TPU v7x, 32 devices: a whole 2x2x4 slice. The times are simulated.
32 devices in a mesh: grp: 8 (over z, core), cls: 4 (over y, x).
Axes of the slice: x: 2, y: 2, z: 4, core: 2. Of those that a mesh axis runs over, the one named last changes fastest.
Arguments:
- particles: bfloat16 [512, 16384], P(('grp', 'cls')), may hold values from -6 to 6
- candidates: int32 [512, 8], P(('grp', 'cls')), may hold values from 0 to 207, all different within a row; in each aligned block of 16 rows (0 to 15, 16 to 31, ...) at most 2 rows name the same one
- group_ids: int32 [512], P(('grp', 'cls')), may hold values from 0 to 63
- ctf_ids: int32 [512], P(('grp', 'cls')), may hold values from 0 to 255
- ctf_table: float32 [256, 64], replicated, may hold values from -1 to 1
- noise_prec: float32 [64, 64], replicated, may hold values from 0.02 to 0.2
- references: bfloat16 [208, 16384], P('cls'), may hold values from -3 to 3
- log_prior: bfloat16 [208], P('cls'), may hold values from -4 to 4
- reg: float32 [64], replicated, may hold values from 0.1 to 1
Outputs:
- averages: float32 [208, 16384], P('cls')
- class_share: float32 [208], P('cls')
- log_mass: float32 [512], P(('grp', 'cls'))
Inputs may be any that keep to these rules, and one draw needn't show every extreme that they name: `candidates`: the 8 classes of a particle are distinct. Among the pairs of the rows of one device no class is named more than 2 times, a bound that some block reaches.
All inputs are finite; a program needn't handle non-finite values.
Results may differ from a plain program's by a relative error of at most 0.0046.
Values may be sent and summed in bfloat16 or wider, within the bound.
No kernel may reach another device: no remote copies, remote signals or barrier semaphores. Data moves between devices by JAX's collectives and lax.ppermute only.
A program may use at most 128 MiB of HBM per device.

v0:
```python
import math

import jax
import jax.numpy as jnp
from jax import lax
from jax.sharding import PartitionSpec as P

SHELLS = 64
FREQ = 128
FEAT = 16384
ROTS = 64
K = 208
CAND = 8
MOST = 2


def phase_tables():
    turns = jnp.arange(ROTS, dtype=jnp.int32)[:, None]
    orders = jnp.arange(FREQ, dtype=jnp.int32)[None, :]
    angles = (turns * orders % ROTS).astype(jnp.float32) * (2.0 * math.pi / ROTS)
    return (jnp.cos(angles), jnp.sin(angles))


def shell_terms(particles, group_ids, ctf_ids, ctf_table, noise_prec):
    upper_limit = lax.Precision.HIGHEST
    group_hot = (
        group_ids[:, None] == jnp.arange(noise_prec.shape[0], dtype=jnp.int32)[None, :]
    ).astype(jnp.float32)
    table_hot = (
        ctf_ids[:, None] == jnp.arange(ctf_table.shape[0], dtype=jnp.int32)[None, :]
    ).astype(jnp.float32)
    precision_rows = jnp.dot(group_hot, noise_prec, precision=upper_limit)
    ctf_rows = jnp.dot(table_hot, ctf_table, precision=upper_limit)
    count = particles.shape[0]
    shell_weight = precision_rows * ctf_rows
    weighted = (
        particles.astype(jnp.float32).reshape(count, 2, SHELLS, FREQ)
        * shell_weight[:, None, :, None]
    ).reshape(count, FEAT)
    return (
        weighted.astype(jnp.bfloat16),
        (precision_rows * ctf_rows * ctf_rows).astype(jnp.bfloat16),
    )


def swapped_parts(images):
    count = images.shape[0]
    particle_pieces = images.reshape(count, 2, SHELLS, FREQ)
    return (particle_pieces, jnp.stack([particle_pieces[:, 1], -particle_pieces[:, 0]], axis=1))


def rotation_scores(inner_loop, outer_loop, cos_tab, sin_tab):
    upper_limit = lax.Precision.HIGHEST
    return jnp.einsum("...f,jf->...j", inner_loop, cos_tab, precision=upper_limit) + jnp.einsum(
        "...f,jf->...j", outer_loop, sin_tab, precision=upper_limit
    )


def posterior(scores):
    best = jnp.max(scores, axis=1, keepdims=True)
    exponent = jnp.exp(scores - best)
    total_mass = jnp.sum(exponent, axis=1, keepdims=True)
    return ((exponent / total_mass).astype(jnp.bfloat16), jnp.log(total_mass[:, 0]))


def phase_sums(weight_wide, cos_tab, sin_tab):
    upper_limit = lax.Precision.HIGHEST
    wcos = jnp.einsum("...j,jf->...f", weight_wide, cos_tab, precision=upper_limit).astype(
        jnp.bfloat16
    )
    wsin = jnp.einsum("...j,jf->...f", weight_wide, sin_tab, precision=upper_limit).astype(
        jnp.bfloat16
    )
    return (wcos, wsin)


def slot_plan(flat_class, first, count):
    pairs = flat_class.shape[0]
    pair_iota = jnp.arange(pairs, dtype=jnp.int32)
    earlier = (flat_class[:, None] == flat_class[None, :]) & (
        pair_iota[None, :] < pair_iota[:, None]
    )
    pair_rank = jnp.sum(earlier.astype(jnp.int32), axis=1)
    slot_of_pair = (flat_class - first) * MOST + pair_rank
    slot_match = slot_of_pair[None, :] == jnp.arange(count * MOST, dtype=jnp.int32)[:, None]
    filled = jnp.any(slot_match, axis=1)
    pair_of_slot = jnp.sum(jnp.where(slot_match, pair_iota[None, :], 0), axis=1)
    return (slot_of_pair, filled, pair_of_slot)


def with_blank(rows):
    return jnp.concatenate([rows, jnp.zeros((1, rows.shape[1]), rows.dtype)], axis=0)


def score_slots(got_rows, got_side, references, log_prior, cos_tab, sin_tab):
    owners = got_rows.shape[0]
    cls_dev = references.shape[0]
    row_blocks = got_rows.reshape(owners, cls_dev, MOST, 2, SHELLS, FREQ)
    particle_pieces, exchanged_rows = swapped_parts(references)
    both_images = jnp.stack([particle_pieces, exchanged_rows], axis=1)
    both_sums = jnp.einsum(
        "scmxrf,cyxrf->scmyf", row_blocks, both_images, preferred_element_type=jnp.float32
    )
    correlation = rotation_scores(both_sums[..., 0, :], both_sums[..., 1, :], cos_tab, sin_tab)
    shell_power = jnp.sum(
        jnp.square(references.astype(jnp.float32)).reshape(cls_dev, 2, SHELLS, FREQ), axis=(1, 3)
    )
    side_wide = got_side.reshape(owners, cls_dev, MOST, SHELLS).astype(jnp.float32)
    penalty = jnp.sum(side_wide * shell_power[None, :, None, :], axis=-1)
    scores = (
        correlation - 0.5 * penalty[..., None] + log_prior.astype(jnp.float32)[None, :, None, None]
    )
    return scores.reshape(owners, cls_dev * MOST, ROTS)


def outgoing_weights(returned, slot_of_pair, filled, pair_of_slot, part_dev):
    owners = returned.shape[0]
    pair_scores = returned.reshape(K * MOST, ROTS)[slot_of_pair].reshape(part_dev, CAND * ROTS)
    weights, log_mass = posterior(pair_scores)
    pair_rows = weights.reshape(part_dev * CAND, ROTS)
    outgoing = jnp.where(filled[:, None], pair_rows[pair_of_slot], jnp.zeros((), jnp.bfloat16))
    return (outgoing.reshape(owners, K * MOST // owners, ROTS), log_mass)


def owner_sums(got_rows, got_side, got_weights, cos_tab, sin_tab):
    owners = got_rows.shape[0]
    cls_dev = got_rows.shape[1] // MOST
    weight_wide = got_weights.reshape(owners, cls_dev, MOST, ROTS).astype(jnp.float32)
    wcos, wsin = phase_sums(weight_wide, cos_tab, sin_tab)
    particle_pieces = got_rows.reshape(owners, cls_dev, MOST, 2, SHELLS, FREQ)
    real_row = jnp.stack([wcos, wsin], axis=-2)
    imag_row = jnp.stack([-wsin, wcos], axis=-2)
    factors = jnp.stack([real_row, imag_row], axis=-3)
    numerator = jnp.einsum(
        "scmxrf,scmxyf->cyrf", particle_pieces, factors, preferred_element_type=jnp.float32
    ).reshape(cls_dev, FEAT)
    side_wide = got_side.reshape(owners, cls_dev, MOST, SHELLS).astype(jnp.float32)
    pair_sums = jnp.sum(weight_wide, axis=-1)
    denominator = jnp.einsum("scm,scmr->cr", pair_sums, side_wide, precision=lax.Precision.HIGHEST)
    class_mass = jnp.sum(pair_sums, axis=(0, 2))
    return (numerator, denominator, class_mass)


def owner_plan(weighted, shell_side, candidates, references, log_prior, cos_tab, sin_tab):
    part_dev = weighted.shape[0]
    cls_dev = references.shape[0]
    owners = lax.axis_size("cls")
    flat_class = candidates.reshape(part_dev * CAND)
    slot_of_pair, filled, pair_of_slot = slot_plan(flat_class, 0, K)
    row_of_slot = jnp.where(filled, pair_of_slot // CAND, part_dev)
    send_rows = with_blank(weighted)[row_of_slot].reshape(owners, cls_dev * MOST, FEAT)
    send_side = with_blank(shell_side)[row_of_slot].reshape(owners, cls_dev * MOST, SHELLS)
    got_rows, got_side = (
        lax.all_to_all(send_rows, "cls", split_axis=0, concat_axis=0, tiled=True),
        lax.all_to_all(send_side, "cls", split_axis=0, concat_axis=0, tiled=True),
    )
    scores = score_slots(got_rows, got_side, references, log_prior, cos_tab, sin_tab)
    returned = lax.all_to_all(scores, "cls", split_axis=0, concat_axis=0, tiled=True)
    outgoing, log_mass = outgoing_weights(returned, slot_of_pair, filled, pair_of_slot, part_dev)
    got_weights = lax.all_to_all(outgoing, "cls", split_axis=0, concat_axis=0, tiled=True)
    numerator, denominator, class_mass = owner_sums(
        got_rows, got_side, got_weights, cos_tab, sin_tab
    )
    return (numerator, denominator, class_mass, log_mass)


def divide(numerator, denominator, reg):
    width = numerator.shape[1]
    columns = jnp.arange(width, dtype=jnp.int32)
    shell_index = columns // FREQ % SHELLS
    divisor = jnp.take(denominator, shell_index, axis=1) + jnp.take(reg, shell_index)[None, :]
    return numerator / divisor


def per_device(
    particles, candidates, group_ids, ctf_ids, ctf_table, noise_prec, references, log_prior, reg
):
    cos_tab, sin_tab = phase_tables()
    weighted, shell_side = shell_terms(particles, group_ids, ctf_ids, ctf_table, noise_prec)
    numerator, denominator, class_mass, log_mass = owner_plan(
        weighted, shell_side, candidates, references, log_prior, cos_tab, sin_tab
    )
    numerator, denominator, class_mass = lax.psum((numerator, denominator, class_mass), "grp")
    averages = divide(numerator, denominator, reg)
    particle_total = particles.shape[0] * lax.axis_size("grp") * lax.axis_size("cls")
    class_share = class_mass * (K / particle_total)
    return (averages, class_share, log_mass)


def solution(mesh):
    return jax.shard_map(
        per_device,
        mesh=mesh,
        in_specs=(
            P(("grp", "cls"), None),
            P(("grp", "cls"), None),
            P(("grp", "cls")),
            P(("grp", "cls")),
            P(),
            P(),
            P("cls", None),
            P("cls"),
            P(),
        ),
        out_specs=(P("cls", None), P("cls"), P(("grp", "cls"))),
        check_vma=False,
    )
```

profile of v0, /device:TPU:0, one launch (start us, length us, event | category | flops | bytes accessed | tf_op | source)
XLA Modules:
  0.0 688.1 jit_solution(4216927527309744453)
XLA Ops:
  7.2 0.8 copy.86
  8.8 0.8 fusion.33
  9.6 1.0 multiply_convert_fusion
  10.6 1.5 gather_fusion.1
  12.8 5.2 all-to-all-start.1
  18.2 1.6 fusion.5
  19.9 13.5 %gather_fusion = bf16[416,16384]{1,0:T(8,128)(2,1)} fusion(bf16[17,16384]{1,0:T(8,128)(2,1)S(1)} %concatenate.6, s32[1024]{0:T(1024)S(1)} %pad_clamp_fusion.2), kind=kCustom, calls=%fused_computation | custom fusion | bytes 27264640 | tf_op jit(solution)/shard_map/gather | solution.py:151
  33.4 6.8 all-to-all-start
  41.2 11.2 %copy.88 = bf16[52,1,2,64,128]{3,1,2,4,0:T(2,128)(2,1)} copy(bf16[52,1,2,64,128]{4,3,2,0,1:T(8,128)(2,1)S(1)} %maximum_bitcast_fusion.2) | data formatting | bytes 3407872 | tf_op jit(solution)/shard_map/stack | solution.py:100
  52.5 11.3 %copy.87 = bf16[52,1,2,64,128]{3,1,2,4,0:T(2,128)(2,1)} copy(bf16[52,1,2,64,128]{4,3,2,0,1:T(8,128)(2,1)S(1)} %bitcast.174) | data formatting | bytes 3407872 | tf_op jit(solution)/shard_map/stack;reshape | solution.py:100
  63.8 1.7 convert_multiply_fusion
  69.7 119.0 %all-to-all-done = bf16[4,104,16384]{2,1,0:T(8,128)(2,1)} async-done(((bf16[4,104,16384]{2,1,0:T(8,128)(2,1)}), bf16[4,104,16384]{2,1,0:T(8,128)(2,1)}, u32[]{:S(2)}, u32[]{:S(2)}) %all-to-all-start) | async-done | bytes 13631520 | tf_op jit(solution)/shard_map/all_to_all | solution.py:154
  188.7 10.8 %copy.135 = bf16[52,8,128,128]{3,2,1,0:T(8,128)(2,1)} copy(bf16[52,8,128,128]{3,1,2,0:T(8,128)(2,1)} %bitcast.125) | data formatting | bytes 27262976
  199.5 41.8 %copy.89 = bf16[4,52,2,2,64,128]{4,0,3,2,5,1:T(4,128)(2,1)} copy(bf16[4,52,2,2,64,128]{5,4,3,2,1,0:T(8,128)(2,1)} %bitcast.168) | data formatting | bytes 27262976 | tf_op jit(solution)/shard_map/reshape | solution.py:98
  241.4 125.9 %convolution_bitcast_fusion = f32[4,52,2,2,128]{0,3,2,4,1:T(2,128)} fusion(bf16[4,52,2,2,64,128]{4,0,3,2,5,1:T(4,128)(2,1)} %copy.89, bf16[52,1,2,64,128]{3,1,2,4,0:T(2,128)(2,1)} %copy.88, bf16[52,1,2,64,128]{3,1,2,4,0:T(2,128)(2,1)} %copy.87), kind=kOutput, calls=%fused_computation.5 | convolution fusion | flops 34078720 | bytes 17465344 | tf_op jit(solution)/shard_map/scmxrf,cyxrf->scmyf/dot_general | solution.py:101
  367.3 17.5 %fusion.54 = (f32[4,52,2,1,128]{0,3,2,4,1:T(1,128)}, f32[4,52,2,1,128]{0,3,2,4,1:T(1,128)}) fusion(f32[4,52,2,2,128]{0,3,2,4,1:T(2,128)} %convolution_bitcast_fusion), kind=kLoop, calls=%fused_computation.123 | loop fusion | bytes 851968 | tf_op jit(solution)/shard_map/slice | solution.py:104
  384.9 6.3 copy.90
  391.7 6.1 copy.91
  399.2 3.3 all-to-all-start.2
  402.5 5.0 all-to-all-done.2
  409.5 1.5 gather_fusion.3
  411.7 3.3 all-to-all-start.3
  415.8 4.0 all-to-all-done.3
  420.8 16.7 %copy.105 = bf16[4,52,2,2,2,128]{0,4,3,2,5,1:T(2,128)(2,1)} copy(bf16[4,52,2,2,2,128]{5,1,2,0,4,3:T(8,128)(2,1)S(1)} %pad_maximum_fusion) | data formatting | bytes 851968 | tf_op jit(solution)/shard_map/stack | solution.py:133
  437.5 37.6 %convolution_bitcast_fusion.1 = f32[52,2,64,128]{2,1,3,0:T(2,128)} fusion(bf16[4,52,2,2,2,128]{0,4,3,2,5,1:T(2,128)(2,1)} %copy.105, bf16[4,52,2,2,64,128]{4,0,3,2,5,1:T(4,128)(2,1)} %copy.89), kind=kOutput, calls=%fused_computation.10 | convolution fusion | flops 27262976 | bytes 17465344 | tf_op jit(solution)/shard_map/scmxrf,scmxyf->cyrf/dot_general | solution.py:134
  475.1 13.4 %copy.126 = f32[52,2,64,128]{0,3,2,1:T(8,128)} copy(f32[52,2,64,128]{2,1,3,0:T(2,128)} %convolution_bitcast_fusion.1) | data formatting | bytes 6815744 | tf_op jit(solution)/shard_map/reshape | solution.py:136
  489.2 40.5 %select_select_fusion = f32[16384]{0:T(1024)S(1)} fusion(s32[16384]{0:T(1024)S(1)} %bitcast.184, f32[]{:T(128)} %bitcast.43, f32[]{:T(128)} %bitcast.44, f32[]{:T(128)} %bitcast.45, f32[]{:T(128)} %bitcast.46, f32[]{:T(128)} %bitcast.47, f32[]{:T(128)} %bitcast.48, f32[]{:T(128)} %bitcast.49, f32[]{:T(128)} %bitcast.50, f32[]{:T(128)} %bitcast.51, ...), kind=kLoop, calls=%fused_computation.56 | loop fusion | flops 2490368 | bytes 131328 | tf_op jit(solution)/shard_map/jit(_take)/select_n | solution.py:171
  531.6 28.9 %all-reduce.2 = (f32[52,64]{0,1:T(8,128)S(1)}, f32[52]{0:T(128)S(1)}) all-reduce(f32[52,64]{0,1:T(8,128)S(1)} %copy.125, f32[52]{0:T(128)S(1)} %reduce_sum.96), channel_id=1, replica_groups=mesh['grp'=8,'cls'=4] {'grp'}, use_global_device_ids=true, to_apply=%region_11.12 | all-reduce | flops 3380 | bytes 27040 | tf_op jit(solution)/shard_map/psum | solution.py:183
  560.5 54.4 %gather_fusion.4 = f32[16384,52]{1,0:T(8,128)} fusion(f32[52,64]{0,1:T(8,128)S(1)} %get-tuple-element.20, s32[16384]{0:T(1024)S(1)} %broadcast_clamp_fusion), kind=kCustom, calls=%fused_computation.4 | custom fusion | bytes 6881280 | tf_op jit(solution)/shard_map/jit(_take)/gather | solution.py:171
  615.4 49.6 %all-reduce.5.cloned.1.call-done = f32[52,16384]{0,1:T(8,128)} async-done(((f32[52,16384]{0,1:T(8,128)}), f32[52,16384]{0,1:T(8,128)}) %all-reduce.5.cloned.1.call-update) | async-done | bytes 3407888 | tf_op jit(solution)/shard_map/psum | solution.py:183
  665.0 9.5 %bitcast_divide_fusion = f32[52,16384]{0,1:T(8,128)} fusion(f32[52,16384]{0,1:T(8,128)} %all-reduce.5.cloned.1.call-done, f32[16384,52]{1,0:T(8,128)} %gather_fusion.4, f32[16384]{0:T(1024)S(1)} %select_select_fusion, pred[16384]{0:T(1024)(128)(4,1)S(1)} %compare_and_fusion), kind=kLoop, calls=%fused_computation.6 | loop fusion | flops 2555904 | bytes 10305536 | tf_op jit(solution)/shard_map/div | solution.py:172
  674.5 6.7 copy.112
  (91 shorter events, 16.2 us)
Async XLA Ops:
  7.2 1.6 copy-start
  8.2 0.5 copy-start.6
  12.8 20.5 %all-to-all-start.1 = ((bf16[4,104,64]{1,2,0:T(8,128)(2,1)}), bf16[4,104,64]{1,2,0:T(8,128)(2,1)S(1)}, u32[]{:S(2)}, u32[]{:S(2)}) async-start(bf16[4,104,64]{1,2,0:T(8,128)(2,1)} %copy.92), calls=%async_computation.1 | async-start | bytes 131072 | tf_op jit(solution)/shard_map/all_to_all | solution.py:155
  33.4 6.9 %copy-start.2 = (bf16[52,16384]{1,0:T(8,128)(2,1)S(1)}, bf16[52,16384]{1,0:T(8,128)(2,1)}, u32[]{:S(2)}) copy-start(bf16[52,16384]{1,0:T(8,128)(2,1)} %param.15) | copy-start | bytes 5111812
  33.4 155.4 %all-to-all-start = ((bf16[4,104,16384]{2,1,0:T(8,128)(2,1)}), bf16[4,104,16384]{2,1,0:T(8,128)(2,1)}, u32[]{:S(2)}, u32[]{:S(2)}) async-start(bf16[4,104,16384]{2,1,0:T(8,128)(2,1)} %bitcast.169), calls=%async_computation | async-start | bytes 27262976 | tf_op jit(solution)/shard_map/all_to_all | solution.py:154
  41.2 22.5 %copy-start.5 = (bf16[52]{0:T(256)(128)(2,1)S(1)}, bf16[52]{0:T(256)(128)(2,1)}, u32[]{:S(2)}) copy-start(bf16[52]{0:T(256)(128)(2,1)} %param.16) | copy-start | bytes 316
  65.5 1.5 copy-start.4
  65.5 2.4 copy-start.3
  399.2 8.3 %all-to-all-start.2 = ((f32[4,104,64]{1,2,0:T(8,128)}), f32[4,104,64]{1,2,0:T(8,128)S(1)}, u32[]{:S(2)}, u32[]{:S(2)}) async-start(f32[4,104,64]{1,2,0:T(8,128)} %copy.98), calls=%async_computation.2 | async-start | bytes 262144 | tf_op jit(solution)/shard_map/all_to_all | solution.py:158
  411.7 8.1 %all-to-all-start.3 = ((bf16[4,104,64]{1,2,0:T(8,128)(2,1)}), bf16[4,104,64]{1,2,0:T(8,128)(2,1)S(1)}, u32[]{:S(2)}, u32[]{:S(2)}) async-start(bf16[4,104,64]{1,2,0:T(8,128)(2,1)} %broadcast_select_fusion), calls=%async_computation.3 | async-start | bytes 131072 | tf_op jit(solution)/shard_map/all_to_all | solution.py:160
  415.0 250.0 %all-reduce.5.cloned.1.call-start = ((), (), s32[]{:S(2)}) async-start(), calls=%async_computation.4 | async-start | bytes 16777216 | tf_op jit(solution)/shard_map/psum | solution.py:183
  665.0 16.3 %copy-start.1 = (f32[256,64]{0,1:T(8,128)S(1)}, f32[256,64]{0,1:T(8,128)}, u32[]{:S(2)}) copy-start(f32[256,64]{0,1:T(8,128)} %param.13) | copy-start | bytes 196612
Sparse Core Ops, SparseCore 0:
  488.7 176.3 all-reduce.4
where the time goes:
time: 691 us; the launch traced here: 688 us
  local copies, waits for them, and re-layouts  223 us (32%)
  waiting for transfers between devices  178 us (26%)
  matrix products  167 us (24%)
  other arithmetic  57.9 us (8%)
  blocking collectives  28.9 us (4%)
  starting transfers between devices  18.6 us (3%)
  between operations  14.5 us (2%)
    dot_general x1, matrix products, score_slots(): jnp.einsum('scmxrf,cyxrf->scmyf', row_blocks, both_images, preferred_elem...  126 us
    all_to_all x1, waiting for transfers between devices, owner_plan(): lax.all_to_all(send_rows, 'cls', split_axis=0, concat_axis=0, tiled=True)  119 us
    gather x1, local copies, waits for them, and re-layouts, divide(): jnp.take(denominator, shell_index, axis=1)  54.4 us
    psum x1, waiting for transfers between devices, per_device(): lax.psum((numerator, denominator, class_mass), 'grp')  49.6 us
    reshape x1, local copies, waits for them, and re-layouts, score_slots(): row_blocks = got_rows.reshape(owners, cls_dev, MOST, 2, SHELLS, FREQ)  41.8 us
    select_n x1, other arithmetic, divide(): jnp.take(reg, shell_index)[None, :]  40.5 us
    dot_general x1, matrix products, owner_sums(): jnp.einsum('scmxrf,scmxyf->cyrf', particle_pieces, factors, preferred_ele...  37.6 us
    psum x1, blocking collectives, per_device(): lax.psum((numerator, denominator, class_mass), 'grp')  28.9 us
  transfers between devices with their start and end apart: 5, of which 4 were waited for; matrix products, arithmetic and copies ran while one was open for 21% of the time, Pallas kernels for 0%

commit v1 on v0

v1 whole, which is shorter than its diff:
```python
import functools
import math

import jax
import jax.numpy as jnp
import numpy as np
from jax import lax
from jax.experimental import pallas as pl
from jax.experimental.pallas import tpu as pltpu
from jax.sharding import PartitionSpec as P

SHELLS = 64
FREQ = 128
FEAT = 16384
ROTS = 64
K = 208
CAND = 8
IMG = 2 * SHELLS
UNROLL = 4
LOW = -1e30
HIGH = lax.Precision.HIGHEST
VMEM = pltpu.VMEM
SMEM = pltpu.SMEM


def tables():
    turns = np.arange(ROTS)[:, None]
    orders = np.arange(FREQ)[None, :]
    angles = ((turns * orders) % ROTS).astype(np.float32) * np.float32(2.0 * math.pi / ROTS)
    cos_tab = np.cos(angles).astype(np.float32)
    sin_tab = np.sin(angles).astype(np.float32)
    last = np.zeros((FREQ, ROTS), np.float32)
    last[:SHELLS] = -0.5
    last[SHELLS] = 1.0
    scoring = np.concatenate([cos_tab.T, sin_tab.T, last], axis=0)
    phases = np.concatenate([cos_tab, sin_tab], axis=1)
    return scoring, phases


def lanes_of(shape):
    return lax.broadcasted_iota(jnp.int32, shape, len(shape) - 1)


def prep_kernel(
    ids_s, ids_v, ctf, prec, refs, prior, first_s, rf_out, sw_out, side_out, pow_out, cls_out,
    rows_out, locs_out, counts_out, spread,
):
    count = ids_v.shape[0]
    cls_dev = refs.shape[0]
    pad = spread.shape[0] // IMG
    rows = count * CAND
    blocks = counts_out.shape[0]
    per = count // blocks
    first = first_s[0]
    slots = rows_out.shape[0] // blocks

    def block_list(b, _):
        def one(i, n):
            for t in range(CAND):
                local = ids_s[b * per + i, t] - first
                good = jnp.logical_and(local >= 0, local < cls_dev)
                rows_out[b * slots + n] = (b * per + i) * CAND + t
                locs_out[b * slots + n] = local
                n = n + good.astype(jnp.int32)
            return n

        n = lax.fori_loop(0, per, one, jnp.int32(0))
        for extra in range(UNROLL):
            rows_out[b * slots + n + extra] = rows
            locs_out[b * slots + n + extra] = 0
        counts_out[b] = (n + UNROLL - 1) // UNROLL
        return 0

    lax.fori_loop(0, blocks, block_list, 0)

    ids = ids_v[...]
    groups = (ids[:, CAND : CAND + 1] == lanes_of((count, prec.shape[0]))).astype(jnp.float32)
    entries = (ids[:, CAND + 1 : CAND + 2] == lanes_of((count, ctf.shape[0]))).astype(jnp.float32)
    prec_rows = jnp.dot(groups, prec[...], precision=HIGH, preferred_element_type=jnp.float32)
    ctf_rows = jnp.dot(entries, ctf[...], precision=HIGH, preferred_element_type=jnp.float32)
    weight = prec_rows * ctf_rows
    sw_out[...] = weight
    side = (weight * ctf_rows).astype(jnp.bfloat16).astype(jnp.float32)
    side_out[:, :SHELLS] = side
    side_out[:, SHELLS:] = (lanes_of((count, SHELLS)) == 0).astype(jnp.float32)

    cand = ids[:, :CAND].astype(jnp.float32)
    wide = jnp.broadcast_to(cand[:, None, :], (count, CAND, CAND)).reshape(rows, CAND)
    own = lax.broadcasted_iota(jnp.int32, (rows, CAND), 0) % CAND == lanes_of((rows, CAND))
    column = jnp.sum(jnp.where(own, wide, 0.0), axis=1, keepdims=True) - first.astype(jnp.float32)
    cls_out[...] = jnp.broadcast_to(column, (rows, FREQ))

    def shell(r, power):
        parts = []
        for x in range(2):
            piece = refs[:, pl.ds(pl.multiple_of((x * SHELLS + r) * FREQ, FREQ), FREQ)].astype(
                jnp.float32
            )
            spread[pl.ds(pl.multiple_of((x * SHELLS + r) * pad, 8), cls_dev), :] = piece
            parts.append(piece * piece)
        total = jnp.sum(parts[0] + parts[1], axis=1, keepdims=True)
        return jnp.where(lanes_of((cls_dev, FREQ)) == r, total, power)

    power = lax.fori_loop(0, SHELLS, shell, jnp.zeros((cls_dev, FREQ), jnp.float32))
    pow_out[...] = jnp.where(
        lanes_of((cls_dev, FREQ)) == SHELLS, prior[...].astype(jnp.float32), power
    )

    def image(k, _):
        rf_out[k] = spread[pl.ds(k, IMG, stride=pad), :]
        return 0

    lax.fori_loop(0, cls_dev, image, 0)


def score_kernel(
    blocks, rows_s, locs_s, counts_s, *refs,
):
    pieces = refs[:blocks]
    sw, side, power, rf, cls_f, scoring, w_out, scores_out, stats_out, spread, w32, ex = refs[blocks:]
    per = pieces[0].shape[0]
    count = per * blocks
    rows = count * CAND
    cls_dev = rf.shape[0]
    slots = rows_s.shape[0] // blocks

    for b in range(blocks):
        weight = sw[b * per : (b + 1) * per, :]
        for r in range(SHELLS):
            factor = weight[:, r : r + 1]
            for x in range(2):
                at = x * SHELLS + r
                piece = pieces[b][:, at * FREQ : (at + 1) * FREQ].astype(jnp.float32) * factor
                spread[at * per : (at + 1) * per, :] = piece.astype(jnp.bfloat16).astype(jnp.float32)

        def image(i, _):
            whole = spread[pl.ds(i, IMG, stride=per), :]
            w32[b * per + i] = whole
            w_out[b * per + i] = whole.astype(jnp.bfloat16)
            return 0

        lax.fori_loop(0, per, image, 0)

        def pairs(step, _):
            for u in range(UNROLL):
                row = rows_s[b * slots + step * UNROLL + u]
                k = locs_s[b * slots + step * UNROLL + u]
                i = jnp.minimum(row // CAND, count - 1)
                w_re, w_im = w32[i, :SHELLS], w32[i, SHELLS:]
                a_re, a_im = rf[k, :SHELLS], rf[k, SHELLS:]
                inner = jnp.sum(w_re * a_re + w_im * a_im, axis=0, keepdims=True)
                outer = jnp.sum(w_re * a_im - w_im * a_re, axis=0, keepdims=True)
                ex[0, pl.ds(row, 1), :] = inner
                ex[1, pl.ds(row, 1), :] = outer
                ex[2, pl.ds(row, 1), :] = side[pl.ds(i, 1), :] * power[pl.ds(k, 1), :]
            return 0

        lax.fori_loop(0, counts_s[b], pairs, 0)

    local = cls_f[:, :ROTS]
    good = jnp.logical_and(local >= 0, local < cls_dev)
    table = scoring[...]
    values = jnp.zeros((rows, ROTS), jnp.float32)
    for part in range(3):
        values = values + jnp.dot(
            jnp.where(good[:, :1], ex[part, :rows, :], 0.0),
            table[part * FREQ : (part + 1) * FREQ],
            precision=HIGH,
            preferred_element_type=jnp.float32,
        )
    scores = jnp.where(good, values, LOW)
    scores_out[...] = scores
    top = jnp.broadcast_to(jnp.max(scores, axis=1, keepdims=True), (rows, ROTS))
    best = jnp.max(top.reshape(count, CAND, ROTS), axis=1)
    best_rows = jnp.broadcast_to(best[:, None, :], (count, CAND, ROTS)).reshape(rows, ROTS)
    mass = jnp.where(good, jnp.exp(scores - best_rows), 0.0)
    mass = jnp.broadcast_to(jnp.sum(mass, axis=1, keepdims=True), (rows, ROTS))
    total = jnp.sum(mass.reshape(count, CAND, ROTS), axis=1)
    stats_out[:, :ROTS] = best
    stats_out[:, ROTS:] = total


def sum_kernel(
    blocks, slices, rows_s, locs_s, counts_s, *refs,
):
    stats = refs[:blocks]
    scores, w_in, side, cls_f, phases, msg_out, mass_out, wcs, num = refs[blocks:]
    count = w_in.shape[0]
    per = count // blocks
    rows = count * CAND
    cls_dev = num.shape[0]
    slots = rows_s.shape[0] // blocks
    width = SHELLS // slices

    best = stats[0][:, :ROTS]
    for one in stats[1:]:
        best = jnp.maximum(best, one[:, :ROTS])
    total = jnp.zeros((count, ROTS), jnp.float32)
    for one in stats:
        total = total + one[:, ROTS:] * jnp.exp(one[:, :ROTS] - best)
    mass_out[...] = jnp.log(total[:per, :])

    def over_rows(v):
        return jnp.broadcast_to(v[:, None, :], (count, CAND, ROTS)).reshape(rows, ROTS)

    local = cls_f[...]
    good = jnp.logical_and(local >= 0, local < cls_dev)
    weights = jnp.exp(scores[...] - over_rows(best)) / over_rows(total)
    weights = jnp.where(good[:, :ROTS], weights, 0.0).astype(jnp.bfloat16).astype(jnp.float32)
    both = jnp.dot(weights, phases[...], precision=HIGH, preferred_element_type=jnp.float32)
    both = both.astype(jnp.bfloat16).astype(jnp.float32)
    for part in range(2):
        wcs[part, :rows, :] = both[:, part * FREQ : (part + 1) * FREQ]
        wcs[part, rows:, :] = jnp.zeros((8, FREQ), jnp.float32)

    pair_sum = jnp.sum(weights, axis=1, keepdims=True)
    twice = (lanes_of((rows, FREQ)) % ROTS).astype(jnp.float32)
    chosen = jnp.where(twice == local, pair_sum, 0.0)
    by_particle = jnp.sum(chosen.reshape(count, CAND, FREQ), axis=1)
    den = lax.dot_general(
        side[...], by_particle, (((0,), (0,)), ((), ())), precision=HIGH,
        preferred_element_type=jnp.float32,
    )

    num[...] = jnp.zeros_like(num)

    for b in range(blocks):
        def pairs(step, _):
            for u in range(UNROLL):
                row = rows_s[b * slots + step * UNROLL + u]
                k = locs_s[b * slots + step * UNROLL + u]
                i = jnp.minimum(row // CAND, count - 1)
                c = wcs[0, pl.ds(row, 1), :]
                s = wcs[1, pl.ds(row, 1), :]
                w_re = w_in[i, :SHELLS].astype(jnp.float32)
                w_im = w_in[i, SHELLS:].astype(jnp.float32)
                num[k, :SHELLS] += w_re * c - w_im * s
                num[k, SHELLS:] += w_re * s + w_im * c
            return 0

        lax.fori_loop(0, counts_s[b], pairs, 0)

    def pack(k, _):
        for s in range(slices):
            msg_out[s, k, :width] = num[k, s * width : (s + 1) * width].astype(jnp.bfloat16)
            msg_out[s, k, width:] = num[
                k, SHELLS + s * width : SHELLS + (s + 1) * width
            ].astype(jnp.bfloat16)
        return 0

    lax.fori_loop(0, cls_dev, pack, 0)
    left = lanes_of((SHELLS, FREQ)) < ROTS
    high = den[:SHELLS].astype(jnp.bfloat16)
    low = (den[:SHELLS] - high.astype(jnp.float32)).astype(jnp.bfloat16)
    halves = jnp.where(left, high.astype(jnp.float32), low.astype(jnp.float32))
    mass = jnp.broadcast_to(jnp.sum(by_particle, axis=0, keepdims=True), (width, FREQ))
    mass_high = mass.astype(jnp.bfloat16).astype(jnp.float32)
    mass_low = (mass - mass_high).astype(jnp.bfloat16).astype(jnp.float32)
    mass_halves = jnp.where(left[:width], mass_high, mass_low)
    for s in range(slices):
        msg_out[s, cls_dev, :width] = halves[s * width : (s + 1) * width].astype(jnp.bfloat16)
        msg_out[s, cls_dev, width:] = mass_halves.astype(jnp.bfloat16)


def divide_kernel(scale, got, reg, avg_out, share_out):
    sources = got.shape[0]
    cls_dev = avg_out.shape[0]
    width = avg_out.shape[1] // 2
    tile = got[0, cls_dev].astype(jnp.float32)
    for s in range(1, sources):
        tile = tile + got[s, cls_dev].astype(jnp.float32)
    tile = tile + pltpu.roll(tile, ROTS, 1)
    divisor = tile[:width] + reg[...]
    share_out[...] = tile[width : width + 1] * scale
    inverse = 1.0 / divisor
    for k in range(cls_dev):
        total = got[0, k].astype(jnp.float32)
        for s in range(1, sources):
            total = total + got[s, k].astype(jnp.float32)
        factor = jnp.concatenate([inverse[:, k : k + 1]] * 2, axis=0)
        avg_out[k] = (total * factor).astype(jnp.bfloat16)


def spread_kernel(got, out, wide):
    slices, cls_dev, height, _ = got.shape
    width = height // 2
    pad = wide.shape[0] // IMG

    def one(k, _):
        for s in range(slices):
            piece = got[s, k].astype(jnp.float32)
            for x in range(2):
                at = x * SHELLS + s * width
                wide[pl.ds(k + at * pad, width, stride=pad), :] = piece[x * width : (x + 1) * width]
        return 0

    lax.fori_loop(0, cls_dev, one, 0)
    for at in range(IMG):
        out[:, at * FREQ : (at + 1) * FREQ] = wide[at * pad : at * pad + cls_dev, :]


def whole(space):
    return pl.BlockSpec(memory_space=space)


def params(mib):
    return pltpu.CompilerParams(vmem_limit_bytes=mib * 2**20)


def swap(value, axis, distance):
    size = lax.axis_size(axis)
    return lax.ppermute(value, axis, [(i, i ^ distance) for i in range(size)])


def per_device(
    particles, candidates, group_ids, ctf_ids, ctf_table, noise_prec, references, log_prior, reg
):
    n_cls = lax.axis_size("cls")
    n_grp = lax.axis_size("grp")
    per = particles.shape[0]
    cls_dev = references.shape[0]
    count = per * n_cls
    rows = count * CAND
    slots = per * CAND + 2 * UNROLL
    pad = -(-cls_dev // 8) * 8
    width = SHELLS // n_grp
    scoring, phases = (jnp.asarray(t) for t in tables())
    f32 = jnp.float32
    bf16 = jnp.bfloat16
    shape = jax.ShapeDtypeStruct

    ids = jnp.concatenate(
        [
            candidates,
            group_ids[:, None],
            ctf_ids[:, None],
            jnp.zeros((per, CAND - 2), jnp.int32),
        ],
        axis=1,
    )
    pieces = [particles] + [swap(particles, "cls", d) for d in range(1, n_cls)]
    all_ids = jnp.concatenate([ids] + [swap(ids, "cls", d) for d in range(1, n_cls)], axis=0)
    first = (lax.axis_index("cls") * cls_dev).astype(jnp.int32).reshape(1)

    rf, sw, side, power, cls_f, row_list, loc_list, counts = pl.pallas_call(
        prep_kernel,
        out_shape=(
            shape((cls_dev, IMG, FREQ), f32),
            shape((count, SHELLS), f32),
            shape((count, FREQ), f32),
            shape((cls_dev, FREQ), f32),
            shape((rows, FREQ), f32),
            shape((n_cls * slots,), jnp.int32),
            shape((n_cls * slots,), jnp.int32),
            shape((n_cls,), jnp.int32),
        ),
        in_specs=[whole(SMEM)] + [whole(VMEM)] * 5 + [whole(SMEM)],
        out_specs=tuple([whole(VMEM)] * 5 + [whole(SMEM)] * 3),
        scratch_shapes=[VMEM((IMG * pad, FREQ), f32)],
        compiler_params=params(40),
        name="prep",
    )(all_ids, all_ids, ctf_table, noise_prec, references, log_prior[:, None], first)

    weighted, scores, stats = pl.pallas_call(
        functools.partial(score_kernel, n_cls),
        out_shape=(
            shape((count, IMG, FREQ), bf16),
            shape((rows, ROTS), f32),
            shape((count, FREQ), f32),
        ),
        in_specs=[whole(SMEM)] * 3 + [whole(VMEM)] * (n_cls + 6),
        out_specs=tuple([whole(VMEM)] * 3),
        scratch_shapes=[
            VMEM((IMG * per, FREQ), f32),
            VMEM((count, IMG, FREQ), f32),
            VMEM((3, rows + 8, FREQ), f32),
        ],
        compiler_params=params(56),
        name="score",
    )(row_list, loc_list, counts, *pieces, sw, side, power, rf, cls_f, scoring)

    all_stats = [stats]
    for d in range(1, n_cls):
        got = swap(stats, "cls", d).reshape(n_cls, per, FREQ)
        order = [e ^ d for e in range(n_cls)]
        all_stats.append(jnp.concatenate([got[e] for e in order], axis=0))

    message, mass = pl.pallas_call(
        functools.partial(sum_kernel, n_cls, n_grp),
        out_shape=(
            shape((n_grp, cls_dev + 1, 2 * width, FREQ), bf16),
            shape((per, ROTS), f32),
        ),
        in_specs=[whole(SMEM)] * 3 + [whole(VMEM)] * (n_cls + 5),
        out_specs=tuple([whole(VMEM)] * 2),
        scratch_shapes=[
            VMEM((2, rows + 8, FREQ), f32),
            VMEM((cls_dev, IMG, FREQ), f32),
        ],
        compiler_params=params(56),
        name="sum",
    )(row_list, loc_list, counts, *all_stats, scores, weighted, side, cls_f, phases)

    received = lax.all_to_all(message, "grp", split_axis=0, concat_axis=0, tiled=True)
    own_reg = lax.dynamic_slice(reg, (lax.axis_index("grp") * width,), (width,))
    particle_total = per * n_grp * n_cls
    averaged, share = pl.pallas_call(
        functools.partial(divide_kernel, K / particle_total),
        out_shape=(
            shape((cls_dev, 2 * width, FREQ), bf16),
            shape((1, FREQ), f32),
        ),
        in_specs=[whole(VMEM)] * 2,
        out_specs=tuple([whole(VMEM)] * 2),
        compiler_params=params(40),
        name="divide",
    )(received, jnp.broadcast_to(own_reg[:, None], (width, FREQ)))
    gathered = lax.all_gather(averaged, "grp")
    averages = pl.pallas_call(
        spread_kernel,
        out_shape=shape((cls_dev, FEAT), f32),
        in_specs=[whole(VMEM)],
        out_specs=whole(VMEM),
        scratch_shapes=[VMEM((IMG * pad, FREQ), f32)],
        compiler_params=params(40),
        name="spread",
    )(gathered)
    return (averages, share[0, :cls_dev], mass[:, 0])


def solution(mesh):
    return jax.shard_map(
        per_device,
        mesh=mesh,
        in_specs=(
            P(("grp", "cls"), None),
            P(("grp", "cls"), None),
            P(("grp", "cls")),
            P(("grp", "cls")),
            P(),
            P(),
            P("cls", None),
            P("cls"),
            P(),
        ),
        out_specs=(P("cls", None), P("cls"), P(("grp", "cls"))),
        check_vma=False,
    )
```

time: 691 us -> 168 us (0.24)
  local copies, waits for them, and re-layouts: 223 us -> 13.8 us
  matrix products: 167 us -> 0 us
  waiting for transfers between devices: 178 us -> 85.1 us
  other arithmetic: 57.9 us -> 2.75 us
  Pallas kernels: 0 us -> 32.8 us
  blocking collectives: 28.9 us -> 0 us
    dot_general x8 -> x0, matrix products: 167 us -> none  [the longest x1 126 us: score_slots(): jnp.einsum('scmxrf,cyxrf->scmyf', row_blocks, both_images, preferred_elem...]
    all_to_all x4 -> x1, waiting for transfers between devices: 128 us -> 41.2 us  [per_device(): lax.all_to_all(message, 'grp', split_axis=0, concat_axis=0, tiled=True)]
    gather x10 -> x0, local copies, waits for them, and re-layouts: 74.4 us -> none  [the longest x1 54.4 us: divide(): jnp.take(denominator, shell_index, axis=1)]
    reshape x5 -> x0, local copies, waits for them, and re-layouts: 56.8 us -> none  [the longest x1 41.8 us: score_slots(): row_blocks = got_rows.reshape(owners, cls_dev, MOST, 2, SHELLS, FREQ)]
    psum x1 -> x0, waiting for transfers between devices: 49.6 us -> none  [per_device(): lax.psum((numerator, denominator, class_mass), 'grp')]
    select_n x5 -> x0, other arithmetic: 41.9 us -> none  [the longest x1 40.5 us: divide(): jnp.take(reg, shell_index)[None, :]]
    another operation x3 -> x0, local copies, waits for them, and re-layouts: 39.2 us -> none  [the longest x2 22.5 us: score_slots(): both_images = jnp.stack([particle_pieces, exchanged_rows], axis=1)]
    pallas_call x0 -> x5, Pallas kernels: none -> 32.8 us  [the longest x1 11.2 us: per_device(): pl.pallas_call(prep_kernel, out_shape=(shape((cls_dev, IMG, FREQ), f32),...]
  transfers between devices with their start and end apart: 5 -> 11, of which waited for: 4 -> 6; matrix products, arithmetic and copies ran while one was open for 21% -> 3% of each run, Pallas kernels for 0% -> 7%
where the time goes in v1:
time: 168 us; the launch traced here: 167 us
  waiting for transfers between devices  85.1 us (51%)
  Pallas kernels  32.8 us (20%)
  starting transfers between devices  18.6 us (11%)
  between operations  14.1 us (8%)
  local copies, waits for them, and re-layouts  13.8 us (8%)
  other arithmetic  2.75 us (2%)
    all_to_all x1, waiting for transfers between devices, per_device(): lax.all_to_all(message, 'grp', split_axis=0, concat_axis=0, tiled=True)  41.2 us
    all_gather x1, waiting for transfers between devices, per_device(): gathered = lax.all_gather(averaged, 'grp')  22.8 us
    ppermute x9, waiting for transfers between devices, swap(): return lax.ppermute(value, axis, [(i, i ^ distance) for i in range(size)])  21.1 us
    ppermute x9, starting transfers between devices, swap(): return lax.ppermute(value, axis, [(i, i ^ distance) for i in range(size)])  14.2 us
    unnamed x33, local copies, waits for them, and re-layouts  11.7 us
    pallas_call x1, Pallas kernels, per_device(): pl.pallas_call(prep_kernel, out_shape=(shape((cls_dev, IMG, FREQ), f32),...  11.2 us
    pallas_call x1, Pallas kernels, per_device(): pl.pallas_call(functools.partial(score_kernel, n_cls), out_shape=(shape((...  10.8 us
    pallas_call x1, Pallas kernels, per_device(): pl.pallas_call(functools.partial(sum_kernel, n_cls, n_grp), out_shape=(sh...  6.82 us
  transfers between devices with their start and end apart: 11, of which 6 were waited for; matrix products, arithmetic and copies ran while one was open for 3% of the time, Pallas kernels for 7%

profile of v1, /device:TPU:0, one launch (start us, length us, event | category | flops | bytes accessed | tf_op | source)
XLA Modules:
  0.0 167.2 jit_solution(12045882717805570861)
XLA Ops:
  7.2 3.0 %collective-permute-start.3 = (bf16[16,16384]{1,0:T(8,128)(2,1)}, bf16[16,16384]{1,0:T(8,128)(2,1)S(1)}, u32[]{:S(2)}, u32[]{:S(2)}) collective-permute-start(bf16[16,16384]{1,0:T(8,128)(2,1)} %refs_0_.1), channel_id=1, source_target_pairs={{0,1},{1,0},{2,3},{3,2},{4,5},{5,4},{6,7},{7,6},{8,9},{9,8},{10,11... | collective-permute-start | bytes 1572872 | tf_op jit(solution)/shard_map/ppermute | solution.py:312
  10.2 1.5 collective-permute-start.4
  11.7 0.7 pad_add_fusion
  12.4 2.0 %collective-permute-start = (s32[16,16]{0,1:T(8,128)S(1)}, s32[16,16]{0,1:T(8,128)S(1)}, u32[]{:S(2)}, u32[]{:S(2)}) collective-permute-start(s32[16,16]{0,1:T(8,128)S(1)} %pad_add_fusion), channel_id=1, source_target_pairs={{0,1},{1,0},{2,3},{3,2},{4,5},{5,4},{6,7},{7,6},{8,9},{9,8},{10,11... | collective-permute-start | bytes 3080 | tf_op jit(solution)/shard_map/ppermute | solution.py:312
  14.4 1.5 collective-permute-start.1
  15.9 17.8 %collective-permute-done = s32[16,16]{0,1:T(8,128)S(1)} collective-permute-done((s32[16,16]{0,1:T(8,128)S(1)}, s32[16,16]{0,1:T(8,128)S(1)}, u32[]{:S(2)}, u32[]{:S(2)}) %collective-permute-start) | collective-permute-done | bytes 1056 | tf_op jit(solution)/shard_map/ppermute | solution.py:312
  33.8 2.6 %collective-permute-start.2 = (s32[16,16]{0,1:T(8,128)S(1)}, s32[16,16]{0,1:T(8,128)S(1)}, u32[]{:S(2)}, u32[]{:S(2)}) collective-permute-start(s32[16,16]{0,1:T(8,128)S(1)} %pad_add_fusion), channel_id=1, source_target_pairs={{0,3},{1,2},{2,1},{3,0},{4,7},{5,6},{6,5},{7,4},{8,11},{9,10},{10,... | collective-permute-start | bytes 3080 | tf_op jit(solution)/shard_map/ppermute | solution.py:312
  36.4 0.9 copy.26.ctf
  37.3 0.8 copy.27.prior
  38.3 0.8 pad_add_fusion.1
  39.2 1.5 copy-done.1
  40.7 0.8 copy-done.5
  41.5 11.2 %prep.1 = (f32[52,128,128]{2,1,0:T(8,128)S(1)}, f32[64,64]{1,0:T(8,128)S(1)}, f32[64,128]{1,0:T(8,128)S(1)}, f32[52,128]{1,0:T(8,128)S(1)}, f32[512,128]{1,0:T(8...) custom-call(s32[64,16]{1,0:T(8,128)S(1)} %copy.24.ids_s.ids_v, s32[64,16]{1,0:T(8,128)S(1)} %copy.24.ids_s.ids_v, ...), custom_call_target="tpu_custom_call" | custom-call | tf_op jit(solution)/shard_map/prep/pallas_call | solution.py:345
  52.7 1.7 %copy-done = f32[52,128,128]{2,1,0:T(8,128)} copy-done((f32[52,128,128]{2,1,0:T(8,128)}, f32[52,128,128]{2,1,0:T(8,128)S(1)}, u32[]{:S(2)}) %copy-start) | copy-done | bytes 3407896
  54.5 0.7 copy-done.3
  56.4 0.6 copy-done.7
  58.7 0.8 copy-done.11
  59.8 10.8 %score.1 = (bf16[64,128,128]{2,1,0:T(8,128)(2,1)}, f32[512,64]{1,0:T(8,128)}, f32[64,128]{1,0:T(8,128)}) custom-call(s32[544]{0:T(1024)} %copy-done.8, s32[544]{0:T(1024)} %copy-done.9, s32[4]{0:T(128)} %copy-done.10, bf16[16,16384]{1,0:T(8,128)(2,1)} %refs_0_.1, bf16[16,16384]{1,0:T(8,128)(2,1)} %copy-done.11, bf16[16,16384]{1,0:T(8,128)(2,1)} %copy-done.12, ...), custom_call_target="tpu_custom_call" | custom-call | tf_op jit(solution)/shard_map/score/pallas_call | solution.py:364
  70.6 2.4 %collective-permute-start.8 = (f32[64,128]{1,0:T(8,128)}, f32[64,128]{1,0:T(8,128)S(1)}, u32[]{:S(2)}, u32[]{:S(2)}) collective-permute-start(f32[64,128]{1,0:T(8,128)} %get-tuple-element.26.refs_0_), channel_id=1, source_target_pairs={{0,3},{1,2},{2,1},{3,0},{4,7},{5,6},{6,5},{7,4},{8,11},{9,10},{10,... | collective-permute-start | bytes 98312 | tf_op jit(solution)/shard_map/ppermute | solution.py:312
  73.0 1.0 collective-permute-start.6
  74.1 1.5 collective-permute-done.8
  75.6 1.5 collective-permute-done.7
  77.2 0.6 pad_maximum_fusion.2.refs_3_
  77.8 0.6 pad_maximum_fusion
  78.4 6.8 %sum.1 = (bf16[8,53,16,128]{3,2,1,0:T(8,128)(2,1)}, f32[16,64]{1,0:T(8,128)}) custom-call(s32[544]{0:T(1024)} %copy-done.8, s32[544]{0:T(1024)} %copy-done.9, s32[4]{0:T(128)} %copy-done.10, f32[64,128]{1,0:T(8,128)} %get-tuple-element.26.refs_0_, f32[64,128]{1,0:T(8,128)} %get-tuple-element.43.refs_1_, f32[64,128]{1,0:T(8,128)} %get-tuple-element.44.refs_2_, ...), custom_call_target="tpu_custom_call" | custom-call | tf_op jit(solution)/shard_map/sum/pallas_call | solution.py:388
  85.2 4.4 %all-to-all-start = ((bf16[8,53,16,128]{3,2,1,0:T(8,128)(2,1)}), bf16[8,53,16,128]{3,2,1,0:T(8,128)(2,1)S(1)}, u32[]{:S(2)}, u32[]{:S(2)}) async-start(bf16[8,53,16,128]{3,2,1,0:T(8,128)(2,1)} %get-tuple-element.29), calls=%async_computation | async-start | bytes 3473408 | tf_op jit(solution)/shard_map/all_to_all | solution.py:404
  89.7 41.2 %all-to-all-done.got = bf16[8,53,16,128]{3,2,1,0:T(8,128)(2,1)S(1)} async-done(((bf16[8,53,16,128]{3,2,1,0:T(8,128)(2,1)}), bf16[8,53,16,128]{3,2,1,0:T(8,128)(2,1)S(1)}, u32[]{:S(2)}, u32[]{:S(2)}) %all-to-all-start) | async-done | bytes 1736736 | tf_op jit(solution)/shard_map/all_to_all | solution.py:404
  131.0 1.0 divide.1
  132.0 0.6 slice_reduce_fusion
  133.2 22.8 %all-gather.3.cloned.1.call-done = bf16[416,16,128]{2,1,0:T(8,128)(2,1)} async-done(((bf16[52,16,128]{2,1,0:T(8,128)(2,1)}), bf16[416,16,128]{2,1,0:T(8,128)(2,1)}) %all-gather.3.cloned.1.call-update) | async-done | bytes 1703952 | tf_op jit(solution)/shard_map/all_gather | solution.py:418
  156.0 1.5 copy-done.2
  157.4 3.0 %spread.1 = f32[52,16384]{1,0:T(8,128)} custom-call(bf16[8,52,16,128]{3,2,1,0:T(8,128)(2,1)S(1)} %bitcast.7), custom_call_target="tpu_custom_call" | custom-call | tf_op jit(solution)/shard_map/spread/pallas_call | solution.py:419
  (43 shorter events, 4.3 us)
Async XLA Ops:
  7.2 51.5 %collective-permute-start.3 = (bf16[16,16384]{1,0:T(8,128)(2,1)}, bf16[16,16384]{1,0:T(8,128)(2,1)S(1)}, u32[]{:S(2)}, u32[]{:S(2)}) collective-permute-start(bf16[16,16384]{1,0:T(8,128)(2,1)} %refs_0_.1), channel_id=1, source_target_pairs={{0,1},{1,0},{2,3},{3,2},{4,5},{5,4},{6,7},{7,6},{8,9},{9,8},{10,11... | collective-permute-start | bytes 1572872 | tf_op jit(solution)/shard_map/ppermute | solution.py:312
  10.2 48.5 %collective-permute-start.4 = (bf16[16,16384]{1,0:T(8,128)(2,1)}, bf16[16,16384]{1,0:T(8,128)(2,1)S(1)}, u32[]{:S(2)}, u32[]{:S(2)}) collective-permute-start(bf16[16,16384]{1,0:T(8,128)(2,1)} %refs_0_.1), channel_id=1, source_target_pairs={{0,2},{1,3},{2,0},{3,1},{4,6},{5,7},{6,4},{7,5},{8,10},{9,11},{10,... | collective-permute-start | bytes 1572872 | tf_op jit(solution)/shard_map/ppermute | solution.py:312
  11.7 47.0 %collective-permute-start.5 = (bf16[16,16384]{1,0:T(8,128)(2,1)}, bf16[16,16384]{1,0:T(8,128)(2,1)S(1)}, u32[]{:S(2)}, u32[]{:S(2)}) collective-permute-start(bf16[16,16384]{1,0:T(8,128)(2,1)} %refs_0_.1), channel_id=1, source_target_pairs={{0,3},{1,2},{2,1},{3,0},{4,7},{5,6},{6,5},{7,4},{8,11},{9,10},{10,... | collective-permute-start | bytes 1572872 | tf_op jit(solution)/shard_map/ppermute | solution.py:312
  12.4 21.3 %collective-permute-start = (s32[16,16]{0,1:T(8,128)S(1)}, s32[16,16]{0,1:T(8,128)S(1)}, u32[]{:S(2)}, u32[]{:S(2)}) collective-permute-start(s32[16,16]{0,1:T(8,128)S(1)} %pad_add_fusion), channel_id=1, source_target_pairs={{0,1},{1,0},{2,3},{3,2},{4,5},{5,4},{6,7},{7,6},{8,9},{9,8},{10,11... | collective-permute-start | bytes 3080 | tf_op jit(solution)/shard_map/ppermute | solution.py:312
  14.4 23.7 %collective-permute-start.1 = (s32[16,16]{0,1:T(8,128)S(1)}, s32[16,16]{0,1:T(8,128)S(1)}, u32[]{:S(2)}, u32[]{:S(2)}) collective-permute-start(s32[16,16]{0,1:T(8,128)S(1)} %pad_add_fusion), channel_id=1, source_target_pairs={{0,2},{1,3},{2,0},{3,1},{4,6},{5,7},{6,4},{7,5},{8,10},{9,11},{10,... | collective-permute-start | bytes 3080 | tf_op jit(solution)/shard_map/ppermute | solution.py:312
  33.8 4.5 %collective-permute-start.2 = (s32[16,16]{0,1:T(8,128)S(1)}, s32[16,16]{0,1:T(8,128)S(1)}, u32[]{:S(2)}, u32[]{:S(2)}) collective-permute-start(s32[16,16]{0,1:T(8,128)S(1)} %pad_add_fusion), channel_id=1, source_target_pairs={{0,3},{1,2},{2,1},{3,0},{4,7},{5,6},{6,5},{7,4},{8,11},{9,10},{10,... | collective-permute-start | bytes 3080 | tf_op jit(solution)/shard_map/ppermute | solution.py:312
  39.2 1.5 copy-start.1
  40.7 0.8 copy-start.5
  52.7 1.8 %copy-start = (f32[52,128,128]{2,1,0:T(8,128)}, f32[52,128,128]{2,1,0:T(8,128)S(1)}, u32[]{:S(2)}) copy-start(f32[52,128,128]{2,1,0:T(8,128)S(1)} %get-tuple-element.24.refs_7_) | copy-start | bytes 10223620
  54.5 0.7 copy-start.3
  55.2 0.6 copy-start.4
  55.8 0.6 copy-start.6
  56.3 0.6 copy-start.7
  57.0 0.6 copy-start.8
  57.5 0.6 copy-start.9
  58.1 0.5 copy-start.10
  58.6 0.8 copy-start.11
  58.7 1.0 copy-start.12
  58.7 1.1 copy-start.13
  70.6 5.0 %collective-permute-start.8 = (f32[64,128]{1,0:T(8,128)}, f32[64,128]{1,0:T(8,128)S(1)}, u32[]{:S(2)}, u32[]{:S(2)}) collective-permute-start(f32[64,128]{1,0:T(8,128)} %get-tuple-element.26.refs_0_), channel_id=1, source_target_pairs={{0,3},{1,2},{2,1},{3,0},{4,7},{5,6},{6,5},{7,4},{8,11},{9,10},{10,... | collective-permute-start | bytes 98312 | tf_op jit(solution)/shard_map/ppermute | solution.py:312
  73.0 4.1 %collective-permute-start.7 = (f32[64,128]{1,0:T(8,128)}, f32[64,128]{1,0:T(8,128)S(1)}, u32[]{:S(2)}, u32[]{:S(2)}) collective-permute-start(f32[64,128]{1,0:T(8,128)} %get-tuple-element.26.refs_0_), channel_id=1, source_target_pairs={{0,2},{1,3},{2,0},{3,1},{4,6},{5,7},{6,4},{7,5},{8,10},{9,11},{10,... | collective-permute-start | bytes 98312 | tf_op jit(solution)/shard_map/ppermute | solution.py:312
  73.0 4.7 %collective-permute-start.6 = (f32[64,128]{1,0:T(8,128)}, f32[64,128]{1,0:T(8,128)S(1)}, u32[]{:S(2)}, u32[]{:S(2)}) collective-permute-start(f32[64,128]{1,0:T(8,128)} %get-tuple-element.26.refs_0_), channel_id=1, source_target_pairs={{0,1},{1,0},{2,3},{3,2},{4,5},{5,4},{6,7},{7,6},{8,9},{9,8},{10,11... | collective-permute-start | bytes 98312 | tf_op jit(solution)/shard_map/ppermute | solution.py:312
  85.2 4.4 %copy-start.15 = (f32[64]{0:T(128)S(1)}, f32[64]{0:T(128)}, u32[]{:S(2)}) copy-start(f32[64]{0:T(128)} %param.19) | copy-start | bytes 772
  85.2 45.7 %all-to-all-start = ((bf16[8,53,16,128]{3,2,1,0:T(8,128)(2,1)}), bf16[8,53,16,128]{3,2,1,0:T(8,128)(2,1)S(1)}, u32[]{:S(2)}, u32[]{:S(2)}) async-start(bf16[8,53,16,128]{3,2,1,0:T(8,128)(2,1)} %get-tuple-element.29), calls=%async_computation | async-start | bytes 3473408 | tf_op jit(solution)/shard_map/all_to_all | solution.py:404
  89.6 42.4 %copy-start.14 = (f32[16,64]{1,0:T(8,128)S(1)}, f32[16,64]{1,0:T(8,128)}, u32[]{:S(2)}) copy-start(f32[16,64]{1,0:T(8,128)} %get-tuple-element.32) | copy-start | bytes 12292
  89.6 66.4 %all-gather.3.cloned.1.call-start = ((), (), s32[]{:S(2)}) async-start(), calls=%async_computation.1 | async-start | bytes 1916928 | tf_op jit(solution)/shard_map/all_gather | solution.py:418
  156.0 1.5 copy-start.2
Sparse Core Ops, SparseCore 0:
  132.1 23.7 all-gather.2

commit v2 on v0

v2 whole, which is shorter than its diff:
```python
import functools
import math

import jax
import jax.numpy as jnp
import numpy as np
from jax import lax
from jax.experimental import pallas as pl
from jax.experimental.pallas import tpu as pltpu
from jax.sharding import PartitionSpec as P

SHELLS = 64
FREQ = 128
FEAT = 16384
ROTS = 64
K = 208
CAND = 8
IMG = 2 * SHELLS
UNROLL = 4
LOW = -1e30
HIGH = lax.Precision.HIGHEST
VMEM = pltpu.VMEM
SMEM = pltpu.SMEM
HBM = pltpu.HBM
F32 = jnp.float32
BF16 = jnp.bfloat16
SHAPE = jax.ShapeDtypeStruct


def tables():
    turns = np.arange(ROTS)[:, None]
    orders = np.arange(FREQ)[None, :]
    angles = ((turns * orders) % ROTS).astype(np.float32) * np.float32(2.0 * math.pi / ROTS)
    cos_tab = np.cos(angles).astype(np.float32)
    sin_tab = np.sin(angles).astype(np.float32)
    last = np.zeros((FREQ, ROTS), np.float32)
    last[:SHELLS] = -0.5
    last[SHELLS] = 1.0
    scoring = np.concatenate([cos_tab.T, sin_tab.T, last], axis=0)
    phases = np.concatenate([cos_tab, sin_tab], axis=1)
    return scoring, phases


def lanes_of(shape):
    return lax.broadcasted_iota(jnp.int32, shape, len(shape) - 1)


def rounded(v):
    return v.astype(BF16).astype(F32)


def chunks_of(cls_dev):
    cut = cls_dev // 2 // 8 * 8
    return ((cut, cls_dev - cut), (0, cut)) if cut else ((0, cls_dev),)


def weigh_kernel(
    particles_h, cand_h, groups_h, entries_h, ctf_h, prec_h, low_out, high_out,
    particles, cand, groups, entries, ctf, prec, hot_g, hot_e, spread, sem,
):
    copies = [
        pltpu.make_async_copy(a, b, sem.at[n])
        for n, (a, b) in enumerate(
            (
                (groups_h, groups), (entries_h, entries), (ctf_h, ctf), (prec_h, prec),
                (cand_h, cand), (particles_h, particles),
            )
        )
    ]
    for copy in copies:
        copy.start()
    per = particles.shape[0]
    half = per // 2
    for copy in copies[:2]:
        copy.wait()
    for i in range(per):
        hot_g[i : i + 1, :] = (lanes_of((1, hot_g.shape[1])) == groups[i]).astype(F32)
        hot_e[i : i + 1, :] = (lanes_of((1, hot_e.shape[1])) == entries[i]).astype(F32)
    for copy in copies[2:5]:
        copy.wait()
    p = jnp.dot(hot_g[...], prec[...], precision=HIGH, preferred_element_type=F32)
    c = lax.dot_general(
        hot_e[...], ctf[...], (((1,), (1,)), ((), ())), precision=HIGH, preferred_element_type=F32
    )
    eye = (lanes_of((per, per)) == lax.broadcasted_iota(jnp.int32, (per, per), 0)).astype(F32)
    named = lax.dot_general(
        eye, cand[...].astype(F32), (((1,), (1,)), ((), ())), precision=HIGH,
        preferred_element_type=F32,
    )
    factors = p * c
    extra = jnp.concatenate(
        [factors * c, named, jnp.zeros((per, FREQ - SHELLS - CAND), F32)], axis=1
    )
    low_out[half * IMG :, :] = extra.astype(BF16)
    copies[5].wait()
    for r in range(SHELLS):
        factor = jnp.broadcast_to(factors[:, r : r + 1], (per, FREQ))
        for x in range(2):
            at = x * SHELLS + r
            piece = particles[:, at * FREQ : (at + 1) * FREQ].astype(F32) * factor
            spread[at * per : (at + 1) * per, :] = rounded(piece)
    for i in range(per):
        out, at = (low_out, i) if i < half else (high_out, i - half)
        out[at * IMG : (at + 1) * IMG, :] = spread[i : i + IMG * per : per, :].astype(BF16)


def prep_kernel(
    refs_h, scoring_h, phases_h, prior, rf_out, pow_out, scoring_out, phases_out, refs, spread, sem
):
    cls_dev = refs.shape[0]
    pad = spread.shape[0] // IMG
    parts = sem.shape[0] - 2
    step = FEAT // parts
    tables_in = [
        pltpu.make_async_copy(scoring_h, scoring_out, sem.at[parts]),
        pltpu.make_async_copy(phases_h, phases_out, sem.at[parts + 1]),
    ]
    copies = [
        pltpu.make_async_copy(
            refs_h.at[:, pl.ds(n * step, step)], refs.at[:, pl.ds(n * step, step)], sem.at[n]
        )
        for n in range(parts)
    ]
    for copy in copies + tables_in:
        copy.start()
    for copy in copies:
        copy.wait()

    def shell(r, power):
        parts = []
        for x in range(2):
            at = x * SHELLS + r
            piece = refs[:, pl.ds(pl.multiple_of(at * FREQ, FREQ), FREQ)].astype(F32)
            spread[pl.ds(pl.multiple_of(at * pad, 8), cls_dev), :] = piece
            parts.append(piece * piece)
        total = jnp.sum(parts[0] + parts[1], axis=1, keepdims=True)
        return jnp.where(lanes_of((cls_dev, FREQ)) == r, total, power)

    power = lax.fori_loop(0, SHELLS, shell, jnp.zeros((cls_dev, FREQ), F32), unroll=4)
    pow_out[...] = jnp.where(lanes_of((cls_dev, FREQ)) == SHELLS, prior[...], power)

    def image(k, _):
        rf_out[k] = spread[pl.ds(k, IMG, stride=pad), :]
        return 0

    lax.fori_loop(0, cls_dev, image, 0, unroll=4)
    for copy in tables_in:
        copy.wait()


def score_kernel(blocks, chunks, first_s, *refs):
    messages = refs[: 2 * blocks]
    rf, power, scoring = refs[2 * blocks : 2 * blocks + 3]
    scores_out, stats_out, cls_out, rows_out, locs_out, counts_out = refs[2 * blocks + 3 : -6]
    cand_v, cand_s, side, ex, w32, sem = refs[-6:]
    half = messages[1].shape[0] // IMG
    per = 2 * half
    cls_dev = rf.shape[0]
    block_rows = per * CAND
    slots = rows_out.shape[0] // (blocks * len(chunks))
    first = first_s[0]
    table = scoring[...]

    for b in range(blocks):
        extra = messages[2 * b][half * IMG :, :].astype(F32)
        cand_v[b] = extra.astype(jnp.int32)
        lane = lanes_of((per, FREQ))
        side[b] = jnp.where(lane < SHELLS, extra, (lane == SHELLS).astype(F32))
    copies = [pltpu.make_async_copy(cand_v.at[b], cand_s.at[b], sem.at[b]) for b in range(blocks)]
    for copy in copies:
        copy.start()
    for b in range(blocks):

        def widen(i, _):
            at = pl.multiple_of(i * IMG, IMG)
            w32[b * per + i] = messages[2 * b][pl.ds(at, IMG), :].astype(F32)
            w32[b * per + half + i] = messages[2 * b + 1][pl.ds(at, IMG), :].astype(F32)
            return 0

        lax.fori_loop(0, half, widen, 0)
    for copy in copies:
        copy.wait()

    for b in range(blocks):
        base = b * len(chunks) * slots

        def one(i, n):
            for t in range(CAND):
                local = cand_s[b, i, SHELLS + t] - first
                good = jnp.logical_and(local >= 0, local < cls_dev)
                if len(chunks) == 1:
                    place, n = n[0], (n[0] + good.astype(jnp.int32),)
                else:
                    late = local < chunks[0][0]
                    place = jnp.where(late, slots + n[1], n[0])
                    n = (
                        n[0] + jnp.logical_and(good, jnp.logical_not(late)).astype(jnp.int32),
                        n[1] + jnp.logical_and(good, late).astype(jnp.int32),
                    )
                rows_out[base + place] = i * CAND + t
                locs_out[base + place] = local
            return n

        n = lax.fori_loop(0, per, one, (jnp.int32(0),) * len(chunks))
        for c, (start, _) in enumerate(chunks):
            for spare in range(UNROLL):
                rows_out[base + c * slots + n[c] + spare] = block_rows
                locs_out[base + c * slots + n[c] + spare] = start
            steps = (n[c] + UNROLL - 1) // UNROLL
            counts_out[b * len(chunks) + c] = steps

            def pairs(step, _):
                for u in range(UNROLL):
                    row = rows_out[base + c * slots + step * UNROLL + u]
                    k = locs_out[base + c * slots + step * UNROLL + u]
                    i = jnp.minimum(row // CAND, per - 1)
                    w_re, w_im = w32[b * per + i, :SHELLS], w32[b * per + i, SHELLS:]
                    a_re, a_im = rf[k, :SHELLS], rf[k, SHELLS:]
                    inner = jnp.sum(w_re * a_re + w_im * a_im, axis=0, keepdims=True)
                    outer = jnp.sum(w_re * a_im - w_im * a_re, axis=0, keepdims=True)
                    ex[0, pl.ds(row, 1), :] = inner
                    ex[1, pl.ds(row, 1), :] = outer
                    ex[2, pl.ds(row, 1), :] = side[b, pl.ds(i, 1), :] * power[pl.ds(k, 1), :]
                return 0

            lax.fori_loop(0, steps, pairs, 0)

        wide = jnp.broadcast_to(
            messages[2 * b][half * IMG :, :].astype(F32)[:, None, :], (per, CAND, FREQ)
        ).reshape(block_rows, FREQ)
        own = lanes_of((block_rows, FREQ)) == SHELLS + (
            lax.broadcasted_iota(jnp.int32, (block_rows, FREQ), 0) % CAND
        )
        column = jnp.sum(jnp.where(own, wide, 0.0), axis=1, keepdims=True) - first.astype(F32)
        cls_out[b * block_rows : (b + 1) * block_rows, :] = jnp.broadcast_to(
            column, (block_rows, FREQ)
        )
        good = jnp.logical_and(column >= 0, column < cls_dev)
        values = jnp.zeros((block_rows, ROTS), F32)
        for part in range(3):
            values = values + jnp.dot(
                jnp.where(good, ex[part, :block_rows, :], 0.0),
                table[part * FREQ : (part + 1) * FREQ],
                precision=HIGH,
                preferred_element_type=F32,
            )
        scores = jnp.where(good, values, LOW)
        scores_out[b * block_rows : (b + 1) * block_rows, :] = scores
        top = jnp.broadcast_to(jnp.max(scores, axis=1, keepdims=True), (block_rows, ROTS))
        best = jnp.max(top.reshape(per, CAND, ROTS), axis=1)
        best_rows = jnp.broadcast_to(best[:, None, :], (per, CAND, ROTS)).reshape(block_rows, ROTS)
        mass = jnp.where(good, jnp.exp(scores - best_rows), 0.0)
        mass = jnp.broadcast_to(jnp.sum(mass, axis=1, keepdims=True), (block_rows, ROTS))
        total = jnp.sum(mass.reshape(per, CAND, ROTS), axis=1)
        stats_out[b * per : (b + 1) * per, :ROTS] = best
        stats_out[b * per : (b + 1) * per, ROTS:] = total


def add_pairs(calls, chunk, chunks, messages, wcs, num):
    half = messages[1].shape[0] // IMG
    per = 2 * half
    block_rows = per * CAND
    start = chunks[chunk][0]
    groups, width = num.shape[2], num.shape[3]
    num[...] = jnp.zeros_like(num)
    block = 0
    for rows_s, locs_s, counts_s in calls:
        blocks = counts_s.shape[0] // len(chunks)
        slots = rows_s.shape[0] // (blocks * len(chunks))
        for b in range(blocks):
            low, high = messages[2 * block], messages[2 * block + 1]
            base = (b * len(chunks) + chunk) * slots
            row_base = block * (block_rows + 8)

            def pairs(step, _):
                for u in range(UNROLL):
                    row = rows_s[base + step * UNROLL + u]
                    k = locs_s[base + step * UNROLL + u] - start
                    i = jnp.minimum(row // CAND, per - 1)
                    at = pl.multiple_of((i % half) * IMG, IMG)
                    w = jnp.where(i < half, low[pl.ds(at, IMG), :], high[pl.ds(at, IMG), :])
                    w = w.astype(F32)
                    w_re = w[:SHELLS].reshape(groups, width, FREQ)
                    w_im = w[SHELLS:].reshape(groups, width, FREQ)
                    c = wcs[0, pl.ds(row_base + row, 1), :].reshape(1, 1, FREQ)
                    s = wcs[1, pl.ds(row_base + row, 1), :].reshape(1, 1, FREQ)
                    num[k, 0] += w_re * c - w_im * s
                    num[k, 1] += w_re * s + w_im * c
                return 0

            lax.fori_loop(0, counts_s[b * len(chunks) + chunk], pairs, 0)
            block += 1


def pack_sums(grp, num, own_out, sib_out):
    slices = own_out.shape[0]
    z, h = grp // 2, grp % 2

    def one(k, _):
        for d in range(slices):
            for out, core in ((own_out, h), (sib_out, 1 - h)):
                at = (z ^ d) * 2 + core
                out[d, k] = jnp.concatenate([num[k, 0, at], num[k, 1, at]], axis=0).astype(BF16)
        return 0

    lax.fori_loop(0, num.shape[0], one, 0)


def first_sum_kernel(calls, blocks, chunks, grp_s, *refs):
    lists = [refs[3 * c : 3 * c + 3] for c in range(calls)]
    refs = refs[3 * calls :]
    stats = refs[:blocks]
    scores = refs[blocks : blocks + calls]
    classes = refs[blocks + calls : blocks + 2 * calls]
    messages = refs[blocks + 2 * calls : 3 * blocks + 2 * calls]
    phases, own_out, sib_out, mass_out, wcs, num, halves = refs[3 * blocks + 2 * calls :]
    half = messages[1].shape[0] // IMG
    per = 2 * half
    block_rows = per * CAND
    groups, width = num.shape[2], num.shape[3]
    slices = own_out.shape[0]
    grp = grp_s[0]

    den = jnp.zeros((FREQ, FREQ), F32)
    mass = jnp.zeros((1, FREQ), F32)
    block = 0
    for scores_ref, cls_ref in zip(scores, classes):
        for b in range(scores_ref.shape[0] // block_rows):
            ones = [stats[d][(block ^ d) * per : ((block ^ d) + 1) * per, :] for d in range(blocks)]
            best = functools.reduce(jnp.maximum, [one[:, :ROTS] for one in ones])
            total = sum(one[:, ROTS:] * jnp.exp(one[:, :ROTS] - best) for one in ones)
            if block == 0:
                mass_out[...] = jnp.log(total)

            def over_rows(v):
                return jnp.broadcast_to(v[:, None, :], (per, CAND, ROTS)).reshape(block_rows, ROTS)

            at = slice(b * block_rows, (b + 1) * block_rows)
            weights = jnp.exp(scores_ref[at, :] - over_rows(best)) / over_rows(total)
            local = cls_ref[at, :]
            good = jnp.logical_and(local >= 0, local < sum(n for _, n in chunks))[:, :ROTS]
            weights = rounded(jnp.where(good, weights, 0.0))
            both = rounded(
                jnp.dot(weights, phases[...], precision=HIGH, preferred_element_type=F32)
            )
            row = block * (block_rows + 8)
            for part in range(2):
                wcs[part, row : row + block_rows, :] = both[:, part * FREQ : (part + 1) * FREQ]
                wcs[part, row + block_rows : row + block_rows + 8, :] = jnp.zeros((8, FREQ), F32)
            pair_sum = jnp.sum(weights, axis=1, keepdims=True)
            twice = (lanes_of((block_rows, FREQ)) % ROTS).astype(F32)
            chosen = jnp.where(twice == local, pair_sum, 0.0)
            by_particle = jnp.sum(chosen.reshape(per, CAND, FREQ), axis=1)
            side = messages[2 * block][half * IMG :, :].astype(F32)
            den = den + lax.dot_general(
                side, by_particle, (((0,), (0,)), ((), ())), precision=HIGH,
                preferred_element_type=F32,
            )
            mass = mass + jnp.sum(by_particle, axis=0, keepdims=True)
            block += 1

    add_pairs(lists, 0, chunks, messages, wcs, num)
    pack_sums(grp, num, own_out, sib_out)

    def two(v):
        left = lanes_of(v.shape) < ROTS
        return jnp.where(left, rounded(v), rounded(v - rounded(v)))

    halves[...] = two(den[:SHELLS]).reshape(groups, width, FREQ)
    mass_tile = two(jnp.broadcast_to(mass, (width, FREQ)))
    z, h = grp // 2, grp % 2
    for d in range(slices):
        for out, core in ((own_out, h), (sib_out, 1 - h)):
            tile = halves[(z ^ d) * 2 + core]
            out[d, chunks[0][1]] = jnp.concatenate([tile, mass_tile], axis=0).astype(BF16)


def next_sum_kernel(calls, blocks, chunk, chunks, grp_s, *refs):
    lists = [refs[3 * c : 3 * c + 3] for c in range(calls)]
    messages = refs[3 * calls : 3 * calls + 2 * blocks]
    wcs, own_out, sib_out, num = refs[3 * calls + 2 * blocks :]
    add_pairs(lists, chunk, chunks, messages, wcs, num)
    pack_sums(grp_s[0], num, own_out, sib_out)


def add_kernel(tail, own, sib, *outs):
    for d, out in enumerate(outs):
        out[...] = (own[d].astype(F32) + sib[d].astype(F32)).astype(BF16)
        if tail:
            total = own[d, out.shape[0] - 1].astype(F32) + sib[d, out.shape[0] - 1].astype(F32)
            total = total + pltpu.roll(total, ROTS, 1)
            left = lanes_of(total.shape) < ROTS
            high = rounded(total)
            out[out.shape[0] - 1] = jnp.where(left, high, total - high).astype(BF16)


def divide(got, inverse, start, avg_out):
    for k in range(avg_out.shape[0]):
        total = sum(one[k].astype(F32) for one in got)
        column = inverse[:, start + k : start + k + 1]
        factor = jnp.concatenate([column, column], axis=0)
        avg_out[k] = (total * factor).astype(BF16)


def first_divide_kernel(scale, start, *refs):
    got, (reg, avg_out, share_out, inverse_out) = refs[:-4], refs[-4:]
    cut = avg_out.shape[0]
    width = avg_out.shape[1] // 2
    tile = sum(one[cut].astype(F32) for one in got)
    tile = tile + pltpu.roll(tile, ROTS, 1)
    share_out[...] = tile[width : width + 1] * scale
    inverse = 1.0 / (tile[:width] + reg[...])
    inverse_out[...] = inverse
    divide(got, inverse, start, avg_out)


def next_divide_kernel(start, *refs):
    got, (inverse, avg_out) = refs[:-2], refs[-2:]
    divide(got, inverse[...], start, avg_out)


def spread_kernel(slices, start, has_out, grp_s, *refs):
    got = refs[: 2 * slices]
    out, wide, rows, sem = refs[2 * slices + has_out :]
    cut, height, _ = got[0].shape
    width = height // 2
    pad = wide.shape[0] // IMG
    z, h = grp_s[0] // 2, grp_s[0] % 2

    def one(k, _):
        for d in range(slices):
            for array, core in ((got[d], h), (got[slices + d], 1 - h)):
                piece = array[k].astype(F32)
                for x in range(2):
                    at = (x * SHELLS + ((z ^ d) * 2 + core) * width) * pad
                    wide[pl.ds(at + k, width, stride=pad), :] = piece[
                        x * width : (x + 1) * width
                    ]
        return 0

    lax.fori_loop(0, cut, one, 0)
    for at in range(IMG):
        rows[:, at * FREQ : (at + 1) * FREQ] = wide[at * pad : at * pad + cut, :]
    copy = pltpu.make_async_copy(rows, out.at[pl.ds(start, cut), :], sem)
    copy.start()
    copy.wait()


def whole(space):
    return pl.BlockSpec(memory_space=space)


def in_hbm(value):
    return pltpu.with_memory_space_constraint(value, HBM)


def call(kernel, name, ins, outs, scratch, mib, us, args, **more):
    cost = pl.CostEstimate(flops=0, bytes_accessed=int(us * 3.6e6), transcendentals=0)
    return pl.pallas_call(
        kernel,
        out_shape=tuple(s for s, _ in outs),
        in_specs=[whole(s) for s in ins],
        out_specs=tuple(whole(s) for _, s in outs),
        scratch_shapes=scratch,
        compiler_params=pltpu.CompilerParams(vmem_limit_bytes=mib * 2**20),
        name=name,
        cost_estimate=cost,
        **more,
    )(*args)


def swap(value, axis, distance):
    size = lax.axis_size(axis)
    return lax.ppermute(value, axis, [(i, i ^ distance) for i in range(size)])


def after(value, *others):
    return lax.optimization_barrier((value, *others))[0]


def per_device(
    particles, candidates, group_ids, ctf_ids, ctf_table, noise_prec, references, log_prior, reg
):
    n_cls = lax.axis_size("cls")
    n_grp = lax.axis_size("grp")
    per = particles.shape[0]
    half = per // 2
    cls_dev = references.shape[0]
    block_rows = per * CAND
    chunks = chunks_of(cls_dev)
    slots = block_rows + 2 * UNROLL
    pad = -(-cls_dev // 8) * 8
    width = SHELLS // n_grp
    nz = n_grp // 2
    scoring, phases = (jnp.asarray(t) for t in tables())
    first = (lax.axis_index("cls") * cls_dev).astype(jnp.int32).reshape(1)
    grp = lax.axis_index("grp").astype(jnp.int32).reshape(1)

    low, high = call(
        weigh_kernel, "weigh", [HBM] * 6,
        [(SHAPE((half * IMG + per, FREQ), BF16), VMEM), (SHAPE((half * IMG, FREQ), BF16), VMEM)],
        [
            VMEM(particles.shape, BF16),
            VMEM((CAND, per), jnp.int32),
            SMEM((per,), jnp.int32),
            SMEM((per,), jnp.int32),
            VMEM(ctf_table.shape[::-1], F32),
            VMEM(noise_prec.shape, F32),
            VMEM((per, noise_prec.shape[0]), F32),
            VMEM((per, ctf_table.shape[0]), F32),
            VMEM((IMG * per, FREQ), F32),
            pltpu.SemaphoreType.DMA((6,)),
        ],
        8, 3.0,
        tuple(
            in_hbm(a)
            for a in (particles, candidates.T, group_ids, ctf_ids, ctf_table.T, noise_prec)
        ),
    )

    if n_cls == 4:
        low_1, high_2 = swap(low, "cls", 1), swap(high, "cls", 2)
        high_1, low_2 = swap(high, "cls", 1), swap(low, "cls", 2)

    rf, power, scoring, phases = call(
        prep_kernel, "prep", [HBM, HBM, HBM, VMEM],
        [
            (SHAPE((cls_dev, IMG, FREQ), F32), VMEM),
            (SHAPE((cls_dev, FREQ), F32), VMEM),
            (SHAPE(scoring.shape, F32), VMEM),
            (SHAPE(phases.shape, F32), VMEM),
        ],
        [VMEM(references.shape, BF16), VMEM((IMG * pad, FREQ), F32), pltpu.SemaphoreType.DMA((6,))],
        14, 6.0,
        (
            in_hbm(references), in_hbm(scoring), in_hbm(phases),
            jnp.broadcast_to(log_prior.astype(F32)[:, None], (cls_dev, FREQ)),
        ),
    )

    def score(part):
        blocks = len(part)
        flat = [m for pair in part for m in pair]
        return call(
            functools.partial(score_kernel, blocks, chunks), "score",
            [SMEM] + [VMEM] * (2 * blocks + 3),
            [
                (SHAPE((blocks * block_rows, ROTS), F32), VMEM),
                (SHAPE((blocks * per, FREQ), F32), VMEM),
                (SHAPE((blocks * block_rows, FREQ), F32), VMEM),
                (SHAPE((blocks * len(chunks) * slots,), jnp.int32), SMEM),
                (SHAPE((blocks * len(chunks) * slots,), jnp.int32), SMEM),
                (SHAPE((blocks * len(chunks),), jnp.int32), SMEM),
            ],
            [
                VMEM((blocks, per, FREQ), jnp.int32),
                SMEM((blocks, per, FREQ), jnp.int32),
                VMEM((blocks, per, FREQ), F32),
                VMEM((3, block_rows + 8, FREQ), F32),
                VMEM((blocks * per, IMG, FREQ), F32),
                pltpu.SemaphoreType.DMA((blocks,)),
            ],
            12 if n_cls == 4 else 40, 3.0 * blocks, (first, *flat, rf, power, scoring),
        )

    if n_cls == 4:
        scored = [score([(low, high)])]
        low_1, high_2 = after(low_1, scored[0][1]), after(high_2, scored[0][1])
        low_3, high_3 = swap(low_1, "cls", 2), swap(high_2, "cls", 1)
        messages = [(low, high), (low_1, high_1), (low_2, high_2), (low_3, high_3)]
        scored += [score(messages[1:3]), score(messages[3:])]
    else:
        messages = [(low, high)]
        messages += [(swap(low, "cls", d), swap(high, "cls", d)) for d in range(1, n_cls)]
        scored = [score(messages)]
    stats = jnp.concatenate([s[1] for s in scored], axis=0) if len(scored) > 1 else scored[0][1]
    all_stats = [stats] + [swap(stats, "cls", d) for d in range(1, n_cls)]
    lists = [a for s in scored for a in s[3:]]
    flat = [m for pair in messages for m in pair]
    calls = len(scored)
    all_rows = n_cls * (block_rows + 8)
    tile = (2 * width, FREQ)

    def sums_out(rows):
        return [(SHAPE((nz, rows) + tile, BF16), VMEM)] * 2

    own, sib, mass, wcs = call(
        functools.partial(first_sum_kernel, calls, n_cls, chunks), "sum",
        [SMEM] * (1 + 3 * calls) + [VMEM] * (3 * n_cls + 2 * calls + 1),
        sums_out(chunks[0][1] + 1)
        + [(SHAPE((per, ROTS), F32), VMEM), (SHAPE((2, all_rows, FREQ), F32), VMEM)],
        [VMEM((chunks[0][1], 2, n_grp, width, FREQ), F32), VMEM((n_grp, width, FREQ), F32)],
        16 if n_cls == 4 else 32, 3.8,
        (grp, *lists, *all_stats, *(s[0] for s in scored), *(s[2] for s in scored), *flat, phases),
    )
    sums = [(own, sib)]
    for chunk in range(1, len(chunks)):
        sums.append(
            call(
                functools.partial(next_sum_kernel, calls, n_cls, chunk, chunks), "sum",
                [SMEM] * (1 + 3 * calls) + [VMEM] * (2 * n_cls + 1),
                sums_out(chunks[chunk][1]),
                [VMEM((chunks[chunk][1], 2, n_grp, width, FREQ), F32)],
                16, 3.0, (grp, *lists, *flat, wcs),
            )
        )

    own_reg = lax.dynamic_slice(reg, (lax.axis_index("grp") * width,), (width,))
    own_reg = jnp.broadcast_to(own_reg[:, None], (width, FREQ))
    particle_total = per * n_grp * n_cls
    averages, inverse, share = None, None, None
    for chunk, (own, sib) in enumerate(sums):
        rows = own.shape[1]
        start, cut = chunks[chunk]
        other = swap(sib, "grp", 1)
        added = call(
            functools.partial(add_kernel, chunk == 0), "add", [VMEM] * 2,
            [(SHAPE((rows,) + tile, BF16), VMEM)] * nz, [], 8, 0.8, (own, other),
        )
        got = [added[0]] + [swap(added[d], "grp", 2 * d) for d in range(1, nz)]
        averaged_out = (SHAPE((cut,) + tile, BF16), VMEM)
        if chunk == 0:
            averaged, share, inverse = call(
                functools.partial(first_divide_kernel, K / particle_total, start), "divide",
                [VMEM] * (nz + 1),
                [averaged_out, (SHAPE((1, FREQ), F32), VMEM), (SHAPE((width, FREQ), F32), VMEM)],
                [], 8, 1.0, (*got, own_reg),
            )
        else:
            (averaged,) = call(
                functools.partial(next_divide_kernel, start), "divide", [VMEM] * (nz + 1),
                [averaged_out], [], 8, 1.0, (*got, inverse),
            )
        slices = [averaged] + [swap(averaged, "grp", 2 * d) for d in range(1, nz)]
        slices = slices + [swap(s, "grp", 1) for s in slices]
        has_out = chunk > 0
        (averages,) = call(
            functools.partial(spread_kernel, nz, start, has_out), "spread",
            [SMEM] + [VMEM] * (2 * nz) + [HBM] * has_out,
            [(SHAPE((cls_dev, FEAT), F32), HBM)],
            [
                VMEM((IMG * (-(-cut // 8) * 8), FREQ), F32),
                VMEM((cut, FEAT), F32),
                pltpu.SemaphoreType.DMA,
            ],
            10, 2.0, (grp, *slices) + ((averages,) if has_out else ()),
            input_output_aliases={2 * nz + 1: 0} if has_out else {},
        )
    return (averages, share[0, :cls_dev], mass[:, 0])


def solution(mesh):
    return jax.shard_map(
        per_device,
        mesh=mesh,
        in_specs=(
            P(("grp", "cls"), None),
            P(("grp", "cls"), None),
            P(("grp", "cls")),
            P(("grp", "cls")),
            P(),
            P(),
            P("cls", None),
            P("cls"),
            P(),
        ),
        out_specs=(P("cls", None), P("cls"), P(("grp", "cls"))),
        check_vma=False,
    )
```

time: 691 us -> 95.7 us (0.14)
  local copies, waits for them, and re-layouts: 223 us -> 2.02 us
  matrix products: 167 us -> 0 us
  waiting for transfers between devices: 178 us -> 15.4 us
  other arithmetic: 57.9 us -> 0 us
  starting transfers between devices: 18.6 us -> 48.5 us
  blocking collectives: 28.9 us -> 0 us
  Pallas kernels: 0 us -> 28.5 us
  between operations: 14.5 us -> 0.82 us
    dot_general x8 -> x0, matrix products: 167 us -> none  [the longest x1 126 us: score_slots(): jnp.einsum('scmxrf,cyxrf->scmyf', row_blocks, both_images, preferred_elem...]
    all_to_all x4 -> x0, waiting for transfers between devices: 128 us -> none  [the longest x1 119 us: owner_plan(): lax.all_to_all(send_rows, 'cls', split_axis=0, concat_axis=0, tiled=True)]
    gather x10 -> x0, local copies, waits for them, and re-layouts: 74.4 us -> none  [the longest x1 54.4 us: divide(): jnp.take(denominator, shell_index, axis=1)]
    reshape x5 -> x0, local copies, waits for them, and re-layouts: 56.8 us -> none  [the longest x1 41.8 us: score_slots(): row_blocks = got_rows.reshape(owners, cls_dev, MOST, 2, SHELLS, FREQ)]
    psum x1 -> x0, waiting for transfers between devices: 49.6 us -> none  [per_device(): lax.psum((numerator, denominator, class_mass), 'grp')]
    ppermute x0 -> x31, starting transfers between devices: none -> 48.5 us  [swap(): return lax.ppermute(value, axis, [(i, i ^ distance) for i in range(size)])]
    select_n x5 -> x0, other arithmetic: 41.9 us -> none  [the longest x1 40.5 us: divide(): jnp.take(reg, shell_index)[None, :]]
    another operation x3 -> x0, local copies, waits for them, and re-layouts: 39.2 us -> none  [the longest x2 22.5 us: score_slots(): both_images = jnp.stack([particle_pieces, exchanged_rows], axis=1)]
  transfers between devices with their start and end apart: 5 -> 31, of which waited for: 4 -> 9; matrix products, arithmetic and copies ran while one was open for 21% -> 2% of each run, Pallas kernels for 0% -> 19%
where the time goes in v2:
time: 95.7 us; the launch traced here: 95.3 us
  starting transfers between devices  48.5 us (51%)
  Pallas kernels  28.5 us (30%)
  waiting for transfers between devices  15.4 us (16%)
  local copies, waits for them, and re-layouts  2.02 us (2%)
    ppermute x31, starting transfers between devices, swap(): return lax.ppermute(value, axis, [(i, i ^ distance) for i in range(size)])  48.5 us
    pallas_call x13, Pallas kernels, call(): pl.pallas_call(kernel, out_shape=tuple((s for s, _ in outs)), in_specs=[w...  28.5 us
    ppermute x31, waiting for transfers between devices, swap(): return lax.ppermute(value, axis, [(i, i ^ distance) for i in range(size)])  15.4 us
  transfers between devices with their start and end apart: 31, of which 9 were waited for; matrix products, arithmetic and copies ran while one was open for 2% of the time, Pallas kernels for 19%

profile of v2, /device:TPU:0, one launch (start us, length us, event | category | flops | bytes accessed | tf_op | source)
XLA Modules:
  0.0 95.3 jit_solution(16223718539007654636)
XLA Ops:
  0.6 1.7 %weigh.1 = (bf16[1040,128]{1,0:T(8,128)(2,1)S(1)}, bf16[1024,128]{1,0:T(8,128)(2,1)S(1)}) custom-call(bf16[16,16384]{1,0:T(8,128)(2,1)} %particles_h.1, s32[8,16]{1,0:T(8,128)} %bitcast.7, s32[16]{0:T(128)} %groups_h.1, s32[16]{0:T(128)} %entries_h.1, f32[64,256]{1,0:T(8,128)} %bitcast.6, f32[64,64]{1,0:T(8,128)} %prec_h.1), custom_call_target="tpu_custom_call" | custom-call | bytes 10800000 | tf_op jit(solution)/shard_map/weigh/pallas_call | solution.py:459
  2.4 3.0 %collective-permute-start = (bf16[1040,128]{1,0:T(8,128)(2,1)S(1)}, bf16[1040,128]{1,0:T(8,128)(2,1)S(1)}, u32[]{:S(2)}, u32[]{:S(2)}) collective-permute-start(bf16[1040,128]{1,0:T(8,128)(2,1)S(1)} %get-tuple-element.46.refs_0_.refs_19_.refs_9_), channel_id=1, source_target_pairs={{0,1},{1,0},{2,3},{3,2},{4,5},{5,4},{6,7},{7,6},{8,9},{9,8},{10,11... | collective-permute-start | bytes 798728 | tf_op jit(solution)/shard_map/ppermute | solution.py:474
  5.4 1.5 %collective-permute-start.3 = (bf16[1024,128]{1,0:T(8,128)(2,1)S(1)}, bf16[1024,128]{1,0:T(8,128)(2,1)S(1)}, u32[]{:S(2)}, u32[]{:S(2)}) collective-permute-start(bf16[1024,128]{1,0:T(8,128)(2,1)S(1)} %get-tuple-element.47.refs_1_.refs_20_.refs_10_), channel_id=1, source_target_pairs={{0,2},{1,3},{2,0},{3,1},{4,6},{5,7},{6,4},{7,5},{8,10},{9,11},{10,... | collective-permute-start | bytes 786440 | tf_op jit(solution)/shard_map/ppermute | solution.py:474
  7.5 0.7 broadcast_in_dim.4.prior
  8.2 3.9 %prep.1 = (f32[52,128,128]{2,1,0:T(8,128)S(1)}, f32[52,128]{1,0:T(8,128)S(1)}, f32[384,64]{1,0:T(8,128)S(1)}, f32[64,256]{1,0:T(8,128)S(1)}) custom-call(bf16[52,16384]{1,0:T(8,128)(2,1)} %refs_h.1, f32[384,64]{1,0:T(8,128)} %constant.21.clone.scoring_h, f32[64,256]{1,0:T(8,128)} %constant.22.clone.phases_h, f32[52,128]{1,0:T(8,128)S(1)} %broadcast_in_dim.4.prior), custom_call_target="tpu_custom_call" | custom-call | bytes 21600000 | tf_op jit(solution)/shard_map/prep/pallas_call | solution.py:459
  12.1 2.8 %score.3 = (f32[128,64]{1,0:T(8,128)S(1)}, f32[16,128]{1,0:T(8,128)S(1)}, f32[128,128]{1,0:T(8,128)S(1)}, s32[272]{0:T(512)S(1)}, s32[272]{0:T(512)S(1)}, /*index=5*/s32[2]{0:T(128)S(1)}) custom-call(s32[1]{0:T(128)} %bitcast.1.first_s, bf16[1040,128]{1,0:T(8,128)(2,1)S(1)} %get-tuple-element.46.refs_0_.refs_19_.refs_9_, ...), custom_call_target="tpu_custom_call" | custom-call | bytes 10800000 | tf_op jit(solution)/shard_map/score/pallas_call | solution.py:459
  14.9 2.2 %collective-permute-start.4 = (bf16[1040,128]{1,0:T(8,128)(2,1)S(1)}, bf16[1040,128]{1,0:T(8,128)(2,1)S(1)}, u32[]{:S(2)}, u32[]{:S(2)}) collective-permute-start(bf16[1040,128]{1,0:T(8,128)(2,1)S(1)} %collective-permute-done.refs_0_.refs_21_.refs_11_), channel_id=1, source_target_pairs={{0,2},{1,3},{2,0},{3,1},{4,6},{5,7},{6,4},{7,5},{8,10},{9,11},{10,... | collective-permute-start | bytes 798728 | tf_op jit(solution)/shard_map/ppermute | solution.py:474
  17.1 1.5 %collective-permute-start.5 = (bf16[1024,128]{1,0:T(8,128)(2,1)S(1)}, bf16[1024,128]{1,0:T(8,128)(2,1)S(1)}, u32[]{:S(2)}, u32[]{:S(2)}) collective-permute-start(bf16[1024,128]{1,0:T(8,128)(2,1)S(1)} %collective-permute-done.3.refs_3_.refs_24_.refs_14_), channel_id=1, source_target_pairs={{0,1},{1,0},{2,3},{3,2},{4,5},{5,4},{6,7},{7,6},{8,9},{9,8},{10,11... | collective-permute-start | bytes 786440 | tf_op jit(solution)/shard_map/ppermute | solution.py:474
  18.6 1.7 %collective-permute-done.2.refs_2_.refs_23_.refs_13_ = bf16[1040,128]{1,0:T(8,128)(2,1)S(1)} collective-permute-done((bf16[1040,128]{1,0:T(8,128)(2,1)S(1)}, bf16[1040,128]{1,0:T(8,128)(2,1)S(1)}, u32[]{:S(2)}, u32[]{:S(2)}) %collective-permute-start.2) | collective-permute-done | bytes 266272 | tf_op jit(solution)/shard_map/ppermute | solution.py:474
  20.3 5.2 %score.4 = (f32[256,64]{1,0:T(8,128)S(1)}, f32[32,128]{1,0:T(8,128)S(1)}, f32[256,128]{1,0:T(8,128)S(1)}, s32[544]{0:T(1024)S(1)}, s32[544]{0:T(1024)S(1)}, /*index=5*/s32[4]{0:T(128)S(1)}) custom-call(s32[1]{0:T(128)} %bitcast.1.first_s, bf16[1040,128]{1,0:T(8,128)(2,1)S(1)} %collective-permute-done.refs_0_.refs_21_.refs_11_, ...), custom_call_target="tpu_custom_call" | custom-call | bytes 21600000 | tf_op jit(solution)/shard_map/score/pallas_call | solution.py:459
  25.6 2.9 %score.5 = (f32[128,64]{1,0:T(8,128)S(1)}, f32[16,128]{1,0:T(8,128)S(1)}, f32[128,128]{1,0:T(8,128)S(1)}, s32[272]{0:T(512)S(1)}, s32[272]{0:T(512)S(1)}, /*index=5*/s32[2]{0:T(128)S(1)}) custom-call(s32[1]{0:T(128)} %bitcast.1.first_s, bf16[1040,128]{1,0:T(8,128)(2,1)S(1)} %collective-permute-done.4.refs_0_.refs_25_.refs_15_, ...), custom_call_target="tpu_custom_call" | custom-call | bytes 10800000 | tf_op jit(solution)/shard_map/score/pallas_call | solution.py:459
  28.4 1.4 %collective-permute-start.8 = (f32[64,128]{1,0:T(8,128)S(1)}, f32[64,128]{1,0:T(8,128)S(1)}, u32[]{:S(2)}, u32[]{:S(2)}) collective-permute-start(f32[64,128]{1,0:T(8,128)S(1)} %constant_dynamic-update-slice_fusion.refs_9_), channel_id=1, source_target_pairs={{0,3},{1,2},{2,1},{3,0},{4,7},{5,6},{6,5},{7,4},{8,11},{9,10},{10,... | collective-permute-start | bytes 98312 | tf_op jit(solution)/shard_map/ppermute | solution.py:474
  30.0 2.0 %collective-permute-start.6 = (f32[64,128]{1,0:T(8,128)S(1)}, f32[64,128]{1,0:T(8,128)S(1)}, u32[]{:S(2)}, u32[]{:S(2)}) collective-permute-start(f32[64,128]{1,0:T(8,128)S(1)} %constant_dynamic-update-slice_fusion.refs_9_), channel_id=1, source_target_pairs={{0,1},{1,0},{2,3},{3,2},{4,5},{5,4},{6,7},{7,6},{8,9},{9,8},{10,11... | collective-permute-start | bytes 98312 | tf_op jit(solution)/shard_map/ppermute | solution.py:474
  32.0 1.3 %collective-permute-done.8.refs_12_ = f32[64,128]{1,0:T(8,128)S(1)} collective-permute-done((f32[64,128]{1,0:T(8,128)S(1)}, f32[64,128]{1,0:T(8,128)S(1)}, u32[]{:S(2)}, u32[]{:S(2)}) %collective-permute-start.8) | collective-permute-done | bytes 32800 | tf_op jit(solution)/shard_map/ppermute | solution.py:474
  34.0 3.7 %sum.2 = (bf16[4,29,16,128]{3,2,1,0:T(8,128)(2,1)S(1)}, bf16[4,29,16,128]{3,2,1,0:T(8,128)(2,1)S(1)}, f32[16,64]{1,0:T(8,128)S(1)}, f32[2,544,128]{2,1,0:T(8,128)S(1)}) custom-call(s32[1]{0:T(128)} %bitcast.grp_s, s32[272]{0:T(512)S(1)} %get-tuple-element.51.refs_0_, s32[272]{0:T(512)S(1)} %get-tuple-element.52.refs_1_, s32[2]{0:T(128)S(1)} %get-tuple-element.53.refs_2_, ...), custom_call_target="tpu_custom_call" | custom-call | bytes 13680000 | tf_op jit(solution)/shard_map/sum/pallas_call | solution.py:459
  37.8 2.6 %sum.3 = (bf16[4,24,16,128]{3,2,1,0:T(8,128)(2,1)S(1)}, bf16[4,24,16,128]{3,2,1,0:T(8,128)(2,1)S(1)}) custom-call(s32[1]{0:T(128)} %bitcast.grp_s, s32[272]{0:T(512)S(1)} %get-tuple-element.51.refs_0_, s32[272]{0:T(512)S(1)} %get-tuple-element.52.refs_1_, s32[2]{0:T(128)S(1)} %get-tuple-element.53.refs_2_, s32[544]{0:T(1024)S(1)} %get-tuple-element.57.refs_3_, ...), custom_call_target="tpu_custom_call" | custom-call | bytes 10800000 | tf_op jit(solution)/shard_map/sum/pallas_call | solution.py:459
  40.9 1.8 %collective-permute-start.14 = (bf16[29,16,128]{2,1,0:T(8,128)(2,1)S(1)}, bf16[29,16,128]{2,1,0:T(8,128)(2,1)S(1)}, u32[]{:S(2)}, u32[]{:S(2)}) collective-permute-start(bf16[29,16,128]{2,1,0:T(8,128)(2,1)S(1)} %get-tuple-element.82), channel_id=1, source_target_pairs={{0,8},{4,12},{8,0},{12,4},{16,24},{20,28},{24,16},{28,20},{1,9},{5... | collective-permute-start | bytes 356360 | tf_op jit(solution)/shard_map/ppermute | solution.py:474
  42.8 2.7 %collective-permute-start.15 = (bf16[29,16,128]{2,1,0:T(8,128)(2,1)S(1)}, bf16[29,16,128]{2,1,0:T(8,128)(2,1)S(1)}, u32[]{:S(2)}, u32[]{:S(2)}) collective-permute-start(bf16[29,16,128]{2,1,0:T(8,128)(2,1)S(1)} %get-tuple-element.83), channel_id=1, source_target_pairs={{0,16},{4,20},{8,24},{12,28},{16,0},{20,4},{24,8},{28,12},{1,17},{... | collective-permute-start | bytes 356360 | tf_op jit(solution)/shard_map/ppermute | solution.py:474
  45.6 0.9 collective-permute-start.10
  46.4 3.6 %collective-permute-start.11 = (bf16[24,16,128]{2,1,0:T(8,128)(2,1)S(1)}, bf16[24,16,128]{2,1,0:T(8,128)(2,1)S(1)}, u32[]{:S(2)}, u32[]{:S(2)}) collective-permute-start(bf16[24,16,128]{2,1,0:T(8,128)(2,1)S(1)} %get-tuple-element.77), channel_id=1, source_target_pairs={{0,16},{4,20},{8,24},{12,28},{16,0},{20,4},{24,8},{28,12},{1,17},{... | collective-permute-start | bytes 294920 | tf_op jit(solution)/shard_map/ppermute | solution.py:474
  50.0 1.2 %collective-permute-start.12 = (bf16[24,16,128]{2,1,0:T(8,128)(2,1)S(1)}, bf16[24,16,128]{2,1,0:T(8,128)(2,1)S(1)}, u32[]{:S(2)}, u32[]{:S(2)}) collective-permute-start(bf16[24,16,128]{2,1,0:T(8,128)(2,1)S(1)} %get-tuple-element.78), channel_id=1, source_target_pairs={{0,24},{4,28},{8,16},{12,20},{16,8},{20,12},{24,0},{28,4},{1,25},{... | collective-permute-start | bytes 294920 | tf_op jit(solution)/shard_map/ppermute | solution.py:474
  51.3 3.6 %collective-permute-done.15.refs_2_ = bf16[29,16,128]{2,1,0:T(8,128)(2,1)S(1)} collective-permute-done((bf16[29,16,128]{2,1,0:T(8,128)(2,1)S(1)}, bf16[29,16,128]{2,1,0:T(8,128)(2,1)S(1)}, u32[]{:S(2)}, u32[]{:S(2)}) %collective-permute-start.15) | collective-permute-done | bytes 118816 | tf_op jit(solution)/shard_map/ppermute | solution.py:474
  55.2 7.9 %collective-permute-start.26 = (bf16[28,16,128]{2,1,0:T(8,128)(2,1)S(1)}, bf16[28,16,128]{2,1,0:T(8,128)(2,1)S(1)}, u32[]{:S(2)}, u32[]{:S(2)}) collective-permute-start(bf16[28,16,128]{2,1,0:T(8,128)(2,1)S(1)} %get-tuple-element.86.refs_0_), channel_id=1, source_target_pairs={{0,24},{4,28},{8,16},{12,20},{16,8},{20,12},{24,0},{28,4},{1,25},{... | collective-permute-start | bytes 344072 | tf_op jit(solution)/shard_map/ppermute | solution.py:474
  63.1 2.2 %collective-permute-start.25 = (bf16[28,16,128]{2,1,0:T(8,128)(2,1)S(1)}, bf16[28,16,128]{2,1,0:T(8,128)(2,1)S(1)}, u32[]{:S(2)}, u32[]{:S(2)}) collective-permute-start(bf16[28,16,128]{2,1,0:T(8,128)(2,1)S(1)} %get-tuple-element.86.refs_0_), channel_id=1, source_target_pairs={{0,16},{4,20},{8,24},{12,28},{16,0},{20,4},{24,8},{28,12},{1,17},{... | collective-permute-start | bytes 344072 | tf_op jit(solution)/shard_map/ppermute | solution.py:474
  65.2 3.3 %collective-permute-done.11.refs_2_ = bf16[24,16,128]{2,1,0:T(8,128)(2,1)S(1)} collective-permute-done((bf16[24,16,128]{2,1,0:T(8,128)(2,1)S(1)}, bf16[24,16,128]{2,1,0:T(8,128)(2,1)S(1)}, u32[]{:S(2)}, u32[]{:S(2)}) %collective-permute-start.11) | collective-permute-done | bytes 98336 | tf_op jit(solution)/shard_map/ppermute | solution.py:474
  68.7 7.0 %collective-permute-start.18 = (bf16[24,16,128]{2,1,0:T(8,128)(2,1)S(1)}, bf16[24,16,128]{2,1,0:T(8,128)(2,1)S(1)}, u32[]{:S(2)}, u32[]{:S(2)}) collective-permute-start(bf16[24,16,128]{2,1,0:T(8,128)(2,1)S(1)} %divide.3.refs_0_), channel_id=1, source_target_pairs={{0,16},{4,20},{8,24},{12,28},{16,0},{20,4},{24,8},{28,12},{1,17},{... | collective-permute-start | bytes 294920 | tf_op jit(solution)/shard_map/ppermute | solution.py:474
  75.7 6.8 %collective-permute-start.24 = (bf16[28,16,128]{2,1,0:T(8,128)(2,1)S(1)}, bf16[28,16,128]{2,1,0:T(8,128)(2,1)S(1)}, u32[]{:S(2)}, u32[]{:S(2)}) collective-permute-start(bf16[28,16,128]{2,1,0:T(8,128)(2,1)S(1)} %get-tuple-element.86.refs_0_), channel_id=1, source_target_pairs={{0,8},{4,12},{8,0},{12,4},{16,24},{20,28},{24,16},{28,20},{1,9},{5... | collective-permute-start | bytes 344072 | tf_op jit(solution)/shard_map/ppermute | solution.py:474
  83.1 0.6 slice_reduce_fusion
  83.7 4.1 %collective-permute-done.17.refs_1_ = bf16[24,16,128]{2,1,0:T(8,128)(2,1)S(1)} collective-permute-done((bf16[24,16,128]{2,1,0:T(8,128)(2,1)S(1)}, bf16[24,16,128]{2,1,0:T(8,128)(2,1)S(1)}, u32[]{:S(2)}, u32[]{:S(2)}) %collective-permute-start.17) | collective-permute-done | bytes 98336 | tf_op jit(solution)/shard_map/ppermute | solution.py:474
  89.4 0.7 collective-permute-done.28.refs_5_
  90.1 3.3 %spread.2.refs_8_ = f32[52,16384]{1,0:T(8,128)} custom-call(s32[1]{0:T(128)} %bitcast.grp_s, bf16[28,16,128]{2,1,0:T(8,128)(2,1)S(1)} %get-tuple-element.86.refs_0_, bf16[28,16,128]{2,1,0:T(8,128)(2,1)S(1)} %collective-permute-done.24.refs_1_, bf16[28,16,128]{2,1,0:T(8,128)(2,1)S(1)} %collective-permute-done.25.refs_2_, ...), custom_call_target="tpu_custom_call" | custom-call | bytes 7200000 | tf_op jit(solution)/shard_map/spread/pallas_call | solution.py:459
  93.5 1.8 %spread.3 = f32[52,16384]{1,0:T(8,128)} custom-call(s32[1]{0:T(128)} %bitcast.grp_s, bf16[24,16,128]{2,1,0:T(8,128)(2,1)S(1)} %divide.3.refs_0_, bf16[24,16,128]{2,1,0:T(8,128)(2,1)S(1)} %collective-permute-done.17.refs_1_, bf16[24,16,128]{2,1,0:T(8,128)(2,1)S(1)} %collective-permute-done.18.refs_2_, ...), custom_call_target="tpu_custom_call", output_to_operand_aliasing={{}: (9, {})} | custom-call | bytes 7200000 | tf_op jit(solution)/shard_map/spread/pallas_call | solution.py:459
  (53 shorter events, 4.9 us)
Async XLA Ops:
  2.4 12.5 %collective-permute-start = (bf16[1040,128]{1,0:T(8,128)(2,1)S(1)}, bf16[1040,128]{1,0:T(8,128)(2,1)S(1)}, u32[]{:S(2)}, u32[]{:S(2)}) collective-permute-start(bf16[1040,128]{1,0:T(8,128)(2,1)S(1)} %get-tuple-element.46.refs_0_.refs_19_.refs_9_), channel_id=1, source_target_pairs={{0,1},{1,0},{2,3},{3,2},{4,5},{5,4},{6,7},{7,6},{8,9},{9,8},{10,11... | collective-permute-start | bytes 798728 | tf_op jit(solution)/shard_map/ppermute | solution.py:474
  5.4 11.7 %collective-permute-start.3 = (bf16[1024,128]{1,0:T(8,128)(2,1)S(1)}, bf16[1024,128]{1,0:T(8,128)(2,1)S(1)}, u32[]{:S(2)}, u32[]{:S(2)}) collective-permute-start(bf16[1024,128]{1,0:T(8,128)(2,1)S(1)} %get-tuple-element.47.refs_1_.refs_20_.refs_10_), channel_id=1, source_target_pairs={{0,2},{1,3},{2,0},{3,1},{4,6},{5,7},{6,4},{7,5},{8,10},{9,11},{10,... | collective-permute-start | bytes 786440 | tf_op jit(solution)/shard_map/ppermute | solution.py:474
  6.9 13.4 %collective-permute-start.2 = (bf16[1040,128]{1,0:T(8,128)(2,1)S(1)}, bf16[1040,128]{1,0:T(8,128)(2,1)S(1)}, u32[]{:S(2)}, u32[]{:S(2)}) collective-permute-start(bf16[1040,128]{1,0:T(8,128)(2,1)S(1)} %get-tuple-element.46.refs_0_.refs_19_.refs_9_), channel_id=1, source_target_pairs={{0,2},{1,3},{2,0},{3,1},{4,6},{5,7},{6,4},{7,5},{8,10},{9,11},{10,... | collective-permute-start | bytes 798728 | tf_op jit(solution)/shard_map/ppermute | solution.py:474
  7.4 11.2 %collective-permute-start.1 = (bf16[1024,128]{1,0:T(8,128)(2,1)S(1)}, bf16[1024,128]{1,0:T(8,128)(2,1)S(1)}, u32[]{:S(2)}, u32[]{:S(2)}) collective-permute-start(bf16[1024,128]{1,0:T(8,128)(2,1)S(1)} %get-tuple-element.47.refs_1_.refs_20_.refs_10_), channel_id=1, source_target_pairs={{0,1},{1,0},{2,3},{3,2},{4,5},{5,4},{6,7},{7,6},{8,9},{9,8},{10,11... | collective-permute-start | bytes 786440 | tf_op jit(solution)/shard_map/ppermute | solution.py:474
  14.9 10.6 %collective-permute-start.4 = (bf16[1040,128]{1,0:T(8,128)(2,1)S(1)}, bf16[1040,128]{1,0:T(8,128)(2,1)S(1)}, u32[]{:S(2)}, u32[]{:S(2)}) collective-permute-start(bf16[1040,128]{1,0:T(8,128)(2,1)S(1)} %collective-permute-done.refs_0_.refs_21_.refs_11_), channel_id=1, source_target_pairs={{0,2},{1,3},{2,0},{3,1},{4,6},{5,7},{6,4},{7,5},{8,10},{9,11},{10,... | collective-permute-start | bytes 798728 | tf_op jit(solution)/shard_map/ppermute | solution.py:474
  17.1 8.4 %collective-permute-start.5 = (bf16[1024,128]{1,0:T(8,128)(2,1)S(1)}, bf16[1024,128]{1,0:T(8,128)(2,1)S(1)}, u32[]{:S(2)}, u32[]{:S(2)}) collective-permute-start(bf16[1024,128]{1,0:T(8,128)(2,1)S(1)} %collective-permute-done.3.refs_3_.refs_24_.refs_14_), channel_id=1, source_target_pairs={{0,1},{1,0},{2,3},{3,2},{4,5},{5,4},{6,7},{7,6},{8,9},{9,8},{10,11... | collective-permute-start | bytes 786440 | tf_op jit(solution)/shard_map/ppermute | solution.py:474
  28.4 4.9 %collective-permute-start.8 = (f32[64,128]{1,0:T(8,128)S(1)}, f32[64,128]{1,0:T(8,128)S(1)}, u32[]{:S(2)}, u32[]{:S(2)}) collective-permute-start(f32[64,128]{1,0:T(8,128)S(1)} %constant_dynamic-update-slice_fusion.refs_9_), channel_id=1, source_target_pairs={{0,3},{1,2},{2,1},{3,0},{4,7},{5,6},{6,5},{7,4},{8,11},{9,10},{10,... | collective-permute-start | bytes 98312 | tf_op jit(solution)/shard_map/ppermute | solution.py:474
  29.8 3.9 %collective-permute-start.7 = (f32[64,128]{1,0:T(8,128)S(1)}, f32[64,128]{1,0:T(8,128)S(1)}, u32[]{:S(2)}, u32[]{:S(2)}) collective-permute-start(f32[64,128]{1,0:T(8,128)S(1)} %constant_dynamic-update-slice_fusion.refs_9_), channel_id=1, source_target_pairs={{0,2},{1,3},{2,0},{3,1},{4,6},{5,7},{6,4},{7,5},{8,10},{9,11},{10,... | collective-permute-start | bytes 98312 | tf_op jit(solution)/shard_map/ppermute | solution.py:474
  30.0 3.9 %collective-permute-start.6 = (f32[64,128]{1,0:T(8,128)S(1)}, f32[64,128]{1,0:T(8,128)S(1)}, u32[]{:S(2)}, u32[]{:S(2)}) collective-permute-start(f32[64,128]{1,0:T(8,128)S(1)} %constant_dynamic-update-slice_fusion.refs_9_), channel_id=1, source_target_pairs={{0,1},{1,0},{2,3},{3,2},{4,5},{5,4},{6,7},{7,6},{8,9},{9,8},{10,11... | collective-permute-start | bytes 98312 | tf_op jit(solution)/shard_map/ppermute | solution.py:474
  32.0 19.2 %copy-start = (f32[64]{0:T(128)S(1)}, f32[64]{0:T(128)}, u32[]{:S(2)}) copy-start(f32[64]{0:T(128)} %param.19) | copy-start | bytes 772
  37.7 3.1 %collective-permute-start.13 = (bf16[4,29,16,128]{3,2,1,0:T(8,128)(2,1)S(1)}, bf16[4,29,16,128]{3,2,1,0:T(8,128)(2,1)S(1)}, u32[]{:S(2)}, u32[]{:S(2)}) collective-permute-start(bf16[4,29,16,128]{3,2,1,0:T(8,128)(2,1)S(1)} %get-tuple-element.80), channel_id=1, source_target_pairs={{0,4},{4,0},{8,12},{12,8},{16,20},{20,16},{24,28},{28,24},{1,5},{5... | collective-permute-start | bytes 1425416 | tf_op jit(solution)/shard_map/ppermute | solution.py:474
  40.4 5.1 %collective-permute-start.9 = (bf16[4,24,16,128]{3,2,1,0:T(8,128)(2,1)S(1)}, bf16[4,24,16,128]{3,2,1,0:T(8,128)(2,1)S(1)}, u32[]{:S(2)}, u32[]{:S(2)}) collective-permute-start(bf16[4,24,16,128]{3,2,1,0:T(8,128)(2,1)S(1)} %get-tuple-element.74), channel_id=1, source_target_pairs={{0,4},{4,0},{8,12},{12,8},{16,20},{20,16},{24,28},{28,24},{1,5},{5... | collective-permute-start | bytes 1179656 | tf_op jit(solution)/shard_map/ppermute | solution.py:474
  40.9 9.1 %collective-permute-start.14 = (bf16[29,16,128]{2,1,0:T(8,128)(2,1)S(1)}, bf16[29,16,128]{2,1,0:T(8,128)(2,1)S(1)}, u32[]{:S(2)}, u32[]{:S(2)}) collective-permute-start(bf16[29,16,128]{2,1,0:T(8,128)(2,1)S(1)} %get-tuple-element.82), channel_id=1, source_target_pairs={{0,8},{4,12},{8,0},{12,4},{16,24},{20,28},{24,16},{28,20},{1,9},{5... | collective-permute-start | bytes 356360 | tf_op jit(solution)/shard_map/ppermute | solution.py:474
  42.8 12.1 %collective-permute-start.15 = (bf16[29,16,128]{2,1,0:T(8,128)(2,1)S(1)}, bf16[29,16,128]{2,1,0:T(8,128)(2,1)S(1)}, u32[]{:S(2)}, u32[]{:S(2)}) collective-permute-start(bf16[29,16,128]{2,1,0:T(8,128)(2,1)S(1)} %get-tuple-element.83), channel_id=1, source_target_pairs={{0,16},{4,20},{8,24},{12,28},{16,0},{20,4},{24,8},{28,12},{1,17},{... | collective-permute-start | bytes 356360 | tf_op jit(solution)/shard_map/ppermute | solution.py:474
  45.5 9.4 %collective-permute-start.16 = (bf16[29,16,128]{2,1,0:T(8,128)(2,1)S(1)}, bf16[29,16,128]{2,1,0:T(8,128)(2,1)S(1)}, u32[]{:S(2)}, u32[]{:S(2)}) collective-permute-start(bf16[29,16,128]{2,1,0:T(8,128)(2,1)S(1)} %get-tuple-element.84), channel_id=1, source_target_pairs={{0,24},{4,28},{8,16},{12,20},{16,8},{20,12},{24,0},{28,4},{1,25},{... | collective-permute-start | bytes 356360 | tf_op jit(solution)/shard_map/ppermute | solution.py:474
  45.6 19.7 %collective-permute-start.10 = (bf16[24,16,128]{2,1,0:T(8,128)(2,1)S(1)}, bf16[24,16,128]{2,1,0:T(8,128)(2,1)S(1)}, u32[]{:S(2)}, u32[]{:S(2)}) collective-permute-start(bf16[24,16,128]{2,1,0:T(8,128)(2,1)S(1)} %get-tuple-element.76), channel_id=1, source_target_pairs={{0,8},{4,12},{8,0},{12,4},{16,24},{20,28},{24,16},{28,20},{1,9},{5... | collective-permute-start | bytes 294920 | tf_op jit(solution)/shard_map/ppermute | solution.py:474
  46.4 22.1 %collective-permute-start.11 = (bf16[24,16,128]{2,1,0:T(8,128)(2,1)S(1)}, bf16[24,16,128]{2,1,0:T(8,128)(2,1)S(1)}, u32[]{:S(2)}, u32[]{:S(2)}) collective-permute-start(bf16[24,16,128]{2,1,0:T(8,128)(2,1)S(1)} %get-tuple-element.77), channel_id=1, source_target_pairs={{0,16},{4,20},{8,24},{12,28},{16,0},{20,4},{24,8},{28,12},{1,17},{... | collective-permute-start | bytes 294920 | tf_op jit(solution)/shard_map/ppermute | solution.py:474
  50.0 18.5 %collective-permute-start.12 = (bf16[24,16,128]{2,1,0:T(8,128)(2,1)S(1)}, bf16[24,16,128]{2,1,0:T(8,128)(2,1)S(1)}, u32[]{:S(2)}, u32[]{:S(2)}) collective-permute-start(bf16[24,16,128]{2,1,0:T(8,128)(2,1)S(1)} %get-tuple-element.78), channel_id=1, source_target_pairs={{0,24},{4,28},{8,16},{12,20},{16,8},{20,12},{24,0},{28,4},{1,25},{... | collective-permute-start | bytes 294920 | tf_op jit(solution)/shard_map/ppermute | solution.py:474
  55.2 27.3 %collective-permute-start.26 = (bf16[28,16,128]{2,1,0:T(8,128)(2,1)S(1)}, bf16[28,16,128]{2,1,0:T(8,128)(2,1)S(1)}, u32[]{:S(2)}, u32[]{:S(2)}) collective-permute-start(bf16[28,16,128]{2,1,0:T(8,128)(2,1)S(1)} %get-tuple-element.86.refs_0_), channel_id=1, source_target_pairs={{0,24},{4,28},{8,16},{12,20},{16,8},{20,12},{24,0},{28,4},{1,25},{... | collective-permute-start | bytes 344072 | tf_op jit(solution)/shard_map/ppermute | solution.py:474
  63.1 19.4 %collective-permute-start.25 = (bf16[28,16,128]{2,1,0:T(8,128)(2,1)S(1)}, bf16[28,16,128]{2,1,0:T(8,128)(2,1)S(1)}, u32[]{:S(2)}, u32[]{:S(2)}) collective-permute-start(bf16[28,16,128]{2,1,0:T(8,128)(2,1)S(1)} %get-tuple-element.86.refs_0_), channel_id=1, source_target_pairs={{0,16},{4,20},{8,24},{12,28},{16,0},{20,4},{24,8},{28,12},{1,17},{... | collective-permute-start | bytes 344072 | tf_op jit(solution)/shard_map/ppermute | solution.py:474
  68.6 7.1 %collective-permute-start.19 = (bf16[24,16,128]{2,1,0:T(8,128)(2,1)S(1)}, bf16[24,16,128]{2,1,0:T(8,128)(2,1)S(1)}, u32[]{:S(2)}, u32[]{:S(2)}) collective-permute-start(bf16[24,16,128]{2,1,0:T(8,128)(2,1)S(1)} %divide.3.refs_0_), channel_id=1, source_target_pairs={{0,24},{4,28},{8,16},{12,20},{16,8},{20,12},{24,0},{28,4},{1,25},{... | collective-permute-start | bytes 294920 | tf_op jit(solution)/shard_map/ppermute | solution.py:474
  68.7 14.4 %collective-permute-start.18 = (bf16[24,16,128]{2,1,0:T(8,128)(2,1)S(1)}, bf16[24,16,128]{2,1,0:T(8,128)(2,1)S(1)}, u32[]{:S(2)}, u32[]{:S(2)}) collective-permute-start(bf16[24,16,128]{2,1,0:T(8,128)(2,1)S(1)} %divide.3.refs_0_), channel_id=1, source_target_pairs={{0,16},{4,20},{8,24},{12,28},{16,0},{20,4},{24,8},{28,12},{1,17},{... | collective-permute-start | bytes 294920 | tf_op jit(solution)/shard_map/ppermute | solution.py:474
  75.7 12.1 %collective-permute-start.27 = (bf16[28,16,128]{2,1,0:T(8,128)(2,1)S(1)}, bf16[28,16,128]{2,1,0:T(8,128)(2,1)S(1)}, u32[]{:S(2)}, u32[]{:S(2)}) collective-permute-start(bf16[28,16,128]{2,1,0:T(8,128)(2,1)S(1)} %get-tuple-element.86.refs_0_), channel_id=1, source_target_pairs={{0,4},{4,0},{8,12},{12,8},{16,20},{20,16},{24,28},{28,24},{1,5},{5... | collective-permute-start | bytes 344072 | tf_op jit(solution)/shard_map/ppermute | solution.py:474
  75.7 12.6 %collective-permute-start.24 = (bf16[28,16,128]{2,1,0:T(8,128)(2,1)S(1)}, bf16[28,16,128]{2,1,0:T(8,128)(2,1)S(1)}, u32[]{:S(2)}, u32[]{:S(2)}) collective-permute-start(bf16[28,16,128]{2,1,0:T(8,128)(2,1)S(1)} %get-tuple-element.86.refs_0_), channel_id=1, source_target_pairs={{0,8},{4,12},{8,0},{12,4},{16,24},{20,28},{24,16},{28,20},{1,9},{5... | collective-permute-start | bytes 344072 | tf_op jit(solution)/shard_map/ppermute | solution.py:474
  82.5 5.9 %collective-permute-start.30 = (bf16[28,16,128]{2,1,0:T(8,128)(2,1)S(1)}, bf16[28,16,128]{2,1,0:T(8,128)(2,1)S(1)}, u32[]{:S(2)}, u32[]{:S(2)}) collective-permute-start(bf16[28,16,128]{2,1,0:T(8,128)(2,1)S(1)} %collective-permute-done.26.refs_3_), channel_id=1, source_target_pairs={{0,4},{4,0},{8,12},{12,8},{16,20},{20,16},{24,28},{28,24},{1,5},{5... | collective-permute-start | bytes 344072 | tf_op jit(solution)/shard_map/ppermute | solution.py:474
  82.5 6.3 %collective-permute-start.29 = (bf16[28,16,128]{2,1,0:T(8,128)(2,1)S(1)}, bf16[28,16,128]{2,1,0:T(8,128)(2,1)S(1)}, u32[]{:S(2)}, u32[]{:S(2)}) collective-permute-start(bf16[28,16,128]{2,1,0:T(8,128)(2,1)S(1)} %collective-permute-done.25.refs_2_), channel_id=1, source_target_pairs={{0,4},{4,0},{8,12},{12,8},{16,20},{20,16},{24,28},{28,24},{1,5},{5... | collective-permute-start | bytes 344072 | tf_op jit(solution)/shard_map/ppermute | solution.py:474
  83.1 4.7 %collective-permute-start.17 = (bf16[24,16,128]{2,1,0:T(8,128)(2,1)S(1)}, bf16[24,16,128]{2,1,0:T(8,128)(2,1)S(1)}, u32[]{:S(2)}, u32[]{:S(2)}) collective-permute-start(bf16[24,16,128]{2,1,0:T(8,128)(2,1)S(1)} %divide.3.refs_0_), channel_id=1, source_target_pairs={{0,8},{4,12},{8,0},{12,4},{16,24},{20,28},{24,16},{28,20},{1,9},{5... | collective-permute-start | bytes 294920 | tf_op jit(solution)/shard_map/ppermute | solution.py:474
  87.8 5.7 %collective-permute-start.20 = (bf16[24,16,128]{2,1,0:T(8,128)(2,1)S(1)}, bf16[24,16,128]{2,1,0:T(8,128)(2,1)S(1)}, u32[]{:S(2)}, u32[]{:S(2)}) collective-permute-start(bf16[24,16,128]{2,1,0:T(8,128)(2,1)S(1)} %divide.3.refs_0_), channel_id=1, source_target_pairs={{0,4},{4,0},{8,12},{12,8},{16,20},{20,16},{24,28},{28,24},{1,5},{5... | collective-permute-start | bytes 294920 | tf_op jit(solution)/shard_map/ppermute | solution.py:474
  87.8 5.7 %collective-permute-start.23 = (bf16[24,16,128]{2,1,0:T(8,128)(2,1)S(1)}, bf16[24,16,128]{2,1,0:T(8,128)(2,1)S(1)}, u32[]{:S(2)}, u32[]{:S(2)}) collective-permute-start(bf16[24,16,128]{2,1,0:T(8,128)(2,1)S(1)} %collective-permute-done.19.refs_3_), channel_id=1, source_target_pairs={{0,4},{4,0},{8,12},{12,8},{16,20},{20,16},{24,28},{28,24},{1,5},{5... | collective-permute-start | bytes 294920 | tf_op jit(solution)/shard_map/ppermute | solution.py:474
  88.3 5.2 %collective-permute-start.22 = (bf16[24,16,128]{2,1,0:T(8,128)(2,1)S(1)}, bf16[24,16,128]{2,1,0:T(8,128)(2,1)S(1)}, u32[]{:S(2)}, u32[]{:S(2)}) collective-permute-start(bf16[24,16,128]{2,1,0:T(8,128)(2,1)S(1)} %collective-permute-done.18.refs_2_), channel_id=1, source_target_pairs={{0,4},{4,0},{8,12},{12,8},{16,20},{20,16},{24,28},{28,24},{1,5},{5... | collective-permute-start | bytes 294920 | tf_op jit(solution)/shard_map/ppermute | solution.py:474
  88.4 5.2 %collective-permute-start.21 = (bf16[24,16,128]{2,1,0:T(8,128)(2,1)S(1)}, bf16[24,16,128]{2,1,0:T(8,128)(2,1)S(1)}, u32[]{:S(2)}, u32[]{:S(2)}) collective-permute-start(bf16[24,16,128]{2,1,0:T(8,128)(2,1)S(1)} %collective-permute-done.17.refs_1_), channel_id=1, source_target_pairs={{0,4},{4,0},{8,12},{12,8},{16,20},{20,16},{24,28},{28,24},{1,5},{5... | collective-permute-start | bytes 294920 | tf_op jit(solution)/shard_map/ppermute | solution.py:474
  88.8 1.3 %collective-permute-start.28 = (bf16[28,16,128]{2,1,0:T(8,128)(2,1)S(1)}, bf16[28,16,128]{2,1,0:T(8,128)(2,1)S(1)}, u32[]{:S(2)}, u32[]{:S(2)}) collective-permute-start(bf16[28,16,128]{2,1,0:T(8,128)(2,1)S(1)} %collective-permute-done.24.refs_1_), channel_id=1, source_target_pairs={{0,4},{4,0},{8,12},{12,8},{16,20},{20,16},{24,28},{28,24},{1,5},{5... | collective-permute-start | bytes 344072 | tf_op jit(solution)/shard_map/ppermute | solution.py:474

commit v3 on v2

v3 whole, which is shorter than its diff:
```python
import functools
import math

import jax
import jax.numpy as jnp
import numpy as np
from jax import lax
from jax.experimental import pallas as pl
from jax.experimental.pallas import tpu as pltpu
from jax.sharding import PartitionSpec as P

SHELLS = 64
FREQ = 128
FEAT = 16384
ROTS = 64
K = 208
CAND = 8
MOST = 2
IMG = 2 * SHELLS
UNROLL = 4
LOW = -1e30
HIGH = lax.Precision.HIGHEST
VMEM = pltpu.VMEM
SMEM = pltpu.SMEM
HBM = pltpu.HBM
F32 = jnp.float32
BF16 = jnp.bfloat16
SHAPE = jax.ShapeDtypeStruct


def tables():
    turns = np.arange(ROTS)[:, None]
    orders = np.arange(FREQ)[None, :]
    angles = ((turns * orders) % ROTS).astype(np.float32) * np.float32(2.0 * math.pi / ROTS)
    cos_tab = np.cos(angles).astype(np.float32)
    sin_tab = np.sin(angles).astype(np.float32)
    last = np.zeros((FREQ, ROTS), np.float32)
    last[:SHELLS] = -0.5
    last[SHELLS] = 1.0
    scoring = np.concatenate([cos_tab.T, sin_tab.T, last], axis=0)
    left = np.concatenate([cos_tab, sin_tab], axis=1)
    left = np.concatenate([left, left], axis=0)
    phases = []
    for _ in range(3):
        phases.append(left.astype(jnp.bfloat16))
        left = left - phases[-1].astype(np.float32)
    return (scoring, *phases)


def lanes_of(shape):
    return lax.broadcasted_iota(jnp.int32, shape, len(shape) - 1)


def list_spots(blocks, chunks):
    room = FREQ if max(n for _, n in chunks) * MOST + UNROLL > FREQ // 2 else FREQ // 2
    lines = -(-blocks * len(chunks) * room // FREQ)
    return room, lines, -(-(2 * lines + 1) // 8) * 8


def list_spot(block, chunk, blocks, chunks):
    room, lines, _ = list_spots(blocks, chunks)
    spot = block * len(chunks) + chunk
    line, lane = divmod(spot * room, FREQ)
    return line, lines + line, lane, 2 * lines, spot


def quot(v, n):
    return v >> (n.bit_length() - 1) if n & (n - 1) == 0 else v // n


def rest(v, n):
    return v & (n - 1) if n & (n - 1) == 0 else v % n


def rounded(v):
    return v.astype(BF16).astype(F32)


def row_of(x, r, depth):
    return r // depth * 2 * depth + x * depth + r % depth


def parts_of(image, depth):
    pieces = image.reshape(image.shape[0] // (2 * depth), 2, depth, FREQ)
    return pieces[:, 0], pieces[:, 1]


def chunks_of(cls_dev):
    cut = cls_dev // 2 // 8 * 8
    return ((cut, cls_dev - cut), (0, cut)) if cut else ((0, cls_dev),)


def weigh_kernel(
    slices, grp_s, particles_h, cand_h, groups_h, entries_h, ctf_h, prec_h, message_out, *refs
):
    slice_outs = refs[: slices - 1]
    particles, cand, groups, entries, ctf, prec, hot_g, hot_e, spread, sem = refs[slices - 1 :]
    depth = SHELLS // slices
    z = grp_s[0] // 2
    copies = [
        pltpu.make_async_copy(a, b, sem.at[n])
        for n, (a, b) in enumerate(
            (
                (groups_h, groups), (entries_h, entries), (ctf_h, ctf), (prec_h, prec),
                (cand_h, cand), (particles_h, particles),
            )
        )
    ]
    for copy in copies:
        copy.start()
    per = particles.shape[0]
    for copy in copies[:2]:
        copy.wait()
    for i in range(per):
        hot_g[i : i + 1, :] = (lanes_of((1, hot_g.shape[1])) == groups[i]).astype(F32)
        hot_e[i : i + 1, :] = (lanes_of((1, hot_e.shape[1])) == entries[i]).astype(F32)
    for copy in copies[2:5]:
        copy.wait()
    p = jnp.dot(hot_g[...], prec[...], precision=HIGH, preferred_element_type=F32)
    c = lax.dot_general(
        hot_e[...], ctf[...], (((1,), (1,)), ((), ())), precision=HIGH, preferred_element_type=F32
    )
    eye = (lanes_of((per, per)) == lax.broadcasted_iota(jnp.int32, (per, per), 0)).astype(F32)
    named = lax.dot_general(
        eye, cand[...].astype(F32), (((1,), (1,)), ((), ())), precision=HIGH,
        preferred_element_type=F32,
    )
    factors = p * c
    extra = jnp.concatenate(
        [factors * c, named, jnp.zeros((per, FREQ - SHELLS - CAND), F32)], axis=1
    )
    message_out[per * IMG :, :] = extra.astype(BF16)
    copies[5].wait()
    for r in range(SHELLS):
        factor = jnp.broadcast_to(factors[:, r : r + 1], (per, FREQ))
        for x in range(2):
            at = x * SHELLS + r
            piece = particles[:, at * FREQ : (at + 1) * FREQ].astype(F32) * factor
            at = row_of(x, r, depth)
            spread[at * per : (at + 1) * per, :] = rounded(piece)
    rows = 2 * depth
    for i in range(per):
        message_out[i * IMG : (i + 1) * IMG, :] = spread[i : i + IMG * per : per, :].astype(BF16)
        for d, out in enumerate(slice_outs, start=1):
            row = pl.multiple_of(i * IMG + (z ^ d) * rows, rows)
            out[i * rows : (i + 1) * rows, :] = message_out[pl.ds(row, rows), :]


def prep_kernel(depth, grp_s, refs_h, *rest_refs):
    tables_h, (reg_h, prior), rest_refs = rest_refs[:4], rest_refs[4:6], rest_refs[6:]
    (rf_out, pow_out), tables_out, (reg_out,) = rest_refs[:2], rest_refs[2:6], rest_refs[6:7]
    refs, spread, reg, sem = rest_refs[7:]
    cls_dev = refs.shape[0]
    pad = spread.shape[0] // IMG
    parts = sem.shape[0] - 5
    step = FEAT // parts
    tables_in = [
        pltpu.make_async_copy(a, b, sem.at[parts + n])
        for n, (a, b) in enumerate(zip((*tables_h, reg_h), (*tables_out, reg)))
    ]
    copies = [
        pltpu.make_async_copy(
            refs_h.at[:, pl.ds(n * step, step)], refs.at[:, pl.ds(n * step, step)], sem.at[n]
        )
        for n in range(parts)
    ]
    for copy in copies + tables_in:
        copy.start()
    for copy in copies:
        copy.wait()

    def shell(r, power):
        parts = []
        for x in range(2):
            at = x * SHELLS + r
            piece = refs[:, pl.ds(pl.multiple_of(at * FREQ, FREQ), FREQ)].astype(F32)
            at = row_of(x, r, depth)
            spread[pl.ds(pl.multiple_of(at * pad, 8), cls_dev), :] = piece
            parts.append(piece * piece)
        total = jnp.sum(parts[0] + parts[1], axis=1, keepdims=True)
        return jnp.where(lanes_of((cls_dev, FREQ)) == r, total, power)

    power = lax.fori_loop(0, SHELLS, shell, jnp.zeros((cls_dev, FREQ), F32), unroll=4)
    pow_out[...] = jnp.where(lanes_of((cls_dev, FREQ)) == SHELLS, prior[...], power)

    def image(k, _):
        rf_out[k] = spread[pl.ds(k, IMG, stride=pad), :]
        return 0

    lax.fori_loop(0, cls_dev, image, 0, unroll=4)
    for copy in tables_in:
        copy.wait()
    width = reg_out.shape[0]
    for r in range(width):
        reg_out[r : r + 1, :] = jnp.full((1, FREQ), reg[grp_s[0] * width + r], F32)


def take(refs, counts):
    taken = []
    for count in counts:
        taken.append(refs[:count])
        refs = refs[count:]
    return taken, refs


def score_kernel(arrays, earlier, depth, chunks, first_s, *refs):
    blocks = len(arrays)
    messages, refs = take(refs, arrays)
    (earlier_stats,), refs = take(refs, (earlier,))
    rf, power, scoring = refs[:3]
    scores_out, stats_out, cls_out, ints_out = refs[3:-7]
    cand_v, cand_s, ints_s, side, ex, w32, sem = refs[-7:]
    per = cand_v.shape[1]
    cls_dev = rf.shape[0]
    block_rows = per * CAND
    first = first_s[0]
    table = scoring[...]
    done = 0
    for one in earlier_stats:
        stats_out[done : done + one.shape[0], :] = one[...]
        done += one.shape[0]

    for b in range(blocks):
        extra = messages[b][-1][messages[b][-1].shape[0] - per :, :].astype(F32)
        cand_v[b] = extra.astype(jnp.int32)
        lane = lanes_of((per, FREQ))
        side[b] = jnp.where(lane < SHELLS, extra, (lane == SHELLS).astype(F32))
    copies = [pltpu.make_async_copy(cand_v.at[b], cand_s.at[b], sem.at[b]) for b in range(blocks)]
    for copy in copies:
        copy.start()
    for b in range(blocks):
        begin = 0
        for one in messages[b]:
            count = one.shape[0] // IMG

            def widen(i, _):
                w32[b * per + begin + i] = one[pl.ds(pl.multiple_of(i * IMG, IMG), IMG), :].astype(F32)
                return 0

            lax.fori_loop(0, count, widen, 0, unroll=2)
            begin += count
    for copy in copies:
        copy.wait()

    for b in range(blocks):
        spots = [list_spot(b, c, blocks, chunks) for c in range(len(chunks))]

        def put(place, lane, c, row, local):
            if len(chunks) == 1 or c is not None:
                spot = spots[c or 0]
                ints_s[spot[0], spot[2] + place] = row
                ints_s[spot[1], spot[2] + place] = local
            else:
                ints_s[spots[0][0] + lane[0], lane[1]] = row
                ints_s[spots[0][1] + lane[0], lane[1]] = local

        def one(i, n):
            for t in range(CAND):
                local = cand_s[b, i, SHELLS + t] - first
                good = jnp.logical_and(local >= 0, local < cls_dev)
                if len(chunks) == 1:
                    put(n[0], None, 0, i * CAND + t, local)
                    n = (n[0] + good.astype(jnp.int32),)
                else:
                    late = local < chunks[0][0]
                    line = jnp.where(late, spots[1][0] - spots[0][0], 0)
                    lane = jnp.where(late, spots[1][2] + n[1], spots[0][2] + n[0])
                    put(None, (line, lane), None, i * CAND + t, local)
                    n = (
                        n[0] + jnp.logical_and(good, jnp.logical_not(late)).astype(jnp.int32),
                        n[1] + jnp.logical_and(good, late).astype(jnp.int32),
                    )
            return n

        n = lax.fori_loop(0, per, one, (jnp.int32(0),) * len(chunks))
        for c, (start, _) in enumerate(chunks):
            for spare in range(UNROLL):
                put(n[c] + spare, None, c, block_rows, start)
            ints_s[spots[c][3], spots[c][4]] = quot(n[c] + UNROLL - 1, UNROLL)
    lists_copy = pltpu.make_async_copy(ints_s, ints_out, sem.at[blocks])
    lists_copy.start()

    for b in range(blocks):
        for c in range(len(chunks)):
            spot = list_spot(b, c, blocks, chunks)

            def pairs(step, _):
                for u in range(UNROLL):
                    row = ints_s[spot[0], spot[2] + step * UNROLL + u]
                    k = ints_s[spot[1], spot[2] + step * UNROLL + u]
                    i = jnp.minimum(quot(row, CAND), per - 1)
                    w_re, w_im = parts_of(w32[b * per + i], depth)
                    a_re, a_im = parts_of(rf[k], depth)
                    inner = (w_re * a_re + w_im * a_im).reshape(SHELLS, FREQ)
                    outer = (w_re * a_im - w_im * a_re).reshape(SHELLS, FREQ)
                    ex[0, pl.ds(row, 1), :] = jnp.sum(inner, axis=0, keepdims=True)
                    ex[1, pl.ds(row, 1), :] = jnp.sum(outer, axis=0, keepdims=True)
                    ex[2, pl.ds(row, 1), :] = side[b, pl.ds(i, 1), :] * power[pl.ds(k, 1), :]
                return 0

            lax.fori_loop(0, ints_s[spot[3], spot[4]], pairs, 0)

        wide = jnp.broadcast_to(
            messages[b][-1][messages[b][-1].shape[0] - per :, :].astype(F32)[:, None, :],
            (per, CAND, FREQ),
        ).reshape(block_rows, FREQ)
        own = lanes_of((block_rows, FREQ)) == SHELLS + (
            lax.broadcasted_iota(jnp.int32, (block_rows, FREQ), 0) % CAND
        )
        column = jnp.sum(jnp.where(own, wide, 0.0), axis=1, keepdims=True) - first.astype(F32)
        cls_out[b * block_rows : (b + 1) * block_rows, :] = jnp.broadcast_to(
            column, (block_rows, FREQ)
        )
        good = jnp.logical_and(column >= 0, column < cls_dev)
        values = jnp.zeros((block_rows, ROTS), F32)
        for part in range(3):
            values = values + jnp.dot(
                jnp.where(good, ex[part, :block_rows, :], 0.0),
                table[part * FREQ : (part + 1) * FREQ],
                precision=HIGH,
                preferred_element_type=F32,
            )
        scores = jnp.where(good, values, LOW)
        scores_out[b * block_rows : (b + 1) * block_rows, :] = scores
        top = jnp.broadcast_to(jnp.max(scores, axis=1, keepdims=True), (block_rows, ROTS))
        best = jnp.max(top.reshape(per, CAND, ROTS), axis=1)
        best_rows = jnp.broadcast_to(best[:, None, :], (per, CAND, ROTS)).reshape(block_rows, ROTS)
        mass = jnp.where(good, jnp.exp(scores - best_rows), 0.0)
        mass = jnp.broadcast_to(jnp.sum(mass, axis=1, keepdims=True), (block_rows, ROTS))
        total = jnp.sum(mass.reshape(per, CAND, ROTS), axis=1)
        stats_out[done + b * per : done + (b + 1) * per, :ROTS] = best
        stats_out[done + b * per : done + (b + 1) * per, ROTS:] = total
    lists_copy.wait()


def two(v):
    return jnp.where(lanes_of(v.shape) < ROTS, rounded(v), v - rounded(v))


def one_of_two(v):
    return v + pltpu.roll(v, ROTS, 1)


def weights_kernel(calls, blocks, slices, cls_dev, grp_s, *refs):
    stats = refs[:blocks]
    scores = refs[blocks : blocks + calls]
    classes = refs[blocks + calls : blocks + 2 * calls]
    extras = refs[blocks + 2 * calls : 2 * blocks + 2 * calls]
    refs = refs[2 * blocks + 2 * calls :]
    ints, refs = refs[:calls], refs[calls:]
    own_out, den_out, mass_out, log_out = refs[:4]
    message_outs = refs[4:-2]
    rows_v, den_v = refs[-2:]
    per = log_out.shape[0]
    block_rows = per * CAND
    depth = SHELLS // slices
    z = grp_s[0] // 2

    den = jnp.zeros((FREQ, FREQ), F32)
    mass = jnp.zeros((1, FREQ), F32)
    block = 0
    for scores_ref, cls_ref in zip(scores, classes):
        for b in range(scores_ref.shape[0] // block_rows):
            ones = [stats[d][(block ^ d) * per : ((block ^ d) + 1) * per, :] for d in range(blocks)]
            best = functools.reduce(jnp.maximum, [one[:, :ROTS] for one in ones])
            total = sum(one[:, ROTS:] * jnp.exp(one[:, :ROTS] - best) for one in ones)
            if block == 0:
                log_out[...] = jnp.log(total)

            def over_rows(v):
                return jnp.broadcast_to(v[:, None, :], (per, CAND, ROTS)).reshape(block_rows, ROTS)

            at = slice(b * block_rows, (b + 1) * block_rows)
            weights = jnp.exp(scores_ref[at, :] - over_rows(best)) / over_rows(total)
            local = cls_ref[at, :]
            good = jnp.logical_and(local >= 0, local < cls_dev)[:, :ROTS]
            weights = rounded(jnp.where(good, weights, 0.0))
            rows_v[block * block_rows : (block + 1) * block_rows, :] = weights
            pair_sum = jnp.sum(weights, axis=1, keepdims=True)
            twice = (lanes_of((block_rows, FREQ)) % ROTS).astype(F32)
            chosen = jnp.where(twice == local, pair_sum, 0.0)
            by_particle = jnp.sum(chosen.reshape(per, CAND, FREQ), axis=1)
            side = extras[block][extras[block].shape[0] - per :, :].astype(F32)
            den = den + lax.dot_general(
                side, by_particle, (((0,), (0,)), ((), ())), precision=HIGH,
                preferred_element_type=F32,
            )
            mass = mass + jnp.sum(by_particle, axis=0, keepdims=True)
            block += 1

    lines = rows_v.shape[0] // 2
    packed = jnp.concatenate([rows_v[:lines, :], rows_v[lines:, :]], axis=1).astype(BF16)
    own_out[...] = packed
    den_v[...] = den[:SHELLS].reshape(slices, depth, FREQ)
    mass_rows = jnp.broadcast_to(mass, (8, FREQ))
    mass_out[...] = mass_rows
    den_out[...] = den_v[z]
    tail = [two(mass_rows)] + [one[...].astype(F32) for one in ints]
    tail_rows = depth + sum(one.shape[0] for one in tail)
    spare = message_outs[0].shape[0] - lines - tail_rows
    if spare:
        tail.append(jnp.zeros((spare, FREQ), F32))
    for d, out in enumerate(message_outs, start=1):
        out[:lines, :] = packed
        out[lines:, :] = jnp.concatenate([two(den_v[z ^ d])] + tail, axis=0).astype(BF16)


def phase_rows(packed, phases):
    high, mid, low = phases
    halves = []
    for place in range(2):
        lanes = lanes_of(packed.shape) // ROTS == place
        picked = jnp.where(lanes, packed.astype(F32), 0.0).astype(BF16)
        halves.append(
            rounded(
                sum(
                    jnp.dot(picked, t[...], preferred_element_type=F32) for t in (low, mid, high)
                )
            )
        )
    return halves


def put_phases(packed, phases, wcs, base):
    lines = packed.shape[0]
    for place, both in enumerate(phase_rows(packed, phases)):
        for part in range(2):
            at = base + place * lines
            wcs[part, at : at + lines, :] = both[:, part * FREQ : (part + 1) * FREQ]
    for part in range(2):
        wcs[part, base + 2 * lines : base + 2 * lines + 8, :] = jnp.zeros((8, FREQ), F32)


def add_pair(image, row, k, wcs, num):
    shape = num.shape[1:]
    image = image.astype(F32)
    half = image.shape[0] // 2
    w_re, w_im = image[:half].reshape(shape[1:]), image[half:].reshape(shape[1:])
    c = wcs[0, pl.ds(row, 1), :].reshape(1, 1, FREQ)
    s = wcs[1, pl.ds(row, 1), :].reshape(1, 1, FREQ)
    num[k, 0] += w_re * c - w_im * s
    num[k, 1] += w_re * s + w_im * c


def pick_image(arrays, begin, i, rows, stride, offset):
    def rows_at(one, i):
        return one[pl.ds(pl.multiple_of(i * stride + offset, rows), rows), :]

    held = [one.shape[0] // stride for one in arrays]
    while len(arrays) > 1 and begin >= held[0]:
        arrays, begin, held = arrays[1:], begin - held[0], held[1:]
    if len(arrays) == 1:
        return rows_at(arrays[0], begin + i)
    cut = held[0] - begin
    return jnp.where(
        i < cut,
        rows_at(arrays[0], begin + jnp.minimum(i, cut - 1)),
        rows_at(arrays[1], jnp.maximum(i - cut, 0)),
    )


def own_sum_kernel(chunks, calls, arrays, grp_s, packed, *refs):
    (ints,), refs = take(refs, (len(calls),))
    messages, refs = take(refs, arrays)
    phases, (num, wcs, *ints_s, sem) = refs[:3], refs[3:]
    copies = [
        pltpu.make_async_copy(a, b, sem.at[n]) for n, (a, b) in enumerate(zip(ints, ints_s))
    ]
    for copy in copies:
        copy.start()
    per = sum(one.shape[0] for one in messages[0]) // (IMG + 1)
    rows = 2 * num.shape[2] * num.shape[3]
    z = grp_s[0] // 2
    put_phases(packed[...], phases, wcs, 0)
    num[...] = jnp.zeros_like(num)
    for copy in copies:
        copy.wait()
    block = 0
    for held, list_s in zip(calls, ints_s):
        for b in range(held):
            held_in = messages[block]
            base = block * per * CAND
            for c in range(len(chunks)):
                spot = list_spot(b, c, held, chunks)

                def pairs(step, _):
                    for u in range(UNROLL):
                        row = list_s[spot[0], spot[2] + step * UNROLL + u]
                        k = list_s[spot[1], spot[2] + step * UNROLL + u]
                        i = jnp.minimum(quot(row, CAND), per - 1)
                        row = jnp.where(row == per * CAND, wcs.shape[1] - 8, base + row)
                        image = pick_image(held_in, 0, i, rows, IMG, z * rows)
                        add_pair(image, row, k, wcs, num)
                    return 0

                lax.fori_loop(0, list_s[spot[3], spot[4]], pairs, 0)
            block += 1


def join_kernel(*refs):
    out = refs[-1]
    rows = refs[0].shape[0]
    for n, one in enumerate(refs[:-1]):
        out[n * rows : (n + 1) * rows, :] = one[...]


def sum_kernel(chunk, chunks, calls, slices, pieces, grp_s, *refs):
    images, refs = take(refs, pieces)
    messages, refs = refs[: slices - 1], refs[slices - 1 :]
    first, refs = refs[0], refs[1:]
    if chunk == 0:
        phases, (den_own, mass_own), refs = refs[:3], refs[3:5], refs[5:]
        own_out, sib_out, den_out, mass_out, wcs, num, den_v, ints_v, ints_s, sem = refs
    else:
        wcs, own_out, sib_out, num, ints_v, ints_s, sem = refs
    group_rows = wcs.shape[1] // (slices - 1)
    lines = (group_rows - 8) // 2
    core = grp_s[0] % 2
    start, size = chunks[chunk]
    depth = num.shape[2] * num.shape[3]
    rows = 2 * depth
    per = sum(one.shape[0] for one in images[0]) // ((slices - 1) * rows)
    total = ints_v.shape[1]

    for d in range(slices - 1):
        tail = messages[d][lines:, :].astype(F32)
        ints_v[d] = tail[depth + 8 : depth + 8 + total].astype(jnp.int32)
    copies = [
        pltpu.make_async_copy(ints_v.at[d], ints_s.at[d], sem.at[d]) for d in range(slices - 1)
    ]
    for copy in copies:
        copy.start()
    num[...] = first[start : start + size]
    if chunk == 0:
        den, mass = den_own[...], mass_own[...]
        for d in range(slices - 1):
            put_phases(messages[d][:lines, :], phases, wcs, d * group_rows)
            den = den + one_of_two(messages[d][lines:, :].astype(F32)[:depth])
            mass = mass + one_of_two(messages[d][lines:, :].astype(F32)[depth : depth + 8])
    for copy in copies:
        copy.wait()

    for d in range(slices - 1):
        block, line = 0, 0
        for held in calls:
            for b in range(held):
                spot = list_spot(b, chunk, held, chunks)
                held_in = images[block]
                base = d * group_rows + block * per * CAND
                blank = (d + 1) * group_rows - 8

                def pairs(step, _):
                    for u in range(UNROLL):
                        row = ints_s[d, line + spot[0], spot[2] + step * UNROLL + u]
                        k = ints_s[d, line + spot[1], spot[2] + step * UNROLL + u]
                        i = jnp.minimum(quot(row, CAND), per - 1)
                        row = jnp.where(row == per * CAND, blank, base + row)
                        image = pick_image(held_in, d * per, i, rows, rows, 0)
                        add_pair(image, row, k - start, wcs, num)
                    return 0

                lax.fori_loop(0, ints_s[d, line + spot[3], spot[4]], pairs, 0)
                block += 1
            line += list_spots(held, chunks)[2]

    def pack(k, _):
        own_out[k] = jnp.concatenate([num[k, 0, core], num[k, 1, core]], axis=0)
        other = jnp.concatenate([num[k, 0, 1 - core], num[k, 1, 1 - core]], axis=0)
        sib_out[k] = other.astype(BF16)
        return 0

    lax.fori_loop(0, size, pack, 0)
    if chunk == 0:
        width = num.shape[3]
        den_v[...] = den.reshape(2, width, FREQ)
        den_out[...] = den_v[core]
        mass_out[...] = mass
        sib_out[size] = jnp.concatenate([two(den_v[1 - core]), two(mass)[:width]], axis=0).astype(BF16)


def divide(own, sib, inverse, start, avg_out):
    for k in range(avg_out.shape[0]):
        column = inverse[:, start + k : start + k + 1]
        factor = jnp.concatenate([column, column], axis=0)
        avg_out[k] = ((own[k] + sib[k].astype(F32)) * factor).astype(BF16)


def first_divide_kernel(scale, start, own, sib, den, mass, reg, avg_out, share_out, inverse_out):
    cut = avg_out.shape[0]
    width = avg_out.shape[1] // 2
    tile = one_of_two(sib[cut].astype(F32))
    share_out[...] = (tile[width : width + 1] + mass[:1]) * scale
    inverse = 1.0 / (tile[:width] + den[...] + reg[...])
    inverse_out[...] = inverse
    divide(own, sib, inverse, start, avg_out)


def next_divide_kernel(start, own, sib, inverse, avg_out):
    divide(own, sib, inverse[...], start, avg_out)


def spread_kernel(slices, start, has_out, grp_s, *refs):
    got = refs[: 2 * slices]
    out, wide, rows, sem = refs[2 * slices + has_out :]
    cut, height, _ = got[0].shape
    width = height // 2
    pad = wide.shape[0] // IMG
    z, h = grp_s[0] // 2, grp_s[0] % 2

    def one(k, _):
        for d in range(slices):
            for array, core in ((got[d], h), (got[slices + d], 1 - h)):
                piece = array[k].astype(F32)
                for x in range(2):
                    at = (x * SHELLS + ((z ^ d) * 2 + core) * width) * pad
                    wide[pl.ds(at + k, width, stride=pad), :] = piece[
                        x * width : (x + 1) * width
                    ]
        return 0

    lax.fori_loop(0, cut, one, 0)
    for at in range(IMG):
        rows[:, at * FREQ : (at + 1) * FREQ] = wide[at * pad : at * pad + cut, :]
    copy = pltpu.make_async_copy(rows, out.at[pl.ds(start, cut), :], sem)
    copy.start()
    copy.wait()


def whole(space):
    return pl.BlockSpec(memory_space=space)


def in_hbm(value):
    return pltpu.with_memory_space_constraint(value, HBM)


def call(kernel, name, ins, outs, scratch, mib, us, args, **more):
    cost = pl.CostEstimate(flops=0, bytes_accessed=int(us * 3.6e6), transcendentals=0)
    return pl.pallas_call(
        kernel,
        out_shape=tuple(s for s, _ in outs),
        in_specs=[whole(s) for s in ins],
        out_specs=tuple(whole(s) for _, s in outs),
        scratch_shapes=scratch,
        compiler_params=pltpu.CompilerParams(vmem_limit_bytes=mib * 2**20),
        name=name,
        cost_estimate=cost,
        **more,
    )(*args)


def swap(value, axis, distance):
    size = lax.axis_size(axis)
    return lax.ppermute(value, axis, [(i, i ^ distance) for i in range(size)])


def after(value, *others):
    return lax.optimization_barrier((value, *others))[0]


def per_device(
    particles, candidates, group_ids, ctf_ids, ctf_table, noise_prec, references, log_prior, reg
):
    n_cls = lax.axis_size("cls")
    n_grp = lax.axis_size("grp")
    per = particles.shape[0]
    cls_dev = references.shape[0]
    block_rows = per * CAND
    chunks = chunks_of(cls_dev)
    pad = -(-cls_dev // 8) * 8
    width = SHELLS // n_grp
    nz = n_grp // 2
    scoring, *phases = (jnp.asarray(t) for t in tables())
    first = (lax.axis_index("cls") * cls_dev).astype(jnp.int32).reshape(1)
    grp = lax.axis_index("grp").astype(jnp.int32).reshape(1)

    depth = SHELLS // nz
    message, *sliced = call(
        functools.partial(weigh_kernel, nz), "weigh", [SMEM] + [HBM] * 6,
        [(SHAPE((per * (IMG + 1), FREQ), BF16), VMEM)]
        + [(SHAPE((per * 2 * depth, FREQ), BF16), VMEM)] * (nz - 1),
        [
            VMEM(particles.shape, BF16),
            VMEM((CAND, per), jnp.int32),
            SMEM((per,), jnp.int32),
            SMEM((per,), jnp.int32),
            VMEM(ctf_table.shape[::-1], F32),
            VMEM(noise_prec.shape, F32),
            VMEM((per, noise_prec.shape[0]), F32),
            VMEM((per, ctf_table.shape[0]), F32),
            VMEM((IMG * per, FREQ), F32),
            pltpu.SemaphoreType.DMA((6,)),
        ],
        5, 2.0,
        (grp,)
        + tuple(
            in_hbm(a)
            for a in (particles, candidates.T, group_ids, ctf_ids, ctf_table.T, noise_prec)
        ),
    )

    if n_cls == 4:
        message_1, message_2 = swap(message, "cls", 1), swap(message, "cls", 2)
    sliced = [swap(one, "grp", 2 * d) for d, one in enumerate(sliced, start=1)]

    rf, power, scoring, *phases, own_reg = call(
        functools.partial(prep_kernel, depth), "prep", [SMEM] + [HBM] * 6 + [VMEM],
        [(SHAPE((cls_dev, IMG, FREQ), F32), VMEM), (SHAPE((cls_dev, FREQ), F32), VMEM)]
        + [(SHAPE(t.shape, t.dtype), VMEM) for t in (scoring, *phases)]
        + [(SHAPE((width, FREQ), F32), VMEM)],
        [
            VMEM(references.shape, BF16),
            VMEM((IMG * pad, FREQ), F32),
            SMEM(reg.shape, F32),
            pltpu.SemaphoreType.DMA((9,)),
        ],
        8, 4.0,
        (grp,)
        + tuple(in_hbm(a) for a in (references, scoring, *phases, reg))
        + (jnp.broadcast_to(log_prior.astype(F32)[:, None], (cls_dev, FREQ)),),
    )

    def score(part, earlier=()):
        blocks = len(part)
        flat = [m for arrays in part for m in arrays]
        earlier = tuple(s[1] for s in earlier)
        ahead = sum(s.shape[0] for s in earlier)
        counts = tuple(len(arrays) for arrays in part)
        return call(
            functools.partial(score_kernel, counts, len(earlier), depth, chunks), "score",
            [SMEM] + [VMEM] * (len(flat) + len(earlier) + 3),
            [
                (SHAPE((blocks * block_rows, ROTS), F32), VMEM),
                (SHAPE((ahead + blocks * per, FREQ), F32), VMEM),
                (SHAPE((blocks * block_rows, FREQ), F32), VMEM),
                (SHAPE((list_spots(blocks, chunks)[2], FREQ), jnp.int32), VMEM),
            ],
            [
                VMEM((blocks, per, FREQ), jnp.int32),
                SMEM((blocks, per, FREQ), jnp.int32),
                SMEM((list_spots(blocks, chunks)[2], FREQ), jnp.int32),
                VMEM((blocks, per, FREQ), F32),
                VMEM((3, block_rows + 8, FREQ), F32),
                VMEM((blocks * per, IMG, FREQ), F32),
                pltpu.SemaphoreType.DMA((blocks + 1,)),
            ],
            6 if n_cls == 4 else 40, 3.0 * blocks, (first, *flat, *earlier, rf, power, scoring),
        )

    def join(got):
        (joined,) = call(
            join_kernel, "join", [VMEM] * (nz - 1),
            [(SHAPE(((nz - 1) * per * 2 * depth, FREQ), BF16), VMEM)], [], 2, 0.5, got,
        )
        return joined

    if n_cls == 4:
        cut = per // 2 * IMG
        scored = [score([(after(message, sliced[0]),)])]
        ready = (scored[0][1], sliced[1])
        message_1, message_2 = after(message_1, *ready), after(message_2, *ready)
        message_3 = (swap(message_1[:cut], "cls", 2), swap(message_2[cut:], "cls", 1))
        messages = [(message,), (message_1,), (message_2,), message_3]
        scored += [score(messages[1:3])]
        joined = join([after(sliced[0], scored[1][1], *message_3)] + sliced[1:])
        joined_1, joined_2 = swap(joined, "cls", 1), swap(joined, "cls", 2)
        scored += [score(messages[3:], scored)]
    else:
        messages = [(message,)] + [(swap(message, "cls", d),) for d in range(1, n_cls)]
        scored = [score(messages)]
        joined = join(sliced)
        images = [joined] + [swap(joined, "cls", d) for d in range(1, n_cls)]
        pieces = (1,) * n_cls
    calls = (1, 2, 1) if n_cls == 4 else (n_cls,)
    arrays = tuple(len(m) for m in messages)
    stats = scored[-1][1]
    all_stats = [stats] + [swap(stats, "cls", d) for d in range(1, n_cls)]
    ints = [s[3] for s in scored]
    list_lines = sum(one.shape[0] for one in ints)
    flat = [m for held in messages for m in held]

    lines = n_cls * block_rows // 2
    packed, den, mass, log_mass, *outgoing = call(
        functools.partial(weights_kernel, len(calls), n_cls, nz, cls_dev), "weights",
        [SMEM] + [VMEM] * (2 * n_cls + 3 * len(calls)),
        [
            (SHAPE((lines, FREQ), BF16), VMEM),
            (SHAPE((depth, FREQ), F32), VMEM),
            (SHAPE((8, FREQ), F32), VMEM),
            (SHAPE((per, ROTS), F32), VMEM),
        ]
        + [(SHAPE((-(-(lines + depth + 8 + list_lines) // 16) * 16, FREQ), BF16), VMEM)] * (nz - 1),
        [VMEM((2 * lines, ROTS), F32), VMEM((nz, depth, FREQ), F32)],
        4 if n_cls == 4 else 12, 2.0,
        (
            grp, *all_stats, *(s[0] for s in scored), *(s[2] for s in scored),
            *(held[-1] for held in messages), *ints,
        ),
    )
    incoming = [swap(one, "grp", 2 * d) for d, one in enumerate(outgoing, start=1)]
    if n_cls == 4:
        cut = joined.shape[0] // 2
        joined_1, joined_2 = after(joined_1, packed), after(joined_2, packed)
        joined_3 = [swap(joined_1[:cut], "cls", 2), swap(joined_2[cut:], "cls", 1)]
        images = [joined, joined_1, joined_2, *joined_3]
        pieces = (1, 1, 1, 2)
    (first_sums,) = call(
        functools.partial(own_sum_kernel, chunks, calls, arrays), "own_sum",
        [SMEM] + [VMEM] * (len(flat) + 4 + len(calls)),
        [(SHAPE((cls_dev, 2, 2, width, FREQ), F32), VMEM)],
        [
            VMEM((2, 2 * lines + 8, FREQ), F32),
            *(SMEM(one.shape, jnp.int32) for one in ints),
            pltpu.SemaphoreType.DMA((len(ints),)),
        ],
        4 if n_cls == 4 else 12, 3.0, (grp, packed, *ints, *flat, *phases),
    )
    tile = (2 * width, FREQ)
    sums = []
    for chunk, (start, size) in enumerate(chunks):
        more = chunk == 0
        outs = [
            (SHAPE((size,) + tile, F32), VMEM),
            (SHAPE((size + more,) + tile, BF16), VMEM),
        ]
        scratch = [
            VMEM((size, 2, 2, width, FREQ), F32),
            VMEM((nz - 1, list_lines, FREQ), jnp.int32),
            SMEM((nz - 1, list_lines, FREQ), jnp.int32),
            pltpu.SemaphoreType.DMA((nz - 1,)),
        ]
        if more:
            outs += [
                (SHAPE((width, FREQ), F32), VMEM),
                (SHAPE((8, FREQ), F32), VMEM),
                (SHAPE((2, (nz - 1) * (2 * lines + 8), FREQ), F32), VMEM),
            ]
            scratch = scratch[:1] + [VMEM((2, width, FREQ), F32)] + scratch[1:]
            args = (grp, *images, *incoming, first_sums, *phases, den, mass)
        else:
            args = (grp, *images, *incoming, first_sums, wcs)
        own, sib, *others = call(
            functools.partial(sum_kernel, chunk, chunks, calls, nz, pieces), "sum",
            [SMEM] + [VMEM] * (len(args) - 1), outs, scratch, 3 if n_cls == 4 else 24, 3.0, args,
        )
        if more:
            den, mass, wcs = others
        sums.append((own, sib))

    particle_total = per * n_grp * n_cls
    divided, inverse, share = [], None, None
    for chunk, (own, sib) in enumerate(sums):
        start, cut = chunks[chunk]
        other = swap(sib, "grp", 1)
        averaged_out = (SHAPE((cut,) + tile, BF16), VMEM)
        if chunk == 0:
            averaged, share, inverse = call(
                functools.partial(first_divide_kernel, K / particle_total, start), "divide",
                [VMEM] * 5,
                [averaged_out, (SHAPE((1, FREQ), F32), VMEM), (SHAPE((width, FREQ), F32), VMEM)],
                [], 2, 1.0, (own, other, den, mass, own_reg),
            )
        else:
            (averaged,) = call(
                functools.partial(next_divide_kernel, start), "divide", [VMEM] * 3,
                [averaged_out], [], 2, 1.0, (own, other, inverse),
            )
        divided.append(averaged)

    averages = None
    for chunk, averaged in enumerate(divided):
        start, cut = chunks[chunk]
        if nz == 4:
            across = swap(averaged, "grp", 4)
            across = after(across, averages if chunk > 0 else divided[-1])
            slices = [averaged, swap(averaged, "grp", 2), across, swap(across, "grp", 2)]
        else:
            slices = [averaged] + [swap(averaged, "grp", 2 * d) for d in range(1, nz)]
        has_out = chunk > 0
        slices = slices + [swap(s, "grp", 1) for s in slices]
        (averages,) = call(
            functools.partial(spread_kernel, nz, start, has_out), "spread",
            [SMEM] + [VMEM] * (2 * nz) + [HBM] * has_out,
            [(SHAPE((cls_dev, FEAT), F32), HBM)],
            [
                VMEM((IMG * (-(-cut // 8) * 8), FREQ), F32),
                VMEM((cut, FEAT), F32),
                pltpu.SemaphoreType.DMA,
            ],
            6, 2.0, (grp, *slices) + ((averages,) if has_out else ()),
            input_output_aliases={2 * nz + 1: 0} if has_out else {},
        )
    return (averages, share[0, :cls_dev], log_mass[:, 0])


def solution(mesh):
    return jax.shard_map(
        per_device,
        mesh=mesh,
        in_specs=(
            P(("grp", "cls"), None),
            P(("grp", "cls"), None),
            P(("grp", "cls")),
            P(("grp", "cls")),
            P(),
            P(),
            P("cls", None),
            P("cls"),
            P(),
        ),
        out_specs=(P("cls", None), P("cls"), P(("grp", "cls"))),
        check_vma=False,
    )
```

time: 95.7 us -> 87.9 us (0.918)
  starting transfers between devices: 48.5 us -> 31.9 us
  Pallas kernels: 28.5 us -> 33.2 us
  waiting for transfers between devices: 15.4 us -> 19.5 us
    ppermute x31 -> x33, starting transfers between devices: 48.5 us -> 31.9 us  [swap(): return lax.ppermute(value, axis, [(i, i ^ distance) for i in range(size)])]
    pallas_call x13 -> x14, Pallas kernels: 28.5 us -> 33.2 us  [call(): pl.pallas_call(kernel, out_shape=tuple((s for s, _ in outs)), in_specs=[w...]
    ppermute x31 -> x33, waiting for transfers between devices: 15.4 us -> 19.5 us  [swap(): return lax.ppermute(value, axis, [(i, i ^ distance) for i in range(size)])]
  transfers between devices with their start and end apart: 31 -> 33, of which waited for: 9 -> 9; matrix products, arithmetic and copies ran while one was open for 2% -> 2% of each run, Pallas kernels for 19% -> 29%
where the time goes in v3:
time: 87.9 us; the launch traced here: 87.5 us
  Pallas kernels  33.2 us (38%)
  starting transfers between devices  31.9 us (36%)
  waiting for transfers between devices  19.5 us (22%)
  local copies, waits for them, and re-layouts  1.93 us (2%)
  between operations  0.88 us (1%)
    pallas_call x14, Pallas kernels, call(): pl.pallas_call(kernel, out_shape=tuple((s for s, _ in outs)), in_specs=[w...  33.2 us
    ppermute x33, starting transfers between devices, swap(): return lax.ppermute(value, axis, [(i, i ^ distance) for i in range(size)])  31.9 us
    ppermute x33, waiting for transfers between devices, swap(): return lax.ppermute(value, axis, [(i, i ^ distance) for i in range(size)])  19.5 us
  transfers between devices with their start and end apart: 33, of which 9 were waited for; matrix products, arithmetic and copies ran while one was open for 2% of the time, Pallas kernels for 29%

profile of v3, /device:TPU:0, one launch (start us, length us, event | category | flops | bytes accessed | tf_op | source)
XLA Modules:
  0.0 87.5 jit_solution(3226546035529417039)
XLA Ops:
  0.6 1.9 %weigh.1 = (bf16[2064,128]{1,0:T(8,128)(2,1)S(1)}, bf16[512,128]{1,0:T(8,128)(2,1)S(1)}, bf16[512,128]{1,0:T(8,128)(2,1)S(1)}, bf16[512,128]{1,0:T(8,128)(2,1)S(1)}) custom-call(s32[1]{0:T(128)} %bitcast.grp_s, bf16[16,16384]{1,0:T(8,128)(2,1)} %particles_h.1, s32[8,16]{1,0:T(8,128)} %bitcast.7, s32[16]{0:T(128)} %groups_h.1, s32[16]{0:T(128)} %entries_h.1, ...), custom_call_target="tpu_custom_call" | custom-call | bytes 7200000 | tf_op jit(solution)/shard_map/weigh/pallas_call | solution.py:639
  2.5 3.0 %collective-permute-start.3 = (bf16[2064,128]{1,0:T(8,128)(2,1)S(1)}, bf16[2064,128]{1,0:T(8,128)(2,1)S(1)}, u32[]{:S(2)}, u32[]{:S(2)}) collective-permute-start(bf16[2064,128]{1,0:T(8,128)(2,1)S(1)} %get-tuple-element.53.refs_0_.refs_10_.refs_3_), channel_id=1, source_target_pairs={{0,2},{1,3},{2,0},{3,1},{4,6},{5,7},{6,4},{7,5},{8,10},{9,11},{10,... | collective-permute-start | bytes 1585160 | tf_op jit(solution)/shard_map/ppermute | solution.py:654
  5.6 1.5 %collective-permute-start.1 = (bf16[2064,128]{1,0:T(8,128)(2,1)S(1)}, bf16[2064,128]{1,0:T(8,128)(2,1)S(1)}, u32[]{:S(2)}, u32[]{:S(2)}) collective-permute-start(bf16[2064,128]{1,0:T(8,128)(2,1)S(1)} %get-tuple-element.53.refs_0_.refs_10_.refs_3_), channel_id=1, source_target_pairs={{0,1},{1,0},{2,3},{3,2},{4,5},{5,4},{6,7},{7,6},{8,9},{9,8},{10,11... | collective-permute-start | bytes 1585160 | tf_op jit(solution)/shard_map/ppermute | solution.py:654
  7.1 1.6 %collective-permute-start = (bf16[512,128]{1,0:T(8,128)(2,1)S(1)}, bf16[512,128]{1,0:T(8,128)(2,1)S(1)}, u32[]{:S(2)}, u32[]{:S(2)}) collective-permute-start(bf16[512,128]{1,0:T(8,128)(2,1)S(1)} %get-tuple-element.51), channel_id=1, source_target_pairs={{0,8},{4,12},{8,0},{12,4},{16,24},{20,28},{24,16},{28,20},{1,9},{5... | collective-permute-start | bytes 393224 | tf_op jit(solution)/shard_map/ppermute | solution.py:654
  8.6 2.6 %collective-permute-start.2 = (bf16[512,128]{1,0:T(8,128)(2,1)S(1)}, bf16[512,128]{1,0:T(8,128)(2,1)S(1)}, u32[]{:S(2)}, u32[]{:S(2)}) collective-permute-start(bf16[512,128]{1,0:T(8,128)(2,1)S(1)} %get-tuple-element.58), channel_id=1, source_target_pairs={{0,16},{4,20},{8,24},{12,28},{16,0},{20,4},{24,8},{28,12},{1,17},{... | collective-permute-start | bytes 393224 | tf_op jit(solution)/shard_map/ppermute | solution.py:654
  12.0 4.0 %prep.1 = (f32[52,128,128]{2,1,0:T(8,128)S(1)}, f32[52,128]{1,0:T(8,128)S(1)}, f32[384,64]{1,0:T(8,128)S(1)}, bf16[128,256]{1,0:T(8,128)(2,1)S(1)}, bf16[128,256...) custom-call(s32[1]{0:T(128)} %bitcast.grp_s, bf16[52,16384]{1,0:T(8,128)(2,1)} %refs_h.1, ...), custom_call_target="tpu_custom_call" | custom-call | bytes 14400000 | tf_op jit(solution)/shard_map/prep/pallas_call | solution.py:639
  16.0 2.9 %score.3 = (f32[128,64]{1,0:T(8,128)S(1)}, f32[16,128]{1,0:T(8,128)S(1)}, f32[128,128]{1,0:T(8,128)S(1)}, s32[8,128]{1,0:T(8,128)S(1)}) custom-call(s32[1]{0:T(128)} %bitcast.3.first_s, bf16[2064,128]{1,0:T(8,128)(2,1)S(1)} %get-tuple-element.53.refs_0_.refs_10_.refs_3_, f32[52,128,128]{2,1,0:T(8,128)S(1)} %get-tuple-element.54.refs_1_.refs_2_.refs_4_, ...), custom_call_target="tpu_custom_call" | custom-call | bytes 10800000 | tf_op jit(solution)/shard_map/score/pallas_call | solution.py:639
  19.5 1.5 %collective-permute-start.4 = (bf16[1024,128]{1,0:T(8,128)(2,1)S(1)}, bf16[1024,128]{1,0:T(8,128)(2,1)S(1)}, u32[]{:S(2)}, u32[]{:S(2)}) collective-permute-start(bf16[1024,128]{1,0:T(8,128)(2,1)S(1)} %slice.18), channel_id=1, source_target_pairs={{0,2},{1,3},{2,0},{3,1},{4,6},{5,7},{6,4},{7,5},{8,10},{9,11},{10,... | collective-permute-start | bytes 786440 | tf_op jit(solution)/shard_map/ppermute | solution.py:654
  21.0 3.6 %collective-permute-start.6 = (bf16[512,128]{1,0:T(8,128)(2,1)S(1)}, bf16[512,128]{1,0:T(8,128)(2,1)S(1)}, u32[]{:S(2)}, u32[]{:S(2)}) collective-permute-start(bf16[512,128]{1,0:T(8,128)(2,1)S(1)} %get-tuple-element.63), channel_id=1, source_target_pairs={{0,24},{4,28},{8,16},{12,20},{16,8},{20,12},{24,0},{28,4},{1,25},{... | collective-permute-start | bytes 393224 | tf_op jit(solution)/shard_map/ppermute | solution.py:654
  24.6 5.7 %score.4 = (f32[256,64]{1,0:T(8,128)S(1)}, f32[32,128]{1,0:T(8,128)S(1)}, f32[256,128]{1,0:T(8,128)S(1)}, s32[8,128]{1,0:T(8,128)S(1)}) custom-call(s32[1]{0:T(128)} %bitcast.3.first_s, bf16[2064,128]{1,0:T(8,128)(2,1)S(1)} %collective-permute-done.1.refs_0_.refs_11_.refs_4_, bf16[2064,128]{1,0:T(8,128)(2,1)S(1)} %collective-permute-done.3.refs_1_.refs_12_.refs_5_, ...), custom_call_target="tpu_custom_call" | custom-call | bytes 21600000 | tf_op jit(solution)/shard_map/score/pallas_call | solution.py:639
  30.7 1.2 %collective-permute-start.7 = (bf16[1536,128]{1,0:T(8,128)(2,1)S(1)}, bf16[1536,128]{1,0:T(8,128)(2,1)S(1)}, u32[]{:S(2)}, u32[]{:S(2)}) collective-permute-start(bf16[1536,128]{1,0:T(8,128)(2,1)S(1)} %join.1.refs_0_), channel_id=1, source_target_pairs={{0,1},{1,0},{2,3},{3,2},{4,5},{5,4},{6,7},{7,6},{8,9},{9,8},{10,11... | collective-permute-start | bytes 1179656 | tf_op jit(solution)/shard_map/ppermute | solution.py:654
  31.9 2.9 %score.5 = (f32[128,64]{1,0:T(8,128)S(1)}, f32[64,128]{1,0:T(8,128)S(1)}, f32[128,128]{1,0:T(8,128)S(1)}, s32[8,128]{1,0:T(8,128)S(1)}) custom-call(s32[1]{0:T(128)} %bitcast.3.first_s, bf16[1024,128]{1,0:T(8,128)(2,1)S(1)} %collective-permute-done.4.refs_0_.refs_6_, bf16[1040,128]{1,0:T(8,128)(2,1)S(1)} %collective-permute-done.5.refs_1_.refs_13_.refs_7_, ...), custom_call_target="tpu_custom_call" | custom-call | bytes 10800000 | tf_op jit(solution)/shard_map/score/pallas_call | solution.py:639
  34.8 2.0 %collective-permute-start.10 = (f32[64,128]{1,0:T(8,128)S(1)}, f32[64,128]{1,0:T(8,128)S(1)}, u32[]{:S(2)}, u32[]{:S(2)}) collective-permute-start(f32[64,128]{1,0:T(8,128)S(1)} %get-tuple-element.64.refs_0_), channel_id=1, source_target_pairs={{0,3},{1,2},{2,1},{3,0},{4,7},{5,6},{6,5},{7,4},{8,11},{9,10},{10,... | collective-permute-start | bytes 98312 | tf_op jit(solution)/shard_map/ppermute | solution.py:654
  37.1 1.3 %collective-permute-start.8 = (f32[64,128]{1,0:T(8,128)S(1)}, f32[64,128]{1,0:T(8,128)S(1)}, u32[]{:S(2)}, u32[]{:S(2)}) collective-permute-start(f32[64,128]{1,0:T(8,128)S(1)} %get-tuple-element.64.refs_0_), channel_id=1, source_target_pairs={{0,1},{1,0},{2,3},{3,2},{4,5},{5,4},{6,7},{7,6},{8,9},{9,8},{10,11... | collective-permute-start | bytes 98312 | tf_op jit(solution)/shard_map/ppermute | solution.py:654
  38.4 3.3 %collective-permute-done.10.refs_3_ = f32[64,128]{1,0:T(8,128)S(1)} collective-permute-done((f32[64,128]{1,0:T(8,128)S(1)}, f32[64,128]{1,0:T(8,128)S(1)}, u32[]{:S(2)}, u32[]{:S(2)}) %collective-permute-start.10) | collective-permute-done | bytes 32800 | tf_op jit(solution)/shard_map/ppermute | solution.py:654
  43.2 1.1 %collective-permute-start.12 = (bf16[768,128]{1,0:T(8,128)(2,1)S(1)}, bf16[768,128]{1,0:T(8,128)(2,1)S(1)}, u32[]{:S(2)}, u32[]{:S(2)}) collective-permute-start(bf16[768,128]{1,0:T(8,128)(2,1)S(1)} %slice.20), channel_id=1, source_target_pairs={{0,2},{1,3},{2,0},{3,1},{4,6},{5,7},{6,4},{7,5},{8,10},{9,11},{10,... | collective-permute-start | bytes 589832 | tf_op jit(solution)/shard_map/ppermute | solution.py:654
  44.3 2.1 %collective-permute-start.15 = (bf16[304,128]{1,0:T(8,128)(2,1)S(1)}, bf16[304,128]{1,0:T(8,128)(2,1)S(1)}, u32[]{:S(2)}, u32[]{:S(2)}) collective-permute-start(bf16[304,128]{1,0:T(8,128)(2,1)S(1)} %get-tuple-element.78), channel_id=1, source_target_pairs={{0,16},{4,20},{8,24},{12,28},{16,0},{20,4},{24,8},{28,12},{1,17},{... | collective-permute-start | bytes 233480 | tf_op jit(solution)/shard_map/ppermute | solution.py:654
  46.3 2.3 %collective-permute-start.16 = (bf16[304,128]{1,0:T(8,128)(2,1)S(1)}, bf16[304,128]{1,0:T(8,128)(2,1)S(1)}, u32[]{:S(2)}, u32[]{:S(2)}) collective-permute-start(bf16[304,128]{1,0:T(8,128)(2,1)S(1)} %get-tuple-element.79), channel_id=1, source_target_pairs={{0,24},{4,28},{8,16},{12,20},{16,8},{20,12},{24,0},{28,4},{1,25},{... | collective-permute-start | bytes 233480 | tf_op jit(solution)/shard_map/ppermute | solution.py:654
  48.7 2.2 %own_sum.1.refs_8_ = f32[52,2,2,8,128]{4,3,2,1,0:T(8,128)S(1)} custom-call(s32[1]{0:T(128)} %bitcast.grp_s, bf16[256,128]{1,0:T(8,128)(2,1)S(1)} %get-tuple-element.74.packed, s32[8,128]{1,0:T(8,128)S(1)} %get-tuple-element.71.refs_14_.refs_0_, s32[8,128]{1,0:T(8,128)S(1)} %get-tuple-element.72.refs_15_.refs_1_, ...), custom_call_target="tpu_custom_call" | custom-call | bytes 10800000 | tf_op jit(solution)/shard_map/own_sum/pallas_call | solution.py:639
  50.9 1.7 %collective-permute-done.16.refs_7_ = bf16[304,128]{1,0:T(8,128)(2,1)S(1)} collective-permute-done((bf16[304,128]{1,0:T(8,128)(2,1)S(1)}, bf16[304,128]{1,0:T(8,128)(2,1)S(1)}, u32[]{:S(2)}, u32[]{:S(2)}) %collective-permute-start.16) | collective-permute-done | bytes 77856 | tf_op jit(solution)/shard_map/ppermute | solution.py:654
  52.6 4.1 %sum.2 = (f32[28,16,128]{2,1,0:T(8,128)S(1)}, bf16[29,16,128]{2,1,0:T(8,128)(2,1)S(1)}, f32[8,128]{1,0:T(8,128)S(1)}, f32[8,128]{1,0:T(8,128)S(1)}, f32[2,1560,128]{2,1,0:T(8,128)S(1)}) custom-call(s32[1]{0:T(128)} %bitcast.grp_s, bf16[1536,128]{1,0:T(8,128)(2,1)S(1)} %join.1.refs_0_, bf16[1536,128]{1,0:T(8,128)(2,1)S(1)} %collective-permute-done.7.refs_1_, ...), custom_call_target="tpu_custom_call" | custom-call | bytes 10800000 | tf_op jit(solution)/shard_map/sum/pallas_call | solution.py:639
  56.7 1.3 %collective-permute-done.18.sib = bf16[29,16,128]{2,1,0:T(8,128)(2,1)S(1)} collective-permute-done((bf16[29,16,128]{2,1,0:T(8,128)(2,1)S(1)}, bf16[29,16,128]{2,1,0:T(8,128)(2,1)S(1)}, u32[]{:S(2)}, u32[]{:S(2)}) %collective-permute-start.18) | collective-permute-done | bytes 118816 | tf_op jit(solution)/shard_map/ppermute | solution.py:654
  58.3 3.4 %sum.3 = (f32[24,16,128]{2,1,0:T(8,128)S(1)}, bf16[24,16,128]{2,1,0:T(8,128)(2,1)S(1)}) custom-call(s32[1]{0:T(128)} %bitcast.grp_s, bf16[1536,128]{1,0:T(8,128)(2,1)S(1)} %join.1.refs_0_, bf16[1536,128]{1,0:T(8,128)(2,1)S(1)} %collective-permute-done.7.refs_1_, bf16[1536,128]{1,0:T(8,128)(2,1)S(1)} %collective-permute-done.11.refs_2_, ...), custom_call_target="tpu_custom_call" | custom-call | bytes 10800000 | tf_op jit(solution)/shard_map/sum/pallas_call | solution.py:639
  62.0 2.8 %collective-permute-start.21 = (bf16[28,16,128]{2,1,0:T(8,128)(2,1)S(1)}, bf16[28,16,128]{2,1,0:T(8,128)(2,1)S(1)}, u32[]{:S(2)}, u32[]{:S(2)}) collective-permute-start(bf16[28,16,128]{2,1,0:T(8,128)(2,1)S(1)} %get-tuple-element.94.refs_0_), channel_id=1, source_target_pairs={{0,8},{4,12},{8,0},{12,4},{16,24},{20,28},{24,16},{28,20},{1,9},{5... | collective-permute-start | bytes 344072 | tf_op jit(solution)/shard_map/ppermute | solution.py:654
  64.8 1.8 %collective-permute-done.22.refs_2_ = bf16[28,16,128]{2,1,0:T(8,128)(2,1)S(1)} collective-permute-done((bf16[28,16,128]{2,1,0:T(8,128)(2,1)S(1)}, bf16[28,16,128]{2,1,0:T(8,128)(2,1)S(1)}, u32[]{:S(2)}, u32[]{:S(2)}) %collective-permute-start.22) | collective-permute-done | bytes 114720 | tf_op jit(solution)/shard_map/ppermute | solution.py:654
  67.1 1.9 %collective-permute-done.21.refs_1_ = bf16[28,16,128]{2,1,0:T(8,128)(2,1)S(1)} collective-permute-done((bf16[28,16,128]{2,1,0:T(8,128)(2,1)S(1)}, bf16[28,16,128]{2,1,0:T(8,128)(2,1)S(1)}, u32[]{:S(2)}, u32[]{:S(2)}) %collective-permute-start.21) | collective-permute-done | bytes 114720 | tf_op jit(solution)/shard_map/ppermute | solution.py:654
  69.1 2.5 %collective-permute-done.23.refs_3_ = bf16[28,16,128]{2,1,0:T(8,128)(2,1)S(1)} collective-permute-done((bf16[28,16,128]{2,1,0:T(8,128)(2,1)S(1)}, bf16[28,16,128]{2,1,0:T(8,128)(2,1)S(1)}, u32[]{:S(2)}, u32[]{:S(2)}) %collective-permute-start.23) | collective-permute-done | bytes 114720 | tf_op jit(solution)/shard_map/ppermute | solution.py:654
  71.6 1.2 %collective-permute-start.20 = (bf16[24,16,128]{2,1,0:T(8,128)(2,1)S(1)}, bf16[24,16,128]{2,1,0:T(8,128)(2,1)S(1)}, u32[]{:S(2)}, u32[]{:S(2)}) collective-permute-start(bf16[24,16,128]{2,1,0:T(8,128)(2,1)S(1)} %divide.3.refs_0_), channel_id=1, source_target_pairs={{0,16},{4,20},{8,24},{12,28},{16,0},{20,4},{24,8},{28,12},{1,17},{... | collective-permute-start | bytes 294920 | tf_op jit(solution)/shard_map/ppermute | solution.py:654
  73.7 3.4 %spread.2.refs_8_ = f32[52,16384]{1,0:T(8,128)} custom-call(s32[1]{0:T(128)} %bitcast.grp_s, bf16[28,16,128]{2,1,0:T(8,128)(2,1)S(1)} %get-tuple-element.94.refs_0_, bf16[28,16,128]{2,1,0:T(8,128)(2,1)S(1)} %collective-permute-done.21.refs_1_, bf16[28,16,128]{2,1,0:T(8,128)(2,1)S(1)} %collective-permute-done.22.refs_2_, ...), custom_call_target="tpu_custom_call" | custom-call | bytes 7200000 | tf_op jit(solution)/shard_map/spread/pallas_call | solution.py:639
  77.1 2.7 %collective-permute-done.20.refs_2_ = bf16[24,16,128]{2,1,0:T(8,128)(2,1)S(1)} collective-permute-done((bf16[24,16,128]{2,1,0:T(8,128)(2,1)S(1)}, bf16[24,16,128]{2,1,0:T(8,128)(2,1)S(1)}, u32[]{:S(2)}, u32[]{:S(2)}) %collective-permute-start.20) | collective-permute-done | bytes 98336 | tf_op jit(solution)/shard_map/ppermute | solution.py:654
  81.0 3.5 %collective-permute-done.28.refs_3_ = bf16[24,16,128]{2,1,0:T(8,128)(2,1)S(1)} collective-permute-done((bf16[24,16,128]{2,1,0:T(8,128)(2,1)S(1)}, bf16[24,16,128]{2,1,0:T(8,128)(2,1)S(1)}, u32[]{:S(2)}, u32[]{:S(2)}) %collective-permute-start.28) | collective-permute-done | bytes 98336 | tf_op jit(solution)/shard_map/ppermute | solution.py:654
  85.7 1.8 %spread.3 = f32[52,16384]{1,0:T(8,128)} custom-call(s32[1]{0:T(128)} %bitcast.grp_s, bf16[24,16,128]{2,1,0:T(8,128)(2,1)S(1)} %divide.3.refs_0_, bf16[24,16,128]{2,1,0:T(8,128)(2,1)S(1)} %collective-permute-done.19.refs_1_, bf16[24,16,128]{2,1,0:T(8,128)(2,1)S(1)} %collective-permute-done.20.refs_2_, ...), custom_call_target="tpu_custom_call", output_to_operand_aliasing={{}: (9, {})} | custom-call | bytes 7200000 | tf_op jit(solution)/shard_map/spread/pallas_call | solution.py:639
  (55 shorter events, 8.0 us)
Async XLA Ops:
  2.5 16.4 %collective-permute-start.3 = (bf16[2064,128]{1,0:T(8,128)(2,1)S(1)}, bf16[2064,128]{1,0:T(8,128)(2,1)S(1)}, u32[]{:S(2)}, u32[]{:S(2)}) collective-permute-start(bf16[2064,128]{1,0:T(8,128)(2,1)S(1)} %get-tuple-element.53.refs_0_.refs_10_.refs_3_), channel_id=1, source_target_pairs={{0,2},{1,3},{2,0},{3,1},{4,6},{5,7},{6,4},{7,5},{8,10},{9,11},{10,... | collective-permute-start | bytes 1585160 | tf_op jit(solution)/shard_map/ppermute | solution.py:654
  5.6 13.9 %collective-permute-start.1 = (bf16[2064,128]{1,0:T(8,128)(2,1)S(1)}, bf16[2064,128]{1,0:T(8,128)(2,1)S(1)}, u32[]{:S(2)}, u32[]{:S(2)}) collective-permute-start(bf16[2064,128]{1,0:T(8,128)(2,1)S(1)} %get-tuple-element.53.refs_0_.refs_10_.refs_3_), channel_id=1, source_target_pairs={{0,1},{1,0},{2,3},{3,2},{4,5},{5,4},{6,7},{7,6},{8,9},{9,8},{10,11... | collective-permute-start | bytes 1585160 | tf_op jit(solution)/shard_map/ppermute | solution.py:654
  7.1 8.9 %collective-permute-start = (bf16[512,128]{1,0:T(8,128)(2,1)S(1)}, bf16[512,128]{1,0:T(8,128)(2,1)S(1)}, u32[]{:S(2)}, u32[]{:S(2)}) collective-permute-start(bf16[512,128]{1,0:T(8,128)(2,1)S(1)} %get-tuple-element.51), channel_id=1, source_target_pairs={{0,8},{4,12},{8,0},{12,4},{16,24},{20,28},{24,16},{28,20},{1,9},{5... | collective-permute-start | bytes 393224 | tf_op jit(solution)/shard_map/ppermute | solution.py:654
  8.6 10.2 %collective-permute-start.2 = (bf16[512,128]{1,0:T(8,128)(2,1)S(1)}, bf16[512,128]{1,0:T(8,128)(2,1)S(1)}, u32[]{:S(2)}, u32[]{:S(2)}) collective-permute-start(bf16[512,128]{1,0:T(8,128)(2,1)S(1)} %get-tuple-element.58), channel_id=1, source_target_pairs={{0,16},{4,20},{8,24},{12,28},{16,0},{20,4},{24,8},{28,12},{1,17},{... | collective-permute-start | bytes 393224 | tf_op jit(solution)/shard_map/ppermute | solution.py:654
  18.9 11.4 %collective-permute-start.5 = (bf16[1040,128]{1,0:T(8,128)(2,1)S(1)}, bf16[1040,128]{1,0:T(8,128)(2,1)S(1)}, u32[]{:S(2)}, u32[]{:S(2)}) collective-permute-start(bf16[1040,128]{1,0:T(8,128)(2,1)S(1)} %slice.19), channel_id=1, source_target_pairs={{0,1},{1,0},{2,3},{3,2},{4,5},{5,4},{6,7},{7,6},{8,9},{9,8},{10,11... | collective-permute-start | bytes 798728 | tf_op jit(solution)/shard_map/ppermute | solution.py:654
  19.5 10.8 %collective-permute-start.4 = (bf16[1024,128]{1,0:T(8,128)(2,1)S(1)}, bf16[1024,128]{1,0:T(8,128)(2,1)S(1)}, u32[]{:S(2)}, u32[]{:S(2)}) collective-permute-start(bf16[1024,128]{1,0:T(8,128)(2,1)S(1)} %slice.18), channel_id=1, source_target_pairs={{0,2},{1,3},{2,0},{3,1},{4,6},{5,7},{6,4},{7,5},{8,10},{9,11},{10,... | collective-permute-start | bytes 786440 | tf_op jit(solution)/shard_map/ppermute | solution.py:654
  21.0 9.3 %collective-permute-start.6 = (bf16[512,128]{1,0:T(8,128)(2,1)S(1)}, bf16[512,128]{1,0:T(8,128)(2,1)S(1)}, u32[]{:S(2)}, u32[]{:S(2)}) collective-permute-start(bf16[512,128]{1,0:T(8,128)(2,1)S(1)} %get-tuple-element.63), channel_id=1, source_target_pairs={{0,24},{4,28},{8,16},{12,20},{16,8},{20,12},{24,0},{28,4},{1,25},{... | collective-permute-start | bytes 393224 | tf_op jit(solution)/shard_map/ppermute | solution.py:654
  30.4 12.1 %collective-permute-start.11 = (bf16[1536,128]{1,0:T(8,128)(2,1)S(1)}, bf16[1536,128]{1,0:T(8,128)(2,1)S(1)}, u32[]{:S(2)}, u32[]{:S(2)}) collective-permute-start(bf16[1536,128]{1,0:T(8,128)(2,1)S(1)} %join.1.refs_0_), channel_id=1, source_target_pairs={{0,2},{1,3},{2,0},{3,1},{4,6},{5,7},{6,4},{7,5},{8,10},{9,11},{10,... | collective-permute-start | bytes 1179656 | tf_op jit(solution)/shard_map/ppermute | solution.py:654
  30.7 12.5 %collective-permute-start.7 = (bf16[1536,128]{1,0:T(8,128)(2,1)S(1)}, bf16[1536,128]{1,0:T(8,128)(2,1)S(1)}, u32[]{:S(2)}, u32[]{:S(2)}) collective-permute-start(bf16[1536,128]{1,0:T(8,128)(2,1)S(1)} %join.1.refs_0_), channel_id=1, source_target_pairs={{0,1},{1,0},{2,3},{3,2},{4,5},{5,4},{6,7},{7,6},{8,9},{9,8},{10,11... | collective-permute-start | bytes 1179656 | tf_op jit(solution)/shard_map/ppermute | solution.py:654
  34.8 6.9 %collective-permute-start.10 = (f32[64,128]{1,0:T(8,128)S(1)}, f32[64,128]{1,0:T(8,128)S(1)}, u32[]{:S(2)}, u32[]{:S(2)}) collective-permute-start(f32[64,128]{1,0:T(8,128)S(1)} %get-tuple-element.64.refs_0_), channel_id=1, source_target_pairs={{0,3},{1,2},{2,1},{3,0},{4,7},{5,6},{6,5},{7,4},{8,11},{9,10},{10,... | collective-permute-start | bytes 98312 | tf_op jit(solution)/shard_map/ppermute | solution.py:654
  36.8 4.8 %collective-permute-start.9 = (f32[64,128]{1,0:T(8,128)S(1)}, f32[64,128]{1,0:T(8,128)S(1)}, u32[]{:S(2)}, u32[]{:S(2)}) collective-permute-start(f32[64,128]{1,0:T(8,128)S(1)} %get-tuple-element.64.refs_0_), channel_id=1, source_target_pairs={{0,2},{1,3},{2,0},{3,1},{4,6},{5,7},{6,4},{7,5},{8,10},{9,11},{10,... | collective-permute-start | bytes 98312 | tf_op jit(solution)/shard_map/ppermute | solution.py:654
  37.1 4.6 %collective-permute-start.8 = (f32[64,128]{1,0:T(8,128)S(1)}, f32[64,128]{1,0:T(8,128)S(1)}, u32[]{:S(2)}, u32[]{:S(2)}) collective-permute-start(f32[64,128]{1,0:T(8,128)S(1)} %get-tuple-element.64.refs_0_), channel_id=1, source_target_pairs={{0,1},{1,0},{2,3},{3,2},{4,5},{5,4},{6,7},{7,6},{8,9},{9,8},{10,11... | collective-permute-start | bytes 98312 | tf_op jit(solution)/shard_map/ppermute | solution.py:654
  42.5 10.1 %collective-permute-start.13 = (bf16[768,128]{1,0:T(8,128)(2,1)S(1)}, bf16[768,128]{1,0:T(8,128)(2,1)S(1)}, u32[]{:S(2)}, u32[]{:S(2)}) collective-permute-start(bf16[768,128]{1,0:T(8,128)(2,1)S(1)} %slice.21), channel_id=1, source_target_pairs={{0,1},{1,0},{2,3},{3,2},{4,5},{5,4},{6,7},{7,6},{8,9},{9,8},{10,11... | collective-permute-start | bytes 589832 | tf_op jit(solution)/shard_map/ppermute | solution.py:654
  43.2 9.4 %collective-permute-start.12 = (bf16[768,128]{1,0:T(8,128)(2,1)S(1)}, bf16[768,128]{1,0:T(8,128)(2,1)S(1)}, u32[]{:S(2)}, u32[]{:S(2)}) collective-permute-start(bf16[768,128]{1,0:T(8,128)(2,1)S(1)} %slice.20), channel_id=1, source_target_pairs={{0,2},{1,3},{2,0},{3,1},{4,6},{5,7},{6,4},{7,5},{8,10},{9,11},{10,... | collective-permute-start | bytes 589832 | tf_op jit(solution)/shard_map/ppermute | solution.py:654
  44.3 6.6 %collective-permute-start.14 = (bf16[304,128]{1,0:T(8,128)(2,1)S(1)}, bf16[304,128]{1,0:T(8,128)(2,1)S(1)}, u32[]{:S(2)}, u32[]{:S(2)}) collective-permute-start(bf16[304,128]{1,0:T(8,128)(2,1)S(1)} %get-tuple-element.77), channel_id=1, source_target_pairs={{0,8},{4,12},{8,0},{12,4},{16,24},{20,28},{24,16},{28,20},{1,9},{5... | collective-permute-start | bytes 233480 | tf_op jit(solution)/shard_map/ppermute | solution.py:654
  44.3 6.6 %collective-permute-start.15 = (bf16[304,128]{1,0:T(8,128)(2,1)S(1)}, bf16[304,128]{1,0:T(8,128)(2,1)S(1)}, u32[]{:S(2)}, u32[]{:S(2)}) collective-permute-start(bf16[304,128]{1,0:T(8,128)(2,1)S(1)} %get-tuple-element.78), channel_id=1, source_target_pairs={{0,16},{4,20},{8,24},{12,28},{16,0},{20,4},{24,8},{28,12},{1,17},{... | collective-permute-start | bytes 233480 | tf_op jit(solution)/shard_map/ppermute | solution.py:654
  46.3 6.2 %collective-permute-start.16 = (bf16[304,128]{1,0:T(8,128)(2,1)S(1)}, bf16[304,128]{1,0:T(8,128)(2,1)S(1)}, u32[]{:S(2)}, u32[]{:S(2)}) collective-permute-start(bf16[304,128]{1,0:T(8,128)(2,1)S(1)} %get-tuple-element.79), channel_id=1, source_target_pairs={{0,24},{4,28},{8,16},{12,20},{16,8},{20,12},{24,0},{28,4},{1,25},{... | collective-permute-start | bytes 233480 | tf_op jit(solution)/shard_map/ppermute | solution.py:654
  56.7 1.4 %collective-permute-start.18 = (bf16[29,16,128]{2,1,0:T(8,128)(2,1)S(1)}, bf16[29,16,128]{2,1,0:T(8,128)(2,1)S(1)}, u32[]{:S(2)}, u32[]{:S(2)}) collective-permute-start(bf16[29,16,128]{2,1,0:T(8,128)(2,1)S(1)} %get-tuple-element.89), channel_id=1, source_target_pairs={{0,4},{4,0},{8,12},{12,8},{16,20},{20,16},{24,28},{28,24},{1,5},{5... | collective-permute-start | bytes 356360 | tf_op jit(solution)/shard_map/ppermute | solution.py:654
  58.3 8.3 %collective-permute-start.22 = (bf16[28,16,128]{2,1,0:T(8,128)(2,1)S(1)}, bf16[28,16,128]{2,1,0:T(8,128)(2,1)S(1)}, u32[]{:S(2)}, u32[]{:S(2)}) collective-permute-start(bf16[28,16,128]{2,1,0:T(8,128)(2,1)S(1)} %get-tuple-element.94.refs_0_), channel_id=1, source_target_pairs={{0,16},{4,20},{8,24},{12,28},{16,0},{20,4},{24,8},{28,12},{1,17},{... | collective-permute-start | bytes 344072 | tf_op jit(solution)/shard_map/ppermute | solution.py:654
  61.7 3.0 %collective-permute-start.17 = (bf16[24,16,128]{2,1,0:T(8,128)(2,1)S(1)}, bf16[24,16,128]{2,1,0:T(8,128)(2,1)S(1)}, u32[]{:S(2)}, u32[]{:S(2)}) collective-permute-start(bf16[24,16,128]{2,1,0:T(8,128)(2,1)S(1)} %get-tuple-element.87), channel_id=1, source_target_pairs={{0,4},{4,0},{8,12},{12,8},{16,20},{20,16},{24,28},{28,24},{1,5},{5... | collective-permute-start | bytes 294920 | tf_op jit(solution)/shard_map/ppermute | solution.py:654
  62.0 7.0 %collective-permute-start.21 = (bf16[28,16,128]{2,1,0:T(8,128)(2,1)S(1)}, bf16[28,16,128]{2,1,0:T(8,128)(2,1)S(1)}, u32[]{:S(2)}, u32[]{:S(2)}) collective-permute-start(bf16[28,16,128]{2,1,0:T(8,128)(2,1)S(1)} %get-tuple-element.94.refs_0_), channel_id=1, source_target_pairs={{0,8},{4,12},{8,0},{12,4},{16,24},{20,28},{24,16},{28,20},{1,9},{5... | collective-permute-start | bytes 344072 | tf_op jit(solution)/shard_map/ppermute | solution.py:654
  66.6 5.0 %collective-permute-start.23 = (bf16[28,16,128]{2,1,0:T(8,128)(2,1)S(1)}, bf16[28,16,128]{2,1,0:T(8,128)(2,1)S(1)}, u32[]{:S(2)}, u32[]{:S(2)}) collective-permute-start(bf16[28,16,128]{2,1,0:T(8,128)(2,1)S(1)} %collective-permute-done.22.refs_2_), channel_id=1, source_target_pairs={{0,8},{4,12},{8,0},{12,4},{16,24},{20,28},{24,16},{28,20},{1,9},{5... | collective-permute-start | bytes 344072 | tf_op jit(solution)/shard_map/ppermute | solution.py:654
  66.6 6.3 %collective-permute-start.24 = (bf16[28,16,128]{2,1,0:T(8,128)(2,1)S(1)}, bf16[28,16,128]{2,1,0:T(8,128)(2,1)S(1)}, u32[]{:S(2)}, u32[]{:S(2)}) collective-permute-start(bf16[28,16,128]{2,1,0:T(8,128)(2,1)S(1)} %get-tuple-element.94.refs_0_), channel_id=1, source_target_pairs={{0,4},{4,0},{8,12},{12,8},{16,20},{20,16},{24,28},{28,24},{1,5},{5... | collective-permute-start | bytes 344072 | tf_op jit(solution)/shard_map/ppermute | solution.py:654
  66.6 7.2 %collective-permute-start.26 = (bf16[28,16,128]{2,1,0:T(8,128)(2,1)S(1)}, bf16[28,16,128]{2,1,0:T(8,128)(2,1)S(1)}, u32[]{:S(2)}, u32[]{:S(2)}) collective-permute-start(bf16[28,16,128]{2,1,0:T(8,128)(2,1)S(1)} %collective-permute-done.22.refs_2_), channel_id=1, source_target_pairs={{0,4},{4,0},{8,12},{12,8},{16,20},{20,16},{24,28},{28,24},{1,5},{5... | collective-permute-start | bytes 344072 | tf_op jit(solution)/shard_map/ppermute | solution.py:654
  69.0 4.8 %collective-permute-start.25 = (bf16[28,16,128]{2,1,0:T(8,128)(2,1)S(1)}, bf16[28,16,128]{2,1,0:T(8,128)(2,1)S(1)}, u32[]{:S(2)}, u32[]{:S(2)}) collective-permute-start(bf16[28,16,128]{2,1,0:T(8,128)(2,1)S(1)} %collective-permute-done.21.refs_1_), channel_id=1, source_target_pairs={{0,4},{4,0},{8,12},{12,8},{16,20},{20,16},{24,28},{28,24},{1,5},{5... | collective-permute-start | bytes 344072 | tf_op jit(solution)/shard_map/ppermute | solution.py:654
  71.6 2.1 %collective-permute-start.27 = (bf16[28,16,128]{2,1,0:T(8,128)(2,1)S(1)}, bf16[28,16,128]{2,1,0:T(8,128)(2,1)S(1)}, u32[]{:S(2)}, u32[]{:S(2)}) collective-permute-start(bf16[28,16,128]{2,1,0:T(8,128)(2,1)S(1)} %collective-permute-done.23.refs_3_), channel_id=1, source_target_pairs={{0,4},{4,0},{8,12},{12,8},{16,20},{20,16},{24,28},{28,24},{1,5},{5... | collective-permute-start | bytes 344072 | tf_op jit(solution)/shard_map/ppermute | solution.py:654
  71.6 8.2 %collective-permute-start.20 = (bf16[24,16,128]{2,1,0:T(8,128)(2,1)S(1)}, bf16[24,16,128]{2,1,0:T(8,128)(2,1)S(1)}, u32[]{:S(2)}, u32[]{:S(2)}) collective-permute-start(bf16[24,16,128]{2,1,0:T(8,128)(2,1)S(1)} %divide.3.refs_0_), channel_id=1, source_target_pairs={{0,16},{4,20},{8,24},{12,28},{16,0},{20,4},{24,8},{28,12},{1,17},{... | collective-permute-start | bytes 294920 | tf_op jit(solution)/shard_map/ppermute | solution.py:654
  72.9 7.6 %collective-permute-start.19 = (bf16[24,16,128]{2,1,0:T(8,128)(2,1)S(1)}, bf16[24,16,128]{2,1,0:T(8,128)(2,1)S(1)}, u32[]{:S(2)}, u32[]{:S(2)}) collective-permute-start(bf16[24,16,128]{2,1,0:T(8,128)(2,1)S(1)} %divide.3.refs_0_), channel_id=1, source_target_pairs={{0,8},{4,12},{8,0},{12,4},{16,24},{20,28},{24,16},{28,20},{1,9},{5... | collective-permute-start | bytes 294920 | tf_op jit(solution)/shard_map/ppermute | solution.py:654
  79.8 4.6 %collective-permute-start.28 = (bf16[24,16,128]{2,1,0:T(8,128)(2,1)S(1)}, bf16[24,16,128]{2,1,0:T(8,128)(2,1)S(1)}, u32[]{:S(2)}, u32[]{:S(2)}) collective-permute-start(bf16[24,16,128]{2,1,0:T(8,128)(2,1)S(1)} %collective-permute-done.20.refs_2_), channel_id=1, source_target_pairs={{0,8},{4,12},{8,0},{12,4},{16,24},{20,28},{24,16},{28,20},{1,9},{5... | collective-permute-start | bytes 294920 | tf_op jit(solution)/shard_map/ppermute | solution.py:654
  80.5 4.5 %collective-permute-start.29 = (bf16[24,16,128]{2,1,0:T(8,128)(2,1)S(1)}, bf16[24,16,128]{2,1,0:T(8,128)(2,1)S(1)}, u32[]{:S(2)}, u32[]{:S(2)}) collective-permute-start(bf16[24,16,128]{2,1,0:T(8,128)(2,1)S(1)} %divide.3.refs_0_), channel_id=1, source_target_pairs={{0,4},{4,0},{8,12},{12,8},{16,20},{20,16},{24,28},{28,24},{1,5},{5... | collective-permute-start | bytes 294920 | tf_op jit(solution)/shard_map/ppermute | solution.py:654
  80.5 4.5 %collective-permute-start.30 = (bf16[24,16,128]{2,1,0:T(8,128)(2,1)S(1)}, bf16[24,16,128]{2,1,0:T(8,128)(2,1)S(1)}, u32[]{:S(2)}, u32[]{:S(2)}) collective-permute-start(bf16[24,16,128]{2,1,0:T(8,128)(2,1)S(1)} %collective-permute-done.19.refs_1_), channel_id=1, source_target_pairs={{0,4},{4,0},{8,12},{12,8},{16,20},{20,16},{24,28},{28,24},{1,5},{5... | collective-permute-start | bytes 294920 | tf_op jit(solution)/shard_map/ppermute | solution.py:654
  81.0 4.0 %collective-permute-start.31 = (bf16[24,16,128]{2,1,0:T(8,128)(2,1)S(1)}, bf16[24,16,128]{2,1,0:T(8,128)(2,1)S(1)}, u32[]{:S(2)}, u32[]{:S(2)}) collective-permute-start(bf16[24,16,128]{2,1,0:T(8,128)(2,1)S(1)} %collective-permute-done.20.refs_2_), channel_id=1, source_target_pairs={{0,4},{4,0},{8,12},{12,8},{16,20},{20,16},{24,28},{28,24},{1,5},{5... | collective-permute-start | bytes 294920 | tf_op jit(solution)/shard_map/ppermute | solution.py:654
  (1 other events, 1.3 us)

commit v4 on v3

v4 whole, which is shorter than its diff:
```python
import functools
import math

import jax
import jax.numpy as jnp
import numpy as np
from jax import lax
from jax.experimental import pallas as pl
from jax.experimental.pallas import tpu as pltpu
from jax.sharding import PartitionSpec as P

SHELLS = 64
FREQ = 128
FEAT = 16384
ROTS = 64
K = 208
CAND = 8
MOST = 2
IMG = 2 * SHELLS
UNROLL = 4
LOW = -1e30
HIGH = lax.Precision.HIGHEST
VMEM = pltpu.VMEM
SMEM = pltpu.SMEM
HBM = pltpu.HBM
F32 = jnp.float32
BF16 = jnp.bfloat16
SHAPE = jax.ShapeDtypeStruct


def tables():
    turns = np.arange(ROTS)[:, None]
    orders = np.arange(FREQ)[None, :]
    angles = ((turns * orders) % ROTS).astype(np.float32) * np.float32(2.0 * math.pi / ROTS)
    cos_tab = np.cos(angles).astype(np.float32)
    sin_tab = np.sin(angles).astype(np.float32)
    last = np.zeros((FREQ, ROTS), np.float32)
    last[:SHELLS] = -0.5
    last[SHELLS] = 1.0
    scoring = np.concatenate([cos_tab.T, sin_tab.T, last], axis=0)
    left = np.concatenate([cos_tab, sin_tab], axis=1)
    terms = []
    for _ in range(2):
        term = left.astype(jnp.bfloat16)
        left = left - term.astype(np.float32)
        blank = np.zeros_like(term)
        terms.append(np.block([[term, blank], [blank, term]]))
    return scoring, np.concatenate(terms, axis=0)


def lanes_of(shape):
    return lax.broadcasted_iota(jnp.int32, shape, len(shape) - 1)


def list_room(chunks):
    return FREQ if max(n for _, n in chunks) * MOST + UNROLL > FREQ // 2 else FREQ // 2


def list_lines(owners, chunks):
    lines = -(-owners * len(chunks) * list_room(chunks) // FREQ)
    return lines, -(-(2 * lines + 1) // 16) * 16


def list_spot(owner, chunk, chunks):
    number = owner * len(chunks) + chunk
    at = number * list_room(chunks)
    return number, quot(at, FREQ), rest(at, FREQ)


def quot(v, n):
    return v >> (n.bit_length() - 1) if n & (n - 1) == 0 else v // n


def rest(v, n):
    return v & (n - 1) if n & (n - 1) == 0 else v % n


def odd_tiles(rows):
    return (-(-rows // 8) | 1) * 8


def rounded(v):
    return v.astype(BF16).astype(F32)


def row_of(x, r, depth):
    return r // depth * 2 * depth + x * depth + r % depth


def parts_of(image, depth):
    pieces = image.reshape(image.shape[0] // (2 * depth), 2, depth, FREQ)
    return pieces[:, 0], pieces[:, 1]


def chunks_of(cls_dev):
    cut = cls_dev // 2 // 8 * 8
    return ((cut, cls_dev - cut), (0, cut)) if cut else ((0, cls_dev),)


def block_lists(named, owners, cls_dev, chunks):
    per = named.shape[0]
    pairs = per * CAND
    square = (pairs, pairs)
    wide = jnp.broadcast_to(named[:, None, :], (per, CAND, CAND)).reshape(pairs, CAND)
    own = lax.broadcasted_iota(jnp.int32, wide.shape, 0) % CAND == lanes_of(wide.shape)
    cls = jnp.broadcast_to(jnp.sum(jnp.where(own, wide, 0.0), axis=1, keepdims=True), square)
    owner = sum((cls >= o * cls_dev).astype(F32) for o in range(1, owners))
    local = cls - owner * cls_dev
    number = owner * len(chunks)
    if len(chunks) > 1:
        number = number + (local < chunks[0][0]).astype(F32)
    row = lax.broadcasted_iota(jnp.int32, square, 0)
    lane = lanes_of(square)

    def across(column):
        return jnp.sum(jnp.where(row == lane, column, 0.0), axis=0, keepdims=True)

    earlier = jnp.logical_and(number == across(number), lane < row)
    place = jnp.sum(earlier.astype(F32), axis=1, keepdims=True)
    room = list_room(chunks)
    lines, height = list_lines(owners, chunks)
    slots = lines * FREQ
    target = (number[:, :1] * room + place).astype(jnp.int32)
    hot = (target == lanes_of((pairs, slots))).astype(F32).astype(BF16)
    values = jnp.concatenate(
        [
            lanes_of((1, pairs)).astype(F32), across(local), jnp.ones((1, pairs), F32),
            jnp.zeros((5, pairs), F32),
        ],
        axis=0,
    ).astype(BF16)
    placed = jnp.dot(values, hot, preferred_element_type=F32)
    slot = lanes_of((1, slots))
    start = jnp.zeros((1, slots), F32)
    for c, (first, _) in enumerate(chunks):
        start = jnp.where(quot(slot, room) % len(chunks) == c, float(first), start)
    empty = 1.0 - placed[2:3]
    rows_line = placed[0:1] + empty * pairs
    cls_line = placed[1:2] + empty * start
    counts = jnp.sum((number == lane.astype(F32)).astype(F32), axis=0, keepdims=True)
    counts = quot(counts.astype(jnp.int32) + UNROLL - 1, UNROLL).astype(F32)
    cut = [v[:, n * FREQ : (n + 1) * FREQ] for v in (rows_line, cls_line) for n in range(lines)]
    return jnp.concatenate(
        cut + [counts, jnp.zeros((height - 2 * lines - 1, FREQ), F32)], axis=0
    )


def weigh_kernel(
    slices, owners, cls_dev, chunks, grp_s, particles_h, cand_h, groups_h, entries_h, ctf_h, prec_h, message_out, *refs
):
    slice_outs = refs[: slices - 1]
    particles, cand, groups, entries, ctf, prec, hot_g, hot_e, spread, sem = refs[slices - 1 :]
    depth = SHELLS // slices
    z = grp_s[0] // 2
    copies = [
        pltpu.make_async_copy(a, b, sem.at[n])
        for n, (a, b) in enumerate(
            (
                (groups_h, groups), (entries_h, entries), (ctf_h, ctf), (prec_h, prec),
                (cand_h, cand), (particles_h, particles),
            )
        )
    ]
    for copy in copies:
        copy.start()
    per = particles.shape[0]
    pad = spread.shape[0] // IMG
    for copy in copies[:2]:
        copy.wait()
    for i in range(per):
        hot_g[i : i + 1, :] = (lanes_of((1, hot_g.shape[1])) == groups[i]).astype(F32)
        hot_e[i : i + 1, :] = (lanes_of((1, hot_e.shape[1])) == entries[i]).astype(F32)
    for copy in copies[2:5]:
        copy.wait()
    p = jnp.dot(hot_g[...], prec[...], precision=HIGH, preferred_element_type=F32)
    c = lax.dot_general(
        hot_e[...], ctf[...], (((1,), (1,)), ((), ())), precision=HIGH, preferred_element_type=F32
    )
    eye = (lanes_of((per, per)) == lax.broadcasted_iota(jnp.int32, (per, per), 0)).astype(F32)
    named = lax.dot_general(
        eye, cand[...].astype(F32), (((1,), (1,)), ((), ())), precision=HIGH,
        preferred_element_type=F32,
    )
    factors = p * c
    extra = jnp.concatenate(
        [factors * c, named, jnp.zeros((per, FREQ - SHELLS - CAND), F32)], axis=1
    )
    message_out[per * IMG : per * (IMG + 1), :] = extra.astype(BF16)
    message_out[per * (IMG + 1) :, :] = block_lists(named, owners, cls_dev, chunks).astype(BF16)
    copies[5].wait()
    for r in range(SHELLS):
        factor = jnp.broadcast_to(factors[:, r : r + 1], (per, FREQ))
        for x in range(2):
            at = x * SHELLS + r
            piece = particles[:, at * FREQ : (at + 1) * FREQ].astype(F32) * factor
            at = row_of(x, r, depth)
            spread[at * pad : at * pad + per, :] = rounded(piece)
    rows = 2 * depth
    for i in range(per):
        message_out[i * IMG : (i + 1) * IMG, :] = spread[i : i + IMG * pad : pad, :].astype(BF16)
        for d, out in enumerate(slice_outs, start=1):
            row = pl.multiple_of(i * IMG + (z ^ d) * rows, rows)
            out[i * rows : (i + 1) * rows, :] = message_out[pl.ds(row, rows), :]


def prep_kernel(depth, grp_s, refs_h, *rest_refs):
    tables_h, (reg_h, prior), rest_refs = rest_refs[:2], rest_refs[2:4], rest_refs[4:]
    (rf_out, pow_out), tables_out, (reg_out,) = rest_refs[:2], rest_refs[2:4], rest_refs[4:5]
    refs, spread, reg, sem = rest_refs[5:]
    cls_dev = refs.shape[0]
    pad = spread.shape[0] // IMG
    parts = sem.shape[0] - 3
    step = FEAT // parts
    tables_in = [
        pltpu.make_async_copy(a, b, sem.at[parts + n])
        for n, (a, b) in enumerate(zip((*tables_h, reg_h), (*tables_out, reg)))
    ]
    copies = [
        pltpu.make_async_copy(
            refs_h.at[:, pl.ds(n * step, step)], refs.at[:, pl.ds(n * step, step)], sem.at[n]
        )
        for n in range(parts)
    ]
    turns = parts // 2
    for n in range(turns):
        copies[n].start()
        copies[n + turns].start()
    for copy in tables_in:
        copy.start()

    def shell(r, power):
        parts = []
        for x in range(2):
            at = x * SHELLS + r
            piece = refs[:, pl.ds(pl.multiple_of(at * FREQ, FREQ), FREQ)].astype(F32)
            at = row_of(x, r, depth)
            spread[pl.ds(pl.multiple_of(at * pad, 8), cls_dev), :] = piece
            parts.append(piece * piece)
        total = jnp.sum(parts[0] + parts[1], axis=1, keepdims=True)
        return jnp.where(lanes_of((cls_dev, FREQ)) == r, total, power)

    power = jnp.zeros((cls_dev, FREQ), F32)
    for n in range(turns):
        copies[n].wait()
        copies[n + turns].wait()
        low, high = n * SHELLS // turns, (n + 1) * SHELLS // turns
        power = lax.fori_loop(low, high, shell, power, unroll=4)
    line = jnp.broadcast_to(prior[...].astype(F32).reshape(1, cls_dev), (cls_dev, cls_dev))
    diagonal = lax.broadcasted_iota(jnp.int32, line.shape, 0) == lanes_of(line.shape)
    column = jnp.sum(jnp.where(diagonal, line, 0.0), axis=1, keepdims=True)
    pow_out[...] = jnp.where(lanes_of((cls_dev, FREQ)) == SHELLS, column, power)

    def image(k, _):
        rf_out[k] = spread[pl.ds(k, IMG, stride=pad), :]
        return 0

    lax.fori_loop(0, cls_dev, image, 0, unroll=4)
    for copy in tables_in:
        copy.wait()
    width = reg_out.shape[0]
    for r in range(width):
        reg_out[r : r + 1, :] = jnp.full((1, FREQ), reg[grp_s[0] * width + r], F32)


def take(refs, counts):
    taken = []
    for count in counts:
        taken.append(refs[:count])
        refs = refs[count:]
    return taken, refs


def score_kernel(arrays, earlier, depth, chunks, half, first_s, owner_s, *refs):
    blocks = len(arrays)
    messages, refs = take(refs, arrays)
    (earlier_stats,), refs = take(refs, (earlier,))
    rf, power, scoring = refs[:3]
    scores_out, stats_out, cls_out = refs[3:-6]
    ints_v, ints_s, side, ex, w32, sem = refs[-6:]
    per = side.shape[1]
    height = ints_v.shape[1]
    cls_dev = rf.shape[0]
    block_rows = per * CAND
    first = first_s[0]
    table = scoring[...]
    done = 0
    for one in earlier_stats:
        stats_out[done : done + one.shape[0], :] = one[...]
        done += one.shape[0]

    extras = []
    for b in range(blocks):
        last = messages[b][-1]
        end = last.shape[0] - height
        ints_v[b] = last[end:, :].astype(F32).astype(jnp.int32)
        extras.append(last[end - per : end, :].astype(F32))
    copies = [pltpu.make_async_copy(ints_v.at[b], ints_s.at[b], sem.at[b]) for b in range(blocks)]
    for copy in copies:
        copy.start()
    for b in range(blocks):
        lane = lanes_of((per, FREQ))
        side[b] = jnp.where(lane < SHELLS, extras[b], (lane == SHELLS).astype(F32))
        begin = 0
        for one in messages[b]:
            count = one.shape[0] // IMG

            def widen(i, _):
                w32[b * per + begin + i] = one[pl.ds(pl.multiple_of(i * IMG, IMG), IMG), :].astype(F32)
                return 0

            lax.fori_loop(0, count, widen, 0, unroll=2)
            begin += count
    for copy in copies:
        copy.wait()

    for b in range(blocks):
        for c in range(len(chunks)):
            number, line, lane = list_spot(owner_s[0], c, chunks)

            def pairs(step, _):
                for u in range(UNROLL):
                    row = ints_s[b, line, lane + step * UNROLL + u]
                    k = ints_s[b, line + half, lane + step * UNROLL + u]
                    i = jnp.minimum(quot(row, CAND), per - 1)
                    w_re, w_im = parts_of(w32[b * per + i], depth)
                    a_re, a_im = parts_of(rf[k], depth)
                    inner = (w_re * a_re + w_im * a_im).reshape(SHELLS, FREQ)
                    outer = (w_re * a_im - w_im * a_re).reshape(SHELLS, FREQ)
                    ex[0, pl.ds(row, 1), :] = jnp.sum(inner, axis=0, keepdims=True)
                    ex[1, pl.ds(row, 1), :] = jnp.sum(outer, axis=0, keepdims=True)
                    ex[2, pl.ds(row, 1), :] = side[b, pl.ds(i, 1), :] * power[pl.ds(k, 1), :]
                return 0

            lax.fori_loop(0, ints_s[b, 2 * half, number], pairs, 0)

        wide = jnp.broadcast_to(
            extras[b][:, None, :], (per, CAND, FREQ)
        ).reshape(block_rows, FREQ)
        own = lanes_of((block_rows, FREQ)) == SHELLS + (
            lax.broadcasted_iota(jnp.int32, (block_rows, FREQ), 0) % CAND
        )
        column = jnp.sum(jnp.where(own, wide, 0.0), axis=1, keepdims=True) - first.astype(F32)
        cls_out[b * block_rows : (b + 1) * block_rows, :] = jnp.broadcast_to(
            column, (block_rows, FREQ)
        )
        good = jnp.logical_and(column >= 0, column < cls_dev)
        values = jnp.zeros((block_rows, ROTS), F32)
        for part in range(3):
            values = values + jnp.dot(
                jnp.where(good, ex[part, :block_rows, :], 0.0),
                table[part * FREQ : (part + 1) * FREQ],
                precision=HIGH,
                preferred_element_type=F32,
            )
        scores = jnp.where(good, values, LOW)
        scores_out[b * block_rows : (b + 1) * block_rows, :] = scores
        top = jnp.broadcast_to(jnp.max(scores, axis=1, keepdims=True), (block_rows, ROTS))
        best = jnp.max(top.reshape(per, CAND, ROTS), axis=1)
        best_rows = jnp.broadcast_to(best[:, None, :], (per, CAND, ROTS)).reshape(block_rows, ROTS)
        mass = jnp.where(good, jnp.exp(scores - best_rows), 0.0)
        mass = jnp.broadcast_to(jnp.sum(mass, axis=1, keepdims=True), (block_rows, ROTS))
        total = jnp.sum(mass.reshape(per, CAND, ROTS), axis=1)
        stats_out[done + b * per : done + (b + 1) * per, :ROTS] = best
        stats_out[done + b * per : done + (b + 1) * per, ROTS:] = total


def two(v):
    return jnp.where(lanes_of(v.shape) < ROTS, rounded(v), v - rounded(v))


def one_of_two(v):
    return v + pltpu.roll(v, ROTS, 1)


def weights_kernel(calls, blocks, slices, cls_dev, chunks, grp_s, owner_s, *refs):
    stats = refs[:blocks]
    scores = refs[blocks : blocks + calls]
    classes = refs[blocks + calls : blocks + 2 * calls]
    extras = refs[blocks + 2 * calls : 2 * blocks + 2 * calls]
    refs = refs[2 * blocks + 2 * calls :]
    own_out, den_out, mass_out, log_out, ints_out = refs[:5]
    message_outs = refs[5:-3]
    rows_v, den_v, lists_v = refs[-3:]
    per = log_out.shape[0]
    block_rows = per * CAND
    depth = SHELLS // slices
    z = grp_s[0] // 2

    den = jnp.zeros((FREQ, FREQ), F32)
    mass = jnp.zeros((1, FREQ), F32)
    block = 0
    for scores_ref, cls_ref in zip(scores, classes):
        for b in range(scores_ref.shape[0] // block_rows):
            ones = [stats[d][(block ^ d) * per : ((block ^ d) + 1) * per, :] for d in range(blocks)]
            best = functools.reduce(jnp.maximum, [one[:, :ROTS] for one in ones])
            total = sum(one[:, ROTS:] * jnp.exp(one[:, :ROTS] - best) for one in ones)
            if block == 0:
                log_out[...] = jnp.log(total)

            def over_rows(v):
                return jnp.broadcast_to(v[:, None, :], (per, CAND, ROTS)).reshape(block_rows, ROTS)

            at = slice(b * block_rows, (b + 1) * block_rows)
            weights = jnp.exp(scores_ref[at, :] - over_rows(best)) / over_rows(total)
            local = cls_ref[at, :]
            good = jnp.logical_and(local >= 0, local < cls_dev)[:, :ROTS]
            weights = rounded(jnp.where(good, weights, 0.0))
            rows_v[block * block_rows : (block + 1) * block_rows, :] = weights
            pair_sum = jnp.sum(weights, axis=1, keepdims=True)
            twice = (lanes_of((block_rows, FREQ)) % ROTS).astype(F32)
            chosen = jnp.where(twice == local, pair_sum, 0.0)
            by_particle = jnp.sum(chosen.reshape(per, CAND, FREQ), axis=1)
            end = extras[block].shape[0] - lists_v.shape[0]
            side = extras[block][end - per : end, :].astype(F32)
            den = den + lax.dot_general(
                side, by_particle, (((0,), (0,)), ((), ())), precision=HIGH,
                preferred_element_type=F32,
            )
            mass = mass + jnp.sum(by_particle, axis=0, keepdims=True)
            block += 1

    lines = rows_v.shape[0] // 2
    packed = jnp.concatenate([rows_v[:lines, :], rows_v[lines:, :]], axis=1).astype(BF16)
    own_out[...] = packed
    den_v[...] = den[:SHELLS].reshape(slices, depth, FREQ)
    mass_rows = jnp.broadcast_to(mass, (8, FREQ))
    mass_out[...] = mass_rows
    den_out[...] = den_v[z]
    half = list_lines(blocks, chunks)[0]
    _, line, _ = list_spot(owner_s[0], 0, chunks)
    lists = []
    for one in extras:
        lists_v[...] = one[one.shape[0] - lists_v.shape[0] :, :].astype(F32)
        for at in (line, line + half, 2 * half):
            lists.append(lists_v[pl.ds(at, 1), :])
    if ints_out.shape[0] > len(lists):
        lists.append(jnp.zeros((ints_out.shape[0] - len(lists), FREQ), F32))
    lists = jnp.concatenate(lists, axis=0)
    ints_out[...] = lists.astype(jnp.int32)
    tail = [two(mass_rows), lists]
    tail_rows = depth + sum(one.shape[0] for one in tail)
    spare = message_outs[0].shape[0] - lines - tail_rows
    if spare:
        tail.append(jnp.zeros((spare, FREQ), F32))
    for d, out in enumerate(message_outs, start=1):
        out[:lines, :] = packed
        out[lines:, :] = jnp.concatenate([two(den_v[z ^ d])] + tail, axis=0).astype(BF16)


def put_phases(packed, table, wcs, base):
    lines = packed.shape[0]
    twice = jnp.concatenate([packed, packed], axis=1)
    both = rounded(jnp.dot(twice, table[...], preferred_element_type=F32))
    for place in range(2):
        for part in range(2):
            at = (2 * place + part) * FREQ
            row = base + place * lines
            wcs[part, row : row + lines, :] = both[:, at : at + FREQ]
    for part in range(2):
        wcs[part, base + 2 * lines : base + 2 * lines + 8, :] = jnp.zeros((8, FREQ), F32)


def add_pair(image, row, k, wcs, num):
    shape = num.shape[1:]
    image = image.astype(F32)
    half = image.shape[0] // 2
    w_re, w_im = image[:half].reshape(shape[1:]), image[half:].reshape(shape[1:])
    c = wcs[0, pl.ds(row, 1), :].reshape(1, 1, FREQ)
    s = wcs[1, pl.ds(row, 1), :].reshape(1, 1, FREQ)
    num[k, 0] += w_re * c - w_im * s
    num[k, 1] += w_re * s + w_im * c


def pick_image(arrays, begin, i, rows, stride, offset):
    def rows_at(one, i):
        return one[pl.ds(pl.multiple_of(i * stride + offset, rows), rows), :]

    held = [one.shape[0] // stride for one in arrays]
    while len(arrays) > 1 and begin >= held[0]:
        arrays, begin, held = arrays[1:], begin - held[0], held[1:]
    if len(arrays) == 1:
        return rows_at(arrays[0], begin + i)
    cut = held[0] - begin
    return jnp.where(
        i < cut,
        rows_at(arrays[0], begin + jnp.minimum(i, cut - 1)),
        rows_at(arrays[1], jnp.maximum(i - cut, 0)),
    )


def own_sum_kernel(chunks, arrays, grp_s, owner_s, packed, ints, *refs):
    messages, refs = take(refs, arrays)
    phases, (num, wcs, ints_s, sem) = refs[:1], refs[1:]
    copy = pltpu.make_async_copy(ints, ints_s, sem)
    copy.start()
    per = sum(one.shape[0] for one in messages[0]) // IMG
    rows = 2 * num.shape[2] * num.shape[3]
    z = grp_s[0] // 2
    put_phases(packed[...], phases[0], wcs, 0)
    num[...] = jnp.zeros_like(num)
    copy.wait()
    for block, held_in in enumerate(messages):
        base = block * per * CAND
        for c in range(len(chunks)):
            number, _, lane = list_spot(owner_s[0], c, chunks)

            def pairs(step, _):
                for u in range(UNROLL):
                    row = ints_s[3 * block, lane + step * UNROLL + u]
                    k = ints_s[3 * block + 1, lane + step * UNROLL + u]
                    i = jnp.minimum(quot(row, CAND), per - 1)
                    row = jnp.where(row == per * CAND, wcs.shape[1] - 8, base + row)
                    image = pick_image(held_in, 0, i, rows, IMG, z * rows)
                    add_pair(image, row, k, wcs, num)
                return 0

            lax.fori_loop(0, ints_s[3 * block + 2, number], pairs, 0)


def join_kernel(*refs):
    out = refs[-1]
    rows = refs[0].shape[0]
    for n, one in enumerate(refs[:-1]):
        out[n * rows : (n + 1) * rows, :] = one[...]


def sum_kernel(chunk, chunks, slices, pieces, grp_s, owner_s, *refs):
    images, refs = take(refs, pieces)
    messages, refs = refs[: slices - 1], refs[slices - 1 :]
    first, refs = refs[0], refs[1:]
    if chunk == 0:
        phases, (den_own, mass_own), refs = refs[:1], refs[1:3], refs[3:]
        own_out, sib_out, den_out, mass_out, wcs, ints_s, num, den_v, ints_v, sem = refs
    else:
        wcs, ints_s, own_out, sib_out, num = refs
    group_rows = wcs.shape[1] // (slices - 1)
    lines = (group_rows - 8) // 2
    core = grp_s[0] % 2
    start, size = chunks[chunk]
    depth = num.shape[2] * num.shape[3]
    rows = 2 * depth
    per = sum(one.shape[0] for one in images[0]) // ((slices - 1) * rows)
    if chunk == 0:
        total = ints_v.shape[1]
        for d in range(slices - 1):
            tail = messages[d][lines:, :].astype(F32)
            ints_v[d] = tail[depth + 8 : depth + 8 + total].astype(jnp.int32)
        copies = [
            pltpu.make_async_copy(ints_v.at[d], ints_s.at[d], sem.at[d]) for d in range(slices - 1)
        ]
        for copy in copies:
            copy.start()
    num[...] = first[start : start + size]
    if chunk == 0:
        den, mass = den_own[...], mass_own[...]
        for d in range(slices - 1):
            put_phases(messages[d][:lines, :], phases[0], wcs, d * group_rows)
            den = den + one_of_two(messages[d][lines:, :].astype(F32)[:depth])
            mass = mass + one_of_two(messages[d][lines:, :].astype(F32)[depth : depth + 8])
        for copy in copies:
            copy.wait()

    number, _, lane = list_spot(owner_s[0], chunk, chunks)
    for d in range(slices - 1):
        for block, held_in in enumerate(images):
            base = d * group_rows + block * per * CAND
            blank = (d + 1) * group_rows - 8

            def pairs(step, _):
                for u in range(UNROLL):
                    row = ints_s[d, 3 * block, lane + step * UNROLL + u]
                    k = ints_s[d, 3 * block + 1, lane + step * UNROLL + u]
                    i = jnp.minimum(quot(row, CAND), per - 1)
                    row = jnp.where(row == per * CAND, blank, base + row)
                    image = pick_image(held_in, d * per, i, rows, rows, 0)
                    add_pair(image, row, k - start, wcs, num)
                return 0

            lax.fori_loop(0, ints_s[d, 3 * block + 2, number], pairs, 0)

    def pack(k, _):
        own_out[k] = jnp.concatenate([num[k, 0, core], num[k, 1, core]], axis=0)
        other = jnp.concatenate([num[k, 0, 1 - core], num[k, 1, 1 - core]], axis=0)
        sib_out[k] = other.astype(BF16)
        return 0

    lax.fori_loop(0, size, pack, 0)
    if chunk == 0:
        width = num.shape[3]
        den_v[...] = den.reshape(2, width, FREQ)
        den_out[...] = den_v[core]
        mass_out[...] = mass
        sib_out[size] = jnp.concatenate([two(den_v[1 - core]), two(mass)[:width]], axis=0).astype(BF16)


def divide(own, sib, inverse, start, avg_out):
    for k in range(avg_out.shape[0]):
        column = inverse[:, start + k : start + k + 1]
        factor = jnp.concatenate([column, column], axis=0)
        avg_out[k] = ((own[k] + sib[k].astype(F32)) * factor).astype(BF16)


def first_divide_kernel(scale, start, own, sib, den, mass, reg, avg_out, share_out, inverse_out):
    cut = avg_out.shape[0]
    width = avg_out.shape[1] // 2
    tile = one_of_two(sib[cut].astype(F32))
    share_out[...] = (tile[width : width + 1] + mass[:1]) * scale
    inverse = 1.0 / (tile[:width] + den[...] + reg[...])
    inverse_out[...] = inverse
    divide(own, sib, inverse, start, avg_out)


def next_divide_kernel(start, own, sib, inverse, avg_out):
    divide(own, sib, inverse[...], start, avg_out)


def spread_kernel(planes, chunks, has_out, grp_s, *refs):
    held = 2 * len(planes) * len(chunks)
    arrays, (out, wide, columns, sem) = refs[:held], refs[held + has_out :]
    width = arrays[0].shape[1] // 2
    cls_dev = columns.shape[1]
    pad = wide.shape[0] // (len(planes) * 4 * width)
    z, h = grp_s[0] // 2, grp_s[0] % 2
    copies = []
    for n, d in enumerate(planes):
        for c, (start, cut) in enumerate(chunks):
            pair = arrays[2 * (n * len(chunks) + c) :][:2]

            def one(k, _):
                for side, array in enumerate(pair):
                    piece = array[k].astype(F32)
                    for x in range(2):
                        at = (n * 4 + side * 2 + x) * width * pad + start
                        wide[pl.ds(at + k, width, stride=pad), :] = piece[
                            x * width : (x + 1) * width
                        ]
                return 0

            lax.fori_loop(0, cut, one, 0, unroll=2)
        for side, core in enumerate((h, 1 - h)):
            for x in range(2):
                group = n * 4 + side * 2 + x
                for r in range(width):
                    at = (group * width + r) * pad
                    columns[group, :, r * FREQ : (r + 1) * FREQ] = wide[at : at + cls_dev, :]
                first = (x * SHELLS + ((z ^ d) * 2 + core) * width) * FREQ
                first = pl.multiple_of(first, width * FREQ)
                copies.append(
                    pltpu.make_async_copy(
                        columns.at[group], out.at[:, pl.ds(first, width * FREQ)], sem.at[group]
                    )
                )
                copies[-1].start()
    for copy in copies:
        copy.wait()


def whole(space):
    return pl.BlockSpec(memory_space=space)


def in_hbm(value):
    return pltpu.with_memory_space_constraint(value, HBM)


def call(kernel, name, ins, outs, scratch, mib, us, args, **more):
    cost = pl.CostEstimate(flops=0, bytes_accessed=int(us * 3.6e6), transcendentals=0)
    return pl.pallas_call(
        kernel,
        out_shape=tuple(s for s, _ in outs),
        in_specs=[whole(s) for s in ins],
        out_specs=tuple(whole(s) for _, s in outs),
        scratch_shapes=scratch,
        compiler_params=pltpu.CompilerParams(vmem_limit_bytes=mib * 2**20),
        name=name,
        cost_estimate=cost,
        **more,
    )(*args)


def swap(value, axis, distance):
    size = lax.axis_size(axis)
    return lax.ppermute(value, axis, [(i, i ^ distance) for i in range(size)])


def after(value, *others):
    return lax.optimization_barrier((value, *others))[0]


def per_device(
    particles, candidates, group_ids, ctf_ids, ctf_table, noise_prec, references, log_prior, reg
):
    n_cls = lax.axis_size("cls")
    n_grp = lax.axis_size("grp")
    per = particles.shape[0]
    cls_dev = references.shape[0]
    block_rows = per * CAND
    chunks = chunks_of(cls_dev)
    pad = odd_tiles(cls_dev)
    width = SHELLS // n_grp
    nz = n_grp // 2
    scoring, phases = (jnp.asarray(t) for t in tables())
    owner = lax.axis_index("cls").astype(jnp.int32).reshape(1)
    first = owner * cls_dev
    grp = lax.axis_index("grp").astype(jnp.int32).reshape(1)

    depth = SHELLS // nz
    message, *sliced = call(
        functools.partial(weigh_kernel, nz, n_cls, cls_dev, chunks), "weigh", [SMEM] + [HBM] * 6,
        [(SHAPE((per * (IMG + 1) + list_lines(n_cls, chunks)[1], FREQ), BF16), VMEM)]
        + [(SHAPE((per * 2 * depth, FREQ), BF16), VMEM)] * (nz - 1),
        [
            VMEM(particles.shape, BF16),
            VMEM((CAND, per), jnp.int32),
            SMEM((per,), jnp.int32),
            SMEM((per,), jnp.int32),
            VMEM(ctf_table.shape[::-1], F32),
            VMEM(noise_prec.shape, F32),
            VMEM((per, noise_prec.shape[0]), F32),
            VMEM((per, ctf_table.shape[0]), F32),
            VMEM((IMG * odd_tiles(per), FREQ), F32),
            pltpu.SemaphoreType.DMA((6,)),
        ],
        5, 2.0,
        (grp,)
        + tuple(
            in_hbm(a)
            for a in (particles, candidates.T, group_ids, ctf_ids, ctf_table.T, noise_prec)
        ),
    )

    if n_cls == 4:
        message_1, message_2 = swap(message, "cls", 1), swap(message, "cls", 2)
    sliced = [swap(one, "grp", 2 * d) for d, one in enumerate(sliced, start=1)]

    rf, power, scoring, phases, own_reg = call(
        functools.partial(prep_kernel, depth), "prep", [SMEM] + [HBM] * 4 + [VMEM],
        [(SHAPE((cls_dev, IMG, FREQ), F32), VMEM), (SHAPE((cls_dev, FREQ), F32), VMEM)]
        + [(SHAPE(t.shape, t.dtype), VMEM) for t in (scoring, phases)]
        + [(SHAPE((width, FREQ), F32), VMEM)],
        [
            VMEM(references.shape, BF16),
            VMEM((IMG * pad, FREQ), F32),
            SMEM(reg.shape, F32),
            pltpu.SemaphoreType.DMA((7,)),
        ],
        8, 4.0,
        (grp,)
        + tuple(in_hbm(a) for a in (references, scoring, phases, reg))
        + (log_prior,),
    )

    half, height = list_lines(n_cls, chunks)

    def score(part, earlier=()):
        blocks = len(part)
        flat = [m for arrays in part for m in arrays]
        earlier = tuple(s[1] for s in earlier)
        ahead = sum(s.shape[0] for s in earlier)
        counts = tuple(len(arrays) for arrays in part)
        return call(
            functools.partial(score_kernel, counts, len(earlier), depth, chunks, half), "score",
            [SMEM] * 2 + [VMEM] * (len(flat) + len(earlier) + 3),
            [
                (SHAPE((blocks * block_rows, ROTS), F32), VMEM),
                (SHAPE((ahead + blocks * per, FREQ), F32), VMEM),
                (SHAPE((blocks * block_rows, FREQ), F32), VMEM),
            ],
            [
                VMEM((blocks, height, FREQ), jnp.int32),
                SMEM((blocks, height, FREQ), jnp.int32),
                VMEM((blocks, per, FREQ), F32),
                VMEM((3, block_rows + 8, FREQ), F32),
                VMEM((blocks * per, IMG, FREQ), F32),
                pltpu.SemaphoreType.DMA((blocks,)),
            ],
            6 if n_cls == 4 else 40, 3.0 * blocks, (first, owner, *flat, *earlier, rf, power, scoring),
        )

    def join(got):
        (joined,) = call(
            join_kernel, "join", [VMEM] * (nz - 1),
            [(SHAPE(((nz - 1) * per * 2 * depth, FREQ), BF16), VMEM)], [], 2, 0.5, got,
        )
        return joined

    if n_cls == 4:
        cut = per // 2 * IMG
        scored = [score([(after(message, sliced[0]),)])]
        ready = (scored[0][1], sliced[1])
        message_1, message_2 = after(message_1, *ready), after(message_2, *ready)
        message_3 = (swap(message_1[:cut], "cls", 2), swap(message_2[cut:], "cls", 1))
        messages = [(message,), (message_1,), (message_2,), message_3]
        scored += [score(messages[1:3])]
        joined = join([after(sliced[0], scored[1][1], *message_3)] + sliced[1:])
        joined_1, joined_2 = swap(joined, "cls", 1), swap(joined, "cls", 2)
        scored += [score(messages[3:], scored)]
    else:
        messages = [(message,)] + [(swap(message, "cls", d),) for d in range(1, n_cls)]
        scored = [score(messages)]
        joined = join(sliced)
        images = [joined] + [swap(joined, "cls", d) for d in range(1, n_cls)]
        pieces = (1,) * n_cls
    arrays = tuple(len(m) for m in messages)
    stats = scored[-1][1]
    all_stats = [stats] + [swap(stats, "cls", d) for d in range(1, n_cls)]
    flat = [m for held in messages for m in held]

    lines = n_cls * block_rows // 2
    own_lists = SHAPE((-(-3 * n_cls // 8) * 8, FREQ), jnp.int32)
    outgoing_rows = -(-(lines + depth + 8 + own_lists.shape[0]) // 16) * 16
    packed, den, mass, log_mass, ints, *outgoing = call(
        functools.partial(weights_kernel, len(scored), n_cls, nz, cls_dev, chunks), "weights",
        [SMEM] * 2 + [VMEM] * (2 * n_cls + 2 * len(scored)),
        [
            (SHAPE((lines, FREQ), BF16), VMEM),
            (SHAPE((depth, FREQ), F32), VMEM),
            (SHAPE((8, FREQ), F32), VMEM),
            (SHAPE((per, ROTS), F32), VMEM),
            (own_lists, VMEM),
        ]
        + [(SHAPE((outgoing_rows, FREQ), BF16), VMEM)] * (nz - 1),
        [VMEM((2 * lines, ROTS), F32), VMEM((nz, depth, FREQ), F32), VMEM((height, FREQ), F32)],
        4 if n_cls == 4 else 12, 2.0,
        (
            grp, owner, *all_stats, *(s[0] for s in scored), *(s[2] for s in scored),
            *(held[-1] for held in messages),
        ),
    )
    incoming = [swap(one, "grp", 2 * d) for d, one in enumerate(outgoing, start=1)]
    if n_cls == 4:
        cut = joined.shape[0] // 2
        joined_1, joined_2 = after(joined_1, packed), after(joined_2, packed)
        joined_3 = [swap(joined_1[:cut], "cls", 2), swap(joined_2[cut:], "cls", 1)]
        images = [joined, joined_1, joined_2, *joined_3]
        pieces = (1, 1, 1, 2)
    (first_sums,) = call(
        functools.partial(own_sum_kernel, chunks, arrays), "own_sum",
        [SMEM] * 2 + [VMEM] * (len(flat) + 3),
        [(SHAPE((cls_dev, 2, 2, width, FREQ), F32), VMEM)],
        [
            VMEM((2, 2 * lines + 8, FREQ), F32),
            SMEM(own_lists.shape, jnp.int32),
            pltpu.SemaphoreType.DMA,
        ],
        4 if n_cls == 4 else 12, 3.0, (grp, owner, packed, ints, *flat, phases),
    )
    tile = (2 * width, FREQ)
    sums = []
    for chunk, (start, size) in enumerate(chunks):
        more = chunk == 0
        outs = [
            (SHAPE((size,) + tile, F32), VMEM),
            (SHAPE((size + more,) + tile, BF16), VMEM),
        ]
        scratch = [VMEM((size, 2, 2, width, FREQ), F32)]
        spaces = [SMEM] * 2 + [VMEM] * (sum(pieces) + nz)
        if more:
            outs += [
                (SHAPE((width, FREQ), F32), VMEM),
                (SHAPE((8, FREQ), F32), VMEM),
                (SHAPE((2, (nz - 1) * (2 * lines + 8), FREQ), F32), VMEM),
                (SHAPE((nz - 1,) + own_lists.shape, jnp.int32), SMEM),
            ]
            scratch += [
                VMEM((2, width, FREQ), F32),
                VMEM((nz - 1,) + own_lists.shape, jnp.int32),
                pltpu.SemaphoreType.DMA((nz - 1,)),
            ]
            spaces += [VMEM] * 3
            args = (grp, owner, *images, *incoming, first_sums, phases, den, mass)
        else:
            spaces += [VMEM, SMEM]
            args = (grp, owner, *images, *incoming, first_sums, wcs, lists)
        own, sib, *others = call(
            functools.partial(sum_kernel, chunk, chunks, nz, pieces), "sum",
            spaces, outs, scratch, 3 if n_cls == 4 else 24, 3.0, args,
        )
        if more:
            den, mass, wcs, lists = others
        sums.append((own, sib))

    particle_total = per * n_grp * n_cls
    divided, inverse, share = [], None, None
    for chunk, (own, sib) in enumerate(sums):
        start, cut = chunks[chunk]
        other = swap(sib, "grp", 1)
        averaged_out = (SHAPE((cut,) + tile, BF16), VMEM)
        if chunk == 0:
            averaged, share, inverse = call(
                functools.partial(first_divide_kernel, K / particle_total, start), "divide",
                [VMEM] * 5,
                [averaged_out, (SHAPE((1, FREQ), F32), VMEM), (SHAPE((width, FREQ), F32), VMEM)],
                [], 2, 0.05, (own, other, den, mass, own_reg),
            )
        else:
            (averaged,) = call(
                functools.partial(next_divide_kernel, start), "divide", [VMEM] * 3,
                [averaged_out], [], 2, 0.05, (own, other, inverse),
            )
        divided.append(averaged)

    if nz == 4:
        near = [swap(averaged, "grp", 2) for averaged in divided]
        across = [swap(averaged, "grp", 4) for averaged in divided]
        near, across = lax.optimization_barrier((near, across))
        relayed = [swap(one, "grp", 2) for one in across]
        planes = [list(held) for held in zip(divided, near, across, relayed)]
    else:
        planes = [
            [averaged] + [swap(averaged, "grp", 2 * d) for d in range(1, nz)]
            for averaged in divided
        ]
    averages = None
    for far in ((0, 1, 2), (3,)) if nz == 4 else (tuple(range(nz)),):
        arrays = []
        for d in far:
            for held in planes:
                one = held[d] if averages is None else after(held[d], averages)
                arrays += [one, swap(one, "grp", 1)]
        has_out = averages is not None
        groups = len(far) * 4
        (averages,) = call(
            functools.partial(spread_kernel, far, chunks, has_out), "spread",
            [SMEM] + [VMEM] * len(arrays) + [HBM] * has_out,
            [(SHAPE((cls_dev, FEAT), F32), HBM)],
            [
                VMEM((groups * width * odd_tiles(cls_dev), FREQ), F32),
                VMEM((groups, cls_dev, width * FREQ), F32),
                pltpu.SemaphoreType.DMA((groups,)),
            ],
            8, 0.05, (grp, *arrays) + ((averages,) if has_out else ()),
            input_output_aliases={len(arrays) + 1: 0} if has_out else {},
        )
    return (averages, share[0, :cls_dev], log_mass[:, 0])


def solution(mesh):
    return jax.shard_map(
        per_device,
        mesh=mesh,
        in_specs=(
            P(("grp", "cls"), None),
            P(("grp", "cls"), None),
            P(("grp", "cls")),
            P(("grp", "cls")),
            P(),
            P(),
            P("cls", None),
            P("cls"),
            P(),
        ),
        out_specs=(P("cls", None), P("cls"), P(("grp", "cls"))),
        check_vma=False,
    )
```

time: 87.9 us -> 83.9 us (0.954)
  Pallas kernels: 33.2 us -> 26.9 us
  starting transfers between devices: 31.9 us -> 36 us
  waiting for transfers between devices: 19.5 us -> 17.9 us
    pallas_call x14, Pallas kernels: 33.2 us -> 26.9 us  [call(): pl.pallas_call(kernel, out_shape=tuple((s for s, _ in outs)), in_specs=[w...]
    ppermute x33, starting transfers between devices: 31.9 us -> 36 us  [swap(): return lax.ppermute(value, axis, [(i, i ^ distance) for i in range(size)])]
    ppermute x33, waiting for transfers between devices: 19.5 us -> 17.9 us  [swap(): return lax.ppermute(value, axis, [(i, i ^ distance) for i in range(size)])]
  transfers between devices with their start and end apart: 33 -> 33, of which waited for: 9 -> 9; matrix products, arithmetic and copies ran while one was open for 2% -> 1% of each run, Pallas kernels for 29% -> 23%
where the time goes in v4:
time: 83.9 us; the launch traced here: 83.6 us
  starting transfers between devices  36 us (43%)
  Pallas kernels  26.9 us (32%)
  waiting for transfers between devices  17.9 us (21%)
  local copies, waits for them, and re-layouts  1.86 us (2%)
  between operations  0.86 us (1%)
    ppermute x33, starting transfers between devices, swap(): return lax.ppermute(value, axis, [(i, i ^ distance) for i in range(size)])  36 us
    pallas_call x14, Pallas kernels, call(): pl.pallas_call(kernel, out_shape=tuple((s for s, _ in outs)), in_specs=[w...  26.9 us
    ppermute x33, waiting for transfers between devices, swap(): return lax.ppermute(value, axis, [(i, i ^ distance) for i in range(size)])  17.9 us
  transfers between devices with their start and end apart: 33, of which 9 were waited for; matrix products, arithmetic and copies ran while one was open for 1% of the time, Pallas kernels for 23%

profile of v4, /device:TPU:0, one launch (start us, length us, event | category | flops | bytes accessed | tf_op | source)
XLA Modules:
  0.0 83.6 jit_solution(16185690484581323516)
XLA Ops:
  0.6 2.0 %weigh.1 = (bf16[2080,128]{1,0:T(8,128)(2,1)S(1)}, bf16[512,128]{1,0:T(8,128)(2,1)S(1)}, bf16[512,128]{1,0:T(8,128)(2,1)S(1)}, bf16[512,128]{1,0:T(8,128)(2,1)S(1)}) custom-call(s32[1]{0:T(128)} %bitcast.grp_s, bf16[16,16384]{1,0:T(8,128)(2,1)} %particles_h.1, s32[8,16]{1,0:T(8,128)} %bitcast.7, s32[16]{0:T(128)} %groups_h.1, s32[16]{0:T(128)} %entries_h.1, ...), custom_call_target="tpu_custom_call" | custom-call | bytes 7200000 | tf_op jit(solution)/shard_map/weigh/pallas_call | solution.py:668
  2.7 3.0 %collective-permute-start.3 = (bf16[2080,128]{1,0:T(8,128)(2,1)S(1)}, bf16[2080,128]{1,0:T(8,128)(2,1)S(1)}, u32[]{:S(2)}, u32[]{:S(2)}) collective-permute-start(bf16[2080,128]{1,0:T(8,128)(2,1)S(1)} %get-tuple-element.54.refs_0_.refs_10_), channel_id=1, source_target_pairs={{0,2},{1,3},{2,0},{3,1},{4,6},{5,7},{6,4},{7,5},{8,10},{9,11},{10,... | collective-permute-start | bytes 1597448 | tf_op jit(solution)/shard_map/ppermute | solution.py:683
  5.7 1.5 %collective-permute-start.1 = (bf16[2080,128]{1,0:T(8,128)(2,1)S(1)}, bf16[2080,128]{1,0:T(8,128)(2,1)S(1)}, u32[]{:S(2)}, u32[]{:S(2)}) collective-permute-start(bf16[2080,128]{1,0:T(8,128)(2,1)S(1)} %get-tuple-element.54.refs_0_.refs_10_), channel_id=1, source_target_pairs={{0,1},{1,0},{2,3},{3,2},{4,5},{5,4},{6,7},{7,6},{8,9},{9,8},{10,11... | collective-permute-start | bytes 1597448 | tf_op jit(solution)/shard_map/ppermute | solution.py:683
  7.2 1.6 %collective-permute-start = (bf16[512,128]{1,0:T(8,128)(2,1)S(1)}, bf16[512,128]{1,0:T(8,128)(2,1)S(1)}, u32[]{:S(2)}, u32[]{:S(2)}) collective-permute-start(bf16[512,128]{1,0:T(8,128)(2,1)S(1)} %get-tuple-element.52), channel_id=1, source_target_pairs={{0,8},{4,12},{8,0},{12,4},{16,24},{20,28},{24,16},{28,20},{1,9},{5... | collective-permute-start | bytes 393224 | tf_op jit(solution)/shard_map/ppermute | solution.py:683
  8.8 2.6 %collective-permute-start.2 = (bf16[512,128]{1,0:T(8,128)(2,1)S(1)}, bf16[512,128]{1,0:T(8,128)(2,1)S(1)}, u32[]{:S(2)}, u32[]{:S(2)}) collective-permute-start(bf16[512,128]{1,0:T(8,128)(2,1)S(1)} %get-tuple-element.59), channel_id=1, source_target_pairs={{0,16},{4,20},{8,24},{12,28},{16,0},{20,4},{24,8},{28,12},{1,17},{... | collective-permute-start | bytes 393224 | tf_op jit(solution)/shard_map/ppermute | solution.py:683
  12.0 3.8 %prep.1 = (f32[52,128,128]{2,1,0:T(8,128)S(1)}, f32[52,128]{1,0:T(8,128)S(1)}, f32[384,64]{1,0:T(8,128)S(1)}, bf16[256,512]{1,0:T(8,128)(2,1)S(1)}, f32[8,128]{1,0:T(8,128)S(1)}) custom-call(s32[1]{0:T(128)} %bitcast.grp_s, bf16[52,16384]{1,0:T(8,128)(2,1)} %refs_h.1, f32[384,64]{1,0:T(8,128)} %constant.15.clone.rest_refs_0_, ...), custom_call_target="tpu_custom_call" | custom-call | bytes 14400000 | tf_op jit(solution)/shard_map/prep/pallas_call | solution.py:668
  15.8 1.9 %score.3 = (f32[128,64]{1,0:T(8,128)S(1)}, f32[16,128]{1,0:T(8,128)S(1)}, f32[128,128]{1,0:T(8,128)S(1)}) custom-call(s32[1]{0:T(128)S(6)} %mul.3.first_s, s32[1]{0:T(128)} %bitcast.1.owner_s, bf16[2080,128]{1,0:T(8,128)(2,1)S(1)} %get-tuple-element.54.refs_0_.refs_10_, f32[52,128,128]{2,1,0:T(8,128)S(1)} %get-tuple-element.55.refs_1_.refs_2_.refs_4_, ...), custom_call_target="tpu_custom_call" | custom-call | bytes 10800000 | tf_op jit(solution)/shard_map/score/pallas_call | solution.py:668
  17.8 1.8 %collective-permute-start.5 = (bf16[1056,128]{1,0:T(8,128)(2,1)S(1)}, bf16[1056,128]{1,0:T(8,128)(2,1)S(1)}, u32[]{:S(2)}, u32[]{:S(2)}) collective-permute-start(bf16[1056,128]{1,0:T(8,128)(2,1)S(1)} %slice.19), channel_id=1, source_target_pairs={{0,1},{1,0},{2,3},{3,2},{4,5},{5,4},{6,7},{7,6},{8,9},{9,8},{10,11... | collective-permute-start | bytes 811016 | tf_op jit(solution)/shard_map/ppermute | solution.py:683
  19.6 1.6 %collective-permute-start.4 = (bf16[1024,128]{1,0:T(8,128)(2,1)S(1)}, bf16[1024,128]{1,0:T(8,128)(2,1)S(1)}, u32[]{:S(2)}, u32[]{:S(2)}) collective-permute-start(bf16[1024,128]{1,0:T(8,128)(2,1)S(1)} %slice.18), channel_id=1, source_target_pairs={{0,2},{1,3},{2,0},{3,1},{4,6},{5,7},{6,4},{7,5},{8,10},{9,11},{10,... | collective-permute-start | bytes 786440 | tf_op jit(solution)/shard_map/ppermute | solution.py:683
  21.2 3.6 %collective-permute-start.6 = (bf16[512,128]{1,0:T(8,128)(2,1)S(1)}, bf16[512,128]{1,0:T(8,128)(2,1)S(1)}, u32[]{:S(2)}, u32[]{:S(2)}) collective-permute-start(bf16[512,128]{1,0:T(8,128)(2,1)S(1)} %get-tuple-element.64), channel_id=1, source_target_pairs={{0,24},{4,28},{8,16},{12,20},{16,8},{20,12},{24,0},{28,4},{1,25},{... | collective-permute-start | bytes 393224 | tf_op jit(solution)/shard_map/ppermute | solution.py:683
  24.8 3.4 %score.4 = (f32[256,64]{1,0:T(8,128)S(1)}, f32[32,128]{1,0:T(8,128)S(1)}, f32[256,128]{1,0:T(8,128)S(1)}) custom-call(s32[1]{0:T(128)S(6)} %mul.3.first_s, s32[1]{0:T(128)} %bitcast.1.owner_s, bf16[2080,128]{1,0:T(8,128)(2,1)S(1)} %collective-permute-done.1.refs_0_.refs_11_.refs_1_, bf16[2080,128]{1,0:T(8,128)(2,1)S(1)} %collective-permute-done.3.refs_1_.refs_12_.refs_2_, ...), custom_call_target="tpu_custom_call" | custom-call | bytes 21600000 | tf_op jit(solution)/shard_map/score/pallas_call | solution.py:668
  29.0 1.0 %collective-permute-start.7 = (bf16[1536,128]{1,0:T(8,128)(2,1)S(1)}, bf16[1536,128]{1,0:T(8,128)(2,1)S(1)}, u32[]{:S(2)}, u32[]{:S(2)}) collective-permute-start(bf16[1536,128]{1,0:T(8,128)(2,1)S(1)} %join.1.refs_0_), channel_id=1, source_target_pairs={{0,1},{1,0},{2,3},{3,2},{4,5},{5,4},{6,7},{7,6},{8,9},{9,8},{10,11... | collective-permute-start | bytes 1179656 | tf_op jit(solution)/shard_map/ppermute | solution.py:683
  30.1 1.8 %score.5 = (f32[128,64]{1,0:T(8,128)S(1)}, f32[64,128]{1,0:T(8,128)S(1)}, f32[128,128]{1,0:T(8,128)S(1)}) custom-call(s32[1]{0:T(128)S(6)} %mul.3.first_s, s32[1]{0:T(128)} %bitcast.1.owner_s, bf16[1024,128]{1,0:T(8,128)(2,1)S(1)} %collective-permute-done.4.refs_0_.refs_3_, bf16[1056,128]{1,0:T(8,128)(2,1)S(1)} %collective-permute-done.5.refs_1_.refs_13_.refs_4_, ...), custom_call_target="tpu_custom_call" | custom-call | bytes 10800000 | tf_op jit(solution)/shard_map/score/pallas_call | solution.py:668
  31.9 2.0 %collective-permute-start.10 = (f32[64,128]{1,0:T(8,128)S(1)}, f32[64,128]{1,0:T(8,128)S(1)}, u32[]{:S(2)}, u32[]{:S(2)}) collective-permute-start(f32[64,128]{1,0:T(8,128)S(1)} %get-tuple-element.65.refs_0_), channel_id=1, source_target_pairs={{0,3},{1,2},{2,1},{3,0},{4,7},{5,6},{6,5},{7,4},{8,11},{9,10},{10,... | collective-permute-start | bytes 98312 | tf_op jit(solution)/shard_map/ppermute | solution.py:683
  34.4 1.0 %collective-permute-start.8 = (f32[64,128]{1,0:T(8,128)S(1)}, f32[64,128]{1,0:T(8,128)S(1)}, u32[]{:S(2)}, u32[]{:S(2)}) collective-permute-start(f32[64,128]{1,0:T(8,128)S(1)} %get-tuple-element.65.refs_0_), channel_id=1, source_target_pairs={{0,1},{1,0},{2,3},{3,2},{4,5},{5,4},{6,7},{7,6},{8,9},{9,8},{10,11... | collective-permute-start | bytes 98312 | tf_op jit(solution)/shard_map/ppermute | solution.py:683
  35.4 4.3 %collective-permute-done.10.refs_3_ = f32[64,128]{1,0:T(8,128)S(1)} collective-permute-done((f32[64,128]{1,0:T(8,128)S(1)}, f32[64,128]{1,0:T(8,128)S(1)}, u32[]{:S(2)}, u32[]{:S(2)}) %collective-permute-start.10) | collective-permute-done | bytes 32800 | tf_op jit(solution)/shard_map/ppermute | solution.py:683
  41.2 1.2 %collective-permute-start.12 = (bf16[768,128]{1,0:T(8,128)(2,1)S(1)}, bf16[768,128]{1,0:T(8,128)(2,1)S(1)}, u32[]{:S(2)}, u32[]{:S(2)}) collective-permute-start(bf16[768,128]{1,0:T(8,128)(2,1)S(1)} %slice.20), channel_id=1, source_target_pairs={{0,2},{1,3},{2,0},{3,1},{4,6},{5,7},{6,4},{7,5},{8,10},{9,11},{10,... | collective-permute-start | bytes 589832 | tf_op jit(solution)/shard_map/ppermute | solution.py:683
  42.8 2.9 %collective-permute-start.15 = (bf16[304,128]{1,0:T(8,128)(2,1)S(1)}, bf16[304,128]{1,0:T(8,128)(2,1)S(1)}, u32[]{:S(2)}, u32[]{:S(2)}) collective-permute-start(bf16[304,128]{1,0:T(8,128)(2,1)S(1)} %get-tuple-element.76), channel_id=1, source_target_pairs={{0,16},{4,20},{8,24},{12,28},{16,0},{20,4},{24,8},{28,12},{1,17},{... | collective-permute-start | bytes 233480 | tf_op jit(solution)/shard_map/ppermute | solution.py:683
  45.7 1.1 %collective-permute-start.16 = (bf16[304,128]{1,0:T(8,128)(2,1)S(1)}, bf16[304,128]{1,0:T(8,128)(2,1)S(1)}, u32[]{:S(2)}, u32[]{:S(2)}) collective-permute-start(bf16[304,128]{1,0:T(8,128)(2,1)S(1)} %get-tuple-element.77), channel_id=1, source_target_pairs={{0,24},{4,28},{8,16},{12,20},{16,8},{20,12},{24,0},{28,4},{1,25},{... | collective-permute-start | bytes 233480 | tf_op jit(solution)/shard_map/ppermute | solution.py:683
  46.8 2.1 %own_sum.1.refs_8_ = f32[52,2,2,8,128]{4,3,2,1,0:T(8,128)S(1)} custom-call(s32[1]{0:T(128)} %bitcast.grp_s, s32[1]{0:T(128)} %bitcast.1.owner_s, bf16[256,128]{1,0:T(8,128)(2,1)S(1)} %get-tuple-element.72.packed, s32[16,128]{1,0:T(8,128)S(1)} %get-tuple-element.78.ints, bf16[2080,128]{1,0:T(8,128)(2,1)S(1)} %get-tuple-element.54.refs_0_.refs_10_, ...), custom_call_target="tpu_custom_call" | custom-call | bytes 10800000 | tf_op jit(solution)/shard_map/own_sum/pallas_call | solution.py:668
  48.9 3.0 %collective-permute-done.16.refs_7_ = bf16[304,128]{1,0:T(8,128)(2,1)S(1)} collective-permute-done((bf16[304,128]{1,0:T(8,128)(2,1)S(1)}, bf16[304,128]{1,0:T(8,128)(2,1)S(1)}, u32[]{:S(2)}, u32[]{:S(2)}) %collective-permute-start.16) | collective-permute-done | bytes 77856 | tf_op jit(solution)/shard_map/ppermute | solution.py:683
  51.9 4.6 %sum.2 = (f32[28,16,128]{2,1,0:T(8,128)S(1)}, bf16[29,16,128]{2,1,0:T(8,128)(2,1)S(1)}, f32[8,128]{1,0:T(8,128)S(1)}, f32[8,128]{1,0:T(8,128)S(1)}, f32[2,1560,1...) custom-call(s32[1]{0:T(128)} %bitcast.grp_s, s32[1]{0:T(128)} %bitcast.1.owner_s, bf16[1536,128]{1,0:T(8,128)(2,1)S(1)} %join.1.refs_0_, ...), custom_call_target="tpu_custom_call" | custom-call | bytes 10800000 | tf_op jit(solution)/shard_map/sum/pallas_call | solution.py:668
  56.5 3.0 %sum.3 = (f32[24,16,128]{2,1,0:T(8,128)S(1)}, bf16[24,16,128]{2,1,0:T(8,128)(2,1)S(1)}) custom-call(s32[1]{0:T(128)} %bitcast.grp_s, s32[1]{0:T(128)} %bitcast.1.owner_s, bf16[1536,128]{1,0:T(8,128)(2,1)S(1)} %join.1.refs_0_, bf16[1536,128]{1,0:T(8,128)(2,1)S(1)} %collective-permute-done.7.refs_1_, bf16[1536,128]{1,0:T(8,128)(2,1)S(1)} %collective-permute-done.11.refs_2_, ...), custom_call_target="tpu_custom_call" | custom-call | bytes 10800000 | tf_op jit(solution)/shard_map/sum/pallas_call | solution.py:668
  61.2 1.0 %collective-permute-start.18 = (bf16[28,16,128]{2,1,0:T(8,128)(2,1)S(1)}, bf16[28,16,128]{2,1,0:T(8,128)(2,1)S(1)}, u32[]{:S(2)}, u32[]{:S(2)}) collective-permute-start(bf16[28,16,128]{2,1,0:T(8,128)(2,1)S(1)} %get-tuple-element.87.refs_0_), channel_id=1, source_target_pairs={{0,8},{4,12},{8,0},{12,4},{16,24},{20,28},{24,16},{28,20},{1,9},{5... | collective-permute-start | bytes 344072 | tf_op jit(solution)/shard_map/ppermute | solution.py:683
  62.3 1.3 %collective-permute-start.22 = (bf16[24,16,128]{2,1,0:T(8,128)(2,1)S(1)}, bf16[24,16,128]{2,1,0:T(8,128)(2,1)S(1)}, u32[]{:S(2)}, u32[]{:S(2)}) collective-permute-start(bf16[24,16,128]{2,1,0:T(8,128)(2,1)S(1)} %divide.3.refs_2_), channel_id=1, source_target_pairs={{0,16},{4,20},{8,24},{12,28},{16,0},{20,4},{24,8},{28,12},{1,17},{... | collective-permute-start | bytes 294920 | tf_op jit(solution)/shard_map/ppermute | solution.py:683
  63.6 2.0 %collective-permute-start.20 = (bf16[24,16,128]{2,1,0:T(8,128)(2,1)S(1)}, bf16[24,16,128]{2,1,0:T(8,128)(2,1)S(1)}, u32[]{:S(2)}, u32[]{:S(2)}) collective-permute-start(bf16[24,16,128]{2,1,0:T(8,128)(2,1)S(1)} %divide.3.refs_2_), channel_id=1, source_target_pairs={{0,8},{4,12},{8,0},{12,4},{16,24},{20,28},{24,16},{28,20},{1,9},{5... | collective-permute-start | bytes 294920 | tf_op jit(solution)/shard_map/ppermute | solution.py:683
  65.6 6.1 %collective-permute-done.22.refs_10_ = bf16[24,16,128]{2,1,0:T(8,128)(2,1)S(1)} collective-permute-done((bf16[24,16,128]{2,1,0:T(8,128)(2,1)S(1)}, bf16[24,16,128]{2,1,0:T(8,128)(2,1)S(1)}, u32[]{:S(2)}, u32[]{:S(2)}) %collective-permute-start.22) | collective-permute-done | bytes 98336 | tf_op jit(solution)/shard_map/ppermute | solution.py:683
  71.7 0.9 %collective-permute-done.20.refs_6_ = bf16[24,16,128]{2,1,0:T(8,128)(2,1)S(1)} collective-permute-done((bf16[24,16,128]{2,1,0:T(8,128)(2,1)S(1)}, bf16[24,16,128]{2,1,0:T(8,128)(2,1)S(1)}, u32[]{:S(2)}, u32[]{:S(2)}) %collective-permute-start.20) | collective-permute-done | bytes 98336 | tf_op jit(solution)/shard_map/ppermute | solution.py:683
  73.6 1.7 %collective-permute-start.31 = (bf16[24,16,128]{2,1,0:T(8,128)(2,1)S(1)}, bf16[24,16,128]{2,1,0:T(8,128)(2,1)S(1)}, u32[]{:S(2)}, u32[]{:S(2)}) collective-permute-start(bf16[24,16,128]{2,1,0:T(8,128)(2,1)S(1)} %collective-permute-done.22.refs_10_), channel_id=1, source_target_pairs={{0,8},{4,12},{8,0},{12,4},{16,24},{20,28},{24,16},{28,20},{1,9},{5... | collective-permute-start | bytes 294920 | tf_op jit(solution)/shard_map/ppermute | solution.py:683
  76.6 2.0 %spread.2.refs_4_ = f32[52,16384]{1,0:T(8,128)} custom-call(s32[1]{0:T(128)} %bitcast.grp_s, bf16[28,16,128]{2,1,0:T(8,128)(2,1)S(1)} %get-tuple-element.87.refs_0_, bf16[28,16,128]{2,1,0:T(8,128)(2,1)S(1)} %collective-permute-done.24.refs_1_, bf16[24,16,128]{2,1,0:T(8,128)(2,1)S(1)} %divide.3.refs_2_, ...), custom_call_target="tpu_custom_call" | custom-call | bytes 180000 | tf_op jit(solution)/shard_map/spread/pallas_call | solution.py:668
  78.6 2.2 %collective-permute-done.31.refs_2_ = bf16[24,16,128]{2,1,0:T(8,128)(2,1)S(1)} collective-permute-done((bf16[24,16,128]{2,1,0:T(8,128)(2,1)S(1)}, bf16[24,16,128]{2,1,0:T(8,128)(2,1)S(1)}, u32[]{:S(2)}, u32[]{:S(2)}) %collective-permute-start.31) | collective-permute-done | bytes 98336 | tf_op jit(solution)/shard_map/ppermute | solution.py:683
  82.3 1.2 %spread.3 = f32[52,16384]{1,0:T(8,128)} custom-call(s32[1]{0:T(128)} %bitcast.grp_s, bf16[28,16,128]{2,1,0:T(8,128)(2,1)S(1)} %collective-permute-done.23.refs_0_, bf16[28,16,128]{2,1,0:T(8,128)(2,1)S(1)} %collective-permute-done.30.refs_1_, bf16[24,16,128]{2,1,0:T(8,128)(2,1)S(1)} %collective-permute-done.31.refs_2_, ...), custom_call_target="tpu_custom_call", output_to_operand_aliasing={{}: (5, {})} | custom-call | bytes 180000 | tf_op jit(solution)/shard_map/spread/pallas_call | solution.py:668
  (56 shorter events, 9.5 us)
Async XLA Ops:
  2.7 15.1 %collective-permute-start.3 = (bf16[2080,128]{1,0:T(8,128)(2,1)S(1)}, bf16[2080,128]{1,0:T(8,128)(2,1)S(1)}, u32[]{:S(2)}, u32[]{:S(2)}) collective-permute-start(bf16[2080,128]{1,0:T(8,128)(2,1)S(1)} %get-tuple-element.54.refs_0_.refs_10_), channel_id=1, source_target_pairs={{0,2},{1,3},{2,0},{3,1},{4,6},{5,7},{6,4},{7,5},{8,10},{9,11},{10,... | collective-permute-start | bytes 1597448 | tf_op jit(solution)/shard_map/ppermute | solution.py:683
  5.7 13.9 %collective-permute-start.1 = (bf16[2080,128]{1,0:T(8,128)(2,1)S(1)}, bf16[2080,128]{1,0:T(8,128)(2,1)S(1)}, u32[]{:S(2)}, u32[]{:S(2)}) collective-permute-start(bf16[2080,128]{1,0:T(8,128)(2,1)S(1)} %get-tuple-element.54.refs_0_.refs_10_), channel_id=1, source_target_pairs={{0,1},{1,0},{2,3},{3,2},{4,5},{5,4},{6,7},{7,6},{8,9},{9,8},{10,11... | collective-permute-start | bytes 1597448 | tf_op jit(solution)/shard_map/ppermute | solution.py:683
  7.2 8.6 %collective-permute-start = (bf16[512,128]{1,0:T(8,128)(2,1)S(1)}, bf16[512,128]{1,0:T(8,128)(2,1)S(1)}, u32[]{:S(2)}, u32[]{:S(2)}) collective-permute-start(bf16[512,128]{1,0:T(8,128)(2,1)S(1)} %get-tuple-element.52), channel_id=1, source_target_pairs={{0,8},{4,12},{8,0},{12,4},{16,24},{20,28},{24,16},{28,20},{1,9},{5... | collective-permute-start | bytes 393224 | tf_op jit(solution)/shard_map/ppermute | solution.py:683
  8.8 8.9 %collective-permute-start.2 = (bf16[512,128]{1,0:T(8,128)(2,1)S(1)}, bf16[512,128]{1,0:T(8,128)(2,1)S(1)}, u32[]{:S(2)}, u32[]{:S(2)}) collective-permute-start(bf16[512,128]{1,0:T(8,128)(2,1)S(1)} %get-tuple-element.59), channel_id=1, source_target_pairs={{0,16},{4,20},{8,24},{12,28},{16,0},{20,4},{24,8},{28,12},{1,17},{... | collective-permute-start | bytes 393224 | tf_op jit(solution)/shard_map/ppermute | solution.py:683
  17.8 10.4 %collective-permute-start.5 = (bf16[1056,128]{1,0:T(8,128)(2,1)S(1)}, bf16[1056,128]{1,0:T(8,128)(2,1)S(1)}, u32[]{:S(2)}, u32[]{:S(2)}) collective-permute-start(bf16[1056,128]{1,0:T(8,128)(2,1)S(1)} %slice.19), channel_id=1, source_target_pairs={{0,1},{1,0},{2,3},{3,2},{4,5},{5,4},{6,7},{7,6},{8,9},{9,8},{10,11... | collective-permute-start | bytes 811016 | tf_op jit(solution)/shard_map/ppermute | solution.py:683
  19.6 8.6 %collective-permute-start.4 = (bf16[1024,128]{1,0:T(8,128)(2,1)S(1)}, bf16[1024,128]{1,0:T(8,128)(2,1)S(1)}, u32[]{:S(2)}, u32[]{:S(2)}) collective-permute-start(bf16[1024,128]{1,0:T(8,128)(2,1)S(1)} %slice.18), channel_id=1, source_target_pairs={{0,2},{1,3},{2,0},{3,1},{4,6},{5,7},{6,4},{7,5},{8,10},{9,11},{10,... | collective-permute-start | bytes 786440 | tf_op jit(solution)/shard_map/ppermute | solution.py:683
  21.2 7.0 %collective-permute-start.6 = (bf16[512,128]{1,0:T(8,128)(2,1)S(1)}, bf16[512,128]{1,0:T(8,128)(2,1)S(1)}, u32[]{:S(2)}, u32[]{:S(2)}) collective-permute-start(bf16[512,128]{1,0:T(8,128)(2,1)S(1)} %get-tuple-element.64), channel_id=1, source_target_pairs={{0,24},{4,28},{8,16},{12,20},{16,8},{20,12},{24,0},{28,4},{1,25},{... | collective-permute-start | bytes 393224 | tf_op jit(solution)/shard_map/ppermute | solution.py:683
  28.3 12.3 %collective-permute-start.11 = (bf16[1536,128]{1,0:T(8,128)(2,1)S(1)}, bf16[1536,128]{1,0:T(8,128)(2,1)S(1)}, u32[]{:S(2)}, u32[]{:S(2)}) collective-permute-start(bf16[1536,128]{1,0:T(8,128)(2,1)S(1)} %join.1.refs_0_), channel_id=1, source_target_pairs={{0,2},{1,3},{2,0},{3,1},{4,6},{5,7},{6,4},{7,5},{8,10},{9,11},{10,... | collective-permute-start | bytes 1179656 | tf_op jit(solution)/shard_map/ppermute | solution.py:683
  29.0 12.2 %collective-permute-start.7 = (bf16[1536,128]{1,0:T(8,128)(2,1)S(1)}, bf16[1536,128]{1,0:T(8,128)(2,1)S(1)}, u32[]{:S(2)}, u32[]{:S(2)}) collective-permute-start(bf16[1536,128]{1,0:T(8,128)(2,1)S(1)} %join.1.refs_0_), channel_id=1, source_target_pairs={{0,1},{1,0},{2,3},{3,2},{4,5},{5,4},{6,7},{7,6},{8,9},{9,8},{10,11... | collective-permute-start | bytes 1179656 | tf_op jit(solution)/shard_map/ppermute | solution.py:683
  31.9 7.9 %collective-permute-start.10 = (f32[64,128]{1,0:T(8,128)S(1)}, f32[64,128]{1,0:T(8,128)S(1)}, u32[]{:S(2)}, u32[]{:S(2)}) collective-permute-start(f32[64,128]{1,0:T(8,128)S(1)} %get-tuple-element.65.refs_0_), channel_id=1, source_target_pairs={{0,3},{1,2},{2,1},{3,0},{4,7},{5,6},{6,5},{7,4},{8,11},{9,10},{10,... | collective-permute-start | bytes 98312 | tf_op jit(solution)/shard_map/ppermute | solution.py:683
  33.9 5.9 %collective-permute-start.9 = (f32[64,128]{1,0:T(8,128)S(1)}, f32[64,128]{1,0:T(8,128)S(1)}, u32[]{:S(2)}, u32[]{:S(2)}) collective-permute-start(f32[64,128]{1,0:T(8,128)S(1)} %get-tuple-element.65.refs_0_), channel_id=1, source_target_pairs={{0,2},{1,3},{2,0},{3,1},{4,6},{5,7},{6,4},{7,5},{8,10},{9,11},{10,... | collective-permute-start | bytes 98312 | tf_op jit(solution)/shard_map/ppermute | solution.py:683
  34.4 5.4 %collective-permute-start.8 = (f32[64,128]{1,0:T(8,128)S(1)}, f32[64,128]{1,0:T(8,128)S(1)}, u32[]{:S(2)}, u32[]{:S(2)}) collective-permute-start(f32[64,128]{1,0:T(8,128)S(1)} %get-tuple-element.65.refs_0_), channel_id=1, source_target_pairs={{0,1},{1,0},{2,3},{3,2},{4,5},{5,4},{6,7},{7,6},{8,9},{9,8},{10,11... | collective-permute-start | bytes 98312 | tf_op jit(solution)/shard_map/ppermute | solution.py:683
  40.6 11.3 %collective-permute-start.13 = (bf16[768,128]{1,0:T(8,128)(2,1)S(1)}, bf16[768,128]{1,0:T(8,128)(2,1)S(1)}, u32[]{:S(2)}, u32[]{:S(2)}) collective-permute-start(bf16[768,128]{1,0:T(8,128)(2,1)S(1)} %slice.21), channel_id=1, source_target_pairs={{0,1},{1,0},{2,3},{3,2},{4,5},{5,4},{6,7},{7,6},{8,9},{9,8},{10,11... | collective-permute-start | bytes 589832 | tf_op jit(solution)/shard_map/ppermute | solution.py:683
  41.2 10.7 %collective-permute-start.12 = (bf16[768,128]{1,0:T(8,128)(2,1)S(1)}, bf16[768,128]{1,0:T(8,128)(2,1)S(1)}, u32[]{:S(2)}, u32[]{:S(2)}) collective-permute-start(bf16[768,128]{1,0:T(8,128)(2,1)S(1)} %slice.20), channel_id=1, source_target_pairs={{0,2},{1,3},{2,0},{3,1},{4,6},{5,7},{6,4},{7,5},{8,10},{9,11},{10,... | collective-permute-start | bytes 589832 | tf_op jit(solution)/shard_map/ppermute | solution.py:683
  42.4 6.5 %collective-permute-start.14 = (bf16[304,128]{1,0:T(8,128)(2,1)S(1)}, bf16[304,128]{1,0:T(8,128)(2,1)S(1)}, u32[]{:S(2)}, u32[]{:S(2)}) collective-permute-start(bf16[304,128]{1,0:T(8,128)(2,1)S(1)} %get-tuple-element.75), channel_id=1, source_target_pairs={{0,8},{4,12},{8,0},{12,4},{16,24},{20,28},{24,16},{28,20},{1,9},{5... | collective-permute-start | bytes 233480 | tf_op jit(solution)/shard_map/ppermute | solution.py:683
  42.8 6.0 %collective-permute-start.15 = (bf16[304,128]{1,0:T(8,128)(2,1)S(1)}, bf16[304,128]{1,0:T(8,128)(2,1)S(1)}, u32[]{:S(2)}, u32[]{:S(2)}) collective-permute-start(bf16[304,128]{1,0:T(8,128)(2,1)S(1)} %get-tuple-element.76), channel_id=1, source_target_pairs={{0,16},{4,20},{8,24},{12,28},{16,0},{20,4},{24,8},{28,12},{1,17},{... | collective-permute-start | bytes 233480 | tf_op jit(solution)/shard_map/ppermute | solution.py:683
  45.7 6.2 %collective-permute-start.16 = (bf16[304,128]{1,0:T(8,128)(2,1)S(1)}, bf16[304,128]{1,0:T(8,128)(2,1)S(1)}, u32[]{:S(2)}, u32[]{:S(2)}) collective-permute-start(bf16[304,128]{1,0:T(8,128)(2,1)S(1)} %get-tuple-element.77), channel_id=1, source_target_pairs={{0,24},{4,28},{8,16},{12,20},{16,8},{20,12},{24,0},{28,4},{1,25},{... | collective-permute-start | bytes 233480 | tf_op jit(solution)/shard_map/ppermute | solution.py:683
  56.5 3.7 %collective-permute-start.17 = (bf16[29,16,128]{2,1,0:T(8,128)(2,1)S(1)}, bf16[29,16,128]{2,1,0:T(8,128)(2,1)S(1)}, u32[]{:S(2)}, u32[]{:S(2)}) collective-permute-start(bf16[29,16,128]{2,1,0:T(8,128)(2,1)S(1)} %get-tuple-element.83), channel_id=1, source_target_pairs={{0,4},{4,0},{8,12},{12,8},{16,20},{20,16},{24,28},{28,24},{1,5},{5... | collective-permute-start | bytes 356360 | tf_op jit(solution)/shard_map/ppermute | solution.py:683
  59.6 2.6 %collective-permute-start.19 = (bf16[24,16,128]{2,1,0:T(8,128)(2,1)S(1)}, bf16[24,16,128]{2,1,0:T(8,128)(2,1)S(1)}, u32[]{:S(2)}, u32[]{:S(2)}) collective-permute-start(bf16[24,16,128]{2,1,0:T(8,128)(2,1)S(1)} %get-tuple-element.91), channel_id=1, source_target_pairs={{0,4},{4,0},{8,12},{12,8},{16,20},{20,16},{24,28},{28,24},{1,5},{5... | collective-permute-start | bytes 294920 | tf_op jit(solution)/shard_map/ppermute | solution.py:683
  60.4 12.3 %collective-permute-start.21 = (bf16[28,16,128]{2,1,0:T(8,128)(2,1)S(1)}, bf16[28,16,128]{2,1,0:T(8,128)(2,1)S(1)}, u32[]{:S(2)}, u32[]{:S(2)}) collective-permute-start(bf16[28,16,128]{2,1,0:T(8,128)(2,1)S(1)} %get-tuple-element.87.refs_0_), channel_id=1, source_target_pairs={{0,16},{4,20},{8,24},{12,28},{16,0},{20,4},{24,8},{28,12},{1,17},{... | collective-permute-start | bytes 344072 | tf_op jit(solution)/shard_map/ppermute | solution.py:683
  61.2 11.5 %collective-permute-start.18 = (bf16[28,16,128]{2,1,0:T(8,128)(2,1)S(1)}, bf16[28,16,128]{2,1,0:T(8,128)(2,1)S(1)}, u32[]{:S(2)}, u32[]{:S(2)}) collective-permute-start(bf16[28,16,128]{2,1,0:T(8,128)(2,1)S(1)} %get-tuple-element.87.refs_0_), channel_id=1, source_target_pairs={{0,8},{4,12},{8,0},{12,4},{16,24},{20,28},{24,16},{28,20},{1,9},{5... | collective-permute-start | bytes 344072 | tf_op jit(solution)/shard_map/ppermute | solution.py:683
  62.3 9.4 %collective-permute-start.22 = (bf16[24,16,128]{2,1,0:T(8,128)(2,1)S(1)}, bf16[24,16,128]{2,1,0:T(8,128)(2,1)S(1)}, u32[]{:S(2)}, u32[]{:S(2)}) collective-permute-start(bf16[24,16,128]{2,1,0:T(8,128)(2,1)S(1)} %divide.3.refs_2_), channel_id=1, source_target_pairs={{0,16},{4,20},{8,24},{12,28},{16,0},{20,4},{24,8},{28,12},{1,17},{... | collective-permute-start | bytes 294920 | tf_op jit(solution)/shard_map/ppermute | solution.py:683
  63.6 9.1 %collective-permute-start.20 = (bf16[24,16,128]{2,1,0:T(8,128)(2,1)S(1)}, bf16[24,16,128]{2,1,0:T(8,128)(2,1)S(1)}, u32[]{:S(2)}, u32[]{:S(2)}) collective-permute-start(bf16[24,16,128]{2,1,0:T(8,128)(2,1)S(1)} %divide.3.refs_2_), channel_id=1, source_target_pairs={{0,8},{4,12},{8,0},{12,4},{16,24},{20,28},{24,16},{28,20},{1,9},{5... | collective-permute-start | bytes 294920 | tf_op jit(solution)/shard_map/ppermute | solution.py:683
  65.6 8.0 %collective-permute-start.24 = (bf16[28,16,128]{2,1,0:T(8,128)(2,1)S(1)}, bf16[28,16,128]{2,1,0:T(8,128)(2,1)S(1)}, u32[]{:S(2)}, u32[]{:S(2)}) collective-permute-start(bf16[28,16,128]{2,1,0:T(8,128)(2,1)S(1)} %get-tuple-element.87.refs_0_), channel_id=1, source_target_pairs={{0,4},{4,0},{8,12},{12,8},{16,20},{20,16},{24,28},{28,24},{1,5},{5... | collective-permute-start | bytes 344072 | tf_op jit(solution)/shard_map/ppermute | solution.py:683
  71.7 1.5 %collective-permute-start.25 = (bf16[24,16,128]{2,1,0:T(8,128)(2,1)S(1)}, bf16[24,16,128]{2,1,0:T(8,128)(2,1)S(1)}, u32[]{:S(2)}, u32[]{:S(2)}) collective-permute-start(bf16[24,16,128]{2,1,0:T(8,128)(2,1)S(1)} %divide.3.refs_2_), channel_id=1, source_target_pairs={{0,4},{4,0},{8,12},{12,8},{16,20},{20,16},{24,28},{28,24},{1,5},{5... | collective-permute-start | bytes 294920 | tf_op jit(solution)/shard_map/ppermute | solution.py:683
  72.7 2.6 %collective-permute-start.27 = (bf16[24,16,128]{2,1,0:T(8,128)(2,1)S(1)}, bf16[24,16,128]{2,1,0:T(8,128)(2,1)S(1)}, u32[]{:S(2)}, u32[]{:S(2)}) collective-permute-start(bf16[24,16,128]{2,1,0:T(8,128)(2,1)S(1)} %collective-permute-done.20.refs_6_), channel_id=1, source_target_pairs={{0,4},{4,0},{8,12},{12,8},{16,20},{20,16},{24,28},{28,24},{1,5},{5... | collective-permute-start | bytes 294920 | tf_op jit(solution)/shard_map/ppermute | solution.py:683
  72.7 3.9 %collective-permute-start.26 = (bf16[28,16,128]{2,1,0:T(8,128)(2,1)S(1)}, bf16[28,16,128]{2,1,0:T(8,128)(2,1)S(1)}, u32[]{:S(2)}, u32[]{:S(2)}) collective-permute-start(bf16[28,16,128]{2,1,0:T(8,128)(2,1)S(1)} %collective-permute-done.18.refs_4_), channel_id=1, source_target_pairs={{0,4},{4,0},{8,12},{12,8},{16,20},{20,16},{24,28},{28,24},{1,5},{5... | collective-permute-start | bytes 344072 | tf_op jit(solution)/shard_map/ppermute | solution.py:683
  73.2 3.4 %collective-permute-start.28 = (bf16[28,16,128]{2,1,0:T(8,128)(2,1)S(1)}, bf16[28,16,128]{2,1,0:T(8,128)(2,1)S(1)}, u32[]{:S(2)}, u32[]{:S(2)}) collective-permute-start(bf16[28,16,128]{2,1,0:T(8,128)(2,1)S(1)} %collective-permute-done.21.refs_8_), channel_id=1, source_target_pairs={{0,4},{4,0},{8,12},{12,8},{16,20},{20,16},{24,28},{28,24},{1,5},{5... | collective-permute-start | bytes 344072 | tf_op jit(solution)/shard_map/ppermute | solution.py:683
  73.3 7.6 %collective-permute-start.23 = (bf16[28,16,128]{2,1,0:T(8,128)(2,1)S(1)}, bf16[28,16,128]{2,1,0:T(8,128)(2,1)S(1)}, u32[]{:S(2)}, u32[]{:S(2)}) collective-permute-start(bf16[28,16,128]{2,1,0:T(8,128)(2,1)S(1)} %collective-permute-done.21.refs_8_), channel_id=1, source_target_pairs={{0,8},{4,12},{8,0},{12,4},{16,24},{20,28},{24,16},{28,20},{1,9},{5... | collective-permute-start | bytes 344072 | tf_op jit(solution)/shard_map/ppermute | solution.py:683
  73.6 7.3 %collective-permute-start.31 = (bf16[24,16,128]{2,1,0:T(8,128)(2,1)S(1)}, bf16[24,16,128]{2,1,0:T(8,128)(2,1)S(1)}, u32[]{:S(2)}, u32[]{:S(2)}) collective-permute-start(bf16[24,16,128]{2,1,0:T(8,128)(2,1)S(1)} %collective-permute-done.22.refs_10_), channel_id=1, source_target_pairs={{0,8},{4,12},{8,0},{12,4},{16,24},{20,28},{24,16},{28,20},{1,9},{5... | collective-permute-start | bytes 294920 | tf_op jit(solution)/shard_map/ppermute | solution.py:683
  80.9 1.3 %collective-permute-start.32 = (bf16[24,16,128]{2,1,0:T(8,128)(2,1)S(1)}, bf16[24,16,128]{2,1,0:T(8,128)(2,1)S(1)}, u32[]{:S(2)}, u32[]{:S(2)}) collective-permute-start(bf16[24,16,128]{2,1,0:T(8,128)(2,1)S(1)} %collective-permute-done.31.refs_2_), channel_id=1, source_target_pairs={{0,4},{4,0},{8,12},{12,8},{16,20},{20,16},{24,28},{28,24},{1,5},{5... | collective-permute-start | bytes 294920 | tf_op jit(solution)/shard_map/ppermute | solution.py:683
  80.9 1.5 %collective-permute-start.30 = (bf16[28,16,128]{2,1,0:T(8,128)(2,1)S(1)}, bf16[28,16,128]{2,1,0:T(8,128)(2,1)S(1)}, u32[]{:S(2)}, u32[]{:S(2)}) collective-permute-start(bf16[28,16,128]{2,1,0:T(8,128)(2,1)S(1)} %collective-permute-done.23.refs_0_), channel_id=1, source_target_pairs={{0,4},{4,0},{8,12},{12,8},{16,20},{20,16},{24,28},{28,24},{1,5},{5... | collective-permute-start | bytes 344072 | tf_op jit(solution)/shard_map/ppermute | solution.py:683
  (2 other events, 2.0 us)

commit v5 on v4

--- a/solution.py
+++ b/solution.py
@@ -524,59 +524,86 @@
         out[n * rows : (n + 1) * rows, :] = one[...]
 
 
+def read_tail(message, lines, depth, count):
+    tail = message[lines:, :].astype(F32)
+    den, mass = one_of_two(tail[:depth]), one_of_two(tail[depth : depth + 8])
+    return den, mass, tail[depth + 8 : depth + 8 + count].astype(jnp.int32)
+
+
+def add_plane(d, chunk, chunks, owner, images, ints, base, blank, wcs, num, first_class):
+    number, _, lane = list_spot(owner, chunk, chunks)
+    rows = 2 * num.shape[2] * num.shape[3]
+    per = FREQ // CAND
+    for block, held_in in enumerate(images):
+
+        def pairs(step, _):
+            for u in range(UNROLL):
+                row = ints[3 * block, lane + step * UNROLL + u]
+                k = ints[3 * block + 1, lane + step * UNROLL + u]
+                i = jnp.minimum(quot(row, CAND), per - 1)
+                row = jnp.where(row == per * CAND, blank, base + block * per * CAND + row)
+                image = pick_image(held_in, d * per, i, rows, rows, 0)
+                add_pair(image, row, k - first_class, wcs, num)
+            return 0
+
+        lax.fori_loop(0, ints[3 * block + 2, number], pairs, 0)
+
+
+def near_sum_kernel(chunks, pieces, owner_s, *refs):
+    images, refs = take(refs, pieces)
+    message, first, phases, den_in, mass_in, num, den_out, mass_out, wcs, ints_v, ints_s, sem = refs
+    lines = (wcs.shape[1] - 8) // 2
+    depth = den_in.shape[0]
+    den, mass, ints_v[...] = read_tail(message, lines, depth, ints_v.shape[0])
+    copy = pltpu.make_async_copy(ints_v, ints_s, sem)
+    copy.start()
+    den_out[...] = den_in[...] + den
+    mass_out[...] = mass_in[...] + mass
+    put_phases(message[:lines, :], phases, wcs, 0)
+    num[...] = first[...]
+    copy.wait()
+    for chunk in range(len(chunks)):
+        add_plane(0, chunk, chunks, owner_s[0], images, ints_s, 0, 2 * lines, wcs, num, 0)
+
+
 def sum_kernel(chunk, chunks, slices, pieces, grp_s, owner_s, *refs):
     images, refs = take(refs, pieces)
-    messages, refs = refs[: slices - 1], refs[slices - 1 :]
+    messages, refs = refs[: slices - 2], refs[slices - 2 :]
     first, refs = refs[0], refs[1:]
     if chunk == 0:
-        phases, (den_own, mass_own), refs = refs[:1], refs[1:3], refs[3:]
+        phases, (den_in, mass_in), refs = refs[0], refs[1:3], refs[3:]
         own_out, sib_out, den_out, mass_out, wcs, ints_s, num, den_v, ints_v, sem = refs
     else:
         wcs, ints_s, own_out, sib_out, num = refs
-    group_rows = wcs.shape[1] // (slices - 1)
+    group_rows = wcs.shape[1] // (slices - 2)
     lines = (group_rows - 8) // 2
     core = grp_s[0] % 2
     start, size = chunks[chunk]
     depth = num.shape[2] * num.shape[3]
-    rows = 2 * depth
-    per = sum(one.shape[0] for one in images[0]) // ((slices - 1) * rows)
+
     if chunk == 0:
-        total = ints_v.shape[1]
-        for d in range(slices - 1):
-            tail = messages[d][lines:, :].astype(F32)
-            ints_v[d] = tail[depth + 8 : depth + 8 + total].astype(jnp.int32)
+        den, mass = den_in[...], mass_in[...]
+        for n, message in enumerate(messages):
+            more_den, more_mass, ints_v[n] = read_tail(message, lines, depth, ints_v.shape[1])
+            den, mass = den + more_den, mass + more_mass
         copies = [
-            pltpu.make_async_copy(ints_v.at[d], ints_s.at[d], sem.at[d]) for d in range(slices - 1)
+            pltpu.make_async_copy(ints_v.at[n], ints_s.at[n], sem.at[n])
+            for n in range(slices - 2)
         ]
         for copy in copies:
             copy.start()
+        for n, message in enumerate(messages):
+            put_phases(message[:lines, :], phases, wcs, n * group_rows)
     num[...] = first[start : start + size]
     if chunk == 0:
-        den, mass = den_own[...], mass_own[...]
-        for d in range(slices - 1):
-            put_phases(messages[d][:lines, :], phases[0], wcs, d * group_rows)
-            den = den + one_of_two(messages[d][lines:, :].astype(F32)[:depth])
-            mass = mass + one_of_two(messages[d][lines:, :].astype(F32)[depth : depth + 8])
         for copy in copies:
             copy.wait()
-
-    number, _, lane = list_spot(owner_s[0], chunk, chunks)
-    for d in range(slices - 1):
-        for block, held_in in enumerate(images):
-            base = d * group_rows + block * per * CAND
-            blank = (d + 1) * group_rows - 8
-
-            def pairs(step, _):
-                for u in range(UNROLL):
-                    row = ints_s[d, 3 * block, lane + step * UNROLL + u]
-                    k = ints_s[d, 3 * block + 1, lane + step * UNROLL + u]
-                    i = jnp.minimum(quot(row, CAND), per - 1)
-                    row = jnp.where(row == per * CAND, blank, base + row)
-                    image = pick_image(held_in, d * per, i, rows, rows, 0)
-                    add_pair(image, row, k - start, wcs, num)
-                return 0
-
-            lax.fori_loop(0, ints_s[d, 3 * block + 2, number], pairs, 0)
+    for n in range(slices - 2):
+        base = n * group_rows
+        blank = base + group_rows - 8
+        add_plane(
+            n + 1, chunk, chunks, owner_s[0], images, ints_s.at[n], base, blank, wcs, num, start
+        )
 
     def pack(k, _):
         own_out[k] = jnp.concatenate([num[k, 0, core], num[k, 1, core]], axis=0)
@@ -845,6 +872,23 @@
         ],
         4 if n_cls == 4 else 12, 3.0, (grp, owner, packed, ints, *flat, phases),
     )
+    (near_sums, den, mass) = call(
+        functools.partial(near_sum_kernel, chunks, pieces), "near_sum",
+        [SMEM] + [VMEM] * (sum(pieces) + 5),
+        [
+            (SHAPE((cls_dev, 2, 2, width, FREQ), F32), VMEM),
+            (SHAPE((depth, FREQ), F32), VMEM),
+            (SHAPE((8, FREQ), F32), VMEM),
+        ],
+        [
+            VMEM((2, 2 * lines + 8, FREQ), F32),
+            VMEM(own_lists.shape, jnp.int32),
+            SMEM(own_lists.shape, jnp.int32),
+            pltpu.SemaphoreType.DMA,
+        ],
+        4 if n_cls == 4 else 12, 2.0,
+        (owner, *images, incoming[0], first_sums, phases, den, mass),
+    )
     tile = (2 * width, FREQ)
     sums = []
     for chunk, (start, size) in enumerate(chunks):
@@ -854,24 +898,24 @@
             (SHAPE((size + more,) + tile, BF16), VMEM),
         ]
         scratch = [VMEM((size, 2, 2, width, FREQ), F32)]
-        spaces = [SMEM] * 2 + [VMEM] * (sum(pieces) + nz)
+        spaces = [SMEM] * 2 + [VMEM] * (sum(pieces) + nz - 1)
         if more:
             outs += [
                 (SHAPE((width, FREQ), F32), VMEM),
                 (SHAPE((8, FREQ), F32), VMEM),
-                (SHAPE((2, (nz - 1) * (2 * lines + 8), FREQ), F32), VMEM),
-                (SHAPE((nz - 1,) + own_lists.shape, jnp.int32), SMEM),
+                (SHAPE((2, (nz - 2) * (2 * lines + 8), FREQ), F32), VMEM),
+                (SHAPE((nz - 2,) + own_lists.shape, jnp.int32), SMEM),
             ]
             scratch += [
                 VMEM((2, width, FREQ), F32),
-                VMEM((nz - 1,) + own_lists.shape, jnp.int32),
-                pltpu.SemaphoreType.DMA((nz - 1,)),
+                VMEM((nz - 2,) + own_lists.shape, jnp.int32),
+                pltpu.SemaphoreType.DMA((nz - 2,)),
             ]
             spaces += [VMEM] * 3
-            args = (grp, owner, *images, *incoming, first_sums, phases, den, mass)
+            args = (grp, owner, *images, *incoming[1:], near_sums, phases, den, mass)
         else:
             spaces += [VMEM, SMEM]
-            args = (grp, owner, *images, *incoming, first_sums, wcs, lists)
+            args = (grp, owner, *images, *incoming[1:], near_sums, wcs, lists)
         own, sib, *others = call(
             functools.partial(sum_kernel, chunk, chunks, nz, pieces), "sum",
             spaces, outs, scratch, 3 if n_cls == 4 else 24, 3.0, args,

time: 83.9 us -> 82.1 us (0.979)
  waiting for transfers between devices: 17.9 us -> 15.7 us
    ppermute x33, waiting for transfers between devices: 17.9 us -> 15.7 us  [swap(): return lax.ppermute(value, axis, [(i, i ^ distance) for i in range(size)])]
    pallas_call x14 -> x15, Pallas kernels: 26.9 us -> 27.5 us  [call(): pl.pallas_call(kernel, out_shape=tuple((s for s, _ in outs)), in_specs=[w...]
  transfers between devices with their start and end apart: 33 -> 33, of which waited for: 9 -> 10; matrix products, arithmetic and copies ran while one was open for 1% -> 1% of each run, Pallas kernels for 23% -> 25%
where the time goes in v5:
time: 82.1 us
  starting transfers between devices  36.2 us (44%)
  Pallas kernels  27.5 us (33%)
  waiting for transfers between devices  15.7 us (19%)
  local copies, waits for them, and re-layouts  1.86 us (2%)
  between operations  0.87 us (1%)
    ppermute x33, starting transfers between devices, swap(): return lax.ppermute(value, axis, [(i, i ^ distance) for i in range(size)])  36.2 us
    pallas_call x15, Pallas kernels, call(): pl.pallas_call(kernel, out_shape=tuple((s for s, _ in outs)), in_specs=[w...  27.5 us
    ppermute x33, waiting for transfers between devices, swap(): return lax.ppermute(value, axis, [(i, i ^ distance) for i in range(size)])  15.7 us
  transfers between devices with their start and end apart: 33, of which 10 were waited for; matrix products, arithmetic and copies ran while one was open for 1% of the time, Pallas kernels for 25%

profile of v5, /device:TPU:0, one launch (start us, length us, event | category | flops | bytes accessed | tf_op | source)
XLA Modules:
  0.0 82.1 jit_solution(9210841682589083864)
XLA Ops:
  0.6 2.0 %weigh.1 = (bf16[2080,128]{1,0:T(8,128)(2,1)S(1)}, bf16[512,128]{1,0:T(8,128)(2,1)S(1)}, bf16[512,128]{1,0:T(8,128)(2,1)S(1)}, bf16[512,128]{1,0:T(8,128)(2,1)S(1)}) custom-call(s32[1]{0:T(128)} %bitcast.grp_s, bf16[16,16384]{1,0:T(8,128)(2,1)} %particles_h.1, s32[8,16]{1,0:T(8,128)} %bitcast.7, s32[16]{0:T(128)} %groups_h.1, s32[16]{0:T(128)} %entries_h.1, ...), custom_call_target="tpu_custom_call" | custom-call | bytes 7200000 | tf_op jit(solution)/shard_map/weigh/pallas_call | solution.py:695
  2.7 3.0 %collective-permute-start.3 = (bf16[2080,128]{1,0:T(8,128)(2,1)S(1)}, bf16[2080,128]{1,0:T(8,128)(2,1)S(1)}, u32[]{:S(2)}, u32[]{:S(2)}) collective-permute-start(bf16[2080,128]{1,0:T(8,128)(2,1)S(1)} %get-tuple-element.57.refs_0_.refs_10_), channel_id=1, source_target_pairs={{0,2},{1,3},{2,0},{3,1},{4,6},{5,7},{6,4},{7,5},{8,10},{9,11},{10,... | collective-permute-start | bytes 1597448 | tf_op jit(solution)/shard_map/ppermute | solution.py:710
  5.7 1.5 %collective-permute-start.1 = (bf16[2080,128]{1,0:T(8,128)(2,1)S(1)}, bf16[2080,128]{1,0:T(8,128)(2,1)S(1)}, u32[]{:S(2)}, u32[]{:S(2)}) collective-permute-start(bf16[2080,128]{1,0:T(8,128)(2,1)S(1)} %get-tuple-element.57.refs_0_.refs_10_), channel_id=1, source_target_pairs={{0,1},{1,0},{2,3},{3,2},{4,5},{5,4},{6,7},{7,6},{8,9},{9,8},{10,11... | collective-permute-start | bytes 1597448 | tf_op jit(solution)/shard_map/ppermute | solution.py:710
  7.2 1.6 %collective-permute-start = (bf16[512,128]{1,0:T(8,128)(2,1)S(1)}, bf16[512,128]{1,0:T(8,128)(2,1)S(1)}, u32[]{:S(2)}, u32[]{:S(2)}) collective-permute-start(bf16[512,128]{1,0:T(8,128)(2,1)S(1)} %get-tuple-element.55), channel_id=1, source_target_pairs={{0,8},{4,12},{8,0},{12,4},{16,24},{20,28},{24,16},{28,20},{1,9},{5... | collective-permute-start | bytes 393224 | tf_op jit(solution)/shard_map/ppermute | solution.py:710
  8.8 2.6 %collective-permute-start.2 = (bf16[512,128]{1,0:T(8,128)(2,1)S(1)}, bf16[512,128]{1,0:T(8,128)(2,1)S(1)}, u32[]{:S(2)}, u32[]{:S(2)}) collective-permute-start(bf16[512,128]{1,0:T(8,128)(2,1)S(1)} %get-tuple-element.62), channel_id=1, source_target_pairs={{0,16},{4,20},{8,24},{12,28},{16,0},{20,4},{24,8},{28,12},{1,17},{... | collective-permute-start | bytes 393224 | tf_op jit(solution)/shard_map/ppermute | solution.py:710
  12.0 3.8 %prep.1 = (f32[52,128,128]{2,1,0:T(8,128)S(1)}, f32[52,128]{1,0:T(8,128)S(1)}, f32[384,64]{1,0:T(8,128)S(1)}, bf16[256,512]{1,0:T(8,128)(2,1)S(1)}, f32[8,128]{1,0:T(8,128)S(1)}) custom-call(s32[1]{0:T(128)} %bitcast.grp_s, bf16[52,16384]{1,0:T(8,128)(2,1)} %refs_h.1, f32[384,64]{1,0:T(8,128)} %constant.15.clone.rest_refs_0_, ...), custom_call_target="tpu_custom_call" | custom-call | bytes 14400000 | tf_op jit(solution)/shard_map/prep/pallas_call | solution.py:695
  15.8 1.9 %score.3 = (f32[128,64]{1,0:T(8,128)S(1)}, f32[16,128]{1,0:T(8,128)S(1)}, f32[128,128]{1,0:T(8,128)S(1)}) custom-call(s32[1]{0:T(128)S(6)} %mul.3.first_s, s32[1]{0:T(128)} %bitcast.1.owner_s, bf16[2080,128]{1,0:T(8,128)(2,1)S(1)} %get-tuple-element.57.refs_0_.refs_10_, f32[52,128,128]{2,1,0:T(8,128)S(1)} %get-tuple-element.58.refs_1_.refs_2_.refs_4_, ...), custom_call_target="tpu_custom_call" | custom-call | bytes 10800000 | tf_op jit(solution)/shard_map/score/pallas_call | solution.py:695
  17.8 1.8 %collective-permute-start.5 = (bf16[1056,128]{1,0:T(8,128)(2,1)S(1)}, bf16[1056,128]{1,0:T(8,128)(2,1)S(1)}, u32[]{:S(2)}, u32[]{:S(2)}) collective-permute-start(bf16[1056,128]{1,0:T(8,128)(2,1)S(1)} %slice.19), channel_id=1, source_target_pairs={{0,1},{1,0},{2,3},{3,2},{4,5},{5,4},{6,7},{7,6},{8,9},{9,8},{10,11... | collective-permute-start | bytes 811016 | tf_op jit(solution)/shard_map/ppermute | solution.py:710
  19.6 1.6 %collective-permute-start.4 = (bf16[1024,128]{1,0:T(8,128)(2,1)S(1)}, bf16[1024,128]{1,0:T(8,128)(2,1)S(1)}, u32[]{:S(2)}, u32[]{:S(2)}) collective-permute-start(bf16[1024,128]{1,0:T(8,128)(2,1)S(1)} %slice.18), channel_id=1, source_target_pairs={{0,2},{1,3},{2,0},{3,1},{4,6},{5,7},{6,4},{7,5},{8,10},{9,11},{10,... | collective-permute-start | bytes 786440 | tf_op jit(solution)/shard_map/ppermute | solution.py:710
  21.2 3.6 %collective-permute-start.6 = (bf16[512,128]{1,0:T(8,128)(2,1)S(1)}, bf16[512,128]{1,0:T(8,128)(2,1)S(1)}, u32[]{:S(2)}, u32[]{:S(2)}) collective-permute-start(bf16[512,128]{1,0:T(8,128)(2,1)S(1)} %get-tuple-element.67), channel_id=1, source_target_pairs={{0,24},{4,28},{8,16},{12,20},{16,8},{20,12},{24,0},{28,4},{1,25},{... | collective-permute-start | bytes 393224 | tf_op jit(solution)/shard_map/ppermute | solution.py:710
  24.8 3.5 %score.4 = (f32[256,64]{1,0:T(8,128)S(1)}, f32[32,128]{1,0:T(8,128)S(1)}, f32[256,128]{1,0:T(8,128)S(1)}) custom-call(s32[1]{0:T(128)S(6)} %mul.3.first_s, s32[1]{0:T(128)} %bitcast.1.owner_s, bf16[2080,128]{1,0:T(8,128)(2,1)S(1)} %collective-permute-done.1.refs_0_.refs_11_.refs_1_, bf16[2080,128]{1,0:T(8,128)(2,1)S(1)} %collective-permute-done.3.refs_1_.refs_12_.refs_2_, ...), custom_call_target="tpu_custom_call" | custom-call | bytes 21600000 | tf_op jit(solution)/shard_map/score/pallas_call | solution.py:695
  28.9 1.0 %collective-permute-start.7 = (bf16[1536,128]{1,0:T(8,128)(2,1)S(1)}, bf16[1536,128]{1,0:T(8,128)(2,1)S(1)}, u32[]{:S(2)}, u32[]{:S(2)}) collective-permute-start(bf16[1536,128]{1,0:T(8,128)(2,1)S(1)} %join.1.refs_0_), channel_id=1, source_target_pairs={{0,1},{1,0},{2,3},{3,2},{4,5},{5,4},{6,7},{7,6},{8,9},{9,8},{10,11... | collective-permute-start | bytes 1179656 | tf_op jit(solution)/shard_map/ppermute | solution.py:710
  29.9 1.9 %score.5 = (f32[128,64]{1,0:T(8,128)S(1)}, f32[64,128]{1,0:T(8,128)S(1)}, f32[128,128]{1,0:T(8,128)S(1)}) custom-call(s32[1]{0:T(128)S(6)} %mul.3.first_s, s32[1]{0:T(128)} %bitcast.1.owner_s, bf16[1024,128]{1,0:T(8,128)(2,1)S(1)} %collective-permute-done.4.refs_0_.refs_3_, bf16[1056,128]{1,0:T(8,128)(2,1)S(1)} %collective-permute-done.5.refs_1_.refs_13_.refs_4_, ...), custom_call_target="tpu_custom_call" | custom-call | bytes 10800000 | tf_op jit(solution)/shard_map/score/pallas_call | solution.py:695
  31.8 2.1 %collective-permute-start.10 = (f32[64,128]{1,0:T(8,128)S(1)}, f32[64,128]{1,0:T(8,128)S(1)}, u32[]{:S(2)}, u32[]{:S(2)}) collective-permute-start(f32[64,128]{1,0:T(8,128)S(1)} %get-tuple-element.68.refs_0_), channel_id=1, source_target_pairs={{0,3},{1,2},{2,1},{3,0},{4,7},{5,6},{6,5},{7,4},{8,11},{9,10},{10,... | collective-permute-start | bytes 98312 | tf_op jit(solution)/shard_map/ppermute | solution.py:710
  34.4 1.0 %collective-permute-start.8 = (f32[64,128]{1,0:T(8,128)S(1)}, f32[64,128]{1,0:T(8,128)S(1)}, u32[]{:S(2)}, u32[]{:S(2)}) collective-permute-start(f32[64,128]{1,0:T(8,128)S(1)} %get-tuple-element.68.refs_0_), channel_id=1, source_target_pairs={{0,1},{1,0},{2,3},{3,2},{4,5},{5,4},{6,7},{7,6},{8,9},{9,8},{10,11... | collective-permute-start | bytes 98312 | tf_op jit(solution)/shard_map/ppermute | solution.py:710
  35.4 4.4 %collective-permute-done.10.refs_3_ = f32[64,128]{1,0:T(8,128)S(1)} collective-permute-done((f32[64,128]{1,0:T(8,128)S(1)}, f32[64,128]{1,0:T(8,128)S(1)}, u32[]{:S(2)}, u32[]{:S(2)}) %collective-permute-start.10) | collective-permute-done | bytes 32800 | tf_op jit(solution)/shard_map/ppermute | solution.py:710
  39.8 0.8 weights.1
  41.3 1.1 %collective-permute-start.12 = (bf16[768,128]{1,0:T(8,128)(2,1)S(1)}, bf16[768,128]{1,0:T(8,128)(2,1)S(1)}, u32[]{:S(2)}, u32[]{:S(2)}) collective-permute-start(bf16[768,128]{1,0:T(8,128)(2,1)S(1)} %slice.20), channel_id=1, source_target_pairs={{0,2},{1,3},{2,0},{3,1},{4,6},{5,7},{6,4},{7,5},{8,10},{9,11},{10,... | collective-permute-start | bytes 589832 | tf_op jit(solution)/shard_map/ppermute | solution.py:710
  42.8 2.9 %collective-permute-start.14 = (bf16[304,128]{1,0:T(8,128)(2,1)S(1)}, bf16[304,128]{1,0:T(8,128)(2,1)S(1)}, u32[]{:S(2)}, u32[]{:S(2)}) collective-permute-start(bf16[304,128]{1,0:T(8,128)(2,1)S(1)} %get-tuple-element.78), channel_id=1, source_target_pairs={{0,16},{4,20},{8,24},{12,28},{16,0},{20,4},{24,8},{28,12},{1,17},{... | collective-permute-start | bytes 233480 | tf_op jit(solution)/shard_map/ppermute | solution.py:710
  45.7 1.1 %collective-permute-start.15 = (bf16[304,128]{1,0:T(8,128)(2,1)S(1)}, bf16[304,128]{1,0:T(8,128)(2,1)S(1)}, u32[]{:S(2)}, u32[]{:S(2)}) collective-permute-start(bf16[304,128]{1,0:T(8,128)(2,1)S(1)} %get-tuple-element.79), channel_id=1, source_target_pairs={{0,24},{4,28},{8,16},{12,20},{16,8},{20,12},{24,0},{28,4},{1,25},{... | collective-permute-start | bytes 233480 | tf_op jit(solution)/shard_map/ppermute | solution.py:710
  46.8 2.2 %own_sum.1.refs_6_ = f32[52,2,2,8,128]{4,3,2,1,0:T(8,128)S(1)} custom-call(s32[1]{0:T(128)} %bitcast.grp_s, s32[1]{0:T(128)} %bitcast.1.owner_s, bf16[256,128]{1,0:T(8,128)(2,1)S(1)} %get-tuple-element.75.packed, s32[16,128]{1,0:T(8,128)S(1)} %get-tuple-element.81.ints, bf16[2080,128]{1,0:T(8,128)(2,1)S(1)} %get-tuple-element.57.refs_0_.refs_10_, ...), custom_call_target="tpu_custom_call" | custom-call | bytes 10800000 | tf_op jit(solution)/shard_map/own_sum/pallas_call | solution.py:695
  49.0 2.0 %near_sum.1 = (f32[52,2,2,8,128]{4,3,2,1,0:T(8,128)S(1)}, f32[16,128]{1,0:T(8,128)S(1)}, f32[8,128]{1,0:T(8,128)S(1)}) custom-call(s32[1]{0:T(128)} %bitcast.1.owner_s, bf16[1536,128]{1,0:T(8,128)(2,1)S(1)} %join.1.refs_0_, bf16[1536,128]{1,0:T(8,128)(2,1)S(1)} %collective-permute-done.7.refs_1_, bf16[1536,128]{1,0:T(8,128)(2,1)S(1)} %collective-permute-done.11.refs_2_, ...), custom_call_target="tpu_custom_call" | custom-call | bytes 7200000 | tf_op jit(solution)/shard_map/near_sum/pallas_call | solution.py:695
  50.9 0.9 %collective-permute-done.15.refs_6_ = bf16[304,128]{1,0:T(8,128)(2,1)S(1)} collective-permute-done((bf16[304,128]{1,0:T(8,128)(2,1)S(1)}, bf16[304,128]{1,0:T(8,128)(2,1)S(1)}, u32[]{:S(2)}, u32[]{:S(2)}) %collective-permute-start.15) | collective-permute-done | bytes 77856 | tf_op jit(solution)/shard_map/ppermute | solution.py:710
  51.9 3.6 %sum.2 = (f32[28,16,128]{2,1,0:T(8,128)S(1)}, bf16[29,16,128]{2,1,0:T(8,128)(2,1)S(1)}, f32[8,128]{1,0:T(8,128)S(1)}, f32[8,128]{1,0:T(8,128)S(1)}, f32[2,1040,1...) custom-call(s32[1]{0:T(128)} %bitcast.grp_s, s32[1]{0:T(128)} %bitcast.1.owner_s, bf16[1536,128]{1,0:T(8,128)(2,1)S(1)} %join.1.refs_0_, ...), custom_call_target="tpu_custom_call" | custom-call | bytes 10800000 | tf_op jit(solution)/shard_map/sum/pallas_call | solution.py:695
  55.6 2.4 %sum.3 = (f32[24,16,128]{2,1,0:T(8,128)S(1)}, bf16[24,16,128]{2,1,0:T(8,128)(2,1)S(1)}) custom-call(s32[1]{0:T(128)} %bitcast.grp_s, s32[1]{0:T(128)} %bitcast.1.owner_s, bf16[1536,128]{1,0:T(8,128)(2,1)S(1)} %join.1.refs_0_, bf16[1536,128]{1,0:T(8,128)(2,1)S(1)} %collective-permute-done.7.refs_1_, bf16[1536,128]{1,0:T(8,128)(2,1)S(1)} %collective-permute-done.11.refs_2_, ...), custom_call_target="tpu_custom_call" | custom-call | bytes 10800000 | tf_op jit(solution)/shard_map/sum/pallas_call | solution.py:695
  59.5 1.7 %collective-permute-start.18 = (bf16[28,16,128]{2,1,0:T(8,128)(2,1)S(1)}, bf16[28,16,128]{2,1,0:T(8,128)(2,1)S(1)}, u32[]{:S(2)}, u32[]{:S(2)}) collective-permute-start(bf16[28,16,128]{2,1,0:T(8,128)(2,1)S(1)} %get-tuple-element.93.refs_0_), channel_id=1, source_target_pairs={{0,8},{4,12},{8,0},{12,4},{16,24},{20,28},{24,16},{28,20},{1,9},{5... | collective-permute-start | bytes 344072 | tf_op jit(solution)/shard_map/ppermute | solution.py:710
  62.0 2.0 %collective-permute-start.20 = (bf16[24,16,128]{2,1,0:T(8,128)(2,1)S(1)}, bf16[24,16,128]{2,1,0:T(8,128)(2,1)S(1)}, u32[]{:S(2)}, u32[]{:S(2)}) collective-permute-start(bf16[24,16,128]{2,1,0:T(8,128)(2,1)S(1)} %divide.3.refs_2_), channel_id=1, source_target_pairs={{0,8},{4,12},{8,0},{12,4},{16,24},{20,28},{24,16},{28,20},{1,9},{5... | collective-permute-start | bytes 294920 | tf_op jit(solution)/shard_map/ppermute | solution.py:710
  64.0 6.7 %collective-permute-done.22.refs_10_ = bf16[24,16,128]{2,1,0:T(8,128)(2,1)S(1)} collective-permute-done((bf16[24,16,128]{2,1,0:T(8,128)(2,1)S(1)}, bf16[24,16,128]{2,1,0:T(8,128)(2,1)S(1)}, u32[]{:S(2)}, u32[]{:S(2)}) %collective-permute-start.22) | collective-permute-done | bytes 98336 | tf_op jit(solution)/shard_map/ppermute | solution.py:710
  72.1 2.0 %collective-permute-start.31 = (bf16[24,16,128]{2,1,0:T(8,128)(2,1)S(1)}, bf16[24,16,128]{2,1,0:T(8,128)(2,1)S(1)}, u32[]{:S(2)}, u32[]{:S(2)}) collective-permute-start(bf16[24,16,128]{2,1,0:T(8,128)(2,1)S(1)} %collective-permute-done.22.refs_10_), channel_id=1, source_target_pairs={{0,8},{4,12},{8,0},{12,4},{16,24},{20,28},{24,16},{28,20},{1,9},{5... | collective-permute-start | bytes 294920 | tf_op jit(solution)/shard_map/ppermute | solution.py:710
  75.4 2.0 %spread.2.refs_4_ = f32[52,16384]{1,0:T(8,128)} custom-call(s32[1]{0:T(128)} %bitcast.grp_s, bf16[28,16,128]{2,1,0:T(8,128)(2,1)S(1)} %get-tuple-element.93.refs_0_, bf16[28,16,128]{2,1,0:T(8,128)(2,1)S(1)} %collective-permute-done.24.refs_1_, bf16[24,16,128]{2,1,0:T(8,128)(2,1)S(1)} %divide.3.refs_2_, ...), custom_call_target="tpu_custom_call" | custom-call | bytes 180000 | tf_op jit(solution)/shard_map/spread/pallas_call | solution.py:695
  77.4 2.0 %collective-permute-done.31.refs_2_ = bf16[24,16,128]{2,1,0:T(8,128)(2,1)S(1)} collective-permute-done((bf16[24,16,128]{2,1,0:T(8,128)(2,1)S(1)}, bf16[24,16,128]{2,1,0:T(8,128)(2,1)S(1)}, u32[]{:S(2)}, u32[]{:S(2)}) %collective-permute-start.31) | collective-permute-done | bytes 98336 | tf_op jit(solution)/shard_map/ppermute | solution.py:710
  80.8 1.2 %spread.3 = f32[52,16384]{1,0:T(8,128)} custom-call(s32[1]{0:T(128)} %bitcast.grp_s, bf16[28,16,128]{2,1,0:T(8,128)(2,1)S(1)} %collective-permute-done.23.refs_0_, bf16[28,16,128]{2,1,0:T(8,128)(2,1)S(1)} %collective-permute-done.30.refs_1_, bf16[24,16,128]{2,1,0:T(8,128)(2,1)S(1)} %collective-permute-done.31.refs_2_, ...), custom_call_target="tpu_custom_call", output_to_operand_aliasing={{}: (5, {})} | custom-call | bytes 180000 | tf_op jit(solution)/shard_map/spread/pallas_call | solution.py:695
  (57 shorter events, 9.5 us)
Async XLA Ops:
  2.7 15.1 %collective-permute-start.3 = (bf16[2080,128]{1,0:T(8,128)(2,1)S(1)}, bf16[2080,128]{1,0:T(8,128)(2,1)S(1)}, u32[]{:S(2)}, u32[]{:S(2)}) collective-permute-start(bf16[2080,128]{1,0:T(8,128)(2,1)S(1)} %get-tuple-element.57.refs_0_.refs_10_), channel_id=1, source_target_pairs={{0,2},{1,3},{2,0},{3,1},{4,6},{5,7},{6,4},{7,5},{8,10},{9,11},{10,... | collective-permute-start | bytes 1597448 | tf_op jit(solution)/shard_map/ppermute | solution.py:710
  5.7 13.9 %collective-permute-start.1 = (bf16[2080,128]{1,0:T(8,128)(2,1)S(1)}, bf16[2080,128]{1,0:T(8,128)(2,1)S(1)}, u32[]{:S(2)}, u32[]{:S(2)}) collective-permute-start(bf16[2080,128]{1,0:T(8,128)(2,1)S(1)} %get-tuple-element.57.refs_0_.refs_10_), channel_id=1, source_target_pairs={{0,1},{1,0},{2,3},{3,2},{4,5},{5,4},{6,7},{7,6},{8,9},{9,8},{10,11... | collective-permute-start | bytes 1597448 | tf_op jit(solution)/shard_map/ppermute | solution.py:710
  7.2 8.6 %collective-permute-start = (bf16[512,128]{1,0:T(8,128)(2,1)S(1)}, bf16[512,128]{1,0:T(8,128)(2,1)S(1)}, u32[]{:S(2)}, u32[]{:S(2)}) collective-permute-start(bf16[512,128]{1,0:T(8,128)(2,1)S(1)} %get-tuple-element.55), channel_id=1, source_target_pairs={{0,8},{4,12},{8,0},{12,4},{16,24},{20,28},{24,16},{28,20},{1,9},{5... | collective-permute-start | bytes 393224 | tf_op jit(solution)/shard_map/ppermute | solution.py:710
  8.8 8.9 %collective-permute-start.2 = (bf16[512,128]{1,0:T(8,128)(2,1)S(1)}, bf16[512,128]{1,0:T(8,128)(2,1)S(1)}, u32[]{:S(2)}, u32[]{:S(2)}) collective-permute-start(bf16[512,128]{1,0:T(8,128)(2,1)S(1)} %get-tuple-element.62), channel_id=1, source_target_pairs={{0,16},{4,20},{8,24},{12,28},{16,0},{20,4},{24,8},{28,12},{1,17},{... | collective-permute-start | bytes 393224 | tf_op jit(solution)/shard_map/ppermute | solution.py:710
  17.8 10.5 %collective-permute-start.5 = (bf16[1056,128]{1,0:T(8,128)(2,1)S(1)}, bf16[1056,128]{1,0:T(8,128)(2,1)S(1)}, u32[]{:S(2)}, u32[]{:S(2)}) collective-permute-start(bf16[1056,128]{1,0:T(8,128)(2,1)S(1)} %slice.19), channel_id=1, source_target_pairs={{0,1},{1,0},{2,3},{3,2},{4,5},{5,4},{6,7},{7,6},{8,9},{9,8},{10,11... | collective-permute-start | bytes 811016 | tf_op jit(solution)/shard_map/ppermute | solution.py:710
  19.6 8.7 %collective-permute-start.4 = (bf16[1024,128]{1,0:T(8,128)(2,1)S(1)}, bf16[1024,128]{1,0:T(8,128)(2,1)S(1)}, u32[]{:S(2)}, u32[]{:S(2)}) collective-permute-start(bf16[1024,128]{1,0:T(8,128)(2,1)S(1)} %slice.18), channel_id=1, source_target_pairs={{0,2},{1,3},{2,0},{3,1},{4,6},{5,7},{6,4},{7,5},{8,10},{9,11},{10,... | collective-permute-start | bytes 786440 | tf_op jit(solution)/shard_map/ppermute | solution.py:710
  21.2 7.1 %collective-permute-start.6 = (bf16[512,128]{1,0:T(8,128)(2,1)S(1)}, bf16[512,128]{1,0:T(8,128)(2,1)S(1)}, u32[]{:S(2)}, u32[]{:S(2)}) collective-permute-start(bf16[512,128]{1,0:T(8,128)(2,1)S(1)} %get-tuple-element.67), channel_id=1, source_target_pairs={{0,24},{4,28},{8,16},{12,20},{16,8},{20,12},{24,0},{28,4},{1,25},{... | collective-permute-start | bytes 393224 | tf_op jit(solution)/shard_map/ppermute | solution.py:710
  28.3 12.2 %collective-permute-start.11 = (bf16[1536,128]{1,0:T(8,128)(2,1)S(1)}, bf16[1536,128]{1,0:T(8,128)(2,1)S(1)}, u32[]{:S(2)}, u32[]{:S(2)}) collective-permute-start(bf16[1536,128]{1,0:T(8,128)(2,1)S(1)} %join.1.refs_0_), channel_id=1, source_target_pairs={{0,2},{1,3},{2,0},{3,1},{4,6},{5,7},{6,4},{7,5},{8,10},{9,11},{10,... | collective-permute-start | bytes 1179656 | tf_op jit(solution)/shard_map/ppermute | solution.py:710
  28.9 12.3 %collective-permute-start.7 = (bf16[1536,128]{1,0:T(8,128)(2,1)S(1)}, bf16[1536,128]{1,0:T(8,128)(2,1)S(1)}, u32[]{:S(2)}, u32[]{:S(2)}) collective-permute-start(bf16[1536,128]{1,0:T(8,128)(2,1)S(1)} %join.1.refs_0_), channel_id=1, source_target_pairs={{0,1},{1,0},{2,3},{3,2},{4,5},{5,4},{6,7},{7,6},{8,9},{9,8},{10,11... | collective-permute-start | bytes 1179656 | tf_op jit(solution)/shard_map/ppermute | solution.py:710
  31.8 8.0 %collective-permute-start.10 = (f32[64,128]{1,0:T(8,128)S(1)}, f32[64,128]{1,0:T(8,128)S(1)}, u32[]{:S(2)}, u32[]{:S(2)}) collective-permute-start(f32[64,128]{1,0:T(8,128)S(1)} %get-tuple-element.68.refs_0_), channel_id=1, source_target_pairs={{0,3},{1,2},{2,1},{3,0},{4,7},{5,6},{6,5},{7,4},{8,11},{9,10},{10,... | collective-permute-start | bytes 98312 | tf_op jit(solution)/shard_map/ppermute | solution.py:710
  33.9 5.9 %collective-permute-start.9 = (f32[64,128]{1,0:T(8,128)S(1)}, f32[64,128]{1,0:T(8,128)S(1)}, u32[]{:S(2)}, u32[]{:S(2)}) collective-permute-start(f32[64,128]{1,0:T(8,128)S(1)} %get-tuple-element.68.refs_0_), channel_id=1, source_target_pairs={{0,2},{1,3},{2,0},{3,1},{4,6},{5,7},{6,4},{7,5},{8,10},{9,11},{10,... | collective-permute-start | bytes 98312 | tf_op jit(solution)/shard_map/ppermute | solution.py:710
  34.4 5.4 %collective-permute-start.8 = (f32[64,128]{1,0:T(8,128)S(1)}, f32[64,128]{1,0:T(8,128)S(1)}, u32[]{:S(2)}, u32[]{:S(2)}) collective-permute-start(f32[64,128]{1,0:T(8,128)S(1)} %get-tuple-element.68.refs_0_), channel_id=1, source_target_pairs={{0,1},{1,0},{2,3},{3,2},{4,5},{5,4},{6,7},{7,6},{8,9},{9,8},{10,11... | collective-permute-start | bytes 98312 | tf_op jit(solution)/shard_map/ppermute | solution.py:710
  40.6 8.4 %collective-permute-start.13 = (bf16[768,128]{1,0:T(8,128)(2,1)S(1)}, bf16[768,128]{1,0:T(8,128)(2,1)S(1)}, u32[]{:S(2)}, u32[]{:S(2)}) collective-permute-start(bf16[768,128]{1,0:T(8,128)(2,1)S(1)} %slice.21), channel_id=1, source_target_pairs={{0,1},{1,0},{2,3},{3,2},{4,5},{5,4},{6,7},{7,6},{8,9},{9,8},{10,11... | collective-permute-start | bytes 589832 | tf_op jit(solution)/shard_map/ppermute | solution.py:710
  41.3 7.7 %collective-permute-start.12 = (bf16[768,128]{1,0:T(8,128)(2,1)S(1)}, bf16[768,128]{1,0:T(8,128)(2,1)S(1)}, u32[]{:S(2)}, u32[]{:S(2)}) collective-permute-start(bf16[768,128]{1,0:T(8,128)(2,1)S(1)} %slice.20), channel_id=1, source_target_pairs={{0,2},{1,3},{2,0},{3,1},{4,6},{5,7},{6,4},{7,5},{8,10},{9,11},{10,... | collective-permute-start | bytes 589832 | tf_op jit(solution)/shard_map/ppermute | solution.py:710
  42.4 6.6 %collective-permute-start.16 = (bf16[304,128]{1,0:T(8,128)(2,1)S(1)}, bf16[304,128]{1,0:T(8,128)(2,1)S(1)}, u32[]{:S(2)}, u32[]{:S(2)}) collective-permute-start(bf16[304,128]{1,0:T(8,128)(2,1)S(1)} %get-tuple-element.80), channel_id=1, source_target_pairs={{0,8},{4,12},{8,0},{12,4},{16,24},{20,28},{24,16},{28,20},{1,9},{5... | collective-permute-start | bytes 233480 | tf_op jit(solution)/shard_map/ppermute | solution.py:710
  42.8 8.1 %collective-permute-start.14 = (bf16[304,128]{1,0:T(8,128)(2,1)S(1)}, bf16[304,128]{1,0:T(8,128)(2,1)S(1)}, u32[]{:S(2)}, u32[]{:S(2)}) collective-permute-start(bf16[304,128]{1,0:T(8,128)(2,1)S(1)} %get-tuple-element.78), channel_id=1, source_target_pairs={{0,16},{4,20},{8,24},{12,28},{16,0},{20,4},{24,8},{28,12},{1,17},{... | collective-permute-start | bytes 233480 | tf_op jit(solution)/shard_map/ppermute | solution.py:710
  45.7 6.2 %collective-permute-start.15 = (bf16[304,128]{1,0:T(8,128)(2,1)S(1)}, bf16[304,128]{1,0:T(8,128)(2,1)S(1)}, u32[]{:S(2)}, u32[]{:S(2)}) collective-permute-start(bf16[304,128]{1,0:T(8,128)(2,1)S(1)} %get-tuple-element.79), channel_id=1, source_target_pairs={{0,24},{4,28},{8,16},{12,20},{16,8},{20,12},{24,0},{28,4},{1,25},{... | collective-permute-start | bytes 233480 | tf_op jit(solution)/shard_map/ppermute | solution.py:710
  55.5 3.1 %collective-permute-start.17 = (bf16[29,16,128]{2,1,0:T(8,128)(2,1)S(1)}, bf16[29,16,128]{2,1,0:T(8,128)(2,1)S(1)}, u32[]{:S(2)}, u32[]{:S(2)}) collective-permute-start(bf16[29,16,128]{2,1,0:T(8,128)(2,1)S(1)} %get-tuple-element.89), channel_id=1, source_target_pairs={{0,4},{4,0},{8,12},{12,8},{16,20},{20,16},{24,28},{28,24},{1,5},{5... | collective-permute-start | bytes 356360 | tf_op jit(solution)/shard_map/ppermute | solution.py:710
  58.0 3.2 %collective-permute-start.19 = (bf16[24,16,128]{2,1,0:T(8,128)(2,1)S(1)}, bf16[24,16,128]{2,1,0:T(8,128)(2,1)S(1)}, u32[]{:S(2)}, u32[]{:S(2)}) collective-permute-start(bf16[24,16,128]{2,1,0:T(8,128)(2,1)S(1)} %get-tuple-element.97), channel_id=1, source_target_pairs={{0,4},{4,0},{8,12},{12,8},{16,20},{20,16},{24,28},{28,24},{1,5},{5... | collective-permute-start | bytes 294920 | tf_op jit(solution)/shard_map/ppermute | solution.py:710
  58.8 12.1 %collective-permute-start.21 = (bf16[28,16,128]{2,1,0:T(8,128)(2,1)S(1)}, bf16[28,16,128]{2,1,0:T(8,128)(2,1)S(1)}, u32[]{:S(2)}, u32[]{:S(2)}) collective-permute-start(bf16[28,16,128]{2,1,0:T(8,128)(2,1)S(1)} %get-tuple-element.93.refs_0_), channel_id=1, source_target_pairs={{0,16},{4,20},{8,24},{12,28},{16,0},{20,4},{24,8},{28,12},{1,17},{... | collective-permute-start | bytes 344072 | tf_op jit(solution)/shard_map/ppermute | solution.py:710
  59.5 11.5 %collective-permute-start.18 = (bf16[28,16,128]{2,1,0:T(8,128)(2,1)S(1)}, bf16[28,16,128]{2,1,0:T(8,128)(2,1)S(1)}, u32[]{:S(2)}, u32[]{:S(2)}) collective-permute-start(bf16[28,16,128]{2,1,0:T(8,128)(2,1)S(1)} %get-tuple-element.93.refs_0_), channel_id=1, source_target_pairs={{0,8},{4,12},{8,0},{12,4},{16,24},{20,28},{24,16},{28,20},{1,9},{5... | collective-permute-start | bytes 344072 | tf_op jit(solution)/shard_map/ppermute | solution.py:710
  61.3 9.4 %collective-permute-start.22 = (bf16[24,16,128]{2,1,0:T(8,128)(2,1)S(1)}, bf16[24,16,128]{2,1,0:T(8,128)(2,1)S(1)}, u32[]{:S(2)}, u32[]{:S(2)}) collective-permute-start(bf16[24,16,128]{2,1,0:T(8,128)(2,1)S(1)} %divide.3.refs_2_), channel_id=1, source_target_pairs={{0,16},{4,20},{8,24},{12,28},{16,0},{20,4},{24,8},{28,12},{1,17},{... | collective-permute-start | bytes 294920 | tf_op jit(solution)/shard_map/ppermute | solution.py:710
  62.0 8.9 %collective-permute-start.20 = (bf16[24,16,128]{2,1,0:T(8,128)(2,1)S(1)}, bf16[24,16,128]{2,1,0:T(8,128)(2,1)S(1)}, u32[]{:S(2)}, u32[]{:S(2)}) collective-permute-start(bf16[24,16,128]{2,1,0:T(8,128)(2,1)S(1)} %divide.3.refs_2_), channel_id=1, source_target_pairs={{0,8},{4,12},{8,0},{12,4},{16,24},{20,28},{24,16},{28,20},{1,9},{5... | collective-permute-start | bytes 294920 | tf_op jit(solution)/shard_map/ppermute | solution.py:710
  64.0 8.0 %collective-permute-start.24 = (bf16[28,16,128]{2,1,0:T(8,128)(2,1)S(1)}, bf16[28,16,128]{2,1,0:T(8,128)(2,1)S(1)}, u32[]{:S(2)}, u32[]{:S(2)}) collective-permute-start(bf16[28,16,128]{2,1,0:T(8,128)(2,1)S(1)} %get-tuple-element.93.refs_0_), channel_id=1, source_target_pairs={{0,4},{4,0},{8,12},{12,8},{16,20},{20,16},{24,28},{28,24},{1,5},{5... | collective-permute-start | bytes 344072 | tf_op jit(solution)/shard_map/ppermute | solution.py:710
  71.0 3.1 %collective-permute-start.27 = (bf16[24,16,128]{2,1,0:T(8,128)(2,1)S(1)}, bf16[24,16,128]{2,1,0:T(8,128)(2,1)S(1)}, u32[]{:S(2)}, u32[]{:S(2)}) collective-permute-start(bf16[24,16,128]{2,1,0:T(8,128)(2,1)S(1)} %collective-permute-done.20.refs_6_), channel_id=1, source_target_pairs={{0,4},{4,0},{8,12},{12,8},{16,20},{20,16},{24,28},{28,24},{1,5},{5... | collective-permute-start | bytes 294920 | tf_op jit(solution)/shard_map/ppermute | solution.py:710
  71.3 4.1 %collective-permute-start.26 = (bf16[28,16,128]{2,1,0:T(8,128)(2,1)S(1)}, bf16[28,16,128]{2,1,0:T(8,128)(2,1)S(1)}, u32[]{:S(2)}, u32[]{:S(2)}) collective-permute-start(bf16[28,16,128]{2,1,0:T(8,128)(2,1)S(1)} %collective-permute-done.18.refs_4_), channel_id=1, source_target_pairs={{0,4},{4,0},{8,12},{12,8},{16,20},{20,16},{24,28},{28,24},{1,5},{5... | collective-permute-start | bytes 344072 | tf_op jit(solution)/shard_map/ppermute | solution.py:710
  71.5 3.9 %collective-permute-start.28 = (bf16[28,16,128]{2,1,0:T(8,128)(2,1)S(1)}, bf16[28,16,128]{2,1,0:T(8,128)(2,1)S(1)}, u32[]{:S(2)}, u32[]{:S(2)}) collective-permute-start(bf16[28,16,128]{2,1,0:T(8,128)(2,1)S(1)} %collective-permute-done.21.refs_8_), channel_id=1, source_target_pairs={{0,4},{4,0},{8,12},{12,8},{16,20},{20,16},{24,28},{28,24},{1,5},{5... | collective-permute-start | bytes 344072 | tf_op jit(solution)/shard_map/ppermute | solution.py:710
  72.0 7.3 %collective-permute-start.23 = (bf16[28,16,128]{2,1,0:T(8,128)(2,1)S(1)}, bf16[28,16,128]{2,1,0:T(8,128)(2,1)S(1)}, u32[]{:S(2)}, u32[]{:S(2)}) collective-permute-start(bf16[28,16,128]{2,1,0:T(8,128)(2,1)S(1)} %collective-permute-done.21.refs_8_), channel_id=1, source_target_pairs={{0,8},{4,12},{8,0},{12,4},{16,24},{20,28},{24,16},{28,20},{1,9},{5... | collective-permute-start | bytes 344072 | tf_op jit(solution)/shard_map/ppermute | solution.py:710
  72.1 7.3 %collective-permute-start.31 = (bf16[24,16,128]{2,1,0:T(8,128)(2,1)S(1)}, bf16[24,16,128]{2,1,0:T(8,128)(2,1)S(1)}, u32[]{:S(2)}, u32[]{:S(2)}) collective-permute-start(bf16[24,16,128]{2,1,0:T(8,128)(2,1)S(1)} %collective-permute-done.22.refs_10_), channel_id=1, source_target_pairs={{0,8},{4,12},{8,0},{12,4},{16,24},{20,28},{24,16},{28,20},{1,9},{5... | collective-permute-start | bytes 294920 | tf_op jit(solution)/shard_map/ppermute | solution.py:710
  74.1 1.3 %collective-permute-start.29 = (bf16[24,16,128]{2,1,0:T(8,128)(2,1)S(1)}, bf16[24,16,128]{2,1,0:T(8,128)(2,1)S(1)}, u32[]{:S(2)}, u32[]{:S(2)}) collective-permute-start(bf16[24,16,128]{2,1,0:T(8,128)(2,1)S(1)} %collective-permute-done.22.refs_10_), channel_id=1, source_target_pairs={{0,4},{4,0},{8,12},{12,8},{16,20},{20,16},{24,28},{28,24},{1,5},{5... | collective-permute-start | bytes 294920 | tf_op jit(solution)/shard_map/ppermute | solution.py:710
  79.4 1.3 %collective-permute-start.32 = (bf16[24,16,128]{2,1,0:T(8,128)(2,1)S(1)}, bf16[24,16,128]{2,1,0:T(8,128)(2,1)S(1)}, u32[]{:S(2)}, u32[]{:S(2)}) collective-permute-start(bf16[24,16,128]{2,1,0:T(8,128)(2,1)S(1)} %collective-permute-done.31.refs_2_), channel_id=1, source_target_pairs={{0,4},{4,0},{8,12},{12,8},{16,20},{20,16},{24,28},{28,24},{1,5},{5... | collective-permute-start | bytes 294920 | tf_op jit(solution)/shard_map/ppermute | solution.py:710
  79.4 1.5 %collective-permute-start.30 = (bf16[28,16,128]{2,1,0:T(8,128)(2,1)S(1)}, bf16[28,16,128]{2,1,0:T(8,128)(2,1)S(1)}, u32[]{:S(2)}, u32[]{:S(2)}) collective-permute-start(bf16[28,16,128]{2,1,0:T(8,128)(2,1)S(1)} %collective-permute-done.23.refs_0_), channel_id=1, source_target_pairs={{0,4},{4,0},{8,12},{12,8},{16,20},{20,16},{24,28},{28,24},{1,5},{5... | collective-permute-start | bytes 344072 | tf_op jit(solution)/shard_map/ppermute | solution.py:710
  (2 other events, 2.0 us)

commit v6 on v5

--- a/solution.py
+++ b/solution.py
@@ -93,8 +93,7 @@
 
 
 def chunks_of(cls_dev):
-    cut = cls_dev // 2 // 8 * 8
-    return ((cut, cls_dev - cut), (0, cut)) if cut else ((0, cls_dev),)
+    return ((0, cls_dev),)
 
 
 def block_lists(named, owners, cls_dev, chunks):
@@ -115,8 +114,10 @@
     def across(column):
         return jnp.sum(jnp.where(row == lane, column, 0.0), axis=0, keepdims=True)
 
-    earlier = jnp.logical_and(number == across(number), lane < row)
-    place = jnp.sum(earlier.astype(F32), axis=1, keepdims=True)
+    same = (number == across(number)).astype(F32)
+    place = jnp.sum(jnp.where(lane < row, same, 0.0), axis=1, keepdims=True)
+    held = jnp.sum(same, axis=1, keepdims=True).astype(jnp.int32)
+    place = place + rest(UNROLL - rest(held, UNROLL), UNROLL).astype(F32)
     room = list_room(chunks)
     lines, height = list_lines(owners, chunks)
     slots = lines * FREQ
@@ -130,13 +131,8 @@
         axis=0,
     ).astype(BF16)
     placed = jnp.dot(values, hot, preferred_element_type=F32)
-    slot = lanes_of((1, slots))
-    start = jnp.zeros((1, slots), F32)
-    for c, (first, _) in enumerate(chunks):
-        start = jnp.where(quot(slot, room) % len(chunks) == c, float(first), start)
-    empty = 1.0 - placed[2:3]
-    rows_line = placed[0:1] + empty * pairs
-    cls_line = placed[1:2] + empty * start
+    rows_line = placed[0:1]
+    cls_line = placed[1:2] + (1.0 - placed[2:3]) * cls_dev
     counts = jnp.sum((number == lane.astype(F32)).astype(F32), axis=0, keepdims=True)
     counts = quot(counts.astype(jnp.int32) + UNROLL - 1, UNROLL).astype(F32)
     cut = [v[:, n * FREQ : (n + 1) * FREQ] for v in (rows_line, cls_line) for n in range(lines)]
@@ -208,6 +204,7 @@
     (rf_out, pow_out), tables_out, (reg_out,) = rest_refs[:2], rest_refs[2:4], rest_refs[4:5]
     refs, spread, reg, sem = rest_refs[5:]
     cls_dev = refs.shape[0]
+    pow_out[cls_dev:, :] = jnp.zeros((pow_out.shape[0] - cls_dev, FREQ), F32)
     pad = spread.shape[0] // IMG
     parts = sem.shape[0] - 3
     step = FEAT // parts
@@ -248,7 +245,7 @@
     line = jnp.broadcast_to(prior[...].astype(F32).reshape(1, cls_dev), (cls_dev, cls_dev))
     diagonal = lax.broadcasted_iota(jnp.int32, line.shape, 0) == lanes_of(line.shape)
     column = jnp.sum(jnp.where(diagonal, line, 0.0), axis=1, keepdims=True)
-    pow_out[...] = jnp.where(lanes_of((cls_dev, FREQ)) == SHELLS, column, power)
+    pow_out[:cls_dev, :] = jnp.where(lanes_of((cls_dev, FREQ)) == SHELLS, column, power)
 
     def image(k, _):
         rf_out[k] = spread[pl.ds(k, IMG, stride=pad), :]
@@ -279,7 +276,7 @@
     ints_v, ints_s, side, ex, w32, sem = refs[-6:]
     per = side.shape[1]
     height = ints_v.shape[1]
-    cls_dev = rf.shape[0]
+    cls_dev = rf.shape[0] - 1
     block_rows = per * CAND
     first = first_s[0]
     table = scoring[...]
@@ -321,7 +318,7 @@
                 for u in range(UNROLL):
                     row = ints_s[b, line, lane + step * UNROLL + u]
                     k = ints_s[b, line + half, lane + step * UNROLL + u]
-                    i = jnp.minimum(quot(row, CAND), per - 1)
+                    i = quot(row, CAND)
                     w_re, w_im = parts_of(w32[b * per + i], depth)
                     a_re, a_im = parts_of(rf[k], depth)
                     inner = (w_re * a_re + w_im * a_im).reshape(SHELLS, FREQ)
@@ -456,8 +453,6 @@
             at = (2 * place + part) * FREQ
             row = base + place * lines
             wcs[part, row : row + lines, :] = both[:, at : at + FREQ]
-    for part in range(2):
-        wcs[part, base + 2 * lines : base + 2 * lines + 8, :] = jnp.zeros((8, FREQ), F32)
 
 
 def add_pair(image, row, k, wcs, num):
@@ -508,10 +503,8 @@
                 for u in range(UNROLL):
                     row = ints_s[3 * block, lane + step * UNROLL + u]
                     k = ints_s[3 * block + 1, lane + step * UNROLL + u]
-                    i = jnp.minimum(quot(row, CAND), per - 1)
-                    row = jnp.where(row == per * CAND, wcs.shape[1] - 8, base + row)
-                    image = pick_image(held_in, 0, i, rows, IMG, z * rows)
-                    add_pair(image, row, k, wcs, num)
+                    image = pick_image(held_in, 0, quot(row, CAND), rows, IMG, z * rows)
+                    add_pair(image, base + row, k, wcs, num)
                 return 0
 
             lax.fori_loop(0, ints_s[3 * block + 2, number], pairs, 0)
@@ -530,7 +523,7 @@
     return den, mass, tail[depth + 8 : depth + 8 + count].astype(jnp.int32)
 
 
-def add_plane(d, chunk, chunks, owner, images, ints, base, blank, wcs, num, first_class):
+def add_plane(d, chunk, chunks, owner, images, ints, base, wcs, num):
     number, _, lane = list_spot(owner, chunk, chunks)
     rows = 2 * num.shape[2] * num.shape[3]
     per = FREQ // CAND
@@ -540,10 +533,8 @@
             for u in range(UNROLL):
                 row = ints[3 * block, lane + step * UNROLL + u]
                 k = ints[3 * block + 1, lane + step * UNROLL + u]
-                i = jnp.minimum(quot(row, CAND), per - 1)
-                row = jnp.where(row == per * CAND, blank, base + block * per * CAND + row)
-                image = pick_image(held_in, d * per, i, rows, rows, 0)
-                add_pair(image, row, k - first_class, wcs, num)
+                image = pick_image(held_in, d * per, quot(row, CAND), rows, rows, 0)
+                add_pair(image, base + block * per * CAND + row, k, wcs, num)
             return 0
 
         lax.fori_loop(0, ints[3 * block + 2, number], pairs, 0)
@@ -552,7 +543,7 @@
 def near_sum_kernel(chunks, pieces, owner_s, *refs):
     images, refs = take(refs, pieces)
     message, first, phases, den_in, mass_in, num, den_out, mass_out, wcs, ints_v, ints_s, sem = refs
-    lines = (wcs.shape[1] - 8) // 2
+    lines = wcs.shape[1] // 2
     depth = den_in.shape[0]
     den, mass, ints_v[...] = read_tail(message, lines, depth, ints_v.shape[0])
     copy = pltpu.make_async_copy(ints_v, ints_s, sem)
@@ -563,7 +554,7 @@
     num[...] = first[...]
     copy.wait()
     for chunk in range(len(chunks)):
-        add_plane(0, chunk, chunks, owner_s[0], images, ints_s, 0, 2 * lines, wcs, num, 0)
+        add_plane(0, chunk, chunks, owner_s[0], images, ints_s, 0, wcs, num)
 
 
 def sum_kernel(chunk, chunks, slices, pieces, grp_s, owner_s, *refs):
@@ -576,7 +567,7 @@
     else:
         wcs, ints_s, own_out, sib_out, num = refs
     group_rows = wcs.shape[1] // (slices - 2)
-    lines = (group_rows - 8) // 2
+    lines = group_rows // 2
     core = grp_s[0] % 2
     start, size = chunks[chunk]
     depth = num.shape[2] * num.shape[3]
@@ -594,15 +585,13 @@
             copy.start()
         for n, message in enumerate(messages):
             put_phases(message[:lines, :], phases, wcs, n * group_rows)
-    num[...] = first[start : start + size]
+    num[...] = first[...]
     if chunk == 0:
         for copy in copies:
             copy.wait()
     for n in range(slices - 2):
-        base = n * group_rows
-        blank = base + group_rows - 8
         add_plane(
-            n + 1, chunk, chunks, owner_s[0], images, ints_s.at[n], base, blank, wcs, num, start
+            n + 1, chunk, chunks, owner_s[0], images, ints_s.at[n], n * group_rows, wcs, num
         )
 
     def pack(k, _):
@@ -611,7 +600,7 @@
         sib_out[k] = other.astype(BF16)
         return 0
 
-    lax.fori_loop(0, size, pack, 0)
+    lax.fori_loop(0, size, pack, 0, unroll=4)
     if chunk == 0:
         width = num.shape[3]
         den_v[...] = den.reshape(2, width, FREQ)
@@ -762,7 +751,7 @@
 
     rf, power, scoring, phases, own_reg = call(
         functools.partial(prep_kernel, depth), "prep", [SMEM] + [HBM] * 4 + [VMEM],
-        [(SHAPE((cls_dev, IMG, FREQ), F32), VMEM), (SHAPE((cls_dev, FREQ), F32), VMEM)]
+        [(SHAPE((cls_dev + 1, IMG, FREQ), F32), VMEM), (SHAPE((cls_dev + 1, FREQ), F32), VMEM)]
         + [(SHAPE(t.shape, t.dtype), VMEM) for t in (scoring, phases)]
         + [(SHAPE((width, FREQ), F32), VMEM)],
         [
@@ -797,7 +786,7 @@
                 VMEM((blocks, height, FREQ), jnp.int32),
                 SMEM((blocks, height, FREQ), jnp.int32),
                 VMEM((blocks, per, FREQ), F32),
-                VMEM((3, block_rows + 8, FREQ), F32),
+                VMEM((3, block_rows, FREQ), F32),
                 VMEM((blocks * per, IMG, FREQ), F32),
                 pltpu.SemaphoreType.DMA((blocks,)),
             ],
@@ -864,9 +853,9 @@
     (first_sums,) = call(
         functools.partial(own_sum_kernel, chunks, arrays), "own_sum",
         [SMEM] * 2 + [VMEM] * (len(flat) + 3),
-        [(SHAPE((cls_dev, 2, 2, width, FREQ), F32), VMEM)],
+        [(SHAPE((cls_dev + 1, 2, 2, width, FREQ), F32), VMEM)],
         [
-            VMEM((2, 2 * lines + 8, FREQ), F32),
+            VMEM((2, 2 * lines, FREQ), F32),
             SMEM(own_lists.shape, jnp.int32),
             pltpu.SemaphoreType.DMA,
         ],
@@ -876,12 +865,12 @@
         functools.partial(near_sum_kernel, chunks, pieces), "near_sum",
         [SMEM] + [VMEM] * (sum(pieces) + 5),
         [
-            (SHAPE((cls_dev, 2, 2, width, FREQ), F32), VMEM),
+            (SHAPE((cls_dev + 1, 2, 2, width, FREQ), F32), VMEM),
             (SHAPE((depth, FREQ), F32), VMEM),
             (SHAPE((8, FREQ), F32), VMEM),
         ],
         [
-            VMEM((2, 2 * lines + 8, FREQ), F32),
+            VMEM((2, 2 * lines, FREQ), F32),
             VMEM(own_lists.shape, jnp.int32),
             SMEM(own_lists.shape, jnp.int32),
             pltpu.SemaphoreType.DMA,
@@ -897,13 +886,13 @@
             (SHAPE((size,) + tile, F32), VMEM),
             (SHAPE((size + more,) + tile, BF16), VMEM),
         ]
-        scratch = [VMEM((size, 2, 2, width, FREQ), F32)]
+        scratch = [VMEM((size + 1, 2, 2, width, FREQ), F32)]
         spaces = [SMEM] * 2 + [VMEM] * (sum(pieces) + nz - 1)
         if more:
             outs += [
                 (SHAPE((width, FREQ), F32), VMEM),
                 (SHAPE((8, FREQ), F32), VMEM),
-                (SHAPE((2, (nz - 2) * (2 * lines + 8), FREQ), F32), VMEM),
+                (SHAPE((2, (nz - 2) * (2 * lines), FREQ), F32), VMEM),
                 (SHAPE((nz - 2,) + own_lists.shape, jnp.int32), SMEM),
             ]
             scratch += [

time: 82.1 us -> 81.2 us (0.989)
  waiting for transfers between devices: 15.7 us -> 23 us
  starting transfers between devices: 36.2 us -> 30.3 us
  Pallas kernels: 27.5 us -> 25.1 us
    ppermute x33 -> x25, waiting for transfers between devices: 15.7 us -> 23 us  [swap(): return lax.ppermute(value, axis, [(i, i ^ distance) for i in range(size)])]
    ppermute x33 -> x25, starting transfers between devices: 36.2 us -> 30.3 us  [swap(): return lax.ppermute(value, axis, [(i, i ^ distance) for i in range(size)])]
    pallas_call x15 -> x13, Pallas kernels: 27.5 us -> 25.1 us  [call(): pl.pallas_call(kernel, out_shape=tuple((s for s, _ in outs)), in_specs=[w...]
  transfers between devices with their start and end apart: 33 -> 25, of which waited for: 10 -> 9; matrix products, arithmetic and copies ran while one was open for 1% -> 1% of each run, Pallas kernels for 25% -> 21%
where the time goes in v6:
time: 81.2 us; the launch traced here: 81.1 us
  starting transfers between devices  30.3 us (37%)
  Pallas kernels  25.1 us (31%)
  waiting for transfers between devices  23 us (28%)
  local copies, waits for them, and re-layouts  1.86 us (2%)
  between operations  0.85 us (1%)
    ppermute x25, starting transfers between devices, swap(): return lax.ppermute(value, axis, [(i, i ^ distance) for i in range(size)])  30.3 us
    pallas_call x13, Pallas kernels, call(): pl.pallas_call(kernel, out_shape=tuple((s for s, _ in outs)), in_specs=[w...  25.1 us
    ppermute x25, waiting for transfers between devices, swap(): return lax.ppermute(value, axis, [(i, i ^ distance) for i in range(size)])  23 us
  transfers between devices with their start and end apart: 25, of which 9 were waited for; matrix products, arithmetic and copies ran while one was open for 1% of the time, Pallas kernels for 21%

profile of v6, /device:TPU:0, one launch (start us, length us, event | category | flops | bytes accessed | tf_op | source)
XLA Modules:
  0.0 81.1 jit_solution(13206196433666919273)
XLA Ops:
  0.6 2.0 %weigh.1 = (bf16[2080,128]{1,0:T(8,128)(2,1)S(1)}, bf16[512,128]{1,0:T(8,128)(2,1)S(1)}, bf16[512,128]{1,0:T(8,128)(2,1)S(1)}, bf16[512,128]{1,0:T(8,128)(2,1)S(1)}) custom-call(s32[1]{0:T(128)} %bitcast.grp_s, bf16[16,16384]{1,0:T(8,128)(2,1)} %particles_h.1, s32[8,16]{1,0:T(8,128)} %bitcast.7, s32[16]{0:T(128)} %groups_h.1, s32[16]{0:T(128)} %entries_h.1, ...), custom_call_target="tpu_custom_call" | custom-call | bytes 7200000 | tf_op jit(solution)/shard_map/weigh/pallas_call | solution.py:684
  2.7 3.0 %collective-permute-start.3 = (bf16[2080,128]{1,0:T(8,128)(2,1)S(1)}, bf16[2080,128]{1,0:T(8,128)(2,1)S(1)}, u32[]{:S(2)}, u32[]{:S(2)}) collective-permute-start(bf16[2080,128]{1,0:T(8,128)(2,1)S(1)} %get-tuple-element.49.refs_0_.refs_10_), channel_id=1, source_target_pairs={{0,2},{1,3},{2,0},{3,1},{4,6},{5,7},{6,4},{7,5},{8,10},{9,11},{10,... | collective-permute-start | bytes 1597448 | tf_op jit(solution)/shard_map/ppermute | solution.py:699
  5.7 1.5 %collective-permute-start.1 = (bf16[2080,128]{1,0:T(8,128)(2,1)S(1)}, bf16[2080,128]{1,0:T(8,128)(2,1)S(1)}, u32[]{:S(2)}, u32[]{:S(2)}) collective-permute-start(bf16[2080,128]{1,0:T(8,128)(2,1)S(1)} %get-tuple-element.49.refs_0_.refs_10_), channel_id=1, source_target_pairs={{0,1},{1,0},{2,3},{3,2},{4,5},{5,4},{6,7},{7,6},{8,9},{9,8},{10,11... | collective-permute-start | bytes 1597448 | tf_op jit(solution)/shard_map/ppermute | solution.py:699
  7.2 1.6 %collective-permute-start = (bf16[512,128]{1,0:T(8,128)(2,1)S(1)}, bf16[512,128]{1,0:T(8,128)(2,1)S(1)}, u32[]{:S(2)}, u32[]{:S(2)}) collective-permute-start(bf16[512,128]{1,0:T(8,128)(2,1)S(1)} %get-tuple-element.47), channel_id=1, source_target_pairs={{0,8},{4,12},{8,0},{12,4},{16,24},{20,28},{24,16},{28,20},{1,9},{5... | collective-permute-start | bytes 393224 | tf_op jit(solution)/shard_map/ppermute | solution.py:699
  8.8 2.6 %collective-permute-start.2 = (bf16[512,128]{1,0:T(8,128)(2,1)S(1)}, bf16[512,128]{1,0:T(8,128)(2,1)S(1)}, u32[]{:S(2)}, u32[]{:S(2)}) collective-permute-start(bf16[512,128]{1,0:T(8,128)(2,1)S(1)} %get-tuple-element.54), channel_id=1, source_target_pairs={{0,16},{4,20},{8,24},{12,28},{16,0},{20,4},{24,8},{28,12},{1,17},{... | collective-permute-start | bytes 393224 | tf_op jit(solution)/shard_map/ppermute | solution.py:699
  12.0 3.8 %prep.1 = (f32[53,128,128]{2,1,0:T(8,128)S(1)}, f32[53,128]{1,0:T(8,128)S(1)}, f32[384,64]{1,0:T(8,128)S(1)}, bf16[256,512]{1,0:T(8,128)(2,1)S(1)}, f32[8,128]{1,0:T(8,128)S(1)}) custom-call(s32[1]{0:T(128)} %bitcast.grp_s, bf16[52,16384]{1,0:T(8,128)(2,1)} %refs_h.1, f32[384,64]{1,0:T(8,128)} %constant.15.clone.rest_refs_0_, ...), custom_call_target="tpu_custom_call" | custom-call | bytes 14400000 | tf_op jit(solution)/shard_map/prep/pallas_call | solution.py:684
  15.8 1.8 %score.3 = (f32[128,64]{1,0:T(8,128)S(1)}, f32[16,128]{1,0:T(8,128)S(1)}, f32[128,128]{1,0:T(8,128)S(1)}) custom-call(s32[1]{0:T(128)S(6)} %mul.3.first_s, s32[1]{0:T(128)} %bitcast.1.owner_s, bf16[2080,128]{1,0:T(8,128)(2,1)S(1)} %get-tuple-element.49.refs_0_.refs_10_, f32[53,128,128]{2,1,0:T(8,128)S(1)} %get-tuple-element.50.refs_1_.refs_2_.refs_4_, ...), custom_call_target="tpu_custom_call" | custom-call | bytes 10800000 | tf_op jit(solution)/shard_map/score/pallas_call | solution.py:684
  17.8 1.8 %collective-permute-start.5 = (bf16[1056,128]{1,0:T(8,128)(2,1)S(1)}, bf16[1056,128]{1,0:T(8,128)(2,1)S(1)}, u32[]{:S(2)}, u32[]{:S(2)}) collective-permute-start(bf16[1056,128]{1,0:T(8,128)(2,1)S(1)} %slice.19), channel_id=1, source_target_pairs={{0,1},{1,0},{2,3},{3,2},{4,5},{5,4},{6,7},{7,6},{8,9},{9,8},{10,11... | collective-permute-start | bytes 811016 | tf_op jit(solution)/shard_map/ppermute | solution.py:699
  19.6 1.6 %collective-permute-start.4 = (bf16[1024,128]{1,0:T(8,128)(2,1)S(1)}, bf16[1024,128]{1,0:T(8,128)(2,1)S(1)}, u32[]{:S(2)}, u32[]{:S(2)}) collective-permute-start(bf16[1024,128]{1,0:T(8,128)(2,1)S(1)} %slice.18), channel_id=1, source_target_pairs={{0,2},{1,3},{2,0},{3,1},{4,6},{5,7},{6,4},{7,5},{8,10},{9,11},{10,... | collective-permute-start | bytes 786440 | tf_op jit(solution)/shard_map/ppermute | solution.py:699
  21.2 3.6 %collective-permute-start.6 = (bf16[512,128]{1,0:T(8,128)(2,1)S(1)}, bf16[512,128]{1,0:T(8,128)(2,1)S(1)}, u32[]{:S(2)}, u32[]{:S(2)}) collective-permute-start(bf16[512,128]{1,0:T(8,128)(2,1)S(1)} %get-tuple-element.59), channel_id=1, source_target_pairs={{0,24},{4,28},{8,16},{12,20},{16,8},{20,12},{24,0},{28,4},{1,25},{... | collective-permute-start | bytes 393224 | tf_op jit(solution)/shard_map/ppermute | solution.py:699
  24.8 3.3 %score.4 = (f32[256,64]{1,0:T(8,128)S(1)}, f32[32,128]{1,0:T(8,128)S(1)}, f32[256,128]{1,0:T(8,128)S(1)}) custom-call(s32[1]{0:T(128)S(6)} %mul.3.first_s, s32[1]{0:T(128)} %bitcast.1.owner_s, bf16[2080,128]{1,0:T(8,128)(2,1)S(1)} %collective-permute-done.1.refs_0_.refs_11_.refs_1_, bf16[2080,128]{1,0:T(8,128)(2,1)S(1)} %collective-permute-done.3.refs_1_.refs_12_.refs_2_, ...), custom_call_target="tpu_custom_call" | custom-call | bytes 21600000 | tf_op jit(solution)/shard_map/score/pallas_call | solution.py:684
  28.8 1.3 %collective-permute-start.7 = (bf16[1536,128]{1,0:T(8,128)(2,1)S(1)}, bf16[1536,128]{1,0:T(8,128)(2,1)S(1)}, u32[]{:S(2)}, u32[]{:S(2)}) collective-permute-start(bf16[1536,128]{1,0:T(8,128)(2,1)S(1)} %join.1.refs_0_), channel_id=1, source_target_pairs={{0,1},{1,0},{2,3},{3,2},{4,5},{5,4},{6,7},{7,6},{8,9},{9,8},{10,11... | collective-permute-start | bytes 1179656 | tf_op jit(solution)/shard_map/ppermute | solution.py:699
  30.1 1.8 %score.5 = (f32[128,64]{1,0:T(8,128)S(1)}, f32[64,128]{1,0:T(8,128)S(1)}, f32[128,128]{1,0:T(8,128)S(1)}) custom-call(s32[1]{0:T(128)S(6)} %mul.3.first_s, s32[1]{0:T(128)} %bitcast.1.owner_s, bf16[1024,128]{1,0:T(8,128)(2,1)S(1)} %collective-permute-done.4.refs_0_.refs_3_, bf16[1056,128]{1,0:T(8,128)(2,1)S(1)} %collective-permute-done.5.refs_1_.refs_13_.refs_4_, ...), custom_call_target="tpu_custom_call" | custom-call | bytes 10800000 | tf_op jit(solution)/shard_map/score/pallas_call | solution.py:684
  31.8 1.8 %collective-permute-start.10 = (f32[64,128]{1,0:T(8,128)S(1)}, f32[64,128]{1,0:T(8,128)S(1)}, u32[]{:S(2)}, u32[]{:S(2)}) collective-permute-start(f32[64,128]{1,0:T(8,128)S(1)} %get-tuple-element.60.refs_0_), channel_id=1, source_target_pairs={{0,3},{1,2},{2,1},{3,0},{4,7},{5,6},{6,5},{7,4},{8,11},{9,10},{10,... | collective-permute-start | bytes 98312 | tf_op jit(solution)/shard_map/ppermute | solution.py:699
  34.1 1.3 %collective-permute-start.8 = (f32[64,128]{1,0:T(8,128)S(1)}, f32[64,128]{1,0:T(8,128)S(1)}, u32[]{:S(2)}, u32[]{:S(2)}) collective-permute-start(f32[64,128]{1,0:T(8,128)S(1)} %get-tuple-element.60.refs_0_), channel_id=1, source_target_pairs={{0,1},{1,0},{2,3},{3,2},{4,5},{5,4},{6,7},{7,6},{8,9},{9,8},{10,11... | collective-permute-start | bytes 98312 | tf_op jit(solution)/shard_map/ppermute | solution.py:699
  35.4 4.1 %collective-permute-done.10.refs_3_ = f32[64,128]{1,0:T(8,128)S(1)} collective-permute-done((f32[64,128]{1,0:T(8,128)S(1)}, f32[64,128]{1,0:T(8,128)S(1)}, u32[]{:S(2)}, u32[]{:S(2)}) %collective-permute-start.10) | collective-permute-done | bytes 32800 | tf_op jit(solution)/shard_map/ppermute | solution.py:699
  41.2 1.2 %collective-permute-start.12 = (bf16[768,128]{1,0:T(8,128)(2,1)S(1)}, bf16[768,128]{1,0:T(8,128)(2,1)S(1)}, u32[]{:S(2)}, u32[]{:S(2)}) collective-permute-start(bf16[768,128]{1,0:T(8,128)(2,1)S(1)} %slice.20), channel_id=1, source_target_pairs={{0,2},{1,3},{2,0},{3,1},{4,6},{5,7},{6,4},{7,5},{8,10},{9,11},{10,... | collective-permute-start | bytes 589832 | tf_op jit(solution)/shard_map/ppermute | solution.py:699
  42.8 2.9 %collective-permute-start.14 = (bf16[304,128]{1,0:T(8,128)(2,1)S(1)}, bf16[304,128]{1,0:T(8,128)(2,1)S(1)}, u32[]{:S(2)}, u32[]{:S(2)}) collective-permute-start(bf16[304,128]{1,0:T(8,128)(2,1)S(1)} %get-tuple-element.70), channel_id=1, source_target_pairs={{0,16},{4,20},{8,24},{12,28},{16,0},{20,4},{24,8},{28,12},{1,17},{... | collective-permute-start | bytes 233480 | tf_op jit(solution)/shard_map/ppermute | solution.py:699
  45.7 1.1 %collective-permute-start.15 = (bf16[304,128]{1,0:T(8,128)(2,1)S(1)}, bf16[304,128]{1,0:T(8,128)(2,1)S(1)}, u32[]{:S(2)}, u32[]{:S(2)}) collective-permute-start(bf16[304,128]{1,0:T(8,128)(2,1)S(1)} %get-tuple-element.71), channel_id=1, source_target_pairs={{0,24},{4,28},{8,16},{12,20},{16,8},{20,12},{24,0},{28,4},{1,25},{... | collective-permute-start | bytes 233480 | tf_op jit(solution)/shard_map/ppermute | solution.py:699
  46.8 1.8 %own_sum.1.refs_6_ = f32[53,2,2,8,128]{4,3,2,1,0:T(8,128)S(1)} custom-call(s32[1]{0:T(128)} %bitcast.grp_s, s32[1]{0:T(128)} %bitcast.1.owner_s, bf16[256,128]{1,0:T(8,128)(2,1)S(1)} %get-tuple-element.67.packed, s32[16,128]{1,0:T(8,128)S(1)} %get-tuple-element.73.ints, bf16[2080,128]{1,0:T(8,128)(2,1)S(1)} %get-tuple-element.49.refs_0_.refs_10_, ...), custom_call_target="tpu_custom_call" | custom-call | bytes 10800000 | tf_op jit(solution)/shard_map/own_sum/pallas_call | solution.py:684
  48.6 1.8 %near_sum.1 = (f32[53,2,2,8,128]{4,3,2,1,0:T(8,128)S(1)}, f32[16,128]{1,0:T(8,128)S(1)}, f32[8,128]{1,0:T(8,128)S(1)}) custom-call(s32[1]{0:T(128)} %bitcast.1.owner_s, bf16[1536,128]{1,0:T(8,128)(2,1)S(1)} %join.1.refs_0_, bf16[1536,128]{1,0:T(8,128)(2,1)S(1)} %collective-permute-done.7.refs_1_, bf16[1536,128]{1,0:T(8,128)(2,1)S(1)} %collective-permute-done.11.refs_2_, ...), custom_call_target="tpu_custom_call" | custom-call | bytes 7200000 | tf_op jit(solution)/shard_map/near_sum/pallas_call | solution.py:684
  50.4 1.5 %collective-permute-done.15.refs_6_ = bf16[304,128]{1,0:T(8,128)(2,1)S(1)} collective-permute-done((bf16[304,128]{1,0:T(8,128)(2,1)S(1)}, bf16[304,128]{1,0:T(8,128)(2,1)S(1)}, u32[]{:S(2)}, u32[]{:S(2)}) %collective-permute-start.15) | collective-permute-done | bytes 77856 | tf_op jit(solution)/shard_map/ppermute | solution.py:699
  51.9 4.2 %sum.1 = (f32[52,16,128]{2,1,0:T(8,128)S(1)}, bf16[53,16,128]{2,1,0:T(8,128)(2,1)S(1)}, f32[8,128]{1,0:T(8,128)S(1)}, f32[8,128]{1,0:T(8,128)S(1)}, f32[2,1024,128]{2,1,0:T(8,128)}, /*index=5*/s32[2,16,128]{2,1,0:T(8,128)}) custom-call(s32[1]{0:T(128)} %bitcast.grp_s, s32[1]{0:T(128)} %bitcast.1.owner_s, bf16[1536,128]{1,0:T(8,128)(2,1)S(1)} %join.1.refs_0_, ...), custom_call_target="tpu_custom_call" | custom-call | bytes 10800000 | tf_op jit(solution)/shard_map/sum/pallas_call | solution.py:684
  56.2 1.5 %collective-permute-done.17.sib = bf16[53,16,128]{2,1,0:T(8,128)(2,1)S(1)} collective-permute-done((bf16[53,16,128]{2,1,0:T(8,128)(2,1)S(1)}, bf16[53,16,128]{2,1,0:T(8,128)(2,1)S(1)}, u32[]{:S(2)}, u32[]{:S(2)}) %collective-permute-start.17) | collective-permute-done | bytes 217120 | tf_op jit(solution)/shard_map/ppermute | solution.py:699
  58.3 0.9 %collective-permute-start.19 = (bf16[52,16,128]{2,1,0:T(8,128)(2,1)S(1)}, bf16[52,16,128]{2,1,0:T(8,128)(2,1)S(1)}, u32[]{:S(2)}, u32[]{:S(2)}) collective-permute-start(bf16[52,16,128]{2,1,0:T(8,128)(2,1)S(1)} %get-tuple-element.85.refs_0_), channel_id=1, source_target_pairs={{0,16},{4,20},{8,24},{12,28},{16,0},{20,4},{24,8},{28,12},{1,17},{... | collective-permute-start | bytes 638984 | tf_op jit(solution)/shard_map/ppermute | solution.py:699
  59.2 1.0 %collective-permute-start.18 = (bf16[52,16,128]{2,1,0:T(8,128)(2,1)S(1)}, bf16[52,16,128]{2,1,0:T(8,128)(2,1)S(1)}, u32[]{:S(2)}, u32[]{:S(2)}) collective-permute-start(bf16[52,16,128]{2,1,0:T(8,128)(2,1)S(1)} %get-tuple-element.85.refs_0_), channel_id=1, source_target_pairs={{0,8},{4,12},{8,0},{12,4},{16,24},{20,28},{24,16},{28,20},{1,9},{5... | collective-permute-start | bytes 638984 | tf_op jit(solution)/shard_map/ppermute | solution.py:699
  60.1 9.7 %collective-permute-done.19.refs_4_ = bf16[52,16,128]{2,1,0:T(8,128)(2,1)S(1)} collective-permute-done((bf16[52,16,128]{2,1,0:T(8,128)(2,1)S(1)}, bf16[52,16,128]{2,1,0:T(8,128)(2,1)S(1)}, u32[]{:S(2)}, u32[]{:S(2)}) %collective-permute-start.19) | collective-permute-done | bytes 213024 | tf_op jit(solution)/shard_map/ppermute | solution.py:699
  69.8 0.9 %collective-permute-done.18.refs_2_ = bf16[52,16,128]{2,1,0:T(8,128)(2,1)S(1)} collective-permute-done((bf16[52,16,128]{2,1,0:T(8,128)(2,1)S(1)}, bf16[52,16,128]{2,1,0:T(8,128)(2,1)S(1)}, u32[]{:S(2)}, u32[]{:S(2)}) %collective-permute-start.18) | collective-permute-done | bytes 213024 | tf_op jit(solution)/shard_map/ppermute | solution.py:699
  72.5 2.0 %spread.2.refs_2_ = f32[52,16384]{1,0:T(8,128)} custom-call(s32[1]{0:T(128)} %bitcast.grp_s, bf16[52,16,128]{2,1,0:T(8,128)(2,1)S(1)} %get-tuple-element.85.refs_0_, bf16[52,16,128]{2,1,0:T(8,128)(2,1)S(1)} %collective-permute-done.21.refs_1_, bf16[52,16,128]{2,1,0:T(8,128)(2,1)S(1)} %collective-permute-done.18.refs_2_, ...), custom_call_target="tpu_custom_call" | custom-call | bytes 180000 | tf_op jit(solution)/shard_map/spread/pallas_call | solution.py:684
  74.5 3.9 %collective-permute-done.20.refs_0_ = bf16[52,16,128]{2,1,0:T(8,128)(2,1)S(1)} collective-permute-done((bf16[52,16,128]{2,1,0:T(8,128)(2,1)S(1)}, bf16[52,16,128]{2,1,0:T(8,128)(2,1)S(1)}, u32[]{:S(2)}, u32[]{:S(2)}) %collective-permute-start.20) | collective-permute-done | bytes 213024 | tf_op jit(solution)/shard_map/ppermute | solution.py:699
  78.9 0.9 %collective-permute-done.24.refs_1_ = bf16[52,16,128]{2,1,0:T(8,128)(2,1)S(1)} collective-permute-done((bf16[52,16,128]{2,1,0:T(8,128)(2,1)S(1)}, bf16[52,16,128]{2,1,0:T(8,128)(2,1)S(1)}, u32[]{:S(2)}, u32[]{:S(2)}) %collective-permute-start.24) | collective-permute-done | bytes 213024 | tf_op jit(solution)/shard_map/ppermute | solution.py:699
  79.9 1.2 %spread.3 = f32[52,16384]{1,0:T(8,128)} custom-call(s32[1]{0:T(128)} %bitcast.grp_s, bf16[52,16,128]{2,1,0:T(8,128)(2,1)S(1)} %collective-permute-done.20.refs_0_, bf16[52,16,128]{2,1,0:T(8,128)(2,1)S(1)} %collective-permute-done.24.refs_1_, f32[52,16384]{1,0:T(8,128)} %spread.2.refs_2_), custom_call_target="tpu_custom_call", output_to_operand_aliasing={{}: (3, {})} | custom-call | bytes 180000 | tf_op jit(solution)/shard_map/spread/pallas_call | solution.py:684
  (39 shorter events, 7.1 us)
Async XLA Ops:
  2.7 15.1 %collective-permute-start.3 = (bf16[2080,128]{1,0:T(8,128)(2,1)S(1)}, bf16[2080,128]{1,0:T(8,128)(2,1)S(1)}, u32[]{:S(2)}, u32[]{:S(2)}) collective-permute-start(bf16[2080,128]{1,0:T(8,128)(2,1)S(1)} %get-tuple-element.49.refs_0_.refs_10_), channel_id=1, source_target_pairs={{0,2},{1,3},{2,0},{3,1},{4,6},{5,7},{6,4},{7,5},{8,10},{9,11},{10,... | collective-permute-start | bytes 1597448 | tf_op jit(solution)/shard_map/ppermute | solution.py:699
  5.7 13.9 %collective-permute-start.1 = (bf16[2080,128]{1,0:T(8,128)(2,1)S(1)}, bf16[2080,128]{1,0:T(8,128)(2,1)S(1)}, u32[]{:S(2)}, u32[]{:S(2)}) collective-permute-start(bf16[2080,128]{1,0:T(8,128)(2,1)S(1)} %get-tuple-element.49.refs_0_.refs_10_), channel_id=1, source_target_pairs={{0,1},{1,0},{2,3},{3,2},{4,5},{5,4},{6,7},{7,6},{8,9},{9,8},{10,11... | collective-permute-start | bytes 1597448 | tf_op jit(solution)/shard_map/ppermute | solution.py:699
  7.2 8.6 %collective-permute-start = (bf16[512,128]{1,0:T(8,128)(2,1)S(1)}, bf16[512,128]{1,0:T(8,128)(2,1)S(1)}, u32[]{:S(2)}, u32[]{:S(2)}) collective-permute-start(bf16[512,128]{1,0:T(8,128)(2,1)S(1)} %get-tuple-element.47), channel_id=1, source_target_pairs={{0,8},{4,12},{8,0},{12,4},{16,24},{20,28},{24,16},{28,20},{1,9},{5... | collective-permute-start | bytes 393224 | tf_op jit(solution)/shard_map/ppermute | solution.py:699
  8.8 8.8 %collective-permute-start.2 = (bf16[512,128]{1,0:T(8,128)(2,1)S(1)}, bf16[512,128]{1,0:T(8,128)(2,1)S(1)}, u32[]{:S(2)}, u32[]{:S(2)}) collective-permute-start(bf16[512,128]{1,0:T(8,128)(2,1)S(1)} %get-tuple-element.54), channel_id=1, source_target_pairs={{0,16},{4,20},{8,24},{12,28},{16,0},{20,4},{24,8},{28,12},{1,17},{... | collective-permute-start | bytes 393224 | tf_op jit(solution)/shard_map/ppermute | solution.py:699
  11.4 0.7 copy-start
  17.8 10.3 %collective-permute-start.5 = (bf16[1056,128]{1,0:T(8,128)(2,1)S(1)}, bf16[1056,128]{1,0:T(8,128)(2,1)S(1)}, u32[]{:S(2)}, u32[]{:S(2)}) collective-permute-start(bf16[1056,128]{1,0:T(8,128)(2,1)S(1)} %slice.19), channel_id=1, source_target_pairs={{0,1},{1,0},{2,3},{3,2},{4,5},{5,4},{6,7},{7,6},{8,9},{9,8},{10,11... | collective-permute-start | bytes 811016 | tf_op jit(solution)/shard_map/ppermute | solution.py:699
  19.6 8.5 %collective-permute-start.4 = (bf16[1024,128]{1,0:T(8,128)(2,1)S(1)}, bf16[1024,128]{1,0:T(8,128)(2,1)S(1)}, u32[]{:S(2)}, u32[]{:S(2)}) collective-permute-start(bf16[1024,128]{1,0:T(8,128)(2,1)S(1)} %slice.18), channel_id=1, source_target_pairs={{0,2},{1,3},{2,0},{3,1},{4,6},{5,7},{6,4},{7,5},{8,10},{9,11},{10,... | collective-permute-start | bytes 786440 | tf_op jit(solution)/shard_map/ppermute | solution.py:699
  21.2 6.9 %collective-permute-start.6 = (bf16[512,128]{1,0:T(8,128)(2,1)S(1)}, bf16[512,128]{1,0:T(8,128)(2,1)S(1)}, u32[]{:S(2)}, u32[]{:S(2)}) collective-permute-start(bf16[512,128]{1,0:T(8,128)(2,1)S(1)} %get-tuple-element.59), channel_id=1, source_target_pairs={{0,24},{4,28},{8,16},{12,20},{16,8},{20,12},{24,0},{28,4},{1,25},{... | collective-permute-start | bytes 393224 | tf_op jit(solution)/shard_map/ppermute | solution.py:699
  28.1 12.2 %collective-permute-start.11 = (bf16[1536,128]{1,0:T(8,128)(2,1)S(1)}, bf16[1536,128]{1,0:T(8,128)(2,1)S(1)}, u32[]{:S(2)}, u32[]{:S(2)}) collective-permute-start(bf16[1536,128]{1,0:T(8,128)(2,1)S(1)} %join.1.refs_0_), channel_id=1, source_target_pairs={{0,2},{1,3},{2,0},{3,1},{4,6},{5,7},{6,4},{7,5},{8,10},{9,11},{10,... | collective-permute-start | bytes 1179656 | tf_op jit(solution)/shard_map/ppermute | solution.py:699
  28.8 12.4 %collective-permute-start.7 = (bf16[1536,128]{1,0:T(8,128)(2,1)S(1)}, bf16[1536,128]{1,0:T(8,128)(2,1)S(1)}, u32[]{:S(2)}, u32[]{:S(2)}) collective-permute-start(bf16[1536,128]{1,0:T(8,128)(2,1)S(1)} %join.1.refs_0_), channel_id=1, source_target_pairs={{0,1},{1,0},{2,3},{3,2},{4,5},{5,4},{6,7},{7,6},{8,9},{9,8},{10,11... | collective-permute-start | bytes 1179656 | tf_op jit(solution)/shard_map/ppermute | solution.py:699
  31.8 7.7 %collective-permute-start.10 = (f32[64,128]{1,0:T(8,128)S(1)}, f32[64,128]{1,0:T(8,128)S(1)}, u32[]{:S(2)}, u32[]{:S(2)}) collective-permute-start(f32[64,128]{1,0:T(8,128)S(1)} %get-tuple-element.60.refs_0_), channel_id=1, source_target_pairs={{0,3},{1,2},{2,1},{3,0},{4,7},{5,6},{6,5},{7,4},{8,11},{9,10},{10,... | collective-permute-start | bytes 98312 | tf_op jit(solution)/shard_map/ppermute | solution.py:699
  33.6 5.9 %collective-permute-start.9 = (f32[64,128]{1,0:T(8,128)S(1)}, f32[64,128]{1,0:T(8,128)S(1)}, u32[]{:S(2)}, u32[]{:S(2)}) collective-permute-start(f32[64,128]{1,0:T(8,128)S(1)} %get-tuple-element.60.refs_0_), channel_id=1, source_target_pairs={{0,2},{1,3},{2,0},{3,1},{4,6},{5,7},{6,4},{7,5},{8,10},{9,11},{10,... | collective-permute-start | bytes 98312 | tf_op jit(solution)/shard_map/ppermute | solution.py:699
  34.1 5.5 %collective-permute-start.8 = (f32[64,128]{1,0:T(8,128)S(1)}, f32[64,128]{1,0:T(8,128)S(1)}, u32[]{:S(2)}, u32[]{:S(2)}) collective-permute-start(f32[64,128]{1,0:T(8,128)S(1)} %get-tuple-element.60.refs_0_), channel_id=1, source_target_pairs={{0,1},{1,0},{2,3},{3,2},{4,5},{5,4},{6,7},{7,6},{8,9},{9,8},{10,11... | collective-permute-start | bytes 98312 | tf_op jit(solution)/shard_map/ppermute | solution.py:699
  40.3 8.3 %collective-permute-start.13 = (bf16[768,128]{1,0:T(8,128)(2,1)S(1)}, bf16[768,128]{1,0:T(8,128)(2,1)S(1)}, u32[]{:S(2)}, u32[]{:S(2)}) collective-permute-start(bf16[768,128]{1,0:T(8,128)(2,1)S(1)} %slice.21), channel_id=1, source_target_pairs={{0,1},{1,0},{2,3},{3,2},{4,5},{5,4},{6,7},{7,6},{8,9},{9,8},{10,11... | collective-permute-start | bytes 589832 | tf_op jit(solution)/shard_map/ppermute | solution.py:699
  41.2 7.4 %collective-permute-start.12 = (bf16[768,128]{1,0:T(8,128)(2,1)S(1)}, bf16[768,128]{1,0:T(8,128)(2,1)S(1)}, u32[]{:S(2)}, u32[]{:S(2)}) collective-permute-start(bf16[768,128]{1,0:T(8,128)(2,1)S(1)} %slice.20), channel_id=1, source_target_pairs={{0,2},{1,3},{2,0},{3,1},{4,6},{5,7},{6,4},{7,5},{8,10},{9,11},{10,... | collective-permute-start | bytes 589832 | tf_op jit(solution)/shard_map/ppermute | solution.py:699
  42.4 6.2 %collective-permute-start.16 = (bf16[304,128]{1,0:T(8,128)(2,1)S(1)}, bf16[304,128]{1,0:T(8,128)(2,1)S(1)}, u32[]{:S(2)}, u32[]{:S(2)}) collective-permute-start(bf16[304,128]{1,0:T(8,128)(2,1)S(1)} %get-tuple-element.72), channel_id=1, source_target_pairs={{0,8},{4,12},{8,0},{12,4},{16,24},{20,28},{24,16},{28,20},{1,9},{5... | collective-permute-start | bytes 233480 | tf_op jit(solution)/shard_map/ppermute | solution.py:699
  42.8 7.6 %collective-permute-start.14 = (bf16[304,128]{1,0:T(8,128)(2,1)S(1)}, bf16[304,128]{1,0:T(8,128)(2,1)S(1)}, u32[]{:S(2)}, u32[]{:S(2)}) collective-permute-start(bf16[304,128]{1,0:T(8,128)(2,1)S(1)} %get-tuple-element.70), channel_id=1, source_target_pairs={{0,16},{4,20},{8,24},{12,28},{16,0},{20,4},{24,8},{28,12},{1,17},{... | collective-permute-start | bytes 233480 | tf_op jit(solution)/shard_map/ppermute | solution.py:699
  45.7 6.2 %collective-permute-start.15 = (bf16[304,128]{1,0:T(8,128)(2,1)S(1)}, bf16[304,128]{1,0:T(8,128)(2,1)S(1)}, u32[]{:S(2)}, u32[]{:S(2)}) collective-permute-start(bf16[304,128]{1,0:T(8,128)(2,1)S(1)} %get-tuple-element.71), channel_id=1, source_target_pairs={{0,24},{4,28},{8,16},{12,20},{16,8},{20,12},{24,0},{28,4},{1,25},{... | collective-permute-start | bytes 233480 | tf_op jit(solution)/shard_map/ppermute | solution.py:699
  56.1 1.5 %collective-permute-start.17 = (bf16[53,16,128]{2,1,0:T(8,128)(2,1)S(1)}, bf16[53,16,128]{2,1,0:T(8,128)(2,1)S(1)}, u32[]{:S(2)}, u32[]{:S(2)}) collective-permute-start(bf16[53,16,128]{2,1,0:T(8,128)(2,1)S(1)} %get-tuple-element.81), channel_id=1, source_target_pairs={{0,4},{4,0},{8,12},{12,8},{16,20},{20,16},{24,28},{28,24},{1,5},{5... | collective-permute-start | bytes 651272 | tf_op jit(solution)/shard_map/ppermute | solution.py:699
  58.3 11.5 %collective-permute-start.19 = (bf16[52,16,128]{2,1,0:T(8,128)(2,1)S(1)}, bf16[52,16,128]{2,1,0:T(8,128)(2,1)S(1)}, u32[]{:S(2)}, u32[]{:S(2)}) collective-permute-start(bf16[52,16,128]{2,1,0:T(8,128)(2,1)S(1)} %get-tuple-element.85.refs_0_), channel_id=1, source_target_pairs={{0,16},{4,20},{8,24},{12,28},{16,0},{20,4},{24,8},{28,12},{1,17},{... | collective-permute-start | bytes 638984 | tf_op jit(solution)/shard_map/ppermute | solution.py:699
  59.2 11.6 %collective-permute-start.18 = (bf16[52,16,128]{2,1,0:T(8,128)(2,1)S(1)}, bf16[52,16,128]{2,1,0:T(8,128)(2,1)S(1)}, u32[]{:S(2)}, u32[]{:S(2)}) collective-permute-start(bf16[52,16,128]{2,1,0:T(8,128)(2,1)S(1)} %get-tuple-element.85.refs_0_), channel_id=1, source_target_pairs={{0,8},{4,12},{8,0},{12,4},{16,24},{20,28},{24,16},{28,20},{1,9},{5... | collective-permute-start | bytes 638984 | tf_op jit(solution)/shard_map/ppermute | solution.py:699
  60.1 12.1 %collective-permute-start.21 = (bf16[52,16,128]{2,1,0:T(8,128)(2,1)S(1)}, bf16[52,16,128]{2,1,0:T(8,128)(2,1)S(1)}, u32[]{:S(2)}, u32[]{:S(2)}) collective-permute-start(bf16[52,16,128]{2,1,0:T(8,128)(2,1)S(1)} %get-tuple-element.85.refs_0_), channel_id=1, source_target_pairs={{0,4},{4,0},{8,12},{12,8},{16,20},{20,16},{24,28},{28,24},{1,5},{5... | collective-permute-start | bytes 638984 | tf_op jit(solution)/shard_map/ppermute | solution.py:699
  70.7 1.5 %collective-permute-start.22 = (bf16[52,16,128]{2,1,0:T(8,128)(2,1)S(1)}, bf16[52,16,128]{2,1,0:T(8,128)(2,1)S(1)}, u32[]{:S(2)}, u32[]{:S(2)}) collective-permute-start(bf16[52,16,128]{2,1,0:T(8,128)(2,1)S(1)} %collective-permute-done.18.refs_2_), channel_id=1, source_target_pairs={{0,4},{4,0},{8,12},{12,8},{16,20},{20,16},{24,28},{28,24},{1,5},{5... | collective-permute-start | bytes 638984 | tf_op jit(solution)/shard_map/ppermute | solution.py:699
  70.7 1.8 %collective-permute-start.23 = (bf16[52,16,128]{2,1,0:T(8,128)(2,1)S(1)}, bf16[52,16,128]{2,1,0:T(8,128)(2,1)S(1)}, u32[]{:S(2)}, u32[]{:S(2)}) collective-permute-start(bf16[52,16,128]{2,1,0:T(8,128)(2,1)S(1)} %collective-permute-done.19.refs_4_), channel_id=1, source_target_pairs={{0,4},{4,0},{8,12},{12,8},{16,20},{20,16},{24,28},{28,24},{1,5},{5... | collective-permute-start | bytes 638984 | tf_op jit(solution)/shard_map/ppermute | solution.py:699
  71.2 7.2 %collective-permute-start.20 = (bf16[52,16,128]{2,1,0:T(8,128)(2,1)S(1)}, bf16[52,16,128]{2,1,0:T(8,128)(2,1)S(1)}, u32[]{:S(2)}, u32[]{:S(2)}) collective-permute-start(bf16[52,16,128]{2,1,0:T(8,128)(2,1)S(1)} %collective-permute-done.19.refs_4_), channel_id=1, source_target_pairs={{0,8},{4,12},{8,0},{12,4},{16,24},{20,28},{24,16},{28,20},{1,9},{5... | collective-permute-start | bytes 638984 | tf_op jit(solution)/shard_map/ppermute | solution.py:699
  78.4 1.5 %collective-permute-start.24 = (bf16[52,16,128]{2,1,0:T(8,128)(2,1)S(1)}, bf16[52,16,128]{2,1,0:T(8,128)(2,1)S(1)}, u32[]{:S(2)}, u32[]{:S(2)}) collective-permute-start(bf16[52,16,128]{2,1,0:T(8,128)(2,1)S(1)} %collective-permute-done.20.refs_0_), channel_id=1, source_target_pairs={{0,4},{4,0},{8,12},{12,8},{16,20},{20,16},{24,28},{28,24},{1,5},{5... | collective-permute-start | bytes 638984 | tf_op jit(solution)/shard_map/ppermute | solution.py:699

commit v7 on v6

--- a/solution.py
+++ b/solution.py
@@ -65,6 +65,10 @@
     number = owner * len(chunks) + chunk
     at = number * list_room(chunks)
     return number, quot(at, FREQ), rest(at, FREQ)
+
+
+def list_slots(cls_dev):
+    return -(-cls_dev * MOST // 8) * 8
 
 
 def quot(v, n):
@@ -160,7 +164,7 @@
     for copy in copies:
         copy.start()
     per = particles.shape[0]
-    pad = spread.shape[0] // IMG
+    pad = spread.shape[0] // (IMG + 1)
     for copy in copies[:2]:
         copy.wait()
     for i in range(per):
@@ -205,7 +209,7 @@
     refs, spread, reg, sem = rest_refs[5:]
     cls_dev = refs.shape[0]
     pow_out[cls_dev:, :] = jnp.zeros((pow_out.shape[0] - cls_dev, FREQ), F32)
-    pad = spread.shape[0] // IMG
+    pad = spread.shape[0] // (IMG + 1)
     parts = sem.shape[0] - 3
     step = FEAT // parts
     tables_in = [
@@ -376,12 +380,17 @@
     extras = refs[blocks + 2 * calls : 2 * blocks + 2 * calls]
     refs = refs[2 * blocks + 2 * calls :]
     own_out, den_out, mass_out, log_out, ints_out = refs[:5]
-    message_outs = refs[5:-3]
-    rows_v, den_v, lists_v = refs[-3:]
+    message_outs = refs[5:-4]
+    rows_v, den_v, lists_v, picked_v = refs[-4:]
     per = log_out.shape[0]
     block_rows = per * CAND
     depth = SHELLS // slices
     z = grp_s[0] // 2
+
+    half = list_lines(blocks, chunks)[0]
+    _, line, lane = list_spot(owner_s[0], 0, chunks)
+    slots = list_slots(cls_dev)
+    lists = []
 
     den = jnp.zeros((FREQ, FREQ), F32)
     mass = jnp.zeros((1, FREQ), F32)
@@ -402,7 +411,17 @@
             local = cls_ref[at, :]
             good = jnp.logical_and(local >= 0, local < cls_dev)[:, :ROTS]
             weights = rounded(jnp.where(good, weights, 0.0))
-            rows_v[block * block_rows : (block + 1) * block_rows, :] = weights
+            lists_v[...] = extras[block][extras[block].shape[0] - lists_v.shape[0] :, :].astype(F32)
+            named = jnp.broadcast_to(lists_v[pl.ds(line, 1), :], (block_rows, FREQ))
+            row = lax.broadcasted_iota(jnp.int32, named.shape, 0).astype(F32)
+            picked_v[...] = lax.dot_general(
+                (named == row).astype(F32).astype(BF16), weights.astype(BF16),
+                (((0,), (0,)), ((), ())), preferred_element_type=F32,
+            )
+            at = block * slots
+            rows_v[at : at + slots, :] = picked_v[pl.ds(pl.multiple_of(lane, 8), slots), :]
+            for source in (line, line + half, 2 * half):
+                lists.append(lists_v[pl.ds(source, 1), :])
             pair_sum = jnp.sum(weights, axis=1, keepdims=True)
             twice = (lanes_of((block_rows, FREQ)) % ROTS).astype(F32)
             chosen = jnp.where(twice == local, pair_sum, 0.0)
@@ -423,13 +442,6 @@
     mass_rows = jnp.broadcast_to(mass, (8, FREQ))
     mass_out[...] = mass_rows
     den_out[...] = den_v[z]
-    half = list_lines(blocks, chunks)[0]
-    _, line, _ = list_spot(owner_s[0], 0, chunks)
-    lists = []
-    for one in extras:
-        lists_v[...] = one[one.shape[0] - lists_v.shape[0] :, :].astype(F32)
-        for at in (line, line + half, 2 * half):
-            lists.append(lists_v[pl.ds(at, 1), :])
     if ints_out.shape[0] > len(lists):
         lists.append(jnp.zeros((ints_out.shape[0] - len(lists), FREQ), F32))
     lists = jnp.concatenate(lists, axis=0)
@@ -495,7 +507,7 @@
     num[...] = jnp.zeros_like(num)
     copy.wait()
     for block, held_in in enumerate(messages):
-        base = block * per * CAND
+        base = block * list_slots(num.shape[0] - 1)
         for c in range(len(chunks)):
             number, _, lane = list_spot(owner_s[0], c, chunks)
 
@@ -504,7 +516,7 @@
                     row = ints_s[3 * block, lane + step * UNROLL + u]
                     k = ints_s[3 * block + 1, lane + step * UNROLL + u]
                     image = pick_image(held_in, 0, quot(row, CAND), rows, IMG, z * rows)
-                    add_pair(image, base + row, k, wcs, num)
+                    add_pair(image, base + step * UNROLL + u, k, wcs, num)
                 return 0
 
             lax.fori_loop(0, ints_s[3 * block + 2, number], pairs, 0)
@@ -528,13 +540,14 @@
     rows = 2 * num.shape[2] * num.shape[3]
     per = FREQ // CAND
     for block, held_in in enumerate(images):
+        start = base + block * list_slots(num.shape[0] - 1)
 
         def pairs(step, _):
             for u in range(UNROLL):
                 row = ints[3 * block, lane + step * UNROLL + u]
                 k = ints[3 * block + 1, lane + step * UNROLL + u]
                 image = pick_image(held_in, d * per, quot(row, CAND), rows, rows, 0)
-                add_pair(image, base + block * per * CAND + row, k, wcs, num)
+                add_pair(image, start + step * UNROLL + u, k, wcs, num)
             return 0
 
         lax.fori_loop(0, ints[3 * block + 2, number], pairs, 0)
@@ -635,7 +648,7 @@
     arrays, (out, wide, columns, sem) = refs[:held], refs[held + has_out :]
     width = arrays[0].shape[1] // 2
     cls_dev = columns.shape[1]
-    pad = wide.shape[0] // (len(planes) * 4 * width)
+    pad = wide.shape[0] // (len(planes) * 4 * width + 1)
     z, h = grp_s[0] // 2, grp_s[0] % 2
     copies = []
     for n, d in enumerate(planes):
@@ -734,7 +747,7 @@
             VMEM(noise_prec.shape, F32),
             VMEM((per, noise_prec.shape[0]), F32),
             VMEM((per, ctf_table.shape[0]), F32),
-            VMEM((IMG * odd_tiles(per), FREQ), F32),
+            VMEM(((IMG + 1) * odd_tiles(per), FREQ), F32),
             pltpu.SemaphoreType.DMA((6,)),
         ],
         5, 2.0,
@@ -756,7 +769,7 @@
         + [(SHAPE((width, FREQ), F32), VMEM)],
         [
             VMEM(references.shape, BF16),
-            VMEM((IMG * pad, FREQ), F32),
+            VMEM(((IMG + 1) * pad, FREQ), F32),
             SMEM(reg.shape, F32),
             pltpu.SemaphoreType.DMA((7,)),
         ],
@@ -822,7 +835,7 @@
     all_stats = [stats] + [swap(stats, "cls", d) for d in range(1, n_cls)]
     flat = [m for held in messages for m in held]
 
-    lines = n_cls * block_rows // 2
+    lines = n_cls * list_slots(cls_dev) // 2
     own_lists = SHAPE((-(-3 * n_cls // 8) * 8, FREQ), jnp.int32)
     outgoing_rows = -(-(lines + depth + 8 + own_lists.shape[0]) // 16) * 16
     packed, den, mass, log_mass, ints, *outgoing = call(
@@ -836,7 +849,12 @@
             (own_lists, VMEM),
         ]
         + [(SHAPE((outgoing_rows, FREQ), BF16), VMEM)] * (nz - 1),
-        [VMEM((2 * lines, ROTS), F32), VMEM((nz, depth, FREQ), F32), VMEM((height, FREQ), F32)],
+        [
+            VMEM((2 * lines, ROTS), F32),
+            VMEM((nz, depth, FREQ), F32),
+            VMEM((height, FREQ), F32),
+            VMEM((block_rows, ROTS), F32),
+        ],
         4 if n_cls == 4 else 12, 2.0,
         (
             grp, owner, *all_stats, *(s[0] for s in scored), *(s[2] for s in scored),
@@ -958,7 +976,7 @@
             [SMEM] + [VMEM] * len(arrays) + [HBM] * has_out,
             [(SHAPE((cls_dev, FEAT), F32), HBM)],
             [
-                VMEM((groups * width * odd_tiles(cls_dev), FREQ), F32),
+                VMEM(((groups * width + 1) * odd_tiles(cls_dev), FREQ), F32),
                 VMEM((groups, cls_dev, width * FREQ), F32),
                 pltpu.SemaphoreType.DMA((groups,)),
             ],

time: 81.2 us -> 80.6 us (level)
  no operation moved by 1% of the time
where the time goes in v7:
time: 80.6 us; the launch traced here: 80.5 us
  starting transfers between devices  30 us (37%)
  Pallas kernels  25.2 us (31%)
  waiting for transfers between devices  22.6 us (28%)
  local copies, waits for them, and re-layouts  1.86 us (2%)
  between operations  0.84 us (1%)
    ppermute x25, starting transfers between devices, swap(): return lax.ppermute(value, axis, [(i, i ^ distance) for i in range(size)])  30 us
    pallas_call x13, Pallas kernels, call(): pl.pallas_call(kernel, out_shape=tuple((s for s, _ in outs)), in_specs=[w...  25.2 us
    ppermute x25, waiting for transfers between devices, swap(): return lax.ppermute(value, axis, [(i, i ^ distance) for i in range(size)])  22.6 us
  transfers between devices with their start and end apart: 25, of which 9 were waited for; matrix products, arithmetic and copies ran while one was open for 1% of the time, Pallas kernels for 21%

profile of v7, /device:TPU:0, one launch (start us, length us, event | category | flops | bytes accessed | tf_op | source)
XLA Modules:
  0.0 80.5 jit_solution(16594887847591901724)
XLA Ops:
  0.6 2.0 %weigh.1 = (bf16[2080,128]{1,0:T(8,128)(2,1)S(1)}, bf16[512,128]{1,0:T(8,128)(2,1)S(1)}, bf16[512,128]{1,0:T(8,128)(2,1)S(1)}, bf16[512,128]{1,0:T(8,128)(2,1)S(1)}) custom-call(s32[1]{0:T(128)} %bitcast.grp_s, bf16[16,16384]{1,0:T(8,128)(2,1)} %particles_h.1, s32[8,16]{1,0:T(8,128)} %bitcast.7, s32[16]{0:T(128)} %groups_h.1, s32[16]{0:T(128)} %entries_h.1, ...), custom_call_target="tpu_custom_call" | custom-call | bytes 7200000 | tf_op jit(solution)/shard_map/weigh/pallas_call | solution.py:697
  2.7 3.0 %collective-permute-start.3 = (bf16[2080,128]{1,0:T(8,128)(2,1)S(1)}, bf16[2080,128]{1,0:T(8,128)(2,1)S(1)}, u32[]{:S(2)}, u32[]{:S(2)}) collective-permute-start(bf16[2080,128]{1,0:T(8,128)(2,1)S(1)} %get-tuple-element.49.refs_0_.refs_10_), channel_id=1, source_target_pairs={{0,2},{1,3},{2,0},{3,1},{4,6},{5,7},{6,4},{7,5},{8,10},{9,11},{10,... | collective-permute-start | bytes 1597448 | tf_op jit(solution)/shard_map/ppermute | solution.py:712
  5.7 1.5 %collective-permute-start.1 = (bf16[2080,128]{1,0:T(8,128)(2,1)S(1)}, bf16[2080,128]{1,0:T(8,128)(2,1)S(1)}, u32[]{:S(2)}, u32[]{:S(2)}) collective-permute-start(bf16[2080,128]{1,0:T(8,128)(2,1)S(1)} %get-tuple-element.49.refs_0_.refs_10_), channel_id=1, source_target_pairs={{0,1},{1,0},{2,3},{3,2},{4,5},{5,4},{6,7},{7,6},{8,9},{9,8},{10,11... | collective-permute-start | bytes 1597448 | tf_op jit(solution)/shard_map/ppermute | solution.py:712
  7.2 1.6 %collective-permute-start = (bf16[512,128]{1,0:T(8,128)(2,1)S(1)}, bf16[512,128]{1,0:T(8,128)(2,1)S(1)}, u32[]{:S(2)}, u32[]{:S(2)}) collective-permute-start(bf16[512,128]{1,0:T(8,128)(2,1)S(1)} %get-tuple-element.47), channel_id=1, source_target_pairs={{0,8},{4,12},{8,0},{12,4},{16,24},{20,28},{24,16},{28,20},{1,9},{5... | collective-permute-start | bytes 393224 | tf_op jit(solution)/shard_map/ppermute | solution.py:712
  8.8 2.6 %collective-permute-start.2 = (bf16[512,128]{1,0:T(8,128)(2,1)S(1)}, bf16[512,128]{1,0:T(8,128)(2,1)S(1)}, u32[]{:S(2)}, u32[]{:S(2)}) collective-permute-start(bf16[512,128]{1,0:T(8,128)(2,1)S(1)} %get-tuple-element.54), channel_id=1, source_target_pairs={{0,16},{4,20},{8,24},{12,28},{16,0},{20,4},{24,8},{28,12},{1,17},{... | collective-permute-start | bytes 393224 | tf_op jit(solution)/shard_map/ppermute | solution.py:712
  12.0 3.8 %prep.1 = (f32[53,128,128]{2,1,0:T(8,128)S(1)}, f32[53,128]{1,0:T(8,128)S(1)}, f32[384,64]{1,0:T(8,128)S(1)}, bf16[256,512]{1,0:T(8,128)(2,1)S(1)}, f32[8,128]{1,0:T(8,128)S(1)}) custom-call(s32[1]{0:T(128)} %bitcast.grp_s, bf16[52,16384]{1,0:T(8,128)(2,1)} %refs_h.1, f32[384,64]{1,0:T(8,128)} %constant.15.clone.rest_refs_0_, ...), custom_call_target="tpu_custom_call" | custom-call | bytes 14400000 | tf_op jit(solution)/shard_map/prep/pallas_call | solution.py:697
  15.8 1.8 %score.3 = (f32[128,64]{1,0:T(8,128)S(1)}, f32[16,128]{1,0:T(8,128)S(1)}, f32[128,128]{1,0:T(8,128)S(1)}) custom-call(s32[1]{0:T(128)S(6)} %mul.3.first_s, s32[1]{0:T(128)} %bitcast.1.owner_s, bf16[2080,128]{1,0:T(8,128)(2,1)S(1)} %get-tuple-element.49.refs_0_.refs_10_, f32[53,128,128]{2,1,0:T(8,128)S(1)} %get-tuple-element.50.refs_1_.refs_2_.refs_4_, ...), custom_call_target="tpu_custom_call" | custom-call | bytes 10800000 | tf_op jit(solution)/shard_map/score/pallas_call | solution.py:697
  17.8 1.8 %collective-permute-start.5 = (bf16[1056,128]{1,0:T(8,128)(2,1)S(1)}, bf16[1056,128]{1,0:T(8,128)(2,1)S(1)}, u32[]{:S(2)}, u32[]{:S(2)}) collective-permute-start(bf16[1056,128]{1,0:T(8,128)(2,1)S(1)} %slice.19), channel_id=1, source_target_pairs={{0,1},{1,0},{2,3},{3,2},{4,5},{5,4},{6,7},{7,6},{8,9},{9,8},{10,11... | collective-permute-start | bytes 811016 | tf_op jit(solution)/shard_map/ppermute | solution.py:712
  19.6 1.6 %collective-permute-start.4 = (bf16[1024,128]{1,0:T(8,128)(2,1)S(1)}, bf16[1024,128]{1,0:T(8,128)(2,1)S(1)}, u32[]{:S(2)}, u32[]{:S(2)}) collective-permute-start(bf16[1024,128]{1,0:T(8,128)(2,1)S(1)} %slice.18), channel_id=1, source_target_pairs={{0,2},{1,3},{2,0},{3,1},{4,6},{5,7},{6,4},{7,5},{8,10},{9,11},{10,... | collective-permute-start | bytes 786440 | tf_op jit(solution)/shard_map/ppermute | solution.py:712
  21.2 3.6 %collective-permute-start.6 = (bf16[512,128]{1,0:T(8,128)(2,1)S(1)}, bf16[512,128]{1,0:T(8,128)(2,1)S(1)}, u32[]{:S(2)}, u32[]{:S(2)}) collective-permute-start(bf16[512,128]{1,0:T(8,128)(2,1)S(1)} %get-tuple-element.59), channel_id=1, source_target_pairs={{0,24},{4,28},{8,16},{12,20},{16,8},{20,12},{24,0},{28,4},{1,25},{... | collective-permute-start | bytes 393224 | tf_op jit(solution)/shard_map/ppermute | solution.py:712
  24.8 3.2 %score.4 = (f32[256,64]{1,0:T(8,128)S(1)}, f32[32,128]{1,0:T(8,128)S(1)}, f32[256,128]{1,0:T(8,128)S(1)}) custom-call(s32[1]{0:T(128)S(6)} %mul.3.first_s, s32[1]{0:T(128)} %bitcast.1.owner_s, bf16[2080,128]{1,0:T(8,128)(2,1)S(1)} %collective-permute-done.1.refs_0_.refs_11_.refs_1_, bf16[2080,128]{1,0:T(8,128)(2,1)S(1)} %collective-permute-done.3.refs_1_.refs_12_.refs_2_, ...), custom_call_target="tpu_custom_call" | custom-call | bytes 21600000 | tf_op jit(solution)/shard_map/score/pallas_call | solution.py:697
  28.1 0.9 %collective-permute-start.11 = (bf16[1536,128]{1,0:T(8,128)(2,1)S(1)}, bf16[1536,128]{1,0:T(8,128)(2,1)S(1)}, u32[]{:S(2)}, u32[]{:S(2)}) collective-permute-start(bf16[1536,128]{1,0:T(8,128)(2,1)S(1)} %join.1.refs_0_), channel_id=1, source_target_pairs={{0,2},{1,3},{2,0},{3,1},{4,6},{5,7},{6,4},{7,5},{8,10},{9,11},{10,... | collective-permute-start | bytes 1179656 | tf_op jit(solution)/shard_map/ppermute | solution.py:712
  29.0 0.8 %collective-permute-start.7 = (bf16[1536,128]{1,0:T(8,128)(2,1)S(1)}, bf16[1536,128]{1,0:T(8,128)(2,1)S(1)}, u32[]{:S(2)}, u32[]{:S(2)}) collective-permute-start(bf16[1536,128]{1,0:T(8,128)(2,1)S(1)} %join.1.refs_0_), channel_id=1, source_target_pairs={{0,1},{1,0},{2,3},{3,2},{4,5},{5,4},{6,7},{7,6},{8,9},{9,8},{10,11... | collective-permute-start | bytes 1179656 | tf_op jit(solution)/shard_map/ppermute | solution.py:712
  29.8 1.8 %score.5 = (f32[128,64]{1,0:T(8,128)S(1)}, f32[64,128]{1,0:T(8,128)S(1)}, f32[128,128]{1,0:T(8,128)S(1)}) custom-call(s32[1]{0:T(128)S(6)} %mul.3.first_s, s32[1]{0:T(128)} %bitcast.1.owner_s, bf16[1024,128]{1,0:T(8,128)(2,1)S(1)} %collective-permute-done.4.refs_0_.refs_3_, bf16[1056,128]{1,0:T(8,128)(2,1)S(1)} %collective-permute-done.5.refs_1_.refs_13_.refs_4_, ...), custom_call_target="tpu_custom_call" | custom-call | bytes 10800000 | tf_op jit(solution)/shard_map/score/pallas_call | solution.py:697
  31.6 1.8 %collective-permute-start.10 = (f32[64,128]{1,0:T(8,128)S(1)}, f32[64,128]{1,0:T(8,128)S(1)}, u32[]{:S(2)}, u32[]{:S(2)}) collective-permute-start(f32[64,128]{1,0:T(8,128)S(1)} %get-tuple-element.60.refs_0_), channel_id=1, source_target_pairs={{0,3},{1,2},{2,1},{3,0},{4,7},{5,6},{6,5},{7,4},{8,11},{9,10},{10,... | collective-permute-start | bytes 98312 | tf_op jit(solution)/shard_map/ppermute | solution.py:712
  33.4 0.9 %collective-permute-start.9 = (f32[64,128]{1,0:T(8,128)S(1)}, f32[64,128]{1,0:T(8,128)S(1)}, u32[]{:S(2)}, u32[]{:S(2)}) collective-permute-start(f32[64,128]{1,0:T(8,128)S(1)} %get-tuple-element.60.refs_0_), channel_id=1, source_target_pairs={{0,2},{1,3},{2,0},{3,1},{4,6},{5,7},{6,4},{7,5},{8,10},{9,11},{10,... | collective-permute-start | bytes 98312 | tf_op jit(solution)/shard_map/ppermute | solution.py:712
  35.2 4.5 %collective-permute-done.10.refs_3_ = f32[64,128]{1,0:T(8,128)S(1)} collective-permute-done((f32[64,128]{1,0:T(8,128)S(1)}, f32[64,128]{1,0:T(8,128)S(1)}, u32[]{:S(2)}, u32[]{:S(2)}) %collective-permute-start.10) | collective-permute-done | bytes 32800 | tf_op jit(solution)/shard_map/ppermute | solution.py:712
  39.7 1.0 %weights.1 = (bf16[208,128]{1,0:T(8,128)(2,1)S(1)}, f32[16,128]{1,0:T(8,128)S(1)}, f32[8,128]{1,0:T(8,128)S(1)}, f32[16,64]{1,0:T(8,128)S(1)}, s32[16,128]{1,0:T...) custom-call(s32[1]{0:T(128)} %bitcast.grp_s, ...), custom_call_target="tpu_custom_call" | custom-call | bytes 7200000 | tf_op jit(solution)/shard_map/weights/pallas_call | solution.py:697
  41.4 1.0 %collective-permute-start.12 = (bf16[768,128]{1,0:T(8,128)(2,1)S(1)}, bf16[768,128]{1,0:T(8,128)(2,1)S(1)}, u32[]{:S(2)}, u32[]{:S(2)}) collective-permute-start(bf16[768,128]{1,0:T(8,128)(2,1)S(1)} %slice.20), channel_id=1, source_target_pairs={{0,2},{1,3},{2,0},{3,1},{4,6},{5,7},{6,4},{7,5},{8,10},{9,11},{10,... | collective-permute-start | bytes 589832 | tf_op jit(solution)/shard_map/ppermute | solution.py:712
  43.0 2.8 %collective-permute-start.14 = (bf16[256,128]{1,0:T(8,128)(2,1)S(1)}, bf16[256,128]{1,0:T(8,128)(2,1)S(1)}, u32[]{:S(2)}, u32[]{:S(2)}) collective-permute-start(bf16[256,128]{1,0:T(8,128)(2,1)S(1)} %get-tuple-element.70), channel_id=1, source_target_pairs={{0,16},{4,20},{8,24},{12,28},{16,0},{20,4},{24,8},{28,12},{1,17},{... | collective-permute-start | bytes 196616 | tf_op jit(solution)/shard_map/ppermute | solution.py:712
  45.8 1.0 %collective-permute-start.15 = (bf16[256,128]{1,0:T(8,128)(2,1)S(1)}, bf16[256,128]{1,0:T(8,128)(2,1)S(1)}, u32[]{:S(2)}, u32[]{:S(2)}) collective-permute-start(bf16[256,128]{1,0:T(8,128)(2,1)S(1)} %get-tuple-element.71), channel_id=1, source_target_pairs={{0,24},{4,28},{8,16},{12,20},{16,8},{20,12},{24,0},{28,4},{1,25},{... | collective-permute-start | bytes 196616 | tf_op jit(solution)/shard_map/ppermute | solution.py:712
  46.8 1.8 %own_sum.1.refs_6_ = f32[53,2,2,8,128]{4,3,2,1,0:T(8,128)S(1)} custom-call(s32[1]{0:T(128)} %bitcast.grp_s, s32[1]{0:T(128)} %bitcast.1.owner_s, bf16[208,128]{1,0:T(8,128)(2,1)S(1)} %get-tuple-element.67.packed, s32[16,128]{1,0:T(8,128)S(1)} %get-tuple-element.73.ints, bf16[2080,128]{1,0:T(8,128)(2,1)S(1)} %get-tuple-element.49.refs_0_.refs_10_, ...), custom_call_target="tpu_custom_call" | custom-call | bytes 10800000 | tf_op jit(solution)/shard_map/own_sum/pallas_call | solution.py:697
  48.6 1.8 %near_sum.1 = (f32[53,2,2,8,128]{4,3,2,1,0:T(8,128)S(1)}, f32[16,128]{1,0:T(8,128)S(1)}, f32[8,128]{1,0:T(8,128)S(1)}) custom-call(s32[1]{0:T(128)} %bitcast.1.owner_s, bf16[1536,128]{1,0:T(8,128)(2,1)S(1)} %join.1.refs_0_, bf16[1536,128]{1,0:T(8,128)(2,1)S(1)} %collective-permute-done.7.refs_1_, bf16[1536,128]{1,0:T(8,128)(2,1)S(1)} %collective-permute-done.11.refs_2_, ...), custom_call_target="tpu_custom_call" | custom-call | bytes 7200000 | tf_op jit(solution)/shard_map/near_sum/pallas_call | solution.py:697
  50.4 1.4 %collective-permute-done.15.refs_6_ = bf16[256,128]{1,0:T(8,128)(2,1)S(1)} collective-permute-done((bf16[256,128]{1,0:T(8,128)(2,1)S(1)}, bf16[256,128]{1,0:T(8,128)(2,1)S(1)}, u32[]{:S(2)}, u32[]{:S(2)}) %collective-permute-start.15) | collective-permute-done | bytes 65568 | tf_op jit(solution)/shard_map/ppermute | solution.py:712
  51.8 4.1 %sum.1 = (f32[52,16,128]{2,1,0:T(8,128)S(1)}, bf16[53,16,128]{2,1,0:T(8,128)(2,1)S(1)}, f32[8,128]{1,0:T(8,128)S(1)}, f32[8,128]{1,0:T(8,128)S(1)}, f32[2,832,128]{2,1,0:T(8,128)}, /*index=5*/s32[2,16,128]{2,1,0:T(8,128)}) custom-call(s32[1]{0:T(128)} %bitcast.grp_s, s32[1]{0:T(128)} %bitcast.1.owner_s, bf16[1536,128]{1,0:T(8,128)(2,1)S(1)} %join.1.refs_0_, ...), custom_call_target="tpu_custom_call" | custom-call | bytes 10800000 | tf_op jit(solution)/shard_map/sum/pallas_call | solution.py:697
  56.1 1.5 %collective-permute-done.17.sib = bf16[53,16,128]{2,1,0:T(8,128)(2,1)S(1)} collective-permute-done((bf16[53,16,128]{2,1,0:T(8,128)(2,1)S(1)}, bf16[53,16,128]{2,1,0:T(8,128)(2,1)S(1)}, u32[]{:S(2)}, u32[]{:S(2)}) %collective-permute-start.17) | collective-permute-done | bytes 217120 | tf_op jit(solution)/shard_map/ppermute | solution.py:712
  58.5 1.7 %collective-permute-start.18 = (bf16[52,16,128]{2,1,0:T(8,128)(2,1)S(1)}, bf16[52,16,128]{2,1,0:T(8,128)(2,1)S(1)}, u32[]{:S(2)}, u32[]{:S(2)}) collective-permute-start(bf16[52,16,128]{2,1,0:T(8,128)(2,1)S(1)} %get-tuple-element.85.refs_0_), channel_id=1, source_target_pairs={{0,8},{4,12},{8,0},{12,4},{16,24},{20,28},{24,16},{28,20},{1,9},{5... | collective-permute-start | bytes 638984 | tf_op jit(solution)/shard_map/ppermute | solution.py:712
  60.2 9.7 %collective-permute-done.19.refs_4_ = bf16[52,16,128]{2,1,0:T(8,128)(2,1)S(1)} collective-permute-done((bf16[52,16,128]{2,1,0:T(8,128)(2,1)S(1)}, bf16[52,16,128]{2,1,0:T(8,128)(2,1)S(1)}, u32[]{:S(2)}, u32[]{:S(2)}) %collective-permute-start.19) | collective-permute-done | bytes 213024 | tf_op jit(solution)/shard_map/ppermute | solution.py:712
  71.9 2.0 %spread.2.refs_2_ = f32[52,16384]{1,0:T(8,128)} custom-call(s32[1]{0:T(128)} %bitcast.grp_s, bf16[52,16,128]{2,1,0:T(8,128)(2,1)S(1)} %get-tuple-element.85.refs_0_, bf16[52,16,128]{2,1,0:T(8,128)(2,1)S(1)} %collective-permute-done.21.refs_1_, bf16[52,16,128]{2,1,0:T(8,128)(2,1)S(1)} %collective-permute-done.18.refs_2_, ...), custom_call_target="tpu_custom_call" | custom-call | bytes 180000 | tf_op jit(solution)/shard_map/spread/pallas_call | solution.py:697
  73.9 3.9 %collective-permute-done.20.refs_0_ = bf16[52,16,128]{2,1,0:T(8,128)(2,1)S(1)} collective-permute-done((bf16[52,16,128]{2,1,0:T(8,128)(2,1)S(1)}, bf16[52,16,128]{2,1,0:T(8,128)(2,1)S(1)}, u32[]{:S(2)}, u32[]{:S(2)}) %collective-permute-start.20) | collective-permute-done | bytes 213024 | tf_op jit(solution)/shard_map/ppermute | solution.py:712
  78.3 0.9 %collective-permute-done.24.refs_1_ = bf16[52,16,128]{2,1,0:T(8,128)(2,1)S(1)} collective-permute-done((bf16[52,16,128]{2,1,0:T(8,128)(2,1)S(1)}, bf16[52,16,128]{2,1,0:T(8,128)(2,1)S(1)}, u32[]{:S(2)}, u32[]{:S(2)}) %collective-permute-start.24) | collective-permute-done | bytes 213024 | tf_op jit(solution)/shard_map/ppermute | solution.py:712
  79.3 1.2 %spread.3 = f32[52,16384]{1,0:T(8,128)} custom-call(s32[1]{0:T(128)} %bitcast.grp_s, bf16[52,16,128]{2,1,0:T(8,128)(2,1)S(1)} %collective-permute-done.20.refs_0_, bf16[52,16,128]{2,1,0:T(8,128)(2,1)S(1)} %collective-permute-done.24.refs_1_, f32[52,16384]{1,0:T(8,128)} %spread.2.refs_2_), custom_call_target="tpu_custom_call", output_to_operand_aliasing={{}: (3, {})} | custom-call | bytes 180000 | tf_op jit(solution)/shard_map/spread/pallas_call | solution.py:697
  (39 shorter events, 6.7 us)
Async XLA Ops:
  2.7 15.1 %collective-permute-start.3 = (bf16[2080,128]{1,0:T(8,128)(2,1)S(1)}, bf16[2080,128]{1,0:T(8,128)(2,1)S(1)}, u32[]{:S(2)}, u32[]{:S(2)}) collective-permute-start(bf16[2080,128]{1,0:T(8,128)(2,1)S(1)} %get-tuple-element.49.refs_0_.refs_10_), channel_id=1, source_target_pairs={{0,2},{1,3},{2,0},{3,1},{4,6},{5,7},{6,4},{7,5},{8,10},{9,11},{10,... | collective-permute-start | bytes 1597448 | tf_op jit(solution)/shard_map/ppermute | solution.py:712
  5.7 13.9 %collective-permute-start.1 = (bf16[2080,128]{1,0:T(8,128)(2,1)S(1)}, bf16[2080,128]{1,0:T(8,128)(2,1)S(1)}, u32[]{:S(2)}, u32[]{:S(2)}) collective-permute-start(bf16[2080,128]{1,0:T(8,128)(2,1)S(1)} %get-tuple-element.49.refs_0_.refs_10_), channel_id=1, source_target_pairs={{0,1},{1,0},{2,3},{3,2},{4,5},{5,4},{6,7},{7,6},{8,9},{9,8},{10,11... | collective-permute-start | bytes 1597448 | tf_op jit(solution)/shard_map/ppermute | solution.py:712
  7.2 8.6 %collective-permute-start = (bf16[512,128]{1,0:T(8,128)(2,1)S(1)}, bf16[512,128]{1,0:T(8,128)(2,1)S(1)}, u32[]{:S(2)}, u32[]{:S(2)}) collective-permute-start(bf16[512,128]{1,0:T(8,128)(2,1)S(1)} %get-tuple-element.47), channel_id=1, source_target_pairs={{0,8},{4,12},{8,0},{12,4},{16,24},{20,28},{24,16},{28,20},{1,9},{5... | collective-permute-start | bytes 393224 | tf_op jit(solution)/shard_map/ppermute | solution.py:712
  8.8 8.8 %collective-permute-start.2 = (bf16[512,128]{1,0:T(8,128)(2,1)S(1)}, bf16[512,128]{1,0:T(8,128)(2,1)S(1)}, u32[]{:S(2)}, u32[]{:S(2)}) collective-permute-start(bf16[512,128]{1,0:T(8,128)(2,1)S(1)} %get-tuple-element.54), channel_id=1, source_target_pairs={{0,16},{4,20},{8,24},{12,28},{16,0},{20,4},{24,8},{28,12},{1,17},{... | collective-permute-start | bytes 393224 | tf_op jit(solution)/shard_map/ppermute | solution.py:712
  11.4 0.7 copy-start
  17.8 10.2 %collective-permute-start.5 = (bf16[1056,128]{1,0:T(8,128)(2,1)S(1)}, bf16[1056,128]{1,0:T(8,128)(2,1)S(1)}, u32[]{:S(2)}, u32[]{:S(2)}) collective-permute-start(bf16[1056,128]{1,0:T(8,128)(2,1)S(1)} %slice.19), channel_id=1, source_target_pairs={{0,1},{1,0},{2,3},{3,2},{4,5},{5,4},{6,7},{7,6},{8,9},{9,8},{10,11... | collective-permute-start | bytes 811016 | tf_op jit(solution)/shard_map/ppermute | solution.py:712
  19.6 8.4 %collective-permute-start.4 = (bf16[1024,128]{1,0:T(8,128)(2,1)S(1)}, bf16[1024,128]{1,0:T(8,128)(2,1)S(1)}, u32[]{:S(2)}, u32[]{:S(2)}) collective-permute-start(bf16[1024,128]{1,0:T(8,128)(2,1)S(1)} %slice.18), channel_id=1, source_target_pairs={{0,2},{1,3},{2,0},{3,1},{4,6},{5,7},{6,4},{7,5},{8,10},{9,11},{10,... | collective-permute-start | bytes 786440 | tf_op jit(solution)/shard_map/ppermute | solution.py:712
  21.2 6.9 %collective-permute-start.6 = (bf16[512,128]{1,0:T(8,128)(2,1)S(1)}, bf16[512,128]{1,0:T(8,128)(2,1)S(1)}, u32[]{:S(2)}, u32[]{:S(2)}) collective-permute-start(bf16[512,128]{1,0:T(8,128)(2,1)S(1)} %get-tuple-element.59), channel_id=1, source_target_pairs={{0,24},{4,28},{8,16},{12,20},{16,8},{20,12},{24,0},{28,4},{1,25},{... | collective-permute-start | bytes 393224 | tf_op jit(solution)/shard_map/ppermute | solution.py:712
  28.1 12.5 %collective-permute-start.11 = (bf16[1536,128]{1,0:T(8,128)(2,1)S(1)}, bf16[1536,128]{1,0:T(8,128)(2,1)S(1)}, u32[]{:S(2)}, u32[]{:S(2)}) collective-permute-start(bf16[1536,128]{1,0:T(8,128)(2,1)S(1)} %join.1.refs_0_), channel_id=1, source_target_pairs={{0,2},{1,3},{2,0},{3,1},{4,6},{5,7},{6,4},{7,5},{8,10},{9,11},{10,... | collective-permute-start | bytes 1179656 | tf_op jit(solution)/shard_map/ppermute | solution.py:712
  29.0 12.4 %collective-permute-start.7 = (bf16[1536,128]{1,0:T(8,128)(2,1)S(1)}, bf16[1536,128]{1,0:T(8,128)(2,1)S(1)}, u32[]{:S(2)}, u32[]{:S(2)}) collective-permute-start(bf16[1536,128]{1,0:T(8,128)(2,1)S(1)} %join.1.refs_0_), channel_id=1, source_target_pairs={{0,1},{1,0},{2,3},{3,2},{4,5},{5,4},{6,7},{7,6},{8,9},{9,8},{10,11... | collective-permute-start | bytes 1179656 | tf_op jit(solution)/shard_map/ppermute | solution.py:712
  31.6 8.0 %collective-permute-start.10 = (f32[64,128]{1,0:T(8,128)S(1)}, f32[64,128]{1,0:T(8,128)S(1)}, u32[]{:S(2)}, u32[]{:S(2)}) collective-permute-start(f32[64,128]{1,0:T(8,128)S(1)} %get-tuple-element.60.refs_0_), channel_id=1, source_target_pairs={{0,3},{1,2},{2,1},{3,0},{4,7},{5,6},{6,5},{7,4},{8,11},{9,10},{10,... | collective-permute-start | bytes 98312 | tf_op jit(solution)/shard_map/ppermute | solution.py:712
  33.4 6.2 %collective-permute-start.9 = (f32[64,128]{1,0:T(8,128)S(1)}, f32[64,128]{1,0:T(8,128)S(1)}, u32[]{:S(2)}, u32[]{:S(2)}) collective-permute-start(f32[64,128]{1,0:T(8,128)S(1)} %get-tuple-element.60.refs_0_), channel_id=1, source_target_pairs={{0,2},{1,3},{2,0},{3,1},{4,6},{5,7},{6,4},{7,5},{8,10},{9,11},{10,... | collective-permute-start | bytes 98312 | tf_op jit(solution)/shard_map/ppermute | solution.py:712
  34.4 5.3 %collective-permute-start.8 = (f32[64,128]{1,0:T(8,128)S(1)}, f32[64,128]{1,0:T(8,128)S(1)}, u32[]{:S(2)}, u32[]{:S(2)}) collective-permute-start(f32[64,128]{1,0:T(8,128)S(1)} %get-tuple-element.60.refs_0_), channel_id=1, source_target_pairs={{0,1},{1,0},{2,3},{3,2},{4,5},{5,4},{6,7},{7,6},{8,9},{9,8},{10,11... | collective-permute-start | bytes 98312 | tf_op jit(solution)/shard_map/ppermute | solution.py:712
  40.7 7.9 %collective-permute-start.13 = (bf16[768,128]{1,0:T(8,128)(2,1)S(1)}, bf16[768,128]{1,0:T(8,128)(2,1)S(1)}, u32[]{:S(2)}, u32[]{:S(2)}) collective-permute-start(bf16[768,128]{1,0:T(8,128)(2,1)S(1)} %slice.21), channel_id=1, source_target_pairs={{0,1},{1,0},{2,3},{3,2},{4,5},{5,4},{6,7},{7,6},{8,9},{9,8},{10,11... | collective-permute-start | bytes 589832 | tf_op jit(solution)/shard_map/ppermute | solution.py:712
  41.4 7.2 %collective-permute-start.12 = (bf16[768,128]{1,0:T(8,128)(2,1)S(1)}, bf16[768,128]{1,0:T(8,128)(2,1)S(1)}, u32[]{:S(2)}, u32[]{:S(2)}) collective-permute-start(bf16[768,128]{1,0:T(8,128)(2,1)S(1)} %slice.20), channel_id=1, source_target_pairs={{0,2},{1,3},{2,0},{3,1},{4,6},{5,7},{6,4},{7,5},{8,10},{9,11},{10,... | collective-permute-start | bytes 589832 | tf_op jit(solution)/shard_map/ppermute | solution.py:712
  42.4 6.2 %collective-permute-start.16 = (bf16[256,128]{1,0:T(8,128)(2,1)S(1)}, bf16[256,128]{1,0:T(8,128)(2,1)S(1)}, u32[]{:S(2)}, u32[]{:S(2)}) collective-permute-start(bf16[256,128]{1,0:T(8,128)(2,1)S(1)} %get-tuple-element.72), channel_id=1, source_target_pairs={{0,8},{4,12},{8,0},{12,4},{16,24},{20,28},{24,16},{28,20},{1,9},{5... | collective-permute-start | bytes 196616 | tf_op jit(solution)/shard_map/ppermute | solution.py:712
  43.0 7.5 %collective-permute-start.14 = (bf16[256,128]{1,0:T(8,128)(2,1)S(1)}, bf16[256,128]{1,0:T(8,128)(2,1)S(1)}, u32[]{:S(2)}, u32[]{:S(2)}) collective-permute-start(bf16[256,128]{1,0:T(8,128)(2,1)S(1)} %get-tuple-element.70), channel_id=1, source_target_pairs={{0,16},{4,20},{8,24},{12,28},{16,0},{20,4},{24,8},{28,12},{1,17},{... | collective-permute-start | bytes 196616 | tf_op jit(solution)/shard_map/ppermute | solution.py:712
  45.8 6.1 %collective-permute-start.15 = (bf16[256,128]{1,0:T(8,128)(2,1)S(1)}, bf16[256,128]{1,0:T(8,128)(2,1)S(1)}, u32[]{:S(2)}, u32[]{:S(2)}) collective-permute-start(bf16[256,128]{1,0:T(8,128)(2,1)S(1)} %get-tuple-element.71), channel_id=1, source_target_pairs={{0,24},{4,28},{8,16},{12,20},{16,8},{20,12},{24,0},{28,4},{1,25},{... | collective-permute-start | bytes 196616 | tf_op jit(solution)/shard_map/ppermute | solution.py:712
  56.0 1.5 %collective-permute-start.17 = (bf16[53,16,128]{2,1,0:T(8,128)(2,1)S(1)}, bf16[53,16,128]{2,1,0:T(8,128)(2,1)S(1)}, u32[]{:S(2)}, u32[]{:S(2)}) collective-permute-start(bf16[53,16,128]{2,1,0:T(8,128)(2,1)S(1)} %get-tuple-element.81), channel_id=1, source_target_pairs={{0,4},{4,0},{8,12},{12,8},{16,20},{20,16},{24,28},{28,24},{1,5},{5... | collective-permute-start | bytes 651272 | tf_op jit(solution)/shard_map/ppermute | solution.py:712
  58.2 11.7 %collective-permute-start.19 = (bf16[52,16,128]{2,1,0:T(8,128)(2,1)S(1)}, bf16[52,16,128]{2,1,0:T(8,128)(2,1)S(1)}, u32[]{:S(2)}, u32[]{:S(2)}) collective-permute-start(bf16[52,16,128]{2,1,0:T(8,128)(2,1)S(1)} %get-tuple-element.85.refs_0_), channel_id=1, source_target_pairs={{0,16},{4,20},{8,24},{12,28},{16,0},{20,4},{24,8},{28,12},{1,17},{... | collective-permute-start | bytes 638984 | tf_op jit(solution)/shard_map/ppermute | solution.py:712
  58.5 11.6 %collective-permute-start.18 = (bf16[52,16,128]{2,1,0:T(8,128)(2,1)S(1)}, bf16[52,16,128]{2,1,0:T(8,128)(2,1)S(1)}, u32[]{:S(2)}, u32[]{:S(2)}) collective-permute-start(bf16[52,16,128]{2,1,0:T(8,128)(2,1)S(1)} %get-tuple-element.85.refs_0_), channel_id=1, source_target_pairs={{0,8},{4,12},{8,0},{12,4},{16,24},{20,28},{24,16},{28,20},{1,9},{5... | collective-permute-start | bytes 638984 | tf_op jit(solution)/shard_map/ppermute | solution.py:712
  60.2 11.3 %collective-permute-start.21 = (bf16[52,16,128]{2,1,0:T(8,128)(2,1)S(1)}, bf16[52,16,128]{2,1,0:T(8,128)(2,1)S(1)}, u32[]{:S(2)}, u32[]{:S(2)}) collective-permute-start(bf16[52,16,128]{2,1,0:T(8,128)(2,1)S(1)} %get-tuple-element.85.refs_0_), channel_id=1, source_target_pairs={{0,4},{4,0},{8,12},{12,8},{16,20},{20,16},{24,28},{28,24},{1,5},{5... | collective-permute-start | bytes 638984 | tf_op jit(solution)/shard_map/ppermute | solution.py:712
  70.1 1.5 %collective-permute-start.22 = (bf16[52,16,128]{2,1,0:T(8,128)(2,1)S(1)}, bf16[52,16,128]{2,1,0:T(8,128)(2,1)S(1)}, u32[]{:S(2)}, u32[]{:S(2)}) collective-permute-start(bf16[52,16,128]{2,1,0:T(8,128)(2,1)S(1)} %collective-permute-done.18.refs_2_), channel_id=1, source_target_pairs={{0,4},{4,0},{8,12},{12,8},{16,20},{20,16},{24,28},{28,24},{1,5},{5... | collective-permute-start | bytes 638984 | tf_op jit(solution)/shard_map/ppermute | solution.py:712
  70.1 1.8 %collective-permute-start.23 = (bf16[52,16,128]{2,1,0:T(8,128)(2,1)S(1)}, bf16[52,16,128]{2,1,0:T(8,128)(2,1)S(1)}, u32[]{:S(2)}, u32[]{:S(2)}) collective-permute-start(bf16[52,16,128]{2,1,0:T(8,128)(2,1)S(1)} %collective-permute-done.19.refs_4_), channel_id=1, source_target_pairs={{0,4},{4,0},{8,12},{12,8},{16,20},{20,16},{24,28},{28,24},{1,5},{5... | collective-permute-start | bytes 638984 | tf_op jit(solution)/shard_map/ppermute | solution.py:712
  70.6 7.2 %collective-permute-start.20 = (bf16[52,16,128]{2,1,0:T(8,128)(2,1)S(1)}, bf16[52,16,128]{2,1,0:T(8,128)(2,1)S(1)}, u32[]{:S(2)}, u32[]{:S(2)}) collective-permute-start(bf16[52,16,128]{2,1,0:T(8,128)(2,1)S(1)} %collective-permute-done.19.refs_4_), channel_id=1, source_target_pairs={{0,8},{4,12},{8,0},{12,4},{16,24},{20,28},{24,16},{28,20},{1,9},{5... | collective-permute-start | bytes 638984 | tf_op jit(solution)/shard_map/ppermute | solution.py:712
  77.8 1.5 %collective-permute-start.24 = (bf16[52,16,128]{2,1,0:T(8,128)(2,1)S(1)}, bf16[52,16,128]{2,1,0:T(8,128)(2,1)S(1)}, u32[]{:S(2)}, u32[]{:S(2)}) collective-permute-start(bf16[52,16,128]{2,1,0:T(8,128)(2,1)S(1)} %collective-permute-done.20.refs_0_), channel_id=1, source_target_pairs={{0,4},{4,0},{8,12},{12,8},{16,20},{20,16},{24,28},{28,24},{1,5},{5... | collective-permute-start | bytes 638984 | tf_op jit(solution)/shard_map/ppermute | solution.py:712

commit v8 on v7

--- a/solution.py
+++ b/solution.py
@@ -535,22 +535,31 @@
     return den, mass, tail[depth + 8 : depth + 8 + count].astype(jnp.int32)
 
 
-def add_plane(d, chunk, chunks, owner, images, ints, base, wcs, num):
-    number, _, lane = list_spot(owner, chunk, chunks)
+def add_planes(planes, owner, chunks, images, wcs, *nums):
+    number, _, lane = list_spot(owner, 0, chunks)
+    num = nums[0]
+    slots = list_slots(num.shape[0] - 1)
     rows = 2 * num.shape[2] * num.shape[3]
     per = FREQ // CAND
-    for block, held_in in enumerate(images):
-        start = base + block * list_slots(num.shape[0] - 1)
+    for first in range(0, len(images), 2):
+        group = [
+            (d, ints, base + block * slots, block)
+            for d, ints, base in planes
+            for block in range(first, min(first + 2, len(images)))
+        ]
+        counts = [ints[3 * block + 2, number] for _, ints, _, block in group]
 
         def pairs(step, _):
-            for u in range(UNROLL):
-                row = ints[3 * block, lane + step * UNROLL + u]
-                k = ints[3 * block + 1, lane + step * UNROLL + u]
-                image = pick_image(held_in, d * per, quot(row, CAND), rows, rows, 0)
-                add_pair(image, start + step * UNROLL + u, k, wcs, num)
+            for d, ints, start, block in group:
+                for u in range(UNROLL):
+                    slot = step * UNROLL + u
+                    row = ints[3 * block, lane + slot]
+                    k = ints[3 * block + 1, lane + slot]
+                    image = pick_image(images[block], d * per, quot(row, CAND), rows, rows, 0)
+                    add_pair(image, start + slot, k, wcs, nums[u % len(nums)])
             return 0
 
-        lax.fori_loop(0, ints[3 * block + 2, number], pairs, 0)
+        lax.fori_loop(0, functools.reduce(jnp.maximum, counts), pairs, 0)
 
 
 def near_sum_kernel(chunks, pieces, owner_s, *refs):
@@ -566,8 +575,7 @@
     put_phases(message[:lines, :], phases, wcs, 0)
     num[...] = first[...]
     copy.wait()
-    for chunk in range(len(chunks)):
-        add_plane(0, chunk, chunks, owner_s[0], images, ints_s, 0, wcs, num)
+    add_planes([(0, ints_s, 0)], owner_s[0], chunks, images, wcs, num)
 
 
 def sum_kernel(chunk, chunks, slices, pieces, grp_s, owner_s, *refs):
@@ -576,9 +584,9 @@
     first, refs = refs[0], refs[1:]
     if chunk == 0:
         phases, (den_in, mass_in), refs = refs[0], refs[1:3], refs[3:]
-        own_out, sib_out, den_out, mass_out, wcs, ints_s, num, den_v, ints_v, sem = refs
+        own_out, sib_out, den_out, mass_out, wcs, ints_s, num, more, den_v, ints_v, sem = refs
     else:
-        wcs, ints_s, own_out, sib_out, num = refs
+        wcs, ints_s, own_out, sib_out, num, more = refs
     group_rows = wcs.shape[1] // (slices - 2)
     lines = group_rows // 2
     core = grp_s[0] % 2
@@ -599,18 +607,17 @@
         for n, message in enumerate(messages):
             put_phases(message[:lines, :], phases, wcs, n * group_rows)
     num[...] = first[...]
+    more[...] = jnp.zeros_like(more)
     if chunk == 0:
         for copy in copies:
             copy.wait()
-    for n in range(slices - 2):
-        add_plane(
-            n + 1, chunk, chunks, owner_s[0], images, ints_s.at[n], n * group_rows, wcs, num
-        )
+    planes = [(n + 1, ints_s.at[n], n * group_rows) for n in range(slices - 2)]
+    add_planes(planes, owner_s[0], chunks, images, wcs, num, more)
 
     def pack(k, _):
-        own_out[k] = jnp.concatenate([num[k, 0, core], num[k, 1, core]], axis=0)
-        other = jnp.concatenate([num[k, 0, 1 - core], num[k, 1, 1 - core]], axis=0)
-        sib_out[k] = other.astype(BF16)
+        for out, at in ((own_out, core), (sib_out, 1 - core)):
+            halves = [num[k, x, at] + more[k, x, at] for x in range(2)]
+            out[k] = jnp.concatenate(halves, axis=0).astype(out.dtype)
         return 0
 
     lax.fori_loop(0, size, pack, 0, unroll=4)
@@ -904,7 +911,7 @@
             (SHAPE((size,) + tile, F32), VMEM),
             (SHAPE((size + more,) + tile, BF16), VMEM),
         ]
-        scratch = [VMEM((size + 1, 2, 2, width, FREQ), F32)]
+        scratch = [VMEM((size + 1, 2, 2, width, FREQ), F32)] * 2
         spaces = [SMEM] * 2 + [VMEM] * (sum(pieces) + nz - 1)
         if more:
             outs += [
@@ -925,7 +932,7 @@
             args = (grp, owner, *images, *incoming[1:], near_sums, wcs, lists)
         own, sib, *others = call(
             functools.partial(sum_kernel, chunk, chunks, nz, pieces), "sum",
-            spaces, outs, scratch, 3 if n_cls == 4 else 24, 3.0, args,
+            spaces, outs, scratch, 5 if n_cls == 4 else 24, 3.0, args,
         )
         if more:
             den, mass, wcs, lists = others

time: 80.6 us -> 80.1 us (level)
  transfers between devices with their start and end apart: 25 -> 25, of which waited for: 9 -> 9; matrix products, arithmetic and copies ran while one was open for 1% -> 2% of each run, Pallas kernels for 21% -> 22%
where the time goes in v8:
time: 80.1 us; the launch traced here: 79.9 us
  starting transfers between devices  30.1 us (38%)
  Pallas kernels  24.7 us (31%)
  waiting for transfers between devices  22.3 us (28%)
  local copies, waits for them, and re-layouts  1.86 us (2%)
  between operations  0.85 us (1%)
    ppermute x25, starting transfers between devices, swap(): return lax.ppermute(value, axis, [(i, i ^ distance) for i in range(size)])  30.1 us
    pallas_call x13, Pallas kernels, call(): pl.pallas_call(kernel, out_shape=tuple((s for s, _ in outs)), in_specs=[w...  24.7 us
    ppermute x25, waiting for transfers between devices, swap(): return lax.ppermute(value, axis, [(i, i ^ distance) for i in range(size)])  22.3 us
  transfers between devices with their start and end apart: 25, of which 9 were waited for; matrix products, arithmetic and copies ran while one was open for 2% of the time, Pallas kernels for 22%

profile of v8, /device:TPU:0, one launch (start us, length us, event | category | flops | bytes accessed | tf_op | source)
XLA Modules:
  0.0 79.9 jit_solution(12775800879784318479)
XLA Ops:
  0.6 2.0 %weigh.1 = (bf16[2080,128]{1,0:T(8,128)(2,1)S(1)}, bf16[512,128]{1,0:T(8,128)(2,1)S(1)}, bf16[512,128]{1,0:T(8,128)(2,1)S(1)}, bf16[512,128]{1,0:T(8,128)(2,1)S(1)}) custom-call(s32[1]{0:T(128)} %bitcast.grp_s, bf16[16,16384]{1,0:T(8,128)(2,1)} %particles_h.1, s32[8,16]{1,0:T(8,128)} %bitcast.7, s32[16]{0:T(128)} %groups_h.1, s32[16]{0:T(128)} %entries_h.1, ...), custom_call_target="tpu_custom_call" | custom-call | bytes 7200000 | tf_op jit(solution)/shard_map/weigh/pallas_call | solution.py:704
  2.7 3.0 %collective-permute-start.3 = (bf16[2080,128]{1,0:T(8,128)(2,1)S(1)}, bf16[2080,128]{1,0:T(8,128)(2,1)S(1)}, u32[]{:S(2)}, u32[]{:S(2)}) collective-permute-start(bf16[2080,128]{1,0:T(8,128)(2,1)S(1)} %get-tuple-element.49.refs_0_.refs_10_), channel_id=1, source_target_pairs={{0,2},{1,3},{2,0},{3,1},{4,6},{5,7},{6,4},{7,5},{8,10},{9,11},{10,... | collective-permute-start | bytes 1597448 | tf_op jit(solution)/shard_map/ppermute | solution.py:719
  5.7 1.5 %collective-permute-start.1 = (bf16[2080,128]{1,0:T(8,128)(2,1)S(1)}, bf16[2080,128]{1,0:T(8,128)(2,1)S(1)}, u32[]{:S(2)}, u32[]{:S(2)}) collective-permute-start(bf16[2080,128]{1,0:T(8,128)(2,1)S(1)} %get-tuple-element.49.refs_0_.refs_10_), channel_id=1, source_target_pairs={{0,1},{1,0},{2,3},{3,2},{4,5},{5,4},{6,7},{7,6},{8,9},{9,8},{10,11... | collective-permute-start | bytes 1597448 | tf_op jit(solution)/shard_map/ppermute | solution.py:719
  7.2 1.6 %collective-permute-start = (bf16[512,128]{1,0:T(8,128)(2,1)S(1)}, bf16[512,128]{1,0:T(8,128)(2,1)S(1)}, u32[]{:S(2)}, u32[]{:S(2)}) collective-permute-start(bf16[512,128]{1,0:T(8,128)(2,1)S(1)} %get-tuple-element.47), channel_id=1, source_target_pairs={{0,8},{4,12},{8,0},{12,4},{16,24},{20,28},{24,16},{28,20},{1,9},{5... | collective-permute-start | bytes 393224 | tf_op jit(solution)/shard_map/ppermute | solution.py:719
  8.8 2.6 %collective-permute-start.2 = (bf16[512,128]{1,0:T(8,128)(2,1)S(1)}, bf16[512,128]{1,0:T(8,128)(2,1)S(1)}, u32[]{:S(2)}, u32[]{:S(2)}) collective-permute-start(bf16[512,128]{1,0:T(8,128)(2,1)S(1)} %get-tuple-element.54), channel_id=1, source_target_pairs={{0,16},{4,20},{8,24},{12,28},{16,0},{20,4},{24,8},{28,12},{1,17},{... | collective-permute-start | bytes 393224 | tf_op jit(solution)/shard_map/ppermute | solution.py:719
  12.0 3.8 %prep.1 = (f32[53,128,128]{2,1,0:T(8,128)S(1)}, f32[53,128]{1,0:T(8,128)S(1)}, f32[384,64]{1,0:T(8,128)S(1)}, bf16[256,512]{1,0:T(8,128)(2,1)S(1)}, f32[8,128]{1,0:T(8,128)S(1)}) custom-call(s32[1]{0:T(128)} %bitcast.grp_s, bf16[52,16384]{1,0:T(8,128)(2,1)} %refs_h.1, f32[384,64]{1,0:T(8,128)} %constant.15.clone.rest_refs_0_, ...), custom_call_target="tpu_custom_call" | custom-call | bytes 14400000 | tf_op jit(solution)/shard_map/prep/pallas_call | solution.py:704
  15.8 1.8 %score.3 = (f32[128,64]{1,0:T(8,128)S(1)}, f32[16,128]{1,0:T(8,128)S(1)}, f32[128,128]{1,0:T(8,128)S(1)}) custom-call(s32[1]{0:T(128)S(6)} %mul.3.first_s, s32[1]{0:T(128)} %bitcast.1.owner_s, bf16[2080,128]{1,0:T(8,128)(2,1)S(1)} %get-tuple-element.49.refs_0_.refs_10_, f32[53,128,128]{2,1,0:T(8,128)S(1)} %get-tuple-element.50.refs_1_.refs_2_.refs_4_, ...), custom_call_target="tpu_custom_call" | custom-call | bytes 10800000 | tf_op jit(solution)/shard_map/score/pallas_call | solution.py:704
  17.8 1.8 %collective-permute-start.5 = (bf16[1056,128]{1,0:T(8,128)(2,1)S(1)}, bf16[1056,128]{1,0:T(8,128)(2,1)S(1)}, u32[]{:S(2)}, u32[]{:S(2)}) collective-permute-start(bf16[1056,128]{1,0:T(8,128)(2,1)S(1)} %slice.19), channel_id=1, source_target_pairs={{0,1},{1,0},{2,3},{3,2},{4,5},{5,4},{6,7},{7,6},{8,9},{9,8},{10,11... | collective-permute-start | bytes 811016 | tf_op jit(solution)/shard_map/ppermute | solution.py:719
  19.6 1.6 %collective-permute-start.4 = (bf16[1024,128]{1,0:T(8,128)(2,1)S(1)}, bf16[1024,128]{1,0:T(8,128)(2,1)S(1)}, u32[]{:S(2)}, u32[]{:S(2)}) collective-permute-start(bf16[1024,128]{1,0:T(8,128)(2,1)S(1)} %slice.18), channel_id=1, source_target_pairs={{0,2},{1,3},{2,0},{3,1},{4,6},{5,7},{6,4},{7,5},{8,10},{9,11},{10,... | collective-permute-start | bytes 786440 | tf_op jit(solution)/shard_map/ppermute | solution.py:719
  21.2 3.6 %collective-permute-start.6 = (bf16[512,128]{1,0:T(8,128)(2,1)S(1)}, bf16[512,128]{1,0:T(8,128)(2,1)S(1)}, u32[]{:S(2)}, u32[]{:S(2)}) collective-permute-start(bf16[512,128]{1,0:T(8,128)(2,1)S(1)} %get-tuple-element.59), channel_id=1, source_target_pairs={{0,24},{4,28},{8,16},{12,20},{16,8},{20,12},{24,0},{28,4},{1,25},{... | collective-permute-start | bytes 393224 | tf_op jit(solution)/shard_map/ppermute | solution.py:719
  24.8 3.3 %score.4 = (f32[256,64]{1,0:T(8,128)S(1)}, f32[32,128]{1,0:T(8,128)S(1)}, f32[256,128]{1,0:T(8,128)S(1)}) custom-call(s32[1]{0:T(128)S(6)} %mul.3.first_s, s32[1]{0:T(128)} %bitcast.1.owner_s, bf16[2080,128]{1,0:T(8,128)(2,1)S(1)} %collective-permute-done.1.refs_0_.refs_11_.refs_1_, bf16[2080,128]{1,0:T(8,128)(2,1)S(1)} %collective-permute-done.3.refs_1_.refs_12_.refs_2_, ...), custom_call_target="tpu_custom_call" | custom-call | bytes 21600000 | tf_op jit(solution)/shard_map/score/pallas_call | solution.py:704
  28.7 1.4 %collective-permute-start.7 = (bf16[1536,128]{1,0:T(8,128)(2,1)S(1)}, bf16[1536,128]{1,0:T(8,128)(2,1)S(1)}, u32[]{:S(2)}, u32[]{:S(2)}) collective-permute-start(bf16[1536,128]{1,0:T(8,128)(2,1)S(1)} %join.1.refs_0_), channel_id=1, source_target_pairs={{0,1},{1,0},{2,3},{3,2},{4,5},{5,4},{6,7},{7,6},{8,9},{9,8},{10,11... | collective-permute-start | bytes 1179656 | tf_op jit(solution)/shard_map/ppermute | solution.py:719
  30.1 1.8 %score.5 = (f32[128,64]{1,0:T(8,128)S(1)}, f32[64,128]{1,0:T(8,128)S(1)}, f32[128,128]{1,0:T(8,128)S(1)}) custom-call(s32[1]{0:T(128)S(6)} %mul.3.first_s, s32[1]{0:T(128)} %bitcast.1.owner_s, bf16[1024,128]{1,0:T(8,128)(2,1)S(1)} %collective-permute-done.4.refs_0_.refs_3_, bf16[1056,128]{1,0:T(8,128)(2,1)S(1)} %collective-permute-done.5.refs_1_.refs_13_.refs_4_, ...), custom_call_target="tpu_custom_call" | custom-call | bytes 10800000 | tf_op jit(solution)/shard_map/score/pallas_call | solution.py:704
  31.8 1.9 %collective-permute-start.10 = (f32[64,128]{1,0:T(8,128)S(1)}, f32[64,128]{1,0:T(8,128)S(1)}, u32[]{:S(2)}, u32[]{:S(2)}) collective-permute-start(f32[64,128]{1,0:T(8,128)S(1)} %get-tuple-element.60.refs_0_), channel_id=1, source_target_pairs={{0,3},{1,2},{2,1},{3,0},{4,7},{5,6},{6,5},{7,4},{8,11},{9,10},{10,... | collective-permute-start | bytes 98312 | tf_op jit(solution)/shard_map/ppermute | solution.py:719
  34.0 1.4 %collective-permute-start.8 = (f32[64,128]{1,0:T(8,128)S(1)}, f32[64,128]{1,0:T(8,128)S(1)}, u32[]{:S(2)}, u32[]{:S(2)}) collective-permute-start(f32[64,128]{1,0:T(8,128)S(1)} %get-tuple-element.60.refs_0_), channel_id=1, source_target_pairs={{0,1},{1,0},{2,3},{3,2},{4,5},{5,4},{6,7},{7,6},{8,9},{9,8},{10,11... | collective-permute-start | bytes 98312 | tf_op jit(solution)/shard_map/ppermute | solution.py:719
  35.4 4.2 %collective-permute-done.10.refs_3_ = f32[64,128]{1,0:T(8,128)S(1)} collective-permute-done((f32[64,128]{1,0:T(8,128)S(1)}, f32[64,128]{1,0:T(8,128)S(1)}, u32[]{:S(2)}, u32[]{:S(2)}) %collective-permute-start.10) | collective-permute-done | bytes 32800 | tf_op jit(solution)/shard_map/ppermute | solution.py:719
  39.7 1.0 %weights.1 = (bf16[208,128]{1,0:T(8,128)(2,1)S(1)}, f32[16,128]{1,0:T(8,128)S(1)}, f32[8,128]{1,0:T(8,128)S(1)}, f32[16,64]{1,0:T(8,128)S(1)}, s32[16,128]{1,0:T...) custom-call(s32[1]{0:T(128)} %bitcast.grp_s, ...), custom_call_target="tpu_custom_call" | custom-call | bytes 7200000 | tf_op jit(solution)/shard_map/weights/pallas_call | solution.py:704
  41.3 1.2 %collective-permute-start.12 = (bf16[768,128]{1,0:T(8,128)(2,1)S(1)}, bf16[768,128]{1,0:T(8,128)(2,1)S(1)}, u32[]{:S(2)}, u32[]{:S(2)}) collective-permute-start(bf16[768,128]{1,0:T(8,128)(2,1)S(1)} %slice.20), channel_id=1, source_target_pairs={{0,2},{1,3},{2,0},{3,1},{4,6},{5,7},{6,4},{7,5},{8,10},{9,11},{10,... | collective-permute-start | bytes 589832 | tf_op jit(solution)/shard_map/ppermute | solution.py:719
  43.0 2.7 %collective-permute-start.14 = (bf16[256,128]{1,0:T(8,128)(2,1)S(1)}, bf16[256,128]{1,0:T(8,128)(2,1)S(1)}, u32[]{:S(2)}, u32[]{:S(2)}) collective-permute-start(bf16[256,128]{1,0:T(8,128)(2,1)S(1)} %get-tuple-element.70), channel_id=1, source_target_pairs={{0,16},{4,20},{8,24},{12,28},{16,0},{20,4},{24,8},{28,12},{1,17},{... | collective-permute-start | bytes 196616 | tf_op jit(solution)/shard_map/ppermute | solution.py:719
  45.7 1.2 %collective-permute-start.15 = (bf16[256,128]{1,0:T(8,128)(2,1)S(1)}, bf16[256,128]{1,0:T(8,128)(2,1)S(1)}, u32[]{:S(2)}, u32[]{:S(2)}) collective-permute-start(bf16[256,128]{1,0:T(8,128)(2,1)S(1)} %get-tuple-element.71), channel_id=1, source_target_pairs={{0,24},{4,28},{8,16},{12,20},{16,8},{20,12},{24,0},{28,4},{1,25},{... | collective-permute-start | bytes 196616 | tf_op jit(solution)/shard_map/ppermute | solution.py:719
  46.9 1.8 %own_sum.1.refs_6_ = f32[53,2,2,8,128]{4,3,2,1,0:T(8,128)S(1)} custom-call(s32[1]{0:T(128)} %bitcast.grp_s, s32[1]{0:T(128)} %bitcast.1.owner_s, bf16[208,128]{1,0:T(8,128)(2,1)S(1)} %get-tuple-element.67.packed, s32[16,128]{1,0:T(8,128)S(1)} %get-tuple-element.73.ints, bf16[2080,128]{1,0:T(8,128)(2,1)S(1)} %get-tuple-element.49.refs_0_.refs_10_, ...), custom_call_target="tpu_custom_call" | custom-call | bytes 10800000 | tf_op jit(solution)/shard_map/own_sum/pallas_call | solution.py:704
  48.8 1.7 %near_sum.1 = (f32[53,2,2,8,128]{4,3,2,1,0:T(8,128)S(1)}, f32[16,128]{1,0:T(8,128)S(1)}, f32[8,128]{1,0:T(8,128)S(1)}) custom-call(s32[1]{0:T(128)} %bitcast.1.owner_s, bf16[1536,128]{1,0:T(8,128)(2,1)S(1)} %join.1.refs_0_, bf16[1536,128]{1,0:T(8,128)(2,1)S(1)} %collective-permute-done.7.refs_1_, bf16[1536,128]{1,0:T(8,128)(2,1)S(1)} %collective-permute-done.11.refs_2_, ...), custom_call_target="tpu_custom_call" | custom-call | bytes 7200000 | tf_op jit(solution)/shard_map/near_sum/pallas_call | solution.py:704
  50.5 1.2 %collective-permute-done.15.refs_6_ = bf16[256,128]{1,0:T(8,128)(2,1)S(1)} collective-permute-done((bf16[256,128]{1,0:T(8,128)(2,1)S(1)}, bf16[256,128]{1,0:T(8,128)(2,1)S(1)}, u32[]{:S(2)}, u32[]{:S(2)}) %collective-permute-start.15) | collective-permute-done | bytes 65568 | tf_op jit(solution)/shard_map/ppermute | solution.py:719
  51.7 3.6 %sum.1 = (f32[52,16,128]{2,1,0:T(8,128)S(1)}, bf16[53,16,128]{2,1,0:T(8,128)(2,1)S(1)}, f32[8,128]{1,0:T(8,128)S(1)}, f32[8,128]{1,0:T(8,128)S(1)}, f32[2,832,128]{2,1,0:T(8,128)}, /*index=5*/s32[2,16,128]{2,1,0:T(8,128)}) custom-call(s32[1]{0:T(128)} %bitcast.grp_s, s32[1]{0:T(128)} %bitcast.1.owner_s, bf16[1536,128]{1,0:T(8,128)(2,1)S(1)} %join.1.refs_0_, ...), custom_call_target="tpu_custom_call" | custom-call | bytes 10800000 | tf_op jit(solution)/shard_map/sum/pallas_call | solution.py:704
  55.4 1.5 %collective-permute-done.17.sib = bf16[53,16,128]{2,1,0:T(8,128)(2,1)S(1)} collective-permute-done((bf16[53,16,128]{2,1,0:T(8,128)(2,1)S(1)}, bf16[53,16,128]{2,1,0:T(8,128)(2,1)S(1)}, u32[]{:S(2)}, u32[]{:S(2)}) %collective-permute-start.17) | collective-permute-done | bytes 217120 | tf_op jit(solution)/shard_map/ppermute | solution.py:719
  56.9 0.7 divide.1
  57.9 1.6 %collective-permute-start.18 = (bf16[52,16,128]{2,1,0:T(8,128)(2,1)S(1)}, bf16[52,16,128]{2,1,0:T(8,128)(2,1)S(1)}, u32[]{:S(2)}, u32[]{:S(2)}) collective-permute-start(bf16[52,16,128]{2,1,0:T(8,128)(2,1)S(1)} %get-tuple-element.85.refs_0_), channel_id=1, source_target_pairs={{0,8},{4,12},{8,0},{12,4},{16,24},{20,28},{24,16},{28,20},{1,9},{5... | collective-permute-start | bytes 638984 | tf_op jit(solution)/shard_map/ppermute | solution.py:719
  59.5 9.7 %collective-permute-done.19.refs_4_ = bf16[52,16,128]{2,1,0:T(8,128)(2,1)S(1)} collective-permute-done((bf16[52,16,128]{2,1,0:T(8,128)(2,1)S(1)}, bf16[52,16,128]{2,1,0:T(8,128)(2,1)S(1)}, u32[]{:S(2)}, u32[]{:S(2)}) %collective-permute-start.19) | collective-permute-done | bytes 213024 | tf_op jit(solution)/shard_map/ppermute | solution.py:719
  71.3 2.0 %spread.2.refs_2_ = f32[52,16384]{1,0:T(8,128)} custom-call(s32[1]{0:T(128)} %bitcast.grp_s, bf16[52,16,128]{2,1,0:T(8,128)(2,1)S(1)} %get-tuple-element.85.refs_0_, bf16[52,16,128]{2,1,0:T(8,128)(2,1)S(1)} %collective-permute-done.21.refs_1_, bf16[52,16,128]{2,1,0:T(8,128)(2,1)S(1)} %collective-permute-done.18.refs_2_, ...), custom_call_target="tpu_custom_call" | custom-call | bytes 180000 | tf_op jit(solution)/shard_map/spread/pallas_call | solution.py:704
  73.3 3.9 %collective-permute-done.20.refs_0_ = bf16[52,16,128]{2,1,0:T(8,128)(2,1)S(1)} collective-permute-done((bf16[52,16,128]{2,1,0:T(8,128)(2,1)S(1)}, bf16[52,16,128]{2,1,0:T(8,128)(2,1)S(1)}, u32[]{:S(2)}, u32[]{:S(2)}) %collective-permute-start.20) | collective-permute-done | bytes 213024 | tf_op jit(solution)/shard_map/ppermute | solution.py:719
  77.7 0.9 %collective-permute-done.24.refs_1_ = bf16[52,16,128]{2,1,0:T(8,128)(2,1)S(1)} collective-permute-done((bf16[52,16,128]{2,1,0:T(8,128)(2,1)S(1)}, bf16[52,16,128]{2,1,0:T(8,128)(2,1)S(1)}, u32[]{:S(2)}, u32[]{:S(2)}) %collective-permute-start.24) | collective-permute-done | bytes 213024 | tf_op jit(solution)/shard_map/ppermute | solution.py:719
  78.7 1.2 %spread.3 = f32[52,16384]{1,0:T(8,128)} custom-call(s32[1]{0:T(128)} %bitcast.grp_s, bf16[52,16,128]{2,1,0:T(8,128)(2,1)S(1)} %collective-permute-done.20.refs_0_, bf16[52,16,128]{2,1,0:T(8,128)(2,1)S(1)} %collective-permute-done.24.refs_1_, f32[52,16384]{1,0:T(8,128)} %spread.2.refs_2_), custom_call_target="tpu_custom_call", output_to_operand_aliasing={{}: (3, {})} | custom-call | bytes 180000 | tf_op jit(solution)/shard_map/spread/pallas_call | solution.py:704
  (39 shorter events, 5.9 us)
Async XLA Ops:
  2.7 15.1 %collective-permute-start.3 = (bf16[2080,128]{1,0:T(8,128)(2,1)S(1)}, bf16[2080,128]{1,0:T(8,128)(2,1)S(1)}, u32[]{:S(2)}, u32[]{:S(2)}) collective-permute-start(bf16[2080,128]{1,0:T(8,128)(2,1)S(1)} %get-tuple-element.49.refs_0_.refs_10_), channel_id=1, source_target_pairs={{0,2},{1,3},{2,0},{3,1},{4,6},{5,7},{6,4},{7,5},{8,10},{9,11},{10,... | collective-permute-start | bytes 1597448 | tf_op jit(solution)/shard_map/ppermute | solution.py:719
  5.7 13.9 %collective-permute-start.1 = (bf16[2080,128]{1,0:T(8,128)(2,1)S(1)}, bf16[2080,128]{1,0:T(8,128)(2,1)S(1)}, u32[]{:S(2)}, u32[]{:S(2)}) collective-permute-start(bf16[2080,128]{1,0:T(8,128)(2,1)S(1)} %get-tuple-element.49.refs_0_.refs_10_), channel_id=1, source_target_pairs={{0,1},{1,0},{2,3},{3,2},{4,5},{5,4},{6,7},{7,6},{8,9},{9,8},{10,11... | collective-permute-start | bytes 1597448 | tf_op jit(solution)/shard_map/ppermute | solution.py:719
  7.2 8.6 %collective-permute-start = (bf16[512,128]{1,0:T(8,128)(2,1)S(1)}, bf16[512,128]{1,0:T(8,128)(2,1)S(1)}, u32[]{:S(2)}, u32[]{:S(2)}) collective-permute-start(bf16[512,128]{1,0:T(8,128)(2,1)S(1)} %get-tuple-element.47), channel_id=1, source_target_pairs={{0,8},{4,12},{8,0},{12,4},{16,24},{20,28},{24,16},{28,20},{1,9},{5... | collective-permute-start | bytes 393224 | tf_op jit(solution)/shard_map/ppermute | solution.py:719
  8.8 8.8 %collective-permute-start.2 = (bf16[512,128]{1,0:T(8,128)(2,1)S(1)}, bf16[512,128]{1,0:T(8,128)(2,1)S(1)}, u32[]{:S(2)}, u32[]{:S(2)}) collective-permute-start(bf16[512,128]{1,0:T(8,128)(2,1)S(1)} %get-tuple-element.54), channel_id=1, source_target_pairs={{0,16},{4,20},{8,24},{12,28},{16,0},{20,4},{24,8},{28,12},{1,17},{... | collective-permute-start | bytes 393224 | tf_op jit(solution)/shard_map/ppermute | solution.py:719
  11.4 0.7 copy-start
  17.8 10.3 %collective-permute-start.5 = (bf16[1056,128]{1,0:T(8,128)(2,1)S(1)}, bf16[1056,128]{1,0:T(8,128)(2,1)S(1)}, u32[]{:S(2)}, u32[]{:S(2)}) collective-permute-start(bf16[1056,128]{1,0:T(8,128)(2,1)S(1)} %slice.19), channel_id=1, source_target_pairs={{0,1},{1,0},{2,3},{3,2},{4,5},{5,4},{6,7},{7,6},{8,9},{9,8},{10,11... | collective-permute-start | bytes 811016 | tf_op jit(solution)/shard_map/ppermute | solution.py:719
  19.6 8.5 %collective-permute-start.4 = (bf16[1024,128]{1,0:T(8,128)(2,1)S(1)}, bf16[1024,128]{1,0:T(8,128)(2,1)S(1)}, u32[]{:S(2)}, u32[]{:S(2)}) collective-permute-start(bf16[1024,128]{1,0:T(8,128)(2,1)S(1)} %slice.18), channel_id=1, source_target_pairs={{0,2},{1,3},{2,0},{3,1},{4,6},{5,7},{6,4},{7,5},{8,10},{9,11},{10,... | collective-permute-start | bytes 786440 | tf_op jit(solution)/shard_map/ppermute | solution.py:719
  21.2 7.0 %collective-permute-start.6 = (bf16[512,128]{1,0:T(8,128)(2,1)S(1)}, bf16[512,128]{1,0:T(8,128)(2,1)S(1)}, u32[]{:S(2)}, u32[]{:S(2)}) collective-permute-start(bf16[512,128]{1,0:T(8,128)(2,1)S(1)} %get-tuple-element.59), channel_id=1, source_target_pairs={{0,24},{4,28},{8,16},{12,20},{16,8},{20,12},{24,0},{28,4},{1,25},{... | collective-permute-start | bytes 393224 | tf_op jit(solution)/shard_map/ppermute | solution.py:719
  28.2 12.4 %collective-permute-start.11 = (bf16[1536,128]{1,0:T(8,128)(2,1)S(1)}, bf16[1536,128]{1,0:T(8,128)(2,1)S(1)}, u32[]{:S(2)}, u32[]{:S(2)}) collective-permute-start(bf16[1536,128]{1,0:T(8,128)(2,1)S(1)} %join.1.refs_0_), channel_id=1, source_target_pairs={{0,2},{1,3},{2,0},{3,1},{4,6},{5,7},{6,4},{7,5},{8,10},{9,11},{10,... | collective-permute-start | bytes 1179656 | tf_op jit(solution)/shard_map/ppermute | solution.py:719
  28.7 12.6 %collective-permute-start.7 = (bf16[1536,128]{1,0:T(8,128)(2,1)S(1)}, bf16[1536,128]{1,0:T(8,128)(2,1)S(1)}, u32[]{:S(2)}, u32[]{:S(2)}) collective-permute-start(bf16[1536,128]{1,0:T(8,128)(2,1)S(1)} %join.1.refs_0_), channel_id=1, source_target_pairs={{0,1},{1,0},{2,3},{3,2},{4,5},{5,4},{6,7},{7,6},{8,9},{9,8},{10,11... | collective-permute-start | bytes 1179656 | tf_op jit(solution)/shard_map/ppermute | solution.py:719
  31.8 7.8 %collective-permute-start.10 = (f32[64,128]{1,0:T(8,128)S(1)}, f32[64,128]{1,0:T(8,128)S(1)}, u32[]{:S(2)}, u32[]{:S(2)}) collective-permute-start(f32[64,128]{1,0:T(8,128)S(1)} %get-tuple-element.60.refs_0_), channel_id=1, source_target_pairs={{0,3},{1,2},{2,1},{3,0},{4,7},{5,6},{6,5},{7,4},{8,11},{9,10},{10,... | collective-permute-start | bytes 98312 | tf_op jit(solution)/shard_map/ppermute | solution.py:719
  33.8 5.9 %collective-permute-start.9 = (f32[64,128]{1,0:T(8,128)S(1)}, f32[64,128]{1,0:T(8,128)S(1)}, u32[]{:S(2)}, u32[]{:S(2)}) collective-permute-start(f32[64,128]{1,0:T(8,128)S(1)} %get-tuple-element.60.refs_0_), channel_id=1, source_target_pairs={{0,2},{1,3},{2,0},{3,1},{4,6},{5,7},{6,4},{7,5},{8,10},{9,11},{10,... | collective-permute-start | bytes 98312 | tf_op jit(solution)/shard_map/ppermute | solution.py:719
  34.0 5.6 %collective-permute-start.8 = (f32[64,128]{1,0:T(8,128)S(1)}, f32[64,128]{1,0:T(8,128)S(1)}, u32[]{:S(2)}, u32[]{:S(2)}) collective-permute-start(f32[64,128]{1,0:T(8,128)S(1)} %get-tuple-element.60.refs_0_), channel_id=1, source_target_pairs={{0,1},{1,0},{2,3},{3,2},{4,5},{5,4},{6,7},{7,6},{8,9},{9,8},{10,11... | collective-permute-start | bytes 98312 | tf_op jit(solution)/shard_map/ppermute | solution.py:719
  40.7 8.1 %collective-permute-start.13 = (bf16[768,128]{1,0:T(8,128)(2,1)S(1)}, bf16[768,128]{1,0:T(8,128)(2,1)S(1)}, u32[]{:S(2)}, u32[]{:S(2)}) collective-permute-start(bf16[768,128]{1,0:T(8,128)(2,1)S(1)} %slice.21), channel_id=1, source_target_pairs={{0,1},{1,0},{2,3},{3,2},{4,5},{5,4},{6,7},{7,6},{8,9},{9,8},{10,11... | collective-permute-start | bytes 589832 | tf_op jit(solution)/shard_map/ppermute | solution.py:719
  41.3 7.4 %collective-permute-start.12 = (bf16[768,128]{1,0:T(8,128)(2,1)S(1)}, bf16[768,128]{1,0:T(8,128)(2,1)S(1)}, u32[]{:S(2)}, u32[]{:S(2)}) collective-permute-start(bf16[768,128]{1,0:T(8,128)(2,1)S(1)} %slice.20), channel_id=1, source_target_pairs={{0,2},{1,3},{2,0},{3,1},{4,6},{5,7},{6,4},{7,5},{8,10},{9,11},{10,... | collective-permute-start | bytes 589832 | tf_op jit(solution)/shard_map/ppermute | solution.py:719
  42.5 6.2 %collective-permute-start.16 = (bf16[256,128]{1,0:T(8,128)(2,1)S(1)}, bf16[256,128]{1,0:T(8,128)(2,1)S(1)}, u32[]{:S(2)}, u32[]{:S(2)}) collective-permute-start(bf16[256,128]{1,0:T(8,128)(2,1)S(1)} %get-tuple-element.72), channel_id=1, source_target_pairs={{0,8},{4,12},{8,0},{12,4},{16,24},{20,28},{24,16},{28,20},{1,9},{5... | collective-permute-start | bytes 196616 | tf_op jit(solution)/shard_map/ppermute | solution.py:719
  43.0 7.5 %collective-permute-start.14 = (bf16[256,128]{1,0:T(8,128)(2,1)S(1)}, bf16[256,128]{1,0:T(8,128)(2,1)S(1)}, u32[]{:S(2)}, u32[]{:S(2)}) collective-permute-start(bf16[256,128]{1,0:T(8,128)(2,1)S(1)} %get-tuple-element.70), channel_id=1, source_target_pairs={{0,16},{4,20},{8,24},{12,28},{16,0},{20,4},{24,8},{28,12},{1,17},{... | collective-permute-start | bytes 196616 | tf_op jit(solution)/shard_map/ppermute | solution.py:719
  45.7 6.1 %collective-permute-start.15 = (bf16[256,128]{1,0:T(8,128)(2,1)S(1)}, bf16[256,128]{1,0:T(8,128)(2,1)S(1)}, u32[]{:S(2)}, u32[]{:S(2)}) collective-permute-start(bf16[256,128]{1,0:T(8,128)(2,1)S(1)} %get-tuple-element.71), channel_id=1, source_target_pairs={{0,24},{4,28},{8,16},{12,20},{16,8},{20,12},{24,0},{28,4},{1,25},{... | collective-permute-start | bytes 196616 | tf_op jit(solution)/shard_map/ppermute | solution.py:719
  55.4 1.5 %collective-permute-start.17 = (bf16[53,16,128]{2,1,0:T(8,128)(2,1)S(1)}, bf16[53,16,128]{2,1,0:T(8,128)(2,1)S(1)}, u32[]{:S(2)}, u32[]{:S(2)}) collective-permute-start(bf16[53,16,128]{2,1,0:T(8,128)(2,1)S(1)} %get-tuple-element.81), channel_id=1, source_target_pairs={{0,4},{4,0},{8,12},{12,8},{16,20},{20,16},{24,28},{28,24},{1,5},{5... | collective-permute-start | bytes 651272 | tf_op jit(solution)/shard_map/ppermute | solution.py:719
  57.6 11.6 %collective-permute-start.19 = (bf16[52,16,128]{2,1,0:T(8,128)(2,1)S(1)}, bf16[52,16,128]{2,1,0:T(8,128)(2,1)S(1)}, u32[]{:S(2)}, u32[]{:S(2)}) collective-permute-start(bf16[52,16,128]{2,1,0:T(8,128)(2,1)S(1)} %get-tuple-element.85.refs_0_), channel_id=1, source_target_pairs={{0,16},{4,20},{8,24},{12,28},{16,0},{20,4},{24,8},{28,12},{1,17},{... | collective-permute-start | bytes 638984 | tf_op jit(solution)/shard_map/ppermute | solution.py:719
  57.9 11.6 %collective-permute-start.18 = (bf16[52,16,128]{2,1,0:T(8,128)(2,1)S(1)}, bf16[52,16,128]{2,1,0:T(8,128)(2,1)S(1)}, u32[]{:S(2)}, u32[]{:S(2)}) collective-permute-start(bf16[52,16,128]{2,1,0:T(8,128)(2,1)S(1)} %get-tuple-element.85.refs_0_), channel_id=1, source_target_pairs={{0,8},{4,12},{8,0},{12,4},{16,24},{20,28},{24,16},{28,20},{1,9},{5... | collective-permute-start | bytes 638984 | tf_op jit(solution)/shard_map/ppermute | solution.py:719
  59.5 11.5 %collective-permute-start.21 = (bf16[52,16,128]{2,1,0:T(8,128)(2,1)S(1)}, bf16[52,16,128]{2,1,0:T(8,128)(2,1)S(1)}, u32[]{:S(2)}, u32[]{:S(2)}) collective-permute-start(bf16[52,16,128]{2,1,0:T(8,128)(2,1)S(1)} %get-tuple-element.85.refs_0_), channel_id=1, source_target_pairs={{0,4},{4,0},{8,12},{12,8},{16,20},{20,16},{24,28},{28,24},{1,5},{5... | collective-permute-start | bytes 638984 | tf_op jit(solution)/shard_map/ppermute | solution.py:719
  69.5 1.5 %collective-permute-start.22 = (bf16[52,16,128]{2,1,0:T(8,128)(2,1)S(1)}, bf16[52,16,128]{2,1,0:T(8,128)(2,1)S(1)}, u32[]{:S(2)}, u32[]{:S(2)}) collective-permute-start(bf16[52,16,128]{2,1,0:T(8,128)(2,1)S(1)} %collective-permute-done.18.refs_2_), channel_id=1, source_target_pairs={{0,4},{4,0},{8,12},{12,8},{16,20},{20,16},{24,28},{28,24},{1,5},{5... | collective-permute-start | bytes 638984 | tf_op jit(solution)/shard_map/ppermute | solution.py:719
  69.5 1.8 %collective-permute-start.23 = (bf16[52,16,128]{2,1,0:T(8,128)(2,1)S(1)}, bf16[52,16,128]{2,1,0:T(8,128)(2,1)S(1)}, u32[]{:S(2)}, u32[]{:S(2)}) collective-permute-start(bf16[52,16,128]{2,1,0:T(8,128)(2,1)S(1)} %collective-permute-done.19.refs_4_), channel_id=1, source_target_pairs={{0,4},{4,0},{8,12},{12,8},{16,20},{20,16},{24,28},{28,24},{1,5},{5... | collective-permute-start | bytes 638984 | tf_op jit(solution)/shard_map/ppermute | solution.py:719
  70.0 7.2 %collective-permute-start.20 = (bf16[52,16,128]{2,1,0:T(8,128)(2,1)S(1)}, bf16[52,16,128]{2,1,0:T(8,128)(2,1)S(1)}, u32[]{:S(2)}, u32[]{:S(2)}) collective-permute-start(bf16[52,16,128]{2,1,0:T(8,128)(2,1)S(1)} %collective-permute-done.19.refs_4_), channel_id=1, source_target_pairs={{0,8},{4,12},{8,0},{12,4},{16,24},{20,28},{24,16},{28,20},{1,9},{5... | collective-permute-start | bytes 638984 | tf_op jit(solution)/shard_map/ppermute | solution.py:719
  77.2 1.5 %collective-permute-start.24 = (bf16[52,16,128]{2,1,0:T(8,128)(2,1)S(1)}, bf16[52,16,128]{2,1,0:T(8,128)(2,1)S(1)}, u32[]{:S(2)}, u32[]{:S(2)}) collective-permute-start(bf16[52,16,128]{2,1,0:T(8,128)(2,1)S(1)} %collective-permute-done.20.refs_0_), channel_id=1, source_target_pairs={{0,4},{4,0},{8,12},{12,8},{16,20},{20,16},{24,28},{28,24},{1,5},{5... | collective-permute-start | bytes 638984 | tf_op jit(solution)/shard_map/ppermute | solution.py:719

commit v9 on v8

--- a/solution.py
+++ b/solution.py
@@ -620,7 +620,7 @@
             out[k] = jnp.concatenate(halves, axis=0).astype(out.dtype)
         return 0
 
-    lax.fori_loop(0, size, pack, 0, unroll=4)
+    lax.fori_loop(0, size, pack, 0, unroll=13)
     if chunk == 0:
         width = num.shape[3]
         den_v[...] = den.reshape(2, width, FREQ)
@@ -632,8 +632,11 @@
 def divide(own, sib, inverse, start, avg_out):
     for k in range(avg_out.shape[0]):
         column = inverse[:, start + k : start + k + 1]
-        factor = jnp.concatenate([column, column], axis=0)
-        avg_out[k] = ((own[k] + sib[k].astype(F32)) * factor).astype(BF16)
+        factor = jnp.broadcast_to(column, inverse.shape)
+        total = own[k] + sib[k].astype(F32)
+        width = inverse.shape[0]
+        parts = [total[:width] * factor, total[width:] * factor]
+        avg_out[k] = jnp.concatenate(parts, axis=0).astype(BF16)
 
 
 def first_divide_kernel(scale, start, own, sib, den, mass, reg, avg_out, share_out, inverse_out):

time: 80.1 us -> 79.9 us (level)
  no operation moved by 1% of the time
where the time goes in v9:
time: 79.9 us
  starting transfers between devices  30 us (38%)
  Pallas kernels  24.6 us (31%)
  waiting for transfers between devices  22.5 us (28%)
  local copies, waits for them, and re-layouts  1.86 us (2%)
  between operations  0.85 us (1%)
    ppermute x25, starting transfers between devices, swap(): return lax.ppermute(value, axis, [(i, i ^ distance) for i in range(size)])  30 us
    pallas_call x13, Pallas kernels, call(): pl.pallas_call(kernel, out_shape=tuple((s for s, _ in outs)), in_specs=[w...  24.6 us
    ppermute x25, waiting for transfers between devices, swap(): return lax.ppermute(value, axis, [(i, i ^ distance) for i in range(size)])  22.5 us
  transfers between devices with their start and end apart: 25, of which 9 were waited for; matrix products, arithmetic and copies ran while one was open for 2% of the time, Pallas kernels for 22%

profile of v9, /device:TPU:0, one launch (start us, length us, event | category | flops | bytes accessed | tf_op | source)
XLA Modules:
  0.0 79.9 jit_solution(8079065140819181813)
XLA Ops:
  0.6 2.0 %weigh.1 = (bf16[2080,128]{1,0:T(8,128)(2,1)S(1)}, bf16[512,128]{1,0:T(8,128)(2,1)S(1)}, bf16[512,128]{1,0:T(8,128)(2,1)S(1)}, bf16[512,128]{1,0:T(8,128)(2,1)S(1)}) custom-call(s32[1]{0:T(128)} %bitcast.grp_s, bf16[16,16384]{1,0:T(8,128)(2,1)} %particles_h.1, s32[8,16]{1,0:T(8,128)} %bitcast.7, s32[16]{0:T(128)} %groups_h.1, s32[16]{0:T(128)} %entries_h.1, ...), custom_call_target="tpu_custom_call" | custom-call | bytes 7200000 | tf_op jit(solution)/shard_map/weigh/pallas_call | solution.py:707
  2.7 3.0 %collective-permute-start.3 = (bf16[2080,128]{1,0:T(8,128)(2,1)S(1)}, bf16[2080,128]{1,0:T(8,128)(2,1)S(1)}, u32[]{:S(2)}, u32[]{:S(2)}) collective-permute-start(bf16[2080,128]{1,0:T(8,128)(2,1)S(1)} %get-tuple-element.49.refs_0_.refs_10_), channel_id=1, source_target_pairs={{0,2},{1,3},{2,0},{3,1},{4,6},{5,7},{6,4},{7,5},{8,10},{9,11},{10,... | collective-permute-start | bytes 1597448 | tf_op jit(solution)/shard_map/ppermute | solution.py:722
  5.7 1.5 %collective-permute-start.1 = (bf16[2080,128]{1,0:T(8,128)(2,1)S(1)}, bf16[2080,128]{1,0:T(8,128)(2,1)S(1)}, u32[]{:S(2)}, u32[]{:S(2)}) collective-permute-start(bf16[2080,128]{1,0:T(8,128)(2,1)S(1)} %get-tuple-element.49.refs_0_.refs_10_), channel_id=1, source_target_pairs={{0,1},{1,0},{2,3},{3,2},{4,5},{5,4},{6,7},{7,6},{8,9},{9,8},{10,11... | collective-permute-start | bytes 1597448 | tf_op jit(solution)/shard_map/ppermute | solution.py:722
  7.2 1.6 %collective-permute-start = (bf16[512,128]{1,0:T(8,128)(2,1)S(1)}, bf16[512,128]{1,0:T(8,128)(2,1)S(1)}, u32[]{:S(2)}, u32[]{:S(2)}) collective-permute-start(bf16[512,128]{1,0:T(8,128)(2,1)S(1)} %get-tuple-element.47), channel_id=1, source_target_pairs={{0,8},{4,12},{8,0},{12,4},{16,24},{20,28},{24,16},{28,20},{1,9},{5... | collective-permute-start | bytes 393224 | tf_op jit(solution)/shard_map/ppermute | solution.py:722
  8.8 2.6 %collective-permute-start.2 = (bf16[512,128]{1,0:T(8,128)(2,1)S(1)}, bf16[512,128]{1,0:T(8,128)(2,1)S(1)}, u32[]{:S(2)}, u32[]{:S(2)}) collective-permute-start(bf16[512,128]{1,0:T(8,128)(2,1)S(1)} %get-tuple-element.54), channel_id=1, source_target_pairs={{0,16},{4,20},{8,24},{12,28},{16,0},{20,4},{24,8},{28,12},{1,17},{... | collective-permute-start | bytes 393224 | tf_op jit(solution)/shard_map/ppermute | solution.py:722
  12.0 3.8 %prep.1 = (f32[53,128,128]{2,1,0:T(8,128)S(1)}, f32[53,128]{1,0:T(8,128)S(1)}, f32[384,64]{1,0:T(8,128)S(1)}, bf16[256,512]{1,0:T(8,128)(2,1)S(1)}, f32[8,128]{1,0:T(8,128)S(1)}) custom-call(s32[1]{0:T(128)} %bitcast.grp_s, bf16[52,16384]{1,0:T(8,128)(2,1)} %refs_h.1, f32[384,64]{1,0:T(8,128)} %constant.15.clone.rest_refs_0_, ...), custom_call_target="tpu_custom_call" | custom-call | bytes 14400000 | tf_op jit(solution)/shard_map/prep/pallas_call | solution.py:707
  15.8 1.8 %score.3 = (f32[128,64]{1,0:T(8,128)S(1)}, f32[16,128]{1,0:T(8,128)S(1)}, f32[128,128]{1,0:T(8,128)S(1)}) custom-call(s32[1]{0:T(128)S(6)} %mul.3.first_s, s32[1]{0:T(128)} %bitcast.1.owner_s, bf16[2080,128]{1,0:T(8,128)(2,1)S(1)} %get-tuple-element.49.refs_0_.refs_10_, f32[53,128,128]{2,1,0:T(8,128)S(1)} %get-tuple-element.50.refs_1_.refs_2_.refs_4_, ...), custom_call_target="tpu_custom_call" | custom-call | bytes 10800000 | tf_op jit(solution)/shard_map/score/pallas_call | solution.py:707
  17.8 1.8 %collective-permute-start.5 = (bf16[1056,128]{1,0:T(8,128)(2,1)S(1)}, bf16[1056,128]{1,0:T(8,128)(2,1)S(1)}, u32[]{:S(2)}, u32[]{:S(2)}) collective-permute-start(bf16[1056,128]{1,0:T(8,128)(2,1)S(1)} %slice.19), channel_id=1, source_target_pairs={{0,1},{1,0},{2,3},{3,2},{4,5},{5,4},{6,7},{7,6},{8,9},{9,8},{10,11... | collective-permute-start | bytes 811016 | tf_op jit(solution)/shard_map/ppermute | solution.py:722
  19.6 1.6 %collective-permute-start.4 = (bf16[1024,128]{1,0:T(8,128)(2,1)S(1)}, bf16[1024,128]{1,0:T(8,128)(2,1)S(1)}, u32[]{:S(2)}, u32[]{:S(2)}) collective-permute-start(bf16[1024,128]{1,0:T(8,128)(2,1)S(1)} %slice.18), channel_id=1, source_target_pairs={{0,2},{1,3},{2,0},{3,1},{4,6},{5,7},{6,4},{7,5},{8,10},{9,11},{10,... | collective-permute-start | bytes 786440 | tf_op jit(solution)/shard_map/ppermute | solution.py:722
  21.2 3.6 %collective-permute-start.6 = (bf16[512,128]{1,0:T(8,128)(2,1)S(1)}, bf16[512,128]{1,0:T(8,128)(2,1)S(1)}, u32[]{:S(2)}, u32[]{:S(2)}) collective-permute-start(bf16[512,128]{1,0:T(8,128)(2,1)S(1)} %get-tuple-element.59), channel_id=1, source_target_pairs={{0,24},{4,28},{8,16},{12,20},{16,8},{20,12},{24,0},{28,4},{1,25},{... | collective-permute-start | bytes 393224 | tf_op jit(solution)/shard_map/ppermute | solution.py:722
  24.8 3.3 %score.4 = (f32[256,64]{1,0:T(8,128)S(1)}, f32[32,128]{1,0:T(8,128)S(1)}, f32[256,128]{1,0:T(8,128)S(1)}) custom-call(s32[1]{0:T(128)S(6)} %mul.3.first_s, s32[1]{0:T(128)} %bitcast.1.owner_s, bf16[2080,128]{1,0:T(8,128)(2,1)S(1)} %collective-permute-done.1.refs_0_.refs_11_.refs_1_, bf16[2080,128]{1,0:T(8,128)(2,1)S(1)} %collective-permute-done.3.refs_1_.refs_12_.refs_2_, ...), custom_call_target="tpu_custom_call" | custom-call | bytes 21600000 | tf_op jit(solution)/shard_map/score/pallas_call | solution.py:707
  28.8 1.3 %collective-permute-start.7 = (bf16[1536,128]{1,0:T(8,128)(2,1)S(1)}, bf16[1536,128]{1,0:T(8,128)(2,1)S(1)}, u32[]{:S(2)}, u32[]{:S(2)}) collective-permute-start(bf16[1536,128]{1,0:T(8,128)(2,1)S(1)} %join.1.refs_0_), channel_id=1, source_target_pairs={{0,1},{1,0},{2,3},{3,2},{4,5},{5,4},{6,7},{7,6},{8,9},{9,8},{10,11... | collective-permute-start | bytes 1179656 | tf_op jit(solution)/shard_map/ppermute | solution.py:722
  30.1 1.8 %score.5 = (f32[128,64]{1,0:T(8,128)S(1)}, f32[64,128]{1,0:T(8,128)S(1)}, f32[128,128]{1,0:T(8,128)S(1)}) custom-call(s32[1]{0:T(128)S(6)} %mul.3.first_s, s32[1]{0:T(128)} %bitcast.1.owner_s, bf16[1024,128]{1,0:T(8,128)(2,1)S(1)} %collective-permute-done.4.refs_0_.refs_3_, bf16[1056,128]{1,0:T(8,128)(2,1)S(1)} %collective-permute-done.5.refs_1_.refs_13_.refs_4_, ...), custom_call_target="tpu_custom_call" | custom-call | bytes 10800000 | tf_op jit(solution)/shard_map/score/pallas_call | solution.py:707
  31.9 1.7 %collective-permute-start.10 = (f32[64,128]{1,0:T(8,128)S(1)}, f32[64,128]{1,0:T(8,128)S(1)}, u32[]{:S(2)}, u32[]{:S(2)}) collective-permute-start(f32[64,128]{1,0:T(8,128)S(1)} %get-tuple-element.60.refs_0_), channel_id=1, source_target_pairs={{0,3},{1,2},{2,1},{3,0},{4,7},{5,6},{6,5},{7,4},{8,11},{9,10},{10,... | collective-permute-start | bytes 98312 | tf_op jit(solution)/shard_map/ppermute | solution.py:722
  34.2 1.3 %collective-permute-start.8 = (f32[64,128]{1,0:T(8,128)S(1)}, f32[64,128]{1,0:T(8,128)S(1)}, u32[]{:S(2)}, u32[]{:S(2)}) collective-permute-start(f32[64,128]{1,0:T(8,128)S(1)} %get-tuple-element.60.refs_0_), channel_id=1, source_target_pairs={{0,1},{1,0},{2,3},{3,2},{4,5},{5,4},{6,7},{7,6},{8,9},{9,8},{10,11... | collective-permute-start | bytes 98312 | tf_op jit(solution)/shard_map/ppermute | solution.py:722
  35.5 4.3 %collective-permute-done.10.refs_3_ = f32[64,128]{1,0:T(8,128)S(1)} collective-permute-done((f32[64,128]{1,0:T(8,128)S(1)}, f32[64,128]{1,0:T(8,128)S(1)}, u32[]{:S(2)}, u32[]{:S(2)}) %collective-permute-start.10) | collective-permute-done | bytes 32800 | tf_op jit(solution)/shard_map/ppermute | solution.py:722
  39.7 1.0 %weights.1 = (bf16[208,128]{1,0:T(8,128)(2,1)S(1)}, f32[16,128]{1,0:T(8,128)S(1)}, f32[8,128]{1,0:T(8,128)S(1)}, f32[16,64]{1,0:T(8,128)S(1)}, s32[16,128]{1,0:T...) custom-call(s32[1]{0:T(128)} %bitcast.grp_s, ...), custom_call_target="tpu_custom_call" | custom-call | bytes 7200000 | tf_op jit(solution)/shard_map/weights/pallas_call | solution.py:707
  41.2 1.2 %collective-permute-start.12 = (bf16[768,128]{1,0:T(8,128)(2,1)S(1)}, bf16[768,128]{1,0:T(8,128)(2,1)S(1)}, u32[]{:S(2)}, u32[]{:S(2)}) collective-permute-start(bf16[768,128]{1,0:T(8,128)(2,1)S(1)} %slice.20), channel_id=1, source_target_pairs={{0,2},{1,3},{2,0},{3,1},{4,6},{5,7},{6,4},{7,5},{8,10},{9,11},{10,... | collective-permute-start | bytes 589832 | tf_op jit(solution)/shard_map/ppermute | solution.py:722
  43.0 2.7 %collective-permute-start.14 = (bf16[256,128]{1,0:T(8,128)(2,1)S(1)}, bf16[256,128]{1,0:T(8,128)(2,1)S(1)}, u32[]{:S(2)}, u32[]{:S(2)}) collective-permute-start(bf16[256,128]{1,0:T(8,128)(2,1)S(1)} %get-tuple-element.70), channel_id=1, source_target_pairs={{0,16},{4,20},{8,24},{12,28},{16,0},{20,4},{24,8},{28,12},{1,17},{... | collective-permute-start | bytes 196616 | tf_op jit(solution)/shard_map/ppermute | solution.py:722
  45.7 1.1 %collective-permute-start.15 = (bf16[256,128]{1,0:T(8,128)(2,1)S(1)}, bf16[256,128]{1,0:T(8,128)(2,1)S(1)}, u32[]{:S(2)}, u32[]{:S(2)}) collective-permute-start(bf16[256,128]{1,0:T(8,128)(2,1)S(1)} %get-tuple-element.71), channel_id=1, source_target_pairs={{0,24},{4,28},{8,16},{12,20},{16,8},{20,12},{24,0},{28,4},{1,25},{... | collective-permute-start | bytes 196616 | tf_op jit(solution)/shard_map/ppermute | solution.py:722
  46.8 1.9 %own_sum.1.refs_6_ = f32[53,2,2,8,128]{4,3,2,1,0:T(8,128)S(1)} custom-call(s32[1]{0:T(128)} %bitcast.grp_s, s32[1]{0:T(128)} %bitcast.1.owner_s, bf16[208,128]{1,0:T(8,128)(2,1)S(1)} %get-tuple-element.67.packed, s32[16,128]{1,0:T(8,128)S(1)} %get-tuple-element.73.ints, bf16[2080,128]{1,0:T(8,128)(2,1)S(1)} %get-tuple-element.49.refs_0_.refs_10_, ...), custom_call_target="tpu_custom_call" | custom-call | bytes 10800000 | tf_op jit(solution)/shard_map/own_sum/pallas_call | solution.py:707
  48.6 1.7 %near_sum.1 = (f32[53,2,2,8,128]{4,3,2,1,0:T(8,128)S(1)}, f32[16,128]{1,0:T(8,128)S(1)}, f32[8,128]{1,0:T(8,128)S(1)}) custom-call(s32[1]{0:T(128)} %bitcast.1.owner_s, bf16[1536,128]{1,0:T(8,128)(2,1)S(1)} %join.1.refs_0_, bf16[1536,128]{1,0:T(8,128)(2,1)S(1)} %collective-permute-done.7.refs_1_, bf16[1536,128]{1,0:T(8,128)(2,1)S(1)} %collective-permute-done.11.refs_2_, ...), custom_call_target="tpu_custom_call" | custom-call | bytes 7200000 | tf_op jit(solution)/shard_map/near_sum/pallas_call | solution.py:707
  50.4 1.4 %collective-permute-done.15.refs_6_ = bf16[256,128]{1,0:T(8,128)(2,1)S(1)} collective-permute-done((bf16[256,128]{1,0:T(8,128)(2,1)S(1)}, bf16[256,128]{1,0:T(8,128)(2,1)S(1)}, u32[]{:S(2)}, u32[]{:S(2)}) %collective-permute-start.15) | collective-permute-done | bytes 65568 | tf_op jit(solution)/shard_map/ppermute | solution.py:722
  51.7 3.5 %sum.1 = (f32[52,16,128]{2,1,0:T(8,128)S(1)}, bf16[53,16,128]{2,1,0:T(8,128)(2,1)S(1)}, f32[8,128]{1,0:T(8,128)S(1)}, f32[8,128]{1,0:T(8,128)S(1)}, f32[2,832,128]{2,1,0:T(8,128)}, /*index=5*/s32[2,16,128]{2,1,0:T(8,128)}) custom-call(s32[1]{0:T(128)} %bitcast.grp_s, s32[1]{0:T(128)} %bitcast.1.owner_s, bf16[1536,128]{1,0:T(8,128)(2,1)S(1)} %join.1.refs_0_, ...), custom_call_target="tpu_custom_call" | custom-call | bytes 10800000 | tf_op jit(solution)/shard_map/sum/pallas_call | solution.py:707
  55.3 1.5 %collective-permute-done.17.sib = bf16[53,16,128]{2,1,0:T(8,128)(2,1)S(1)} collective-permute-done((bf16[53,16,128]{2,1,0:T(8,128)(2,1)S(1)}, bf16[53,16,128]{2,1,0:T(8,128)(2,1)S(1)}, u32[]{:S(2)}, u32[]{:S(2)}) %collective-permute-start.17) | collective-permute-done | bytes 217120 | tf_op jit(solution)/shard_map/ppermute | solution.py:722
  56.7 0.7 divide.1
  57.9 1.5 %collective-permute-start.18 = (bf16[52,16,128]{2,1,0:T(8,128)(2,1)S(1)}, bf16[52,16,128]{2,1,0:T(8,128)(2,1)S(1)}, u32[]{:S(2)}, u32[]{:S(2)}) collective-permute-start(bf16[52,16,128]{2,1,0:T(8,128)(2,1)S(1)} %get-tuple-element.85.refs_0_), channel_id=1, source_target_pairs={{0,8},{4,12},{8,0},{12,4},{16,24},{20,28},{24,16},{28,20},{1,9},{5... | collective-permute-start | bytes 638984 | tf_op jit(solution)/shard_map/ppermute | solution.py:722
  59.4 9.7 %collective-permute-done.19.refs_4_ = bf16[52,16,128]{2,1,0:T(8,128)(2,1)S(1)} collective-permute-done((bf16[52,16,128]{2,1,0:T(8,128)(2,1)S(1)}, bf16[52,16,128]{2,1,0:T(8,128)(2,1)S(1)}, u32[]{:S(2)}, u32[]{:S(2)}) %collective-permute-start.19) | collective-permute-done | bytes 213024 | tf_op jit(solution)/shard_map/ppermute | solution.py:722
  71.3 2.0 %spread.2.refs_2_ = f32[52,16384]{1,0:T(8,128)} custom-call(s32[1]{0:T(128)} %bitcast.grp_s, bf16[52,16,128]{2,1,0:T(8,128)(2,1)S(1)} %get-tuple-element.85.refs_0_, bf16[52,16,128]{2,1,0:T(8,128)(2,1)S(1)} %collective-permute-done.21.refs_1_, bf16[52,16,128]{2,1,0:T(8,128)(2,1)S(1)} %collective-permute-done.18.refs_2_, ...), custom_call_target="tpu_custom_call" | custom-call | bytes 180000 | tf_op jit(solution)/shard_map/spread/pallas_call | solution.py:707
  73.3 3.9 %collective-permute-done.20.refs_0_ = bf16[52,16,128]{2,1,0:T(8,128)(2,1)S(1)} collective-permute-done((bf16[52,16,128]{2,1,0:T(8,128)(2,1)S(1)}, bf16[52,16,128]{2,1,0:T(8,128)(2,1)S(1)}, u32[]{:S(2)}, u32[]{:S(2)}) %collective-permute-start.20) | collective-permute-done | bytes 213024 | tf_op jit(solution)/shard_map/ppermute | solution.py:722
  77.7 0.9 %collective-permute-done.24.refs_1_ = bf16[52,16,128]{2,1,0:T(8,128)(2,1)S(1)} collective-permute-done((bf16[52,16,128]{2,1,0:T(8,128)(2,1)S(1)}, bf16[52,16,128]{2,1,0:T(8,128)(2,1)S(1)}, u32[]{:S(2)}, u32[]{:S(2)}) %collective-permute-start.24) | collective-permute-done | bytes 213024 | tf_op jit(solution)/shard_map/ppermute | solution.py:722
  78.7 1.2 %spread.3 = f32[52,16384]{1,0:T(8,128)} custom-call(s32[1]{0:T(128)} %bitcast.grp_s, bf16[52,16,128]{2,1,0:T(8,128)(2,1)S(1)} %collective-permute-done.20.refs_0_, bf16[52,16,128]{2,1,0:T(8,128)(2,1)S(1)} %collective-permute-done.24.refs_1_, f32[52,16384]{1,0:T(8,128)} %spread.2.refs_2_), custom_call_target="tpu_custom_call", output_to_operand_aliasing={{}: (3, {})} | custom-call | bytes 180000 | tf_op jit(solution)/shard_map/spread/pallas_call | solution.py:707
  (39 shorter events, 6.5 us)
Async XLA Ops:
  2.7 15.1 %collective-permute-start.3 = (bf16[2080,128]{1,0:T(8,128)(2,1)S(1)}, bf16[2080,128]{1,0:T(8,128)(2,1)S(1)}, u32[]{:S(2)}, u32[]{:S(2)}) collective-permute-start(bf16[2080,128]{1,0:T(8,128)(2,1)S(1)} %get-tuple-element.49.refs_0_.refs_10_), channel_id=1, source_target_pairs={{0,2},{1,3},{2,0},{3,1},{4,6},{5,7},{6,4},{7,5},{8,10},{9,11},{10,... | collective-permute-start | bytes 1597448 | tf_op jit(solution)/shard_map/ppermute | solution.py:722
  5.7 13.9 %collective-permute-start.1 = (bf16[2080,128]{1,0:T(8,128)(2,1)S(1)}, bf16[2080,128]{1,0:T(8,128)(2,1)S(1)}, u32[]{:S(2)}, u32[]{:S(2)}) collective-permute-start(bf16[2080,128]{1,0:T(8,128)(2,1)S(1)} %get-tuple-element.49.refs_0_.refs_10_), channel_id=1, source_target_pairs={{0,1},{1,0},{2,3},{3,2},{4,5},{5,4},{6,7},{7,6},{8,9},{9,8},{10,11... | collective-permute-start | bytes 1597448 | tf_op jit(solution)/shard_map/ppermute | solution.py:722
  7.2 8.6 %collective-permute-start = (bf16[512,128]{1,0:T(8,128)(2,1)S(1)}, bf16[512,128]{1,0:T(8,128)(2,1)S(1)}, u32[]{:S(2)}, u32[]{:S(2)}) collective-permute-start(bf16[512,128]{1,0:T(8,128)(2,1)S(1)} %get-tuple-element.47), channel_id=1, source_target_pairs={{0,8},{4,12},{8,0},{12,4},{16,24},{20,28},{24,16},{28,20},{1,9},{5... | collective-permute-start | bytes 393224 | tf_op jit(solution)/shard_map/ppermute | solution.py:722
  8.8 8.8 %collective-permute-start.2 = (bf16[512,128]{1,0:T(8,128)(2,1)S(1)}, bf16[512,128]{1,0:T(8,128)(2,1)S(1)}, u32[]{:S(2)}, u32[]{:S(2)}) collective-permute-start(bf16[512,128]{1,0:T(8,128)(2,1)S(1)} %get-tuple-element.54), channel_id=1, source_target_pairs={{0,16},{4,20},{8,24},{12,28},{16,0},{20,4},{24,8},{28,12},{1,17},{... | collective-permute-start | bytes 393224 | tf_op jit(solution)/shard_map/ppermute | solution.py:722
  11.4 0.7 copy-start
  17.8 10.3 %collective-permute-start.5 = (bf16[1056,128]{1,0:T(8,128)(2,1)S(1)}, bf16[1056,128]{1,0:T(8,128)(2,1)S(1)}, u32[]{:S(2)}, u32[]{:S(2)}) collective-permute-start(bf16[1056,128]{1,0:T(8,128)(2,1)S(1)} %slice.19), channel_id=1, source_target_pairs={{0,1},{1,0},{2,3},{3,2},{4,5},{5,4},{6,7},{7,6},{8,9},{9,8},{10,11... | collective-permute-start | bytes 811016 | tf_op jit(solution)/shard_map/ppermute | solution.py:722
  19.6 8.5 %collective-permute-start.4 = (bf16[1024,128]{1,0:T(8,128)(2,1)S(1)}, bf16[1024,128]{1,0:T(8,128)(2,1)S(1)}, u32[]{:S(2)}, u32[]{:S(2)}) collective-permute-start(bf16[1024,128]{1,0:T(8,128)(2,1)S(1)} %slice.18), channel_id=1, source_target_pairs={{0,2},{1,3},{2,0},{3,1},{4,6},{5,7},{6,4},{7,5},{8,10},{9,11},{10,... | collective-permute-start | bytes 786440 | tf_op jit(solution)/shard_map/ppermute | solution.py:722
  21.2 6.9 %collective-permute-start.6 = (bf16[512,128]{1,0:T(8,128)(2,1)S(1)}, bf16[512,128]{1,0:T(8,128)(2,1)S(1)}, u32[]{:S(2)}, u32[]{:S(2)}) collective-permute-start(bf16[512,128]{1,0:T(8,128)(2,1)S(1)} %get-tuple-element.59), channel_id=1, source_target_pairs={{0,24},{4,28},{8,16},{12,20},{16,8},{20,12},{24,0},{28,4},{1,25},{... | collective-permute-start | bytes 393224 | tf_op jit(solution)/shard_map/ppermute | solution.py:722
  28.1 12.5 %collective-permute-start.11 = (bf16[1536,128]{1,0:T(8,128)(2,1)S(1)}, bf16[1536,128]{1,0:T(8,128)(2,1)S(1)}, u32[]{:S(2)}, u32[]{:S(2)}) collective-permute-start(bf16[1536,128]{1,0:T(8,128)(2,1)S(1)} %join.1.refs_0_), channel_id=1, source_target_pairs={{0,2},{1,3},{2,0},{3,1},{4,6},{5,7},{6,4},{7,5},{8,10},{9,11},{10,... | collective-permute-start | bytes 1179656 | tf_op jit(solution)/shard_map/ppermute | solution.py:722
  28.8 12.4 %collective-permute-start.7 = (bf16[1536,128]{1,0:T(8,128)(2,1)S(1)}, bf16[1536,128]{1,0:T(8,128)(2,1)S(1)}, u32[]{:S(2)}, u32[]{:S(2)}) collective-permute-start(bf16[1536,128]{1,0:T(8,128)(2,1)S(1)} %join.1.refs_0_), channel_id=1, source_target_pairs={{0,1},{1,0},{2,3},{3,2},{4,5},{5,4},{6,7},{7,6},{8,9},{9,8},{10,11... | collective-permute-start | bytes 1179656 | tf_op jit(solution)/shard_map/ppermute | solution.py:722
  31.9 7.8 %collective-permute-start.10 = (f32[64,128]{1,0:T(8,128)S(1)}, f32[64,128]{1,0:T(8,128)S(1)}, u32[]{:S(2)}, u32[]{:S(2)}) collective-permute-start(f32[64,128]{1,0:T(8,128)S(1)} %get-tuple-element.60.refs_0_), channel_id=1, source_target_pairs={{0,3},{1,2},{2,1},{3,0},{4,7},{5,6},{6,5},{7,4},{8,11},{9,10},{10,... | collective-permute-start | bytes 98312 | tf_op jit(solution)/shard_map/ppermute | solution.py:722
  33.6 6.1 %collective-permute-start.9 = (f32[64,128]{1,0:T(8,128)S(1)}, f32[64,128]{1,0:T(8,128)S(1)}, u32[]{:S(2)}, u32[]{:S(2)}) collective-permute-start(f32[64,128]{1,0:T(8,128)S(1)} %get-tuple-element.60.refs_0_), channel_id=1, source_target_pairs={{0,2},{1,3},{2,0},{3,1},{4,6},{5,7},{6,4},{7,5},{8,10},{9,11},{10,... | collective-permute-start | bytes 98312 | tf_op jit(solution)/shard_map/ppermute | solution.py:722
  34.2 5.5 %collective-permute-start.8 = (f32[64,128]{1,0:T(8,128)S(1)}, f32[64,128]{1,0:T(8,128)S(1)}, u32[]{:S(2)}, u32[]{:S(2)}) collective-permute-start(f32[64,128]{1,0:T(8,128)S(1)} %get-tuple-element.60.refs_0_), channel_id=1, source_target_pairs={{0,1},{1,0},{2,3},{3,2},{4,5},{5,4},{6,7},{7,6},{8,9},{9,8},{10,11... | collective-permute-start | bytes 98312 | tf_op jit(solution)/shard_map/ppermute | solution.py:722
  40.7 7.9 %collective-permute-start.13 = (bf16[768,128]{1,0:T(8,128)(2,1)S(1)}, bf16[768,128]{1,0:T(8,128)(2,1)S(1)}, u32[]{:S(2)}, u32[]{:S(2)}) collective-permute-start(bf16[768,128]{1,0:T(8,128)(2,1)S(1)} %slice.21), channel_id=1, source_target_pairs={{0,1},{1,0},{2,3},{3,2},{4,5},{5,4},{6,7},{7,6},{8,9},{9,8},{10,11... | collective-permute-start | bytes 589832 | tf_op jit(solution)/shard_map/ppermute | solution.py:722
  41.2 7.5 %collective-permute-start.12 = (bf16[768,128]{1,0:T(8,128)(2,1)S(1)}, bf16[768,128]{1,0:T(8,128)(2,1)S(1)}, u32[]{:S(2)}, u32[]{:S(2)}) collective-permute-start(bf16[768,128]{1,0:T(8,128)(2,1)S(1)} %slice.20), channel_id=1, source_target_pairs={{0,2},{1,3},{2,0},{3,1},{4,6},{5,7},{6,4},{7,5},{8,10},{9,11},{10,... | collective-permute-start | bytes 589832 | tf_op jit(solution)/shard_map/ppermute | solution.py:722
  42.4 6.2 %collective-permute-start.16 = (bf16[256,128]{1,0:T(8,128)(2,1)S(1)}, bf16[256,128]{1,0:T(8,128)(2,1)S(1)}, u32[]{:S(2)}, u32[]{:S(2)}) collective-permute-start(bf16[256,128]{1,0:T(8,128)(2,1)S(1)} %get-tuple-element.72), channel_id=1, source_target_pairs={{0,8},{4,12},{8,0},{12,4},{16,24},{20,28},{24,16},{28,20},{1,9},{5... | collective-permute-start | bytes 196616 | tf_op jit(solution)/shard_map/ppermute | solution.py:722
  43.0 7.4 %collective-permute-start.14 = (bf16[256,128]{1,0:T(8,128)(2,1)S(1)}, bf16[256,128]{1,0:T(8,128)(2,1)S(1)}, u32[]{:S(2)}, u32[]{:S(2)}) collective-permute-start(bf16[256,128]{1,0:T(8,128)(2,1)S(1)} %get-tuple-element.70), channel_id=1, source_target_pairs={{0,16},{4,20},{8,24},{12,28},{16,0},{20,4},{24,8},{28,12},{1,17},{... | collective-permute-start | bytes 196616 | tf_op jit(solution)/shard_map/ppermute | solution.py:722
  45.7 6.1 %collective-permute-start.15 = (bf16[256,128]{1,0:T(8,128)(2,1)S(1)}, bf16[256,128]{1,0:T(8,128)(2,1)S(1)}, u32[]{:S(2)}, u32[]{:S(2)}) collective-permute-start(bf16[256,128]{1,0:T(8,128)(2,1)S(1)} %get-tuple-element.71), channel_id=1, source_target_pairs={{0,24},{4,28},{8,16},{12,20},{16,8},{20,12},{24,0},{28,4},{1,25},{... | collective-permute-start | bytes 196616 | tf_op jit(solution)/shard_map/ppermute | solution.py:722
  55.2 1.5 %collective-permute-start.17 = (bf16[53,16,128]{2,1,0:T(8,128)(2,1)S(1)}, bf16[53,16,128]{2,1,0:T(8,128)(2,1)S(1)}, u32[]{:S(2)}, u32[]{:S(2)}) collective-permute-start(bf16[53,16,128]{2,1,0:T(8,128)(2,1)S(1)} %get-tuple-element.81), channel_id=1, source_target_pairs={{0,4},{4,0},{8,12},{12,8},{16,20},{20,16},{24,28},{28,24},{1,5},{5... | collective-permute-start | bytes 651272 | tf_op jit(solution)/shard_map/ppermute | solution.py:722
  57.4 11.6 %collective-permute-start.19 = (bf16[52,16,128]{2,1,0:T(8,128)(2,1)S(1)}, bf16[52,16,128]{2,1,0:T(8,128)(2,1)S(1)}, u32[]{:S(2)}, u32[]{:S(2)}) collective-permute-start(bf16[52,16,128]{2,1,0:T(8,128)(2,1)S(1)} %get-tuple-element.85.refs_0_), channel_id=1, source_target_pairs={{0,16},{4,20},{8,24},{12,28},{16,0},{20,4},{24,8},{28,12},{1,17},{... | collective-permute-start | bytes 638984 | tf_op jit(solution)/shard_map/ppermute | solution.py:722
  57.9 11.6 %collective-permute-start.18 = (bf16[52,16,128]{2,1,0:T(8,128)(2,1)S(1)}, bf16[52,16,128]{2,1,0:T(8,128)(2,1)S(1)}, u32[]{:S(2)}, u32[]{:S(2)}) collective-permute-start(bf16[52,16,128]{2,1,0:T(8,128)(2,1)S(1)} %get-tuple-element.85.refs_0_), channel_id=1, source_target_pairs={{0,8},{4,12},{8,0},{12,4},{16,24},{20,28},{24,16},{28,20},{1,9},{5... | collective-permute-start | bytes 638984 | tf_op jit(solution)/shard_map/ppermute | solution.py:722
  59.4 11.6 %collective-permute-start.21 = (bf16[52,16,128]{2,1,0:T(8,128)(2,1)S(1)}, bf16[52,16,128]{2,1,0:T(8,128)(2,1)S(1)}, u32[]{:S(2)}, u32[]{:S(2)}) collective-permute-start(bf16[52,16,128]{2,1,0:T(8,128)(2,1)S(1)} %get-tuple-element.85.refs_0_), channel_id=1, source_target_pairs={{0,4},{4,0},{8,12},{12,8},{16,20},{20,16},{24,28},{28,24},{1,5},{5... | collective-permute-start | bytes 638984 | tf_op jit(solution)/shard_map/ppermute | solution.py:722
  69.5 1.5 %collective-permute-start.22 = (bf16[52,16,128]{2,1,0:T(8,128)(2,1)S(1)}, bf16[52,16,128]{2,1,0:T(8,128)(2,1)S(1)}, u32[]{:S(2)}, u32[]{:S(2)}) collective-permute-start(bf16[52,16,128]{2,1,0:T(8,128)(2,1)S(1)} %collective-permute-done.18.refs_2_), channel_id=1, source_target_pairs={{0,4},{4,0},{8,12},{12,8},{16,20},{20,16},{24,28},{28,24},{1,5},{5... | collective-permute-start | bytes 638984 | tf_op jit(solution)/shard_map/ppermute | solution.py:722
  69.5 1.8 %collective-permute-start.23 = (bf16[52,16,128]{2,1,0:T(8,128)(2,1)S(1)}, bf16[52,16,128]{2,1,0:T(8,128)(2,1)S(1)}, u32[]{:S(2)}, u32[]{:S(2)}) collective-permute-start(bf16[52,16,128]{2,1,0:T(8,128)(2,1)S(1)} %collective-permute-done.19.refs_4_), channel_id=1, source_target_pairs={{0,4},{4,0},{8,12},{12,8},{16,20},{20,16},{24,28},{28,24},{1,5},{5... | collective-permute-start | bytes 638984 | tf_op jit(solution)/shard_map/ppermute | solution.py:722
  70.0 7.2 %collective-permute-start.20 = (bf16[52,16,128]{2,1,0:T(8,128)(2,1)S(1)}, bf16[52,16,128]{2,1,0:T(8,128)(2,1)S(1)}, u32[]{:S(2)}, u32[]{:S(2)}) collective-permute-start(bf16[52,16,128]{2,1,0:T(8,128)(2,1)S(1)} %collective-permute-done.19.refs_4_), channel_id=1, source_target_pairs={{0,8},{4,12},{8,0},{12,4},{16,24},{20,28},{24,16},{28,20},{1,9},{5... | collective-permute-start | bytes 638984 | tf_op jit(solution)/shard_map/ppermute | solution.py:722
  77.2 1.5 %collective-permute-start.24 = (bf16[52,16,128]{2,1,0:T(8,128)(2,1)S(1)}, bf16[52,16,128]{2,1,0:T(8,128)(2,1)S(1)}, u32[]{:S(2)}, u32[]{:S(2)}) collective-permute-start(bf16[52,16,128]{2,1,0:T(8,128)(2,1)S(1)} %collective-permute-done.20.refs_0_), channel_id=1, source_target_pairs={{0,4},{4,0},{8,12},{12,8},{16,20},{20,16},{24,28},{28,24},{1,5},{5... | collective-permute-start | bytes 638984 | tf_op jit(solution)/shard_map/ppermute | solution.py:722

commit v10 on v9

--- a/solution.py
+++ b/solution.py
@@ -653,17 +653,19 @@
     divide(own, sib, inverse[...], start, avg_out)
 
 
-def spread_kernel(planes, chunks, has_out, grp_s, *refs):
-    held = 2 * len(planes) * len(chunks)
-    arrays, (out, wide, columns, sem) = refs[:held], refs[held + has_out :]
-    width = arrays[0].shape[1] // 2
+def spread_kernel(planes, counts, has_out, grp_s, *refs):
+    taken, (out, wide, columns, sem) = refs[: 2 * sum(counts)], refs[2 * sum(counts) + has_out :]
+    arrays, _ = take(taken, [2 * count for count in counts])
+    width = taken[0].shape[1] // 2
     cls_dev = columns.shape[1]
     pad = wide.shape[0] // (len(planes) * 4 * width + 1)
     z, h = grp_s[0] // 2, grp_s[0] % 2
     copies = []
     for n, d in enumerate(planes):
-        for c, (start, cut) in enumerate(chunks):
-            pair = arrays[2 * (n * len(chunks) + c) :][:2]
+        start = 0
+        for c in range(counts[n]):
+            pair = arrays[n][2 * c : 2 * c + 2]
+            cut = pair[0].shape[0]
 
             def one(k, _):
                 for side, array in enumerate(pair):
@@ -676,6 +678,7 @@
                 return 0
 
             lax.fori_loop(0, cut, one, 0, unroll=2)
+            start += cut
         for side, core in enumerate((h, 1 - h)):
             for x in range(2):
                 group = n * 4 + side * 2 + x
@@ -961,28 +964,28 @@
             )
         divided.append(averaged)
 
+    (averaged,) = divided
     if nz == 4:
-        near = [swap(averaged, "grp", 2) for averaged in divided]
-        across = [swap(averaged, "grp", 4) for averaged in divided]
-        near, across = lax.optimization_barrier((near, across))
-        relayed = [swap(one, "grp", 2) for one in across]
-        planes = [list(held) for held in zip(divided, near, across, relayed)]
+        near, across = lax.optimization_barrier(
+            (swap(averaged, "grp", 2), swap(averaged, "grp", 4))
+        )
+        cut = cls_dev - cls_dev // 13 * 4
+        relayed = [swap(part, "grp", 2) for part in (across[:cut], across[cut:])]
+        planes = [[averaged], [near], [across], relayed]
     else:
-        planes = [
-            [averaged] + [swap(averaged, "grp", 2 * d) for d in range(1, nz)]
-            for averaged in divided
-        ]
+        planes = [[averaged]] + [[swap(averaged, "grp", 2 * d)] for d in range(1, nz)]
     averages = None
     for far in ((0, 1, 2), (3,)) if nz == 4 else (tuple(range(nz)),):
         arrays = []
         for d in far:
-            for held in planes:
-                one = held[d] if averages is None else after(held[d], averages)
+            for one in planes[d]:
+                one = one if averages is None else after(one, averages)
                 arrays += [one, swap(one, "grp", 1)]
+        counts = tuple(len(planes[d]) for d in far)
         has_out = averages is not None
         groups = len(far) * 4
         (averages,) = call(
-            functools.partial(spread_kernel, far, chunks, has_out), "spread",
+            functools.partial(spread_kernel, far, counts, has_out), "spread",
             [SMEM] + [VMEM] * len(arrays) + [HBM] * has_out,
             [(SHAPE((cls_dev, FEAT), F32), HBM)],
             [

time: 79.9 us -> 80.1 us (level)
  waiting for transfers between devices: 22.5 us -> 20.2 us
  starting transfers between devices: 30 us -> 32.2 us
    ppermute x25 -> x27, waiting for transfers between devices: 22.5 us -> 20.2 us  [swap(): return lax.ppermute(value, axis, [(i, i ^ distance) for i in range(size)])]
    ppermute x25 -> x27, starting transfers between devices: 30 us -> 32.2 us  [swap(): return lax.ppermute(value, axis, [(i, i ^ distance) for i in range(size)])]
  transfers between devices with their start and end apart: 25 -> 27, of which waited for: 9 -> 9; matrix products, arithmetic and copies ran while one was open for 2% -> 2% of each run, Pallas kernels for 22% -> 22%
where the time goes in v10:
time: 80.1 us; the launch traced here: 79.9 us
  starting transfers between devices  32.2 us (40%)
  Pallas kernels  24.7 us (31%)
  waiting for transfers between devices  20.2 us (25%)
  local copies, waits for them, and re-layouts  1.87 us (2%)
  between operations  0.86 us (1%)
    ppermute x27, starting transfers between devices, swap(): return lax.ppermute(value, axis, [(i, i ^ distance) for i in range(size)])  32.2 us
    pallas_call x13, Pallas kernels, call(): pl.pallas_call(kernel, out_shape=tuple((s for s, _ in outs)), in_specs=[w...  24.7 us
    ppermute x27, waiting for transfers between devices, swap(): return lax.ppermute(value, axis, [(i, i ^ distance) for i in range(size)])  20.2 us
  transfers between devices with their start and end apart: 27, of which 9 were waited for; matrix products, arithmetic and copies ran while one was open for 2% of the time, Pallas kernels for 22%

profile of v10, /device:TPU:0, one launch (start us, length us, event | category | flops | bytes accessed | tf_op | source)
XLA Modules:
  0.0 79.9 jit_solution(2315528654724310375)
XLA Ops:
  0.6 2.0 %weigh.1 = (bf16[2080,128]{1,0:T(8,128)(2,1)S(1)}, bf16[512,128]{1,0:T(8,128)(2,1)S(1)}, bf16[512,128]{1,0:T(8,128)(2,1)S(1)}, bf16[512,128]{1,0:T(8,128)(2,1)S(1)}) custom-call(s32[1]{0:T(128)} %bitcast.grp_s, bf16[16,16384]{1,0:T(8,128)(2,1)} %particles_h.1, s32[8,16]{1,0:T(8,128)} %bitcast.7, s32[16]{0:T(128)} %groups_h.1, s32[16]{0:T(128)} %entries_h.1, ...), custom_call_target="tpu_custom_call" | custom-call | bytes 7200000 | tf_op jit(solution)/shard_map/weigh/pallas_call | solution.py:710
  2.7 3.0 %collective-permute-start.3 = (bf16[2080,128]{1,0:T(8,128)(2,1)S(1)}, bf16[2080,128]{1,0:T(8,128)(2,1)S(1)}, u32[]{:S(2)}, u32[]{:S(2)}) collective-permute-start(bf16[2080,128]{1,0:T(8,128)(2,1)S(1)} %get-tuple-element.50.refs_0_.refs_10_), channel_id=1, source_target_pairs={{0,2},{1,3},{2,0},{3,1},{4,6},{5,7},{6,4},{7,5},{8,10},{9,11},{10,... | collective-permute-start | bytes 1597448 | tf_op jit(solution)/shard_map/ppermute | solution.py:725
  5.7 1.5 %collective-permute-start.1 = (bf16[2080,128]{1,0:T(8,128)(2,1)S(1)}, bf16[2080,128]{1,0:T(8,128)(2,1)S(1)}, u32[]{:S(2)}, u32[]{:S(2)}) collective-permute-start(bf16[2080,128]{1,0:T(8,128)(2,1)S(1)} %get-tuple-element.50.refs_0_.refs_10_), channel_id=1, source_target_pairs={{0,1},{1,0},{2,3},{3,2},{4,5},{5,4},{6,7},{7,6},{8,9},{9,8},{10,11... | collective-permute-start | bytes 1597448 | tf_op jit(solution)/shard_map/ppermute | solution.py:725
  7.2 1.6 %collective-permute-start = (bf16[512,128]{1,0:T(8,128)(2,1)S(1)}, bf16[512,128]{1,0:T(8,128)(2,1)S(1)}, u32[]{:S(2)}, u32[]{:S(2)}) collective-permute-start(bf16[512,128]{1,0:T(8,128)(2,1)S(1)} %get-tuple-element.48), channel_id=1, source_target_pairs={{0,8},{4,12},{8,0},{12,4},{16,24},{20,28},{24,16},{28,20},{1,9},{5... | collective-permute-start | bytes 393224 | tf_op jit(solution)/shard_map/ppermute | solution.py:725
  8.8 2.6 %collective-permute-start.2 = (bf16[512,128]{1,0:T(8,128)(2,1)S(1)}, bf16[512,128]{1,0:T(8,128)(2,1)S(1)}, u32[]{:S(2)}, u32[]{:S(2)}) collective-permute-start(bf16[512,128]{1,0:T(8,128)(2,1)S(1)} %get-tuple-element.55), channel_id=1, source_target_pairs={{0,16},{4,20},{8,24},{12,28},{16,0},{20,4},{24,8},{28,12},{1,17},{... | collective-permute-start | bytes 393224 | tf_op jit(solution)/shard_map/ppermute | solution.py:725
  12.0 3.8 %prep.1 = (f32[53,128,128]{2,1,0:T(8,128)S(1)}, f32[53,128]{1,0:T(8,128)S(1)}, f32[384,64]{1,0:T(8,128)S(1)}, bf16[256,512]{1,0:T(8,128)(2,1)S(1)}, f32[8,128]{1,0:T(8,128)S(1)}) custom-call(s32[1]{0:T(128)} %bitcast.grp_s, bf16[52,16384]{1,0:T(8,128)(2,1)} %refs_h.1, f32[384,64]{1,0:T(8,128)} %constant.15.clone.rest_refs_0_, ...), custom_call_target="tpu_custom_call" | custom-call | bytes 14400000 | tf_op jit(solution)/shard_map/prep/pallas_call | solution.py:710
  15.8 1.8 %score.3 = (f32[128,64]{1,0:T(8,128)S(1)}, f32[16,128]{1,0:T(8,128)S(1)}, f32[128,128]{1,0:T(8,128)S(1)}) custom-call(s32[1]{0:T(128)S(6)} %mul.3.first_s, s32[1]{0:T(128)} %bitcast.1.owner_s, bf16[2080,128]{1,0:T(8,128)(2,1)S(1)} %get-tuple-element.50.refs_0_.refs_10_, f32[53,128,128]{2,1,0:T(8,128)S(1)} %get-tuple-element.51.refs_1_.refs_2_.refs_4_, ...), custom_call_target="tpu_custom_call" | custom-call | bytes 10800000 | tf_op jit(solution)/shard_map/score/pallas_call | solution.py:710
  17.8 1.8 %collective-permute-start.5 = (bf16[1056,128]{1,0:T(8,128)(2,1)S(1)}, bf16[1056,128]{1,0:T(8,128)(2,1)S(1)}, u32[]{:S(2)}, u32[]{:S(2)}) collective-permute-start(bf16[1056,128]{1,0:T(8,128)(2,1)S(1)} %slice.25), channel_id=1, source_target_pairs={{0,1},{1,0},{2,3},{3,2},{4,5},{5,4},{6,7},{7,6},{8,9},{9,8},{10,11... | collective-permute-start | bytes 811016 | tf_op jit(solution)/shard_map/ppermute | solution.py:725
  19.6 1.6 %collective-permute-start.4 = (bf16[1024,128]{1,0:T(8,128)(2,1)S(1)}, bf16[1024,128]{1,0:T(8,128)(2,1)S(1)}, u32[]{:S(2)}, u32[]{:S(2)}) collective-permute-start(bf16[1024,128]{1,0:T(8,128)(2,1)S(1)} %slice.24), channel_id=1, source_target_pairs={{0,2},{1,3},{2,0},{3,1},{4,6},{5,7},{6,4},{7,5},{8,10},{9,11},{10,... | collective-permute-start | bytes 786440 | tf_op jit(solution)/shard_map/ppermute | solution.py:725
  21.2 3.6 %collective-permute-start.6 = (bf16[512,128]{1,0:T(8,128)(2,1)S(1)}, bf16[512,128]{1,0:T(8,128)(2,1)S(1)}, u32[]{:S(2)}, u32[]{:S(2)}) collective-permute-start(bf16[512,128]{1,0:T(8,128)(2,1)S(1)} %get-tuple-element.60), channel_id=1, source_target_pairs={{0,24},{4,28},{8,16},{12,20},{16,8},{20,12},{24,0},{28,4},{1,25},{... | collective-permute-start | bytes 393224 | tf_op jit(solution)/shard_map/ppermute | solution.py:725
  24.8 3.3 %score.4 = (f32[256,64]{1,0:T(8,128)S(1)}, f32[32,128]{1,0:T(8,128)S(1)}, f32[256,128]{1,0:T(8,128)S(1)}) custom-call(s32[1]{0:T(128)S(6)} %mul.3.first_s, s32[1]{0:T(128)} %bitcast.1.owner_s, bf16[2080,128]{1,0:T(8,128)(2,1)S(1)} %collective-permute-done.1.refs_0_.refs_11_.refs_1_, bf16[2080,128]{1,0:T(8,128)(2,1)S(1)} %collective-permute-done.3.refs_1_.refs_12_.refs_2_, ...), custom_call_target="tpu_custom_call" | custom-call | bytes 21600000 | tf_op jit(solution)/shard_map/score/pallas_call | solution.py:710
  28.8 1.0 %collective-permute-start.7 = (bf16[1536,128]{1,0:T(8,128)(2,1)S(1)}, bf16[1536,128]{1,0:T(8,128)(2,1)S(1)}, u32[]{:S(2)}, u32[]{:S(2)}) collective-permute-start(bf16[1536,128]{1,0:T(8,128)(2,1)S(1)} %join.1.refs_0_), channel_id=1, source_target_pairs={{0,1},{1,0},{2,3},{3,2},{4,5},{5,4},{6,7},{7,6},{8,9},{9,8},{10,11... | collective-permute-start | bytes 1179656 | tf_op jit(solution)/shard_map/ppermute | solution.py:725
  29.9 1.8 %score.5 = (f32[128,64]{1,0:T(8,128)S(1)}, f32[64,128]{1,0:T(8,128)S(1)}, f32[128,128]{1,0:T(8,128)S(1)}) custom-call(s32[1]{0:T(128)S(6)} %mul.3.first_s, s32[1]{0:T(128)} %bitcast.1.owner_s, bf16[1024,128]{1,0:T(8,128)(2,1)S(1)} %collective-permute-done.4.refs_0_.refs_3_, bf16[1056,128]{1,0:T(8,128)(2,1)S(1)} %collective-permute-done.5.refs_1_.refs_13_.refs_4_, ...), custom_call_target="tpu_custom_call" | custom-call | bytes 10800000 | tf_op jit(solution)/shard_map/score/pallas_call | solution.py:710
  31.7 2.0 %collective-permute-start.10 = (f32[64,128]{1,0:T(8,128)S(1)}, f32[64,128]{1,0:T(8,128)S(1)}, u32[]{:S(2)}, u32[]{:S(2)}) collective-permute-start(f32[64,128]{1,0:T(8,128)S(1)} %get-tuple-element.61.refs_0_), channel_id=1, source_target_pairs={{0,3},{1,2},{2,1},{3,0},{4,7},{5,6},{6,5},{7,4},{8,11},{9,10},{10,... | collective-permute-start | bytes 98312 | tf_op jit(solution)/shard_map/ppermute | solution.py:725
  34.3 1.0 %collective-permute-start.8 = (f32[64,128]{1,0:T(8,128)S(1)}, f32[64,128]{1,0:T(8,128)S(1)}, u32[]{:S(2)}, u32[]{:S(2)}) collective-permute-start(f32[64,128]{1,0:T(8,128)S(1)} %get-tuple-element.61.refs_0_), channel_id=1, source_target_pairs={{0,1},{1,0},{2,3},{3,2},{4,5},{5,4},{6,7},{7,6},{8,9},{9,8},{10,11... | collective-permute-start | bytes 98312 | tf_op jit(solution)/shard_map/ppermute | solution.py:725
  35.3 4.4 %collective-permute-done.10.refs_3_ = f32[64,128]{1,0:T(8,128)S(1)} collective-permute-done((f32[64,128]{1,0:T(8,128)S(1)}, f32[64,128]{1,0:T(8,128)S(1)}, u32[]{:S(2)}, u32[]{:S(2)}) %collective-permute-start.10) | collective-permute-done | bytes 32800 | tf_op jit(solution)/shard_map/ppermute | solution.py:725
  39.7 1.0 %weights.1 = (bf16[208,128]{1,0:T(8,128)(2,1)S(1)}, f32[16,128]{1,0:T(8,128)S(1)}, f32[8,128]{1,0:T(8,128)S(1)}, f32[16,64]{1,0:T(8,128)S(1)}, s32[16,128]{1,0:T...) custom-call(s32[1]{0:T(128)} %bitcast.grp_s, ...), custom_call_target="tpu_custom_call" | custom-call | bytes 7200000 | tf_op jit(solution)/shard_map/weights/pallas_call | solution.py:710
  41.3 1.1 %collective-permute-start.12 = (bf16[768,128]{1,0:T(8,128)(2,1)S(1)}, bf16[768,128]{1,0:T(8,128)(2,1)S(1)}, u32[]{:S(2)}, u32[]{:S(2)}) collective-permute-start(bf16[768,128]{1,0:T(8,128)(2,1)S(1)} %slice.26), channel_id=1, source_target_pairs={{0,2},{1,3},{2,0},{3,1},{4,6},{5,7},{6,4},{7,5},{8,10},{9,11},{10,... | collective-permute-start | bytes 589832 | tf_op jit(solution)/shard_map/ppermute | solution.py:725
  43.0 2.7 %collective-permute-start.14 = (bf16[256,128]{1,0:T(8,128)(2,1)S(1)}, bf16[256,128]{1,0:T(8,128)(2,1)S(1)}, u32[]{:S(2)}, u32[]{:S(2)}) collective-permute-start(bf16[256,128]{1,0:T(8,128)(2,1)S(1)} %get-tuple-element.71), channel_id=1, source_target_pairs={{0,16},{4,20},{8,24},{12,28},{16,0},{20,4},{24,8},{28,12},{1,17},{... | collective-permute-start | bytes 196616 | tf_op jit(solution)/shard_map/ppermute | solution.py:725
  45.7 1.2 %collective-permute-start.15 = (bf16[256,128]{1,0:T(8,128)(2,1)S(1)}, bf16[256,128]{1,0:T(8,128)(2,1)S(1)}, u32[]{:S(2)}, u32[]{:S(2)}) collective-permute-start(bf16[256,128]{1,0:T(8,128)(2,1)S(1)} %get-tuple-element.72), channel_id=1, source_target_pairs={{0,24},{4,28},{8,16},{12,20},{16,8},{20,12},{24,0},{28,4},{1,25},{... | collective-permute-start | bytes 196616 | tf_op jit(solution)/shard_map/ppermute | solution.py:725
  46.9 1.9 %own_sum.1.refs_6_ = f32[53,2,2,8,128]{4,3,2,1,0:T(8,128)S(1)} custom-call(s32[1]{0:T(128)} %bitcast.grp_s, s32[1]{0:T(128)} %bitcast.1.owner_s, bf16[208,128]{1,0:T(8,128)(2,1)S(1)} %get-tuple-element.68.packed, s32[16,128]{1,0:T(8,128)S(1)} %get-tuple-element.74.ints, bf16[2080,128]{1,0:T(8,128)(2,1)S(1)} %get-tuple-element.50.refs_0_.refs_10_, ...), custom_call_target="tpu_custom_call" | custom-call | bytes 10800000 | tf_op jit(solution)/shard_map/own_sum/pallas_call | solution.py:710
  48.8 1.7 %near_sum.1 = (f32[53,2,2,8,128]{4,3,2,1,0:T(8,128)S(1)}, f32[16,128]{1,0:T(8,128)S(1)}, f32[8,128]{1,0:T(8,128)S(1)}) custom-call(s32[1]{0:T(128)} %bitcast.1.owner_s, bf16[1536,128]{1,0:T(8,128)(2,1)S(1)} %join.1.refs_0_, bf16[1536,128]{1,0:T(8,128)(2,1)S(1)} %collective-permute-done.7.refs_1_, bf16[1536,128]{1,0:T(8,128)(2,1)S(1)} %collective-permute-done.11.refs_2_, ...), custom_call_target="tpu_custom_call" | custom-call | bytes 7200000 | tf_op jit(solution)/shard_map/near_sum/pallas_call | solution.py:710
  50.5 1.2 %collective-permute-done.15.refs_6_ = bf16[256,128]{1,0:T(8,128)(2,1)S(1)} collective-permute-done((bf16[256,128]{1,0:T(8,128)(2,1)S(1)}, bf16[256,128]{1,0:T(8,128)(2,1)S(1)}, u32[]{:S(2)}, u32[]{:S(2)}) %collective-permute-start.15) | collective-permute-done | bytes 65568 | tf_op jit(solution)/shard_map/ppermute | solution.py:725
  51.7 3.5 %sum.1 = (f32[52,16,128]{2,1,0:T(8,128)S(1)}, bf16[53,16,128]{2,1,0:T(8,128)(2,1)S(1)}, f32[8,128]{1,0:T(8,128)S(1)}, f32[8,128]{1,0:T(8,128)S(1)}, f32[2,832,128]{2,1,0:T(8,128)}, /*index=5*/s32[2,16,128]{2,1,0:T(8,128)}) custom-call(s32[1]{0:T(128)} %bitcast.grp_s, s32[1]{0:T(128)} %bitcast.1.owner_s, bf16[1536,128]{1,0:T(8,128)(2,1)S(1)} %join.1.refs_0_, ...), custom_call_target="tpu_custom_call" | custom-call | bytes 10800000 | tf_op jit(solution)/shard_map/sum/pallas_call | solution.py:710
  55.3 1.5 %collective-permute-done.17.sib = bf16[53,16,128]{2,1,0:T(8,128)(2,1)S(1)} collective-permute-done((bf16[53,16,128]{2,1,0:T(8,128)(2,1)S(1)}, bf16[53,16,128]{2,1,0:T(8,128)(2,1)S(1)}, u32[]{:S(2)}, u32[]{:S(2)}) %collective-permute-start.17) | collective-permute-done | bytes 217120 | tf_op jit(solution)/shard_map/ppermute | solution.py:725
  56.8 0.7 divide.1
  57.8 1.6 %collective-permute-start.18 = (bf16[52,16,128]{2,1,0:T(8,128)(2,1)S(1)}, bf16[52,16,128]{2,1,0:T(8,128)(2,1)S(1)}, u32[]{:S(2)}, u32[]{:S(2)}) collective-permute-start(bf16[52,16,128]{2,1,0:T(8,128)(2,1)S(1)} %get-tuple-element.86.refs_0_), channel_id=1, source_target_pairs={{0,8},{4,12},{8,0},{12,4},{16,24},{20,28},{24,16},{28,20},{1,9},{5... | collective-permute-start | bytes 638984 | tf_op jit(solution)/shard_map/ppermute | solution.py:725
  59.4 9.7 %collective-permute-done.19.refs_4_ = bf16[52,16,128]{2,1,0:T(8,128)(2,1)S(1)} collective-permute-done((bf16[52,16,128]{2,1,0:T(8,128)(2,1)S(1)}, bf16[52,16,128]{2,1,0:T(8,128)(2,1)S(1)}, u32[]{:S(2)}, u32[]{:S(2)}) %collective-permute-start.19) | collective-permute-done | bytes 213024 | tf_op jit(solution)/shard_map/ppermute | solution.py:725
  70.3 1.7 %collective-permute-start.25 = (bf16[16,16,128]{2,1,0:T(8,128)(2,1)S(1)}, bf16[16,16,128]{2,1,0:T(8,128)(2,1)S(1)}, u32[]{:S(2)}, u32[]{:S(2)}) collective-permute-start(bf16[16,16,128]{2,1,0:T(8,128)(2,1)S(1)} %slice.29), channel_id=1, source_target_pairs={{0,8},{4,12},{8,0},{12,4},{16,24},{20,28},{24,16},{28,20},{1,9},{5... | collective-permute-start | bytes 196616 | tf_op jit(solution)/shard_map/ppermute | solution.py:725
  72.6 2.0 %spread.2.refs_4_ = f32[52,16384]{1,0:T(8,128)} custom-call(s32[1]{0:T(128)} %bitcast.grp_s, bf16[52,16,128]{2,1,0:T(8,128)(2,1)S(1)} %get-tuple-element.86.refs_0_, bf16[52,16,128]{2,1,0:T(8,128)(2,1)S(1)} %collective-permute-done.21.refs_1_, bf16[52,16,128]{2,1,0:T(8,128)(2,1)S(1)} %collective-permute-done.18.refs_2_, ...), custom_call_target="tpu_custom_call" | custom-call | bytes 180000 | tf_op jit(solution)/shard_map/spread/pallas_call | solution.py:710
  74.7 2.5 %collective-permute-done.25.refs_2_ = bf16[16,16,128]{2,1,0:T(8,128)(2,1)S(1)} collective-permute-done((bf16[16,16,128]{2,1,0:T(8,128)(2,1)S(1)}, bf16[16,16,128]{2,1,0:T(8,128)(2,1)S(1)}, u32[]{:S(2)}, u32[]{:S(2)}) %collective-permute-start.25) | collective-permute-done | bytes 65568 | tf_op jit(solution)/shard_map/ppermute | solution.py:725
  78.7 1.2 %spread.3 = f32[52,16384]{1,0:T(8,128)} custom-call(s32[1]{0:T(128)} %bitcast.grp_s, bf16[36,16,128]{2,1,0:T(8,128)(2,1)S(1)} %collective-permute-done.20.refs_0_, bf16[36,16,128]{2,1,0:T(8,128)(2,1)S(1)} %collective-permute-done.24.refs_1_, bf16[16,16,128]{2,1,0:T(8,128)(2,1)S(1)} %collective-permute-done.25.refs_2_, ...), custom_call_target="tpu_custom_call", output_to_operand_aliasing={{}: (5, {})} | custom-call | bytes 180000 | tf_op jit(solution)/shard_map/spread/pallas_call | solution.py:710
  (45 shorter events, 7.2 us)
Async XLA Ops:
  2.7 15.1 %collective-permute-start.3 = (bf16[2080,128]{1,0:T(8,128)(2,1)S(1)}, bf16[2080,128]{1,0:T(8,128)(2,1)S(1)}, u32[]{:S(2)}, u32[]{:S(2)}) collective-permute-start(bf16[2080,128]{1,0:T(8,128)(2,1)S(1)} %get-tuple-element.50.refs_0_.refs_10_), channel_id=1, source_target_pairs={{0,2},{1,3},{2,0},{3,1},{4,6},{5,7},{6,4},{7,5},{8,10},{9,11},{10,... | collective-permute-start | bytes 1597448 | tf_op jit(solution)/shard_map/ppermute | solution.py:725
  5.7 13.9 %collective-permute-start.1 = (bf16[2080,128]{1,0:T(8,128)(2,1)S(1)}, bf16[2080,128]{1,0:T(8,128)(2,1)S(1)}, u32[]{:S(2)}, u32[]{:S(2)}) collective-permute-start(bf16[2080,128]{1,0:T(8,128)(2,1)S(1)} %get-tuple-element.50.refs_0_.refs_10_), channel_id=1, source_target_pairs={{0,1},{1,0},{2,3},{3,2},{4,5},{5,4},{6,7},{7,6},{8,9},{9,8},{10,11... | collective-permute-start | bytes 1597448 | tf_op jit(solution)/shard_map/ppermute | solution.py:725
  7.2 8.6 %collective-permute-start = (bf16[512,128]{1,0:T(8,128)(2,1)S(1)}, bf16[512,128]{1,0:T(8,128)(2,1)S(1)}, u32[]{:S(2)}, u32[]{:S(2)}) collective-permute-start(bf16[512,128]{1,0:T(8,128)(2,1)S(1)} %get-tuple-element.48), channel_id=1, source_target_pairs={{0,8},{4,12},{8,0},{12,4},{16,24},{20,28},{24,16},{28,20},{1,9},{5... | collective-permute-start | bytes 393224 | tf_op jit(solution)/shard_map/ppermute | solution.py:725
  8.8 8.8 %collective-permute-start.2 = (bf16[512,128]{1,0:T(8,128)(2,1)S(1)}, bf16[512,128]{1,0:T(8,128)(2,1)S(1)}, u32[]{:S(2)}, u32[]{:S(2)}) collective-permute-start(bf16[512,128]{1,0:T(8,128)(2,1)S(1)} %get-tuple-element.55), channel_id=1, source_target_pairs={{0,16},{4,20},{8,24},{12,28},{16,0},{20,4},{24,8},{28,12},{1,17},{... | collective-permute-start | bytes 393224 | tf_op jit(solution)/shard_map/ppermute | solution.py:725
  11.4 0.7 copy-start
  17.8 10.3 %collective-permute-start.5 = (bf16[1056,128]{1,0:T(8,128)(2,1)S(1)}, bf16[1056,128]{1,0:T(8,128)(2,1)S(1)}, u32[]{:S(2)}, u32[]{:S(2)}) collective-permute-start(bf16[1056,128]{1,0:T(8,128)(2,1)S(1)} %slice.25), channel_id=1, source_target_pairs={{0,1},{1,0},{2,3},{3,2},{4,5},{5,4},{6,7},{7,6},{8,9},{9,8},{10,11... | collective-permute-start | bytes 811016 | tf_op jit(solution)/shard_map/ppermute | solution.py:725
  19.6 8.5 %collective-permute-start.4 = (bf16[1024,128]{1,0:T(8,128)(2,1)S(1)}, bf16[1024,128]{1,0:T(8,128)(2,1)S(1)}, u32[]{:S(2)}, u32[]{:S(2)}) collective-permute-start(bf16[1024,128]{1,0:T(8,128)(2,1)S(1)} %slice.24), channel_id=1, source_target_pairs={{0,2},{1,3},{2,0},{3,1},{4,6},{5,7},{6,4},{7,5},{8,10},{9,11},{10,... | collective-permute-start | bytes 786440 | tf_op jit(solution)/shard_map/ppermute | solution.py:725
  21.2 7.0 %collective-permute-start.6 = (bf16[512,128]{1,0:T(8,128)(2,1)S(1)}, bf16[512,128]{1,0:T(8,128)(2,1)S(1)}, u32[]{:S(2)}, u32[]{:S(2)}) collective-permute-start(bf16[512,128]{1,0:T(8,128)(2,1)S(1)} %get-tuple-element.60), channel_id=1, source_target_pairs={{0,24},{4,28},{8,16},{12,20},{16,8},{20,12},{24,0},{28,4},{1,25},{... | collective-permute-start | bytes 393224 | tf_op jit(solution)/shard_map/ppermute | solution.py:725
  28.2 12.4 %collective-permute-start.11 = (bf16[1536,128]{1,0:T(8,128)(2,1)S(1)}, bf16[1536,128]{1,0:T(8,128)(2,1)S(1)}, u32[]{:S(2)}, u32[]{:S(2)}) collective-permute-start(bf16[1536,128]{1,0:T(8,128)(2,1)S(1)} %join.1.refs_0_), channel_id=1, source_target_pairs={{0,2},{1,3},{2,0},{3,1},{4,6},{5,7},{6,4},{7,5},{8,10},{9,11},{10,... | collective-permute-start | bytes 1179656 | tf_op jit(solution)/shard_map/ppermute | solution.py:725
  28.8 12.5 %collective-permute-start.7 = (bf16[1536,128]{1,0:T(8,128)(2,1)S(1)}, bf16[1536,128]{1,0:T(8,128)(2,1)S(1)}, u32[]{:S(2)}, u32[]{:S(2)}) collective-permute-start(bf16[1536,128]{1,0:T(8,128)(2,1)S(1)} %join.1.refs_0_), channel_id=1, source_target_pairs={{0,1},{1,0},{2,3},{3,2},{4,5},{5,4},{6,7},{7,6},{8,9},{9,8},{10,11... | collective-permute-start | bytes 1179656 | tf_op jit(solution)/shard_map/ppermute | solution.py:725
  31.7 7.9 %collective-permute-start.10 = (f32[64,128]{1,0:T(8,128)S(1)}, f32[64,128]{1,0:T(8,128)S(1)}, u32[]{:S(2)}, u32[]{:S(2)}) collective-permute-start(f32[64,128]{1,0:T(8,128)S(1)} %get-tuple-element.61.refs_0_), channel_id=1, source_target_pairs={{0,3},{1,2},{2,1},{3,0},{4,7},{5,6},{6,5},{7,4},{8,11},{9,10},{10,... | collective-permute-start | bytes 98312 | tf_op jit(solution)/shard_map/ppermute | solution.py:725
  33.7 6.0 %collective-permute-start.9 = (f32[64,128]{1,0:T(8,128)S(1)}, f32[64,128]{1,0:T(8,128)S(1)}, u32[]{:S(2)}, u32[]{:S(2)}) collective-permute-start(f32[64,128]{1,0:T(8,128)S(1)} %get-tuple-element.61.refs_0_), channel_id=1, source_target_pairs={{0,2},{1,3},{2,0},{3,1},{4,6},{5,7},{6,4},{7,5},{8,10},{9,11},{10,... | collective-permute-start | bytes 98312 | tf_op jit(solution)/shard_map/ppermute | solution.py:725
  34.3 5.4 %collective-permute-start.8 = (f32[64,128]{1,0:T(8,128)S(1)}, f32[64,128]{1,0:T(8,128)S(1)}, u32[]{:S(2)}, u32[]{:S(2)}) collective-permute-start(f32[64,128]{1,0:T(8,128)S(1)} %get-tuple-element.61.refs_0_), channel_id=1, source_target_pairs={{0,1},{1,0},{2,3},{3,2},{4,5},{5,4},{6,7},{7,6},{8,9},{9,8},{10,11... | collective-permute-start | bytes 98312 | tf_op jit(solution)/shard_map/ppermute | solution.py:725
  40.7 8.1 %collective-permute-start.13 = (bf16[768,128]{1,0:T(8,128)(2,1)S(1)}, bf16[768,128]{1,0:T(8,128)(2,1)S(1)}, u32[]{:S(2)}, u32[]{:S(2)}) collective-permute-start(bf16[768,128]{1,0:T(8,128)(2,1)S(1)} %slice.27), channel_id=1, source_target_pairs={{0,1},{1,0},{2,3},{3,2},{4,5},{5,4},{6,7},{7,6},{8,9},{9,8},{10,11... | collective-permute-start | bytes 589832 | tf_op jit(solution)/shard_map/ppermute | solution.py:725
  41.3 7.5 %collective-permute-start.12 = (bf16[768,128]{1,0:T(8,128)(2,1)S(1)}, bf16[768,128]{1,0:T(8,128)(2,1)S(1)}, u32[]{:S(2)}, u32[]{:S(2)}) collective-permute-start(bf16[768,128]{1,0:T(8,128)(2,1)S(1)} %slice.26), channel_id=1, source_target_pairs={{0,2},{1,3},{2,0},{3,1},{4,6},{5,7},{6,4},{7,5},{8,10},{9,11},{10,... | collective-permute-start | bytes 589832 | tf_op jit(solution)/shard_map/ppermute | solution.py:725
  42.5 6.3 %collective-permute-start.16 = (bf16[256,128]{1,0:T(8,128)(2,1)S(1)}, bf16[256,128]{1,0:T(8,128)(2,1)S(1)}, u32[]{:S(2)}, u32[]{:S(2)}) collective-permute-start(bf16[256,128]{1,0:T(8,128)(2,1)S(1)} %get-tuple-element.73), channel_id=1, source_target_pairs={{0,8},{4,12},{8,0},{12,4},{16,24},{20,28},{24,16},{28,20},{1,9},{5... | collective-permute-start | bytes 196616 | tf_op jit(solution)/shard_map/ppermute | solution.py:725
  43.0 7.6 %collective-permute-start.14 = (bf16[256,128]{1,0:T(8,128)(2,1)S(1)}, bf16[256,128]{1,0:T(8,128)(2,1)S(1)}, u32[]{:S(2)}, u32[]{:S(2)}) collective-permute-start(bf16[256,128]{1,0:T(8,128)(2,1)S(1)} %get-tuple-element.71), channel_id=1, source_target_pairs={{0,16},{4,20},{8,24},{12,28},{16,0},{20,4},{24,8},{28,12},{1,17},{... | collective-permute-start | bytes 196616 | tf_op jit(solution)/shard_map/ppermute | solution.py:725
  45.7 6.1 %collective-permute-start.15 = (bf16[256,128]{1,0:T(8,128)(2,1)S(1)}, bf16[256,128]{1,0:T(8,128)(2,1)S(1)}, u32[]{:S(2)}, u32[]{:S(2)}) collective-permute-start(bf16[256,128]{1,0:T(8,128)(2,1)S(1)} %get-tuple-element.72), channel_id=1, source_target_pairs={{0,24},{4,28},{8,16},{12,20},{16,8},{20,12},{24,0},{28,4},{1,25},{... | collective-permute-start | bytes 196616 | tf_op jit(solution)/shard_map/ppermute | solution.py:725
  55.2 1.5 %collective-permute-start.17 = (bf16[53,16,128]{2,1,0:T(8,128)(2,1)S(1)}, bf16[53,16,128]{2,1,0:T(8,128)(2,1)S(1)}, u32[]{:S(2)}, u32[]{:S(2)}) collective-permute-start(bf16[53,16,128]{2,1,0:T(8,128)(2,1)S(1)} %get-tuple-element.82), channel_id=1, source_target_pairs={{0,4},{4,0},{8,12},{12,8},{16,20},{20,16},{24,28},{28,24},{1,5},{5... | collective-permute-start | bytes 651272 | tf_op jit(solution)/shard_map/ppermute | solution.py:725
  57.4 11.6 %collective-permute-start.19 = (bf16[52,16,128]{2,1,0:T(8,128)(2,1)S(1)}, bf16[52,16,128]{2,1,0:T(8,128)(2,1)S(1)}, u32[]{:S(2)}, u32[]{:S(2)}) collective-permute-start(bf16[52,16,128]{2,1,0:T(8,128)(2,1)S(1)} %get-tuple-element.86.refs_0_), channel_id=1, source_target_pairs={{0,16},{4,20},{8,24},{12,28},{16,0},{20,4},{24,8},{28,12},{1,17},{... | collective-permute-start | bytes 638984 | tf_op jit(solution)/shard_map/ppermute | solution.py:725
  57.8 11.6 %collective-permute-start.18 = (bf16[52,16,128]{2,1,0:T(8,128)(2,1)S(1)}, bf16[52,16,128]{2,1,0:T(8,128)(2,1)S(1)}, u32[]{:S(2)}, u32[]{:S(2)}) collective-permute-start(bf16[52,16,128]{2,1,0:T(8,128)(2,1)S(1)} %get-tuple-element.86.refs_0_), channel_id=1, source_target_pairs={{0,8},{4,12},{8,0},{12,4},{16,24},{20,28},{24,16},{28,20},{1,9},{5... | collective-permute-start | bytes 638984 | tf_op jit(solution)/shard_map/ppermute | solution.py:725
  59.4 13.3 %collective-permute-start.21 = (bf16[52,16,128]{2,1,0:T(8,128)(2,1)S(1)}, bf16[52,16,128]{2,1,0:T(8,128)(2,1)S(1)}, u32[]{:S(2)}, u32[]{:S(2)}) collective-permute-start(bf16[52,16,128]{2,1,0:T(8,128)(2,1)S(1)} %get-tuple-element.86.refs_0_), channel_id=1, source_target_pairs={{0,4},{4,0},{8,12},{12,8},{16,20},{20,16},{24,28},{28,24},{1,5},{5... | collective-permute-start | bytes 638984 | tf_op jit(solution)/shard_map/ppermute | solution.py:725
  69.4 3.3 %collective-permute-start.22 = (bf16[52,16,128]{2,1,0:T(8,128)(2,1)S(1)}, bf16[52,16,128]{2,1,0:T(8,128)(2,1)S(1)}, u32[]{:S(2)}, u32[]{:S(2)}) collective-permute-start(bf16[52,16,128]{2,1,0:T(8,128)(2,1)S(1)} %collective-permute-done.18.refs_2_), channel_id=1, source_target_pairs={{0,4},{4,0},{8,12},{12,8},{16,20},{20,16},{24,28},{28,24},{1,5},{5... | collective-permute-start | bytes 638984 | tf_op jit(solution)/shard_map/ppermute | solution.py:725
  69.4 3.3 %collective-permute-start.23 = (bf16[52,16,128]{2,1,0:T(8,128)(2,1)S(1)}, bf16[52,16,128]{2,1,0:T(8,128)(2,1)S(1)}, u32[]{:S(2)}, u32[]{:S(2)}) collective-permute-start(bf16[52,16,128]{2,1,0:T(8,128)(2,1)S(1)} %collective-permute-done.19.refs_4_), channel_id=1, source_target_pairs={{0,4},{4,0},{8,12},{12,8},{16,20},{20,16},{24,28},{28,24},{1,5},{5... | collective-permute-start | bytes 638984 | tf_op jit(solution)/shard_map/ppermute | solution.py:725
  69.9 7.2 %collective-permute-start.20 = (bf16[36,16,128]{2,1,0:T(8,128)(2,1)S(1)}, bf16[36,16,128]{2,1,0:T(8,128)(2,1)S(1)}, u32[]{:S(2)}, u32[]{:S(2)}) collective-permute-start(bf16[36,16,128]{2,1,0:T(8,128)(2,1)S(1)} %slice.28), channel_id=1, source_target_pairs={{0,8},{4,12},{8,0},{12,4},{16,24},{20,28},{24,16},{28,20},{1,9},{5... | collective-permute-start | bytes 442376 | tf_op jit(solution)/shard_map/ppermute | solution.py:725
  70.3 6.8 %collective-permute-start.25 = (bf16[16,16,128]{2,1,0:T(8,128)(2,1)S(1)}, bf16[16,16,128]{2,1,0:T(8,128)(2,1)S(1)}, u32[]{:S(2)}, u32[]{:S(2)}) collective-permute-start(bf16[16,16,128]{2,1,0:T(8,128)(2,1)S(1)} %slice.29), channel_id=1, source_target_pairs={{0,8},{4,12},{8,0},{12,4},{16,24},{20,28},{24,16},{28,20},{1,9},{5... | collective-permute-start | bytes 196616 | tf_op jit(solution)/shard_map/ppermute | solution.py:725
  77.1 1.3 %collective-permute-start.26 = (bf16[16,16,128]{2,1,0:T(8,128)(2,1)S(1)}, bf16[16,16,128]{2,1,0:T(8,128)(2,1)S(1)}, u32[]{:S(2)}, u32[]{:S(2)}) collective-permute-start(bf16[16,16,128]{2,1,0:T(8,128)(2,1)S(1)} %collective-permute-done.25.refs_2_), channel_id=1, source_target_pairs={{0,4},{4,0},{8,12},{12,8},{16,20},{20,16},{24,28},{28,24},{1,5},{5... | collective-permute-start | bytes 196616 | tf_op jit(solution)/shard_map/ppermute | solution.py:725
  77.1 1.5 %collective-permute-start.24 = (bf16[36,16,128]{2,1,0:T(8,128)(2,1)S(1)}, bf16[36,16,128]{2,1,0:T(8,128)(2,1)S(1)}, u32[]{:S(2)}, u32[]{:S(2)}) collective-permute-start(bf16[36,16,128]{2,1,0:T(8,128)(2,1)S(1)} %collective-permute-done.20.refs_0_), channel_id=1, source_target_pairs={{0,4},{4,0},{8,12},{12,8},{16,20},{20,16},{24,28},{28,24},{1,5},{5... | collective-permute-start | bytes 442376 | tf_op jit(solution)/shard_map/ppermute | solution.py:725
